TPU v7x, 32 devices: a whole 2x2x4 slice. The times are simulated.
32 devices in a mesh: ctx: 8 (over z, y), exp: 4 (over x, core).
Axes of the slice: x: 2, y: 2, z: 4, core: 2. Of those that a mesh axis runs over, the one named last changes fastest.
Arguments:
- stream_in: bfloat16 [1024, 6144], P('ctx'), may hold values from -41 to 41
- queries: bfloat16 [1024, 8192], P('ctx', 'exp'), may hold values from -6 to 6
- key_proj: bfloat16 [1024, 8192], P('ctx', 'exp'), may hold values from -0.5390625 to 0.5390625
- values: bfloat16 [1024, 8192], P('ctx', 'exp'), may hold values from -6 to 6
- attn_gate: bfloat16 [1024, 8192], P('ctx', 'exp'), may hold values from -6 to 6
- decay_rates: float32 [64], P('exp'), may hold values from 4.8828125e-05 to 0.05
- attn_gain: float32 [8192], P('exp'), may hold values from 0.25 to 1.75
- out_weight: bfloat16 [8192, 6144], P('exp', 'ctx'), may hold values from -0.0625 to 0.0625
- ffn_gain: float32 [6144], replicated, may hold values from 0.25 to 1.75
- routing: int32 [1024, 2], P('ctx'), may hold values from 0 to 31, as said below
- route_weights: float32 [1024, 2], P('ctx'), may hold values from 0.25 to 1
- w_gate: bfloat16 [4, 6144, 9216], P('exp', None, 'ctx'), may hold values from -0.078125 to 0.078125
- w_up: bfloat16 [4, 6144, 9216], P('exp', None, 'ctx'), may hold values from -0.078125 to 0.078125
- w_down: bfloat16 [4, 9216, 6144], P('exp', 'ctx'), may hold values from -0.0625 to 0.0625
Outputs:
- residual_out: bfloat16 [1024, 6144], P(('ctx', 'exp'))
- expert_out: bfloat16 [8, 4, 8, 6144], P('ctx', 'exp')
Inputs may be any that keep to these rules, and one draw needn't show every extreme that they name: `routing`: the two ids of a row differ and at most one of them is below 4. In each aligned block of 128 rows (one context shard) an id below 4 is named by at most 8 rows; one such id, the same for all blocks, is named by exactly 8 rows in every block.
All inputs are finite; a program needn't handle non-finite values.
Results may differ from a plain program's by a relative error of at most 0.025.
Values may be sent and summed in bfloat16 or wider, within the bound.
No kernel may reach another device: no remote copies, remote signals or barrier semaphores. Data moves between devices by JAX's collectives and lax.ppermute only.
A program may use at most 128 MiB of HBM per device.

v0:
```python
import jax
import jax.numpy as jnp
from jax import lax
from jax.sharding import PartitionSpec as P

HIGHEST = lax.Precision.HIGHEST


def entering(value, axis, join, neutral):
    place = lax.axis_index(axis)
    gathered = jax.tree.map(
        lambda a, kind: lax.all_gather(a.astype(kind), axis), value, (jnp.bfloat16, jnp.bfloat16)
    )
    state = jax.tree.map(lambda a, e: jnp.zeros_like(a) + jnp.asarray(e, a.dtype), value, neutral)

    def one(step, state):
        return join(
            state,
            jax.tree.map(
                lambda a, own: lax.dynamic_index_in_dim(a, step, 0, False).astype(own.dtype),
                gathered,
                value,
            ),
        )

    return lax.fori_loop(0, place, one, state)


def normalize_rows(row_block, ffn_gain):
    wide_rows = row_block.astype(jnp.float32)
    inverse = lax.rsqrt(jnp.mean(wide_rows * wide_rows, axis=1, keepdims=True) + 1e-06)
    return (wide_rows * inverse * ffn_gain[None, :]).astype(jnp.bfloat16)


def prefix_combine(earlier_pair, later_pair):
    return (
        earlier_pair[0] * later_pair[0],
        later_pair[0][:, None, None] * earlier_pair[1] + later_pair[1],
    )


def per_device(
    stream_in,
    queries,
    key_proj,
    values,
    attn_gate,
    decay_rates,
    attn_gain,
    out_weight,
    ffn_gain,
    routing,
    route_weights,
    w_gate,
    w_up,
    w_down,
):
    rows_here, model_width = stream_in.shape
    head_count = decay_rates.shape[0]
    head_size = queries.shape[1] // head_count
    exp_count = lax.axis_size("exp")
    ctx_count = lax.axis_size("ctx")
    own_index = lax.axis_index("exp")
    capacity = rows_here // 16
    own_rows = rows_here // exp_count
    per_block = own_rows + capacity
    query_heads = queries.reshape(rows_here, head_count, head_size)
    key_heads = key_proj.reshape(rows_here, head_count, head_size)
    value_heads = values.reshape(rows_here, head_count, head_size)
    positions = jnp.arange(rows_here, dtype=jnp.float32)
    tail_decay = jnp.exp(-decay_rates[None, :] * (rows_here - 1.0 - positions)[:, None])
    weighted_keys = key_heads.astype(jnp.float32) * tail_decay[:, :, None]
    local_state = jnp.einsum(
        "jhd,jhe->hde", weighted_keys, value_heads.astype(jnp.float32), precision=HIGHEST
    )
    span_decay = jnp.exp(-decay_rates * rows_here)
    identity = (jnp.ones_like(span_decay), jnp.zeros_like(local_state))
    prefix_pair = entering((span_decay, local_state), "ctx", prefix_combine, identity)
    prior_state = prefix_pair[1]
    scores = jnp.einsum("ihd,jhd->hij", query_heads, key_heads, preferred_element_type=jnp.float32)
    distance = positions[:, None] - positions[None, :]
    decay_mask = jnp.where(
        distance[None] >= 0.0,
        jnp.exp(-decay_rates[:, None, None] * jnp.maximum(distance, 0.0)[None]),
        0.0,
    )
    near_weights = (scores * decay_mask).astype(jnp.bfloat16)
    near_part = jnp.einsum(
        "hij,jhd->ihd", near_weights, value_heads, preferred_element_type=jnp.float32
    )
    lead_decay = jnp.exp(-decay_rates[None, :] * (positions + 1.0)[:, None])
    far_part = jnp.einsum(
        "ihd,hde->ihe",
        query_heads.astype(jnp.float32) * lead_decay[:, :, None],
        prior_state,
        precision=HIGHEST,
    )
    attended = near_part + far_part
    inverse = lax.rsqrt(jnp.mean(attended * attended, axis=2, keepdims=True) + 1e-06)
    normed = (attended * inverse).reshape(rows_here, head_count * head_size)
    mixed_heads = (
        normed * attn_gain[None, :] * jax.nn.sigmoid(attn_gate.astype(jnp.float32))
    ).astype(jnp.bfloat16)
    held_ids = jnp.arange(exp_count, dtype=jnp.int32)
    hit_mask = routing[:, :, None] == held_ids[None, None, :]
    member = jnp.sum(hit_mask.astype(jnp.int32), axis=1)
    gate_of = jnp.sum(jnp.where(hit_mask, route_weights[:, :, None], 0.0), axis=1)
    slot_rank = jnp.cumsum(member, axis=0) - 1
    slot_index = jnp.arange(capacity, dtype=jnp.int32)
    pick_mask = (member[:, :, None] == 1) & (slot_rank[:, :, None] == slot_index[None, None, :])
    selector = pick_mask.reshape(rows_here, exp_count * capacity).T.astype(jnp.bfloat16)
    slot_weight = jnp.sum(jnp.where(pick_mask, gate_of[:, :, None], 0.0), axis=0)
    slot_mixed = jnp.dot(selector, mixed_heads, preferred_element_type=jnp.float32).astype(
        jnp.bfloat16
    )
    row_blocks = jnp.concatenate(
        [mixed_heads.reshape(exp_count, own_rows, -1), slot_mixed.reshape(exp_count, capacity, -1)],
        axis=1,
    )
    stacked = row_blocks.reshape(exp_count * per_block, head_count * head_size)
    partial_cols = jnp.dot(
        lax.all_gather(stacked, "ctx", axis=0, tiled=True),
        out_weight,
        preferred_element_type=jnp.float32,
    )
    partial_term = partial_cols.reshape(ctx_count, exp_count, per_block, out_weight.shape[1])
    summed = lax.psum_scatter(
        partial_term.astype(jnp.bfloat16), "exp", scatter_dimension=1, tiled=True
    ).astype(jnp.float32)
    swapped = lax.all_to_all(
        summed.astype(jnp.bfloat16), "ctx", split_axis=0, concat_axis=3, tiled=True
    ).astype(summed.dtype)
    projected = swapped.reshape(per_block, model_width)
    stream_own = lax.dynamic_slice_in_dim(stream_in, own_index * own_rows, own_rows, 0)
    own_selector = lax.dynamic_slice_in_dim(selector, own_index * capacity, capacity, 0)
    stream_slots = jnp.dot(own_selector, stream_in, preferred_element_type=jnp.float32)
    residual_rows = jnp.concatenate([stream_own.astype(jnp.float32), stream_slots], axis=0)
    hidden_rows = (residual_rows + projected).astype(jnp.bfloat16)
    residual_out = hidden_rows[:own_rows]
    slot_hidden = hidden_rows[own_rows:]
    outgoing = normalize_rows(slot_hidden, ffn_gain)
    normed_rows = lax.all_gather(outgoing, "ctx", axis=0, tiled=True)
    gate_part = jnp.dot(normed_rows, w_gate[0], preferred_element_type=jnp.float32)
    up_part = jnp.dot(normed_rows, w_up[0], preferred_element_type=jnp.float32)
    activated = (jax.nn.silu(gate_part) * up_part).astype(jnp.bfloat16)
    summed_down = lax.psum_scatter(
        jnp.dot(activated, w_down[0], preferred_element_type=jnp.float32).astype(jnp.bfloat16),
        "ctx",
        scatter_dimension=0,
        tiled=True,
    ).astype(jnp.float32)
    own_weight = lax.dynamic_index_in_dim(slot_weight, own_index, 0, keepdims=False)
    expert_out = (
        (summed_down * own_weight[:, None])
        .astype(jnp.bfloat16)
        .reshape(1, 1, capacity, model_width)
    )
    return (residual_out, expert_out)


def solution(mesh):
    return jax.shard_map(
        per_device,
        mesh=mesh,
        in_specs=(
            P("ctx", None),
            P("ctx", "exp"),
            P("ctx", "exp"),
            P("ctx", "exp"),
            P("ctx", "exp"),
            P("exp"),
            P("exp"),
            P("exp", "ctx"),
            P(),
            P("ctx", None),
            P("ctx", None),
            P("exp", None, "ctx"),
            P("exp", None, "ctx"),
            P("exp", "ctx", None),
        ),
        out_specs=(P(("ctx", "exp"), None), P("ctx", "exp", None, None)),
        check_vma=False,
    )
```

profile of v0, /device:TPU:0, one launch (start us, length us, event | category | flops | bytes accessed | tf_op | source)
XLA Modules:
  0.0 408.1 jit_solution(7213953065315055861)
XLA Ops:
  7.2 0.0 copy-start
  7.2 0.0 all-gather.7.cloned.1.call-start
  7.2 0.8 exponential_convert_fusion
  8.1 2.1 copy.75
  10.2 0.1 multiply_exponential_fusion
  10.3 2.7 convolution_convert_fusion.2
  13.0 0.0 all-gather.7.cloned.1.call-update
  13.0 0.0 all-gather.5.cloned.1.call-start
  13.0 1.2 dynamic-slice.4
  14.9 0.2 dynamic-update-slice
  15.2 23.5 %all-reduce = bf16[128]{0:T(256)(128)(2,1)S(1)} all-reduce(bf16[128]{0:T(256)(128)(2,1)S(1)} %dynamic-update-slice), channel_id=2, replica_groups=mesh['ctx'=8,'exp'=4] {'ctx'}, use_global_device_ids=true, to_apply=%add | all-reduce | flops 128 | bytes 512
  38.7 0.1 reshape.185
  38.8 0.7 convert_reduce_fusion
  39.5 0.1 copy.61
  39.6 0.2 reduce_window_sum.11
  39.8 0.1 copy.62
  39.8 0.1 eq.56
  39.9 0.1 fusion.55
  40.0 3.0 convolution_bitcast_fusion.1
  43.1 46.4 %all-gather.7.cloned.1.call-done = bf16[128,128,128]{2,1,0:T(8,128)(2,1)} async-done(((bf16[16,128,128]{2,1,0:T(8,128)(2,1)}), bf16[128,128,128]{2,1,0:T(8,128)(2,1)}) %all-gather.7.cloned.1.call-update) | async-done | bytes 4194320 | tf_op jit(solution)/shard_map/all_gather | solution.py:12
  89.5 1.1 broadcast_in_dim.35
  90.6 4.0 multiply_reduce_fusion
  94.6 1.1 broadcast_multiply_fusion
  95.6 2.6 copy.70
  98.2 0.0 copy-done.6
  98.2 1.7 multiply_convert_fusion
  99.9 0.2 fusion.15
  100.1 0.9 pad_maximum_fusion
  101.1 0.0 all-gather.5.cloned.1.call-update
  101.1 0.0 copy-start.9
  101.1 0.0 all-reduce.4.cloned.1.call-start
  101.1 102.3 %all-gather.5.cloned.1.call-done = bf16[1280,2048]{1,0:T(8,128)(2,1)} async-done(((bf16[160,2048]{1,0:T(8,128)(2,1)}), bf16[1280,2048]{1,0:T(8,128)(2,1)}) %all-gather.5.cloned.1.call-update) | async-done | bytes 5242896 | tf_op jit(solution)/shard_map/all_gather | solution.py:122
  203.5 0.0 copy-done
  203.5 8.0 %convolution_convert_fusion = bf16[1280,768]{1,0:T(8,128)(2,1)} fusion(bf16[1280,2048]{1,0:T(8,128)(2,1)} %all-gather.5.cloned.1.call-done, bf16[2048,768]{1,0:T(8,128)(2,1)S(1)} %copy-done), kind=kOutput, calls=%fused_computation.9 | convolution fusion | flops 4027514880 | bytes 10354688 | tf_op jit(solution)/shard_map/dot_general | solution.py:121
  211.5 0.0 all-reduce.4.cloned.1.call-update
  211.5 0.0 copy-done.9
  211.6 0.6 dynamic-slice.5
  212.1 0.1 fusion.57
  212.2 46.9 %all-reduce.4.cloned.1.call-done = bf16[8,4,40,768]{3,2,1,0:T(8,128)(2,1)} async-done(((bf16[8,4,40,768]{3,2,1,0:T(8,128)(2,1)}), bf16[8,4,40,768]{3,2,1,0:T(8,128)(2,1)}) %all-reduce.4.cloned.1.call-update) | async-done | bytes 1966096
  259.1 2.5 constant_dynamic-slice_fusion.1
  261.6 5.5 %all-to-all-start = ((bf16[8,1,40,768]{3,2,1,0:T(8,128)(2,1)}), bf16[8,1,40,768]{3,2,1,0:T(8,128)(2,1)}, u32[]{:S(2)}, u32[]{:S(2)}) async-start(bf16[8,1,40,768]{3,2,1,0:T(8,128)(2,1)} %constant_dynamic-slice_fusion.1), calls=%async_computation | async-start | bytes 983040 | tf_op jit(solution)/shard_map/all_to_all | solution.py:130
  267.1 0.0 reduce-scatter.3.cloned.1.call-start
  267.2 0.0 copy-done.3
  267.2 0.3 fusion.58
  267.5 0.1 dynamic-slice_convert_fusion
  267.6 13.4 %all-to-all-done = bf16[8,1,40,768]{3,2,1,0:T(8,128)(2,1)} async-done(((bf16[8,1,40,768]{3,2,1,0:T(8,128)(2,1)}), bf16[8,1,40,768]{3,2,1,0:T(8,128)(2,1)}, u32[]{:S(2)}, u32[]{:S(2)}) %all-to-all-start) | async-done | bytes 491552 | tf_op jit(solution)/shard_map/all_to_all | solution.py:130
  281.0 1.1 fusion.65
  282.1 0.1 copy.78
  282.2 0.1 fusion.25
  282.3 0.2 fusion.49
  282.4 0.6 copy-done.4
  283.1 0.1 fusion.51
  283.1 32.6 %all_gather.23 = bf16[64,6144]{1,0:T(8,128)(2,1)S(1)} all-gather(bf16[8,6144]{1,0:T(8,128)(2,1)S(1)} %fusion.51), channel_id=1, replica_groups=mesh['ctx'=8,'exp'=4] {'ctx'}, dimensions={0}, use_global_device_ids=true | all-gather | bytes 884736 | tf_op jit(solution)/shard_map/all_gather | solution.py:142
  315.8 0.9 copy-done.2
  316.7 7.5 %fusion.4 = f32[64,1152]{1,0:T(8,128)S(1)} fusion(bf16[64,6144]{1,0:T(8,128)(2,1)S(1)} %all_gather.23, bf16[1,6144,1152]{2,1,0:T(8,128)(2,1)} %param.27), kind=kOutput, calls=%fused_computation.6 | convolution fusion | flops 905969664 | bytes 15237120 | tf_op jit(solution)/shard_map/dot_general | solution.py:143
  324.1 0.0 copy-start.7
  324.2 0.0 copy-start.8
  324.2 0.0 copy-start.1
  324.2 15.3 %fusion.6 = bf16[64,6144]{1,0:T(8,128)(2,1)} fusion(bf16[1,1152,6144]{2,1,0:T(8,128)(2,1)} %param.29, bf16[64,6144]{1,0:T(8,128)(2,1)} %copy-done.2, bf16[1,6144,1152]{2,1,0:T(8,128)(2,1)} %param.28, f32[64,1152]{1,0:T(8,128)S(1)} %fusion.4), kind=kOutput, calls=%fused_computation.8 | convolution fusion | flops 1812774912 | bytes 30179328 | tf_op jit(solution)/shard_map/dot_general | solution.py:147
  339.4 0.0 reduce-scatter.3.cloned.1.call-update
  339.5 0.1 select_reduce_fusion
  339.6 1.8 slice.8
  341.4 58.6 %reduce-scatter.3.cloned.1.call-done = bf16[8,6144]{1,0:T(8,128)(2,1)} async-done(((bf16[64,6144]{1,0:T(8,128)(2,1)}), bf16[8,6144]{1,0:T(8,128)(2,1)}) %reduce-scatter.3.cloned.1.call-update) | async-done | bytes 98320 | tf_op jit(solution)/shard_map/reduce_scatter | solution.py:146
  400.0 1.6 fusion.53
  (20 shorter events, 0.1 us)
Async XLA Ops:
  7.2 196.3 %copy-start = (bf16[2048,768]{1,0:T(8,128)(2,1)S(1)}, bf16[2048,768]{1,0:T(8,128)(2,1)}, u32[]{:S(2)}) copy-start(bf16[2048,768]{1,0:T(8,128)(2,1)} %param.23) | copy-start | bytes 9437188
  7.2 82.3 %all-gather.7.cloned.1.call-start = ((), (), s32[]{:S(2)}) async-start(), calls=%async_computation.4 | async-start | bytes 4718592 | tf_op jit(solution)/shard_map/all_gather | solution.py:12
  13.0 190.5 %all-gather.5.cloned.1.call-start = ((), (), s32[]{:S(2)}) async-start(), calls=%async_computation.2 | async-start | bytes 5898240 | tf_op jit(solution)/shard_map/all_gather | solution.py:122
  90.6 7.6 %copy-start.6 = (f32[2048]{0:T(1024)S(1)}, f32[2048]{0:T(1024)}, u32[]{:S(2)}) copy-start(f32[2048]{0:T(1024)} %param.22) | copy-start | bytes 24580
  101.1 110.5 %copy-start.9 = (u32[32]{0:T(128)S(1)}, u32[32]{0:T(128)}, u32[]{:S(2)}) copy-start(u32[32]{0:T(128)} %constant.80) | copy-start | bytes 388
  101.1 158.0 %all-reduce.4.cloned.1.call-start = ((), (), s32[]{:S(2)}) async-start(), calls=%async_computation.5 | async-start | bytes 3932160
  211.5 55.7 %copy-start.3 = (bf16[128,6144]{1,0:T(8,128)(2,1)S(1)}, bf16[128,6144]{1,0:T(8,128)(2,1)}, u32[]{:S(2)}) copy-start(bf16[128,6144]{1,0:T(8,128)(2,1)} %param.16) | copy-start | bytes 4718596
  261.6 19.3 %all-to-all-start = ((bf16[8,1,40,768]{3,2,1,0:T(8,128)(2,1)}), bf16[8,1,40,768]{3,2,1,0:T(8,128)(2,1)}, u32[]{:S(2)}, u32[]{:S(2)}) async-start(bf16[8,1,40,768]{3,2,1,0:T(8,128)(2,1)} %constant_dynamic-slice_fusion.1), calls=%async_computation | async-start | bytes 983040 | tf_op jit(solution)/shard_map/all_to_all | solution.py:130
  267.1 15.9 %copy-start.5 = (f32[6144]{0:T(1024)S(1)}, f32[6144]{0:T(1024)}, u32[]{:S(2)}) copy-start(f32[6144]{0:T(1024)} %param.24) | copy-start | bytes 73732
  267.1 132.8 %reduce-scatter.3.cloned.1.call-start = ((), (), s32[]{:S(2)}) async-start(), calls=%async_computation.3 | async-start | bytes 884736 | tf_op jit(solution)/shard_map/reduce_scatter | solution.py:146
  282.3 0.8 copy-start.4
  315.8 0.9 copy-start.2
  324.1 15.3 %copy-start.7 = (s32[128,2]{0,1:T(2,128)S(1)}, s32[128,2]{0,1:T(2,128)}, u32[]{:S(2)}) copy-start(s32[128,2]{0,1:T(2,128)} %param.25) | copy-start | bytes 3076
  324.2 15.3 %copy-start.8 = (f32[128,2]{0,1:T(2,128)S(1)}, f32[128,2]{0,1:T(2,128)}, u32[]{:S(2)}) copy-start(f32[128,2]{0,1:T(2,128)} %param.26) | copy-start | bytes 3076
  324.2 77.4 %copy-start.1 = (bf16[2048,768]{1,0:T(8,128)(2,1)S(1)}, bf16[2048,768]{1,0:T(8,128)(2,1)}, u32[]{:S(2)}) copy-start(bf16[2048,768]{1,0:T(8,128)(2,1)} %param.23) | copy-start | bytes 9437188
Sparse Core Ops, SparseCore 0:
  13.1 76.3 all-gather.6
  101.2 102.2 all-gather.4
  211.7 47.4 all-reduce.3
  339.6 60.3 reduce-scatter.2
where the time goes:
time: 409 us; the launch traced here: 408 us
  waiting for transfers between devices  268 us (66%)
  blocking collectives  56.1 us (14%)
  matrix products  41 us (10%)
  between operations  14.6 us (4%)
  local copies, waits for them, and re-layouts  14.2 us (3%)
  other arithmetic  8.82 us (2%)
  starting transfers between devices  5.68 us (1%)
    all_gather x1, waiting for transfers between devices, per_device(): lax.all_gather(stacked, 'ctx', axis=0, tiled=True)  102 us
    reduce_scatter x1, waiting for transfers between devices, per_device(): lax.psum_scatter(jnp.dot(activated, w_down[0], preferred_element_type=jnp...  58.6 us
    unnamed x5, waiting for transfers between devices  47 us
    all_gather x1, waiting for transfers between devices, entering(): lax.all_gather(a.astype(kind), axis)  46.4 us
    all_gather x1, blocking collectives, per_device(): normed_rows = lax.all_gather(outgoing, 'ctx', axis=0, tiled=True)  32.6 us
    unnamed x1, blocking collectives  23.5 us
    dot_general x1, matrix products, per_device(): jnp.dot(activated, w_down[0], preferred_element_type=jnp.float32)  15.3 us
    all_to_all x1, waiting for transfers between devices, per_device(): lax.all_to_all(summed.astype(jnp.bfloat16), 'ctx', split_axis=0, concat_a...  13.4 us
  transfers between devices with their start and end apart: 5, of which 5 were waited for; matrix products, arithmetic and copies ran while one was open for 2% of the time, Pallas kernels for 0%

commit v1 on v0

v1 whole, which is shorter than its diff:
```python
import functools

import jax
import jax.numpy as jnp
from jax import lax
from jax.experimental import pallas as pl
from jax.experimental.pallas import tpu as pltpu
from jax.sharding import PartitionSpec as P

CHUNKS = 2
F32 = jnp.float32
BF16 = jnp.bfloat16
VMEM = pl.BlockSpec(memory_space=pltpu.VMEM)
SMEM = pl.BlockSpec(memory_space=pltpu.SMEM)


def rows_iota(shape):
    return lax.broadcasted_iota(jnp.int32, shape, 0).astype(F32)


def cols_iota(shape):
    return lax.broadcasted_iota(jnp.int32, shape, 1).astype(F32)


def lanes(head, size):
    return pl.ds(pl.multiple_of(head * size, size), size)


def state_kernel(per_half, place_ref, decay_ref, k_ref, v_ref, *outs):
    pair = place_ref[0]
    tok, size = k_ref.shape[0], outs[0].shape[1]
    back = (tok - 1.0) - rows_iota((tok, size))
    for chunk in range(CHUNKS):
        for which in range(2):
            out = outs[chunk * 2 + which]
            half = pair if which == 0 else 1 - pair
            for l in range(per_half):
                head = chunk * 2 * per_half + half * per_half + l
                k = k_ref[:, lanes(head, size)].astype(F32)
                k = (k * jnp.exp(-decay_ref[head] * back)).astype(BF16)
                state = lax.dot_general(
                    k,
                    v_ref[:, lanes(head, size)],
                    (((0,), (0,)), ((), ())),
                    preferred_element_type=F32,
                )
                out[l * size : (l + 1) * size, :] = state.astype(BF16)


def near_kernel(heads, decay_ref, q_ref, k_ref, v_ref, near_ref):
    tok = q_ref.shape[0]
    size = q_ref.shape[1] // heads
    gap = rows_iota((tok, tok)) - cols_iota((tok, tok))
    for head in range(heads):
        at = slice(head * size, (head + 1) * size)
        scores = lax.dot_general(
            q_ref[:, at], k_ref[:, at], (((1,), (1,)), ((), ())), preferred_element_type=F32
        )
        mask = jnp.where(gap >= 0.0, jnp.exp(-decay_ref[head] * jnp.maximum(gap, 0.0)), 0.0)
        weights = (scores * mask).astype(BF16)
        near_ref[:, at] = jnp.dot(weights, v_ref[:, at], preferred_element_type=F32)


def mix_kernel(
    chunk, per_half, own_rows, place_ref, decay_ref, q_ref, near_ref, gate_ref, gain_ref, mine_ref, other_ref, out_ref
):
    pair, own = place_ref[0], place_ref[1]
    size = mine_ref.shape[1]
    tok = q_ref.shape[0]
    ahead = rows_iota((tok, size)) + 1.0
    for which in range(2):
        prior = mine_ref if which == 0 else other_ref
        half = pair if which == 0 else 1 - pair
        for l in range(per_half):
            local = half * per_half + l
            head = chunk * 2 * per_half + local
            at = lanes(head, size)
            far = jnp.dot(
                q_ref[:, at], prior[l * size : (l + 1) * size, :], preferred_element_type=F32
            )
            attended = near_ref[:, at] + far * jnp.exp(-decay_ref[head] * ahead)
            inverse = lax.rsqrt(jnp.mean(attended * attended, axis=1, keepdims=True) + 1e-06)
            gate = jax.nn.sigmoid(gate_ref[:, at].astype(F32))
            mixed = (attended * inverse * gain_ref[:, at] * gate).astype(BF16)
            for block in range(tok // own_rows):
                to = pl.multiple_of((block ^ own) * own_rows, own_rows)
                out_ref[pl.ds(to, own_rows), lanes(local, size)] = mixed[
                    block * own_rows : (block + 1) * own_rows
                ]


def per_device(
    stream_in,
    queries,
    key_proj,
    values,
    attn_gate,
    decay_rates,
    attn_gain,
    out_weight,
    ffn_gain,
    routing,
    route_weights,
    w_gate,
    w_up,
    w_down,
):
    tok, width = stream_in.shape
    heads = decay_rates.shape[0]
    size = queries.shape[1] // heads
    n_exp, n_ctx = lax.axis_size("exp"), lax.axis_size("ctx")
    own, place = lax.axis_index("exp"), lax.axis_index("ctx")
    groups = n_ctx // 2
    group, pair = place // 2, place % 2
    cap = tok // 16
    own_rows = tok // n_exp
    cols = out_weight.shape[1]
    per_half = heads // (2 * CHUNKS)
    swap = [(i, i ^ 1) for i in range(n_ctx)]
    line = [(i, i + 2) for i in range(n_ctx - 2)]
    ring = [(i, (i + 2) % n_ctx) for i in range(n_ctx)]
    here = jnp.stack([pair, own]).astype(jnp.int32)

    hit = routing[:, :, None] == jnp.arange(n_exp, dtype=jnp.int32)
    member = jnp.any(hit, axis=1)
    gate_of = jnp.sum(jnp.where(hit, route_weights[:, :, None], 0.0), axis=1)
    position = jnp.arange(tok, dtype=jnp.int32)
    before = (position[:, None] > position[None, :]).astype(BF16)
    rank = jnp.dot(before, member.astype(BF16), preferred_element_type=F32)
    pick = member[:, :, None] & (rank[:, :, None] == jnp.arange(cap, dtype=F32))
    number = jnp.sum(jnp.where(pick, (position + 1).astype(F32)[:, None, None], 0.0), axis=0)
    own_pick = lax.dynamic_index_in_dim(pick, own, 1, keepdims=False)
    own_weight = jnp.sum(
        jnp.where(own_pick, lax.dynamic_index_in_dim(gate_of, own, 1), 0.0), axis=0
    )
    stream_slots = lax.dot_general(
        own_pick.astype(BF16), stream_in, (((0,), (0,)), ((), ())), preferred_element_type=F32
    ).astype(BF16)

    states = pl.pallas_call(
        functools.partial(state_kernel, per_half),
        out_shape=[jax.ShapeDtypeStruct((per_half * size, size), BF16)] * (2 * CHUNKS),
        in_specs=[SMEM, SMEM, VMEM, VMEM],
        out_specs=[VMEM] * (2 * CHUNKS),
        name="shard_state",
    )(here, decay_rates, key_proj, values)
    near = pl.pallas_call(
        functools.partial(near_kernel, heads),
        out_shape=jax.ShapeDtypeStruct((tok, heads * size), F32),
        in_specs=[SMEM, VMEM, VMEM, VMEM],
        out_specs=VMEM,
        name="near_part",
    )(decay_rates, queries, key_proj, values)

    mixed = []
    for chunk in range(CHUNKS):
        keep, send = states[2 * chunk], states[2 * chunk + 1]
        first = chunk * 2 * per_half + pair * per_half
        rate = lax.dynamic_slice_in_dim(decay_rates, first, per_half, 0)
        rate = jnp.repeat(rate, size)[:, None]
        got = lax.ppermute(send, "ctx", swap)
        lower = jnp.where(pair == 0, keep, got).astype(F32)
        upper = jnp.where(pair == 0, got, keep).astype(F32)
        span = jnp.exp(-rate * tok)
        passing = (span * lower + upper).astype(BF16)
        prior = jnp.zeros(passing.shape, F32)
        for step in range(groups - 1):
            passing = lax.ppermute(passing, "ctx", line)
            prior = prior + jnp.exp(-rate * (2 * tok * step)) * passing.astype(F32)
        after = span * prior + lower
        mine = jnp.where(pair == 0, prior, after).astype(BF16)
        theirs = jnp.where(pair == 0, after, prior).astype(BF16)
        other = lax.ppermute(theirs, "ctx", swap)
        mixed.append(
            pl.pallas_call(
                functools.partial(mix_kernel, chunk, per_half, own_rows),
                out_shape=jax.ShapeDtypeStruct((tok, 2 * per_half * size), BF16),
                in_specs=[SMEM, SMEM, VMEM, VMEM, VMEM, VMEM, VMEM, VMEM],
                out_specs=VMEM,
                name="mix_heads",
            )(here, decay_rates, queries, near, attn_gate, attn_gain[None, :], mine, other)
        )

    parcel = stream_slots.reshape(cap, n_ctx, cols).transpose(1, 0, 2)
    label = jnp.pad(number.reshape(1, n_exp * cap), ((0, cap - 1), (0, cols - n_exp * cap)))
    label = jnp.broadcast_to(label.astype(BF16)[None], (n_ctx, cap, cols))
    arrived = lax.all_to_all(
        jnp.concatenate([parcel, label], axis=1), "ctx", split_axis=0, concat_axis=0, tiled=True
    )
    stream_rows = arrived[:, :cap].reshape(n_ctx * cap, cols)
    token = arrived[:, cap, : n_exp * cap].astype(jnp.int32).reshape(n_ctx, n_exp, cap) - 1
    shard = jnp.arange(n_ctx, dtype=jnp.int32)
    block = ((group - shard // 2) % groups) * 2 + (pair ^ (shard % 2))
    token = jnp.stack(
        [lax.dynamic_index_in_dim(token, own ^ j, 1, keepdims=False) for j in range(n_exp)]
    )
    column = block[None, :, None] * tok + ((token // own_rows) ^ own) * own_rows + token % own_rows
    column = jnp.where(token >= 0, column, -1).reshape(-1)
    chosen = (column[:, None] == jnp.arange(n_ctx * tok, dtype=jnp.int32)[None, :]).astype(BF16)

    wide = 2 * per_half * size
    totals = [None] * n_ctx
    for chunk in range(CHUNKS):
        weight = out_weight[chunk * wide : (chunk + 1) * wide]
        current = mixed[chunk]
        for step in range(groups):
            for y, rows in enumerate((current, lax.ppermute(current, "ctx", swap))):
                at = 2 * step + y
                part = jnp.dot(rows, weight, preferred_element_type=F32)
                totals[at] = part if totals[at] is None else totals[at] + part
            if step + 1 < groups:
                current = lax.ppermute(current, "ctx", ring)
    partial = jnp.concatenate([t.astype(BF16) for t in totals], axis=0)

    def add_groups(parts):
        bit = 1
        parts = list(parts)
        while bit < n_exp:
            far = [j for j in range(0, n_exp, bit) if j & bit]
            sent = jnp.stack([parts[j // bit] for j in far])
            got = lax.ppermute(sent, "exp", [(i, i ^ bit) for i in range(n_exp)])
            parts = [
                parts[j // bit - 1].astype(F32) + got[n].astype(F32) for n, j in enumerate(far)
            ]
            bit *= 2
            if bit < n_exp:
                parts = [p.astype(BF16) for p in parts]
        return parts[0]

    slot_rows = jnp.dot(chosen, partial, preferred_element_type=F32).astype(BF16)
    slot_total = add_groups(slot_rows.reshape(n_exp, n_ctx * cap, cols))
    hidden = (slot_total + stream_rows.astype(F32)).astype(BF16)

    def absolute(blocks):
        stacked = jnp.stack(blocks)
        return jnp.take(stacked, block, axis=0)

    pieces = []
    current = hidden
    for step in range(groups):
        pieces += [current, lax.ppermute(current, "ctx", swap)]
        if step + 1 < groups:
            current = lax.ppermute(current, "ctx", ring)
    slot_hidden = absolute(pieces).transpose(1, 0, 2).reshape(n_ctx * cap, width).astype(F32)
    inverse = lax.rsqrt(jnp.mean(slot_hidden * slot_hidden, axis=1, keepdims=True) + 1e-06)
    slot_inputs = (slot_hidden * inverse * ffn_gain[None, :]).astype(BF16)

    gate_part = jnp.dot(slot_inputs, w_gate[0], preferred_element_type=F32)
    up_part = jnp.dot(slot_inputs, w_up[0], preferred_element_type=F32)
    activated = (jax.nn.silu(gate_part) * up_part).astype(BF16)
    down = jnp.dot(activated, w_down[0], preferred_element_type=F32).astype(BF16)
    parts = lax.all_to_all(
        down.reshape(n_ctx, cap, width), "ctx", split_axis=0, concat_axis=0, tiled=True
    )
    summed = jnp.sum(parts.astype(F32), axis=0)
    expert_out = (summed * own_weight[:, None]).astype(BF16).reshape(1, 1, cap, width)

    bulk = partial.reshape(n_ctx, n_exp, own_rows, cols)
    bulk = add_groups([bulk[:, j] for j in range(n_exp)]).astype(BF16)
    back = []
    for step in range(groups):
        for y in range(2):
            piece = bulk[2 * step + y]
            if step or y:
                to = [(i, ((i // 2 - step) % groups) * 2 + ((i % 2) ^ y)) for i in range(n_ctx)]
                piece = lax.ppermute(piece, "ctx", to)
            back.append(piece)
    order = ((shard // 2 - group) % groups) * 2 + (pair ^ (shard % 2))
    projected = jnp.take(jnp.stack(back), order, axis=0).transpose(1, 0, 2).reshape(own_rows, width)
    stream_own = lax.dynamic_slice_in_dim(stream_in, own * own_rows, own_rows, 0)
    residual_out = (stream_own.astype(F32) + projected.astype(F32)).astype(BF16)
    return (residual_out, expert_out)


def solution(mesh):
    return jax.shard_map(
        per_device,
        mesh=mesh,
        in_specs=(
            P("ctx", None),
            P("ctx", "exp"),
            P("ctx", "exp"),
            P("ctx", "exp"),
            P("ctx", "exp"),
            P("exp"),
            P("exp"),
            P("exp", "ctx"),
            P(),
            P("ctx", None),
            P("ctx", None),
            P("exp", None, "ctx"),
            P("exp", None, "ctx"),
            P("exp", "ctx", None),
        ),
        out_specs=(P(("ctx", "exp"), None), P("ctx", "exp", None, None)),
        check_vma=False,
    )
```

time: 409 us -> 196 us (0.48)
  waiting for transfers between devices: 268 us -> 46.7 us
  starting transfers between devices: 5.68 us -> 85 us
  blocking collectives: 56.1 us -> 0 us
  between operations: 14.6 us -> 1.42 us
  Pallas kernels: 0 us -> 12.8 us
  local copies, waits for them, and re-layouts: 14.2 us -> 3.83 us
  matrix products: 41 us -> 34 us
    all_gather x2 -> x0, waiting for transfers between devices: 149 us -> none  [the longest x1 102 us: per_device(): lax.all_gather(stacked, 'ctx', axis=0, tiled=True)]
    ppermute x0 -> x42, starting transfers between devices: none -> 75.2 us  [the longest x7 23.7 us: per_device(): piece = lax.ppermute(piece, 'ctx', to)]
    reduce_scatter x1 -> x0, waiting for transfers between devices: 58.6 us -> none  [per_device(): lax.psum_scatter(jnp.dot(activated, w_down[0], preferred_element_type=jnp...]
    unnamed x5 -> x0, waiting for transfers between devices: 47 us -> none
    ppermute x0 -> x42, waiting for transfers between devices: none -> 46.7 us  [the longest x9 32.8 us: per_device(): current = lax.ppermute(current, 'ctx', ring)]
    all_gather x1 -> x0, blocking collectives: 32.6 us -> none  [per_device(): normed_rows = lax.all_gather(outgoing, 'ctx', axis=0, tiled=True)]
    unnamed x1 -> x0, blocking collectives: 23.5 us -> none
    all_to_all x1 -> x2, waiting for transfers between devices: 13.4 us -> 0.01 us  [the longest x1 0.01 us: per_device(): lax.all_to_all(jnp.concatenate([parcel, label], axis=1), 'ctx', split_axi...]
  transfers between devices with their start and end apart: 5 -> 44, of which waited for: 5 -> 16; matrix products, arithmetic and copies ran while one was open for 2% -> 22% of each run, Pallas kernels for 0% -> 5%
where the time goes in v1:
time: 196 us; the launch traced here: 195 us
  starting transfers between devices  85 us (43%)
  waiting for transfers between devices  46.7 us (24%)
  matrix products  34 us (17%)
  Pallas kernels  12.8 us (7%)
  other arithmetic  11.5 us (6%)
  local copies, waits for them, and re-layouts  3.83 us (2%)
    ppermute x9, waiting for transfers between devices, per_device(): current = lax.ppermute(current, 'ctx', ring)  32.8 us
    ppermute x7, starting transfers between devices, per_device(): piece = lax.ppermute(piece, 'ctx', to)  23.7 us
    ppermute x6, starting transfers between devices, per_device(): passing = lax.ppermute(passing, 'ctx', line)  21.7 us
    dot_general x1, matrix products, per_device(): jnp.dot(activated, w_down[0], preferred_element_type=F32).astype(BF16)  14.9 us
    ppermute x8, starting transfers between devices, per_device(): lax.ppermute(current, 'ctx', swap)  10.9 us
    dot_general x16, matrix products, per_device(): part = jnp.dot(rows, weight, preferred_element_type=F32)  9.13 us
    dot_general x1, matrix products, per_device(): gate_part = jnp.dot(slot_inputs, w_gate[0], preferred_element_type=F32)  7.48 us
    all_to_all x1, starting transfers between devices, per_device(): lax.all_to_all(jnp.concatenate([parcel, label], axis=1), 'ctx', split_axi...  6.26 us
  transfers between devices with their start and end apart: 44, of which 16 were waited for; matrix products, arithmetic and copies ran while one was open for 22% of the time, Pallas kernels for 5%

profile of v1, /device:TPU:0, one launch (start us, length us, event | category | flops | bytes accessed | tf_op | source)
XLA Modules:
  0.0 195.3 jit_solution(13260612820880078553)
XLA Ops:
  1.2 2.4 %shard_state.1 = (bf16[512,128]{1,0:T(8,128)(2,1)}, bf16[512,128]{1,0:T(8,128)(2,1)}, bf16[512,128]{1,0:T(8,128)(2,1)}, bf16[512,128]{1,0:T(8,128)(2,1)}) custom-call(s32[2]{0:T(128)} %pad_add_fusion.1.place_ref, f32[16]{0:T(128)} %decay_ref.7, bf16[128,2048]{1,0:T(8,128)(2,1)} %k_ref.3, bf16[128,2048]{1,0:T(8,128)(2,1)} %v_ref.3), custom_call_target="tpu_custom_call" | custom-call | tf_op jit(solution)/shard_map/shard_state/pallas_call | solution.py:140
  3.6 3.0 %collective-permute-start = (bf16[512,128]{1,0:T(8,128)(2,1)}, bf16[512,128]{1,0:T(8,128)(2,1)S(1)}, u32[]{:S(2)}, u32[]{:S(2)}) collective-permute-start(bf16[512,128]{1,0:T(8,128)(2,1)} %get-tuple-element.7), channel_id=1, source_target_pairs={{0,4},{4,0},{8,12},{12,8},{16,20},{20,16},{24,28},{28,24},{1,5},{5... | collective-permute-start | bytes 393224 | tf_op jit(solution)/shard_map/ppermute | solution.py:161
  6.7 0.7 fusion.92
  7.8 1.7 convolution_convert_fusion
  10.2 6.3 %all-to-all-start = ((bf16[8,16,768]{2,1,0:T(8,128)(2,1)}), bf16[8,16,768]{2,1,0:T(8,128)(2,1)S(1)}, u32[]{:S(2)}, u32[]{:S(2)}) async-start(bf16[8,16,768]{2,1,0:T(8,128)(2,1)} %pad_maximum_fusion.1), calls=%async_computation | async-start | bytes 393216 | tf_op jit(solution)/shard_map/all_to_all | solution.py:187
  17.6 3.9 %collective-permute-start.1 = (bf16[512,128]{1,0:T(8,128)(2,1)S(1)}, bf16[512,128]{1,0:T(8,128)(2,1)S(1)}, u32[]{:S(2)}, u32[]{:S(2)}) collective-permute-start(bf16[512,128]{1,0:T(8,128)(2,1)S(1)} %fusion.74), channel_id=1, source_target_pairs={{0,8},{4,12},{8,16},{12,20},{16,24},{20,28},{1,9},{5,13},{9,17},{1... | collective-permute-start | bytes 393224 | tf_op jit(solution)/shard_map/ppermute | solution.py:168
  21.7 3.4 %collective-permute-start.6 = (bf16[512,128]{1,0:T(8,128)(2,1)S(1)}, bf16[512,128]{1,0:T(8,128)(2,1)S(1)}, u32[]{:S(2)}, u32[]{:S(2)}) collective-permute-start(bf16[512,128]{1,0:T(8,128)(2,1)S(1)} %fusion.76), channel_id=1, source_target_pairs={{0,8},{4,12},{8,16},{12,20},{16,24},{20,28},{1,9},{5,13},{9,17},{1... | collective-permute-start | bytes 393224 | tf_op jit(solution)/shard_map/ppermute | solution.py:168
  25.1 3.7 %collective-permute-start.2 = (bf16[512,128]{1,0:T(8,128)(2,1)S(1)}, bf16[512,128]{1,0:T(8,128)(2,1)S(1)}, u32[]{:S(2)}, u32[]{:S(2)}) collective-permute-start(bf16[512,128]{1,0:T(8,128)(2,1)S(1)} %collective-permute-done.1), channel_id=1, source_target_pairs={{0,8},{4,12},{8,16},{12,20},{16,24},{20,28},{1,9},{5,13},{9,17},{1... | collective-permute-start | bytes 393224 | tf_op jit(solution)/shard_map/ppermute | solution.py:168
  28.8 4.9 %near_part.1.near_ref = f32[128,2048]{1,0:T(8,128)} custom-call(f32[16]{0:T(128)} %decay_ref.7, bf16[128,2048]{1,0:T(8,128)(2,1)} %q_ref.5, bf16[128,2048]{1,0:T(8,128)(2,1)} %k_ref.3, bf16[128,2048]{1,0:T(8,128)(2,1)} %v_ref.3), custom_call_target="tpu_custom_call" | custom-call | tf_op jit(solution)/shard_map/near_part/pallas_call | solution.py:147
  33.9 3.4 %collective-permute-start.7 = (bf16[512,128]{1,0:T(8,128)(2,1)S(1)}, bf16[512,128]{1,0:T(8,128)(2,1)S(1)}, u32[]{:S(2)}, u32[]{:S(2)}) collective-permute-start(bf16[512,128]{1,0:T(8,128)(2,1)S(1)} %collective-permute-done.6), channel_id=1, source_target_pairs={{0,8},{4,12},{8,16},{12,20},{16,24},{20,28},{1,9},{5,13},{9,17},{1... | collective-permute-start | bytes 393224 | tf_op jit(solution)/shard_map/ppermute | solution.py:168
  37.4 4.2 %collective-permute-start.3 = (bf16[512,128]{1,0:T(8,128)(2,1)S(1)}, bf16[512,128]{1,0:T(8,128)(2,1)S(1)}, u32[]{:S(2)}, u32[]{:S(2)}) collective-permute-start(bf16[512,128]{1,0:T(8,128)(2,1)S(1)} %collective-permute-done.2), channel_id=1, source_target_pairs={{0,8},{4,12},{8,16},{12,20},{16,24},{20,28},{1,9},{5,13},{9,17},{1... | collective-permute-start | bytes 393224 | tf_op jit(solution)/shard_map/ppermute | solution.py:168
  41.8 3.1 %collective-permute-start.8 = (bf16[512,128]{1,0:T(8,128)(2,1)S(1)}, bf16[512,128]{1,0:T(8,128)(2,1)S(1)}, u32[]{:S(2)}, u32[]{:S(2)}) collective-permute-start(bf16[512,128]{1,0:T(8,128)(2,1)S(1)} %collective-permute-done.7), channel_id=1, source_target_pairs={{0,8},{4,12},{8,16},{12,20},{16,24},{20,28},{1,9},{5,13},{9,17},{1... | collective-permute-start | bytes 393224 | tf_op jit(solution)/shard_map/ppermute | solution.py:168
  45.0 1.0 select_convert_fusion.2
  46.0 1.7 collective-permute-start.4
  47.7 1.0 select_convert_fusion
  48.7 1.5 collective-permute-start.9
  50.2 0.8 collective-permute-done.4.other_ref
  51.6 2.8 %mix_heads.2 = bf16[128,1024]{1,0:T(8,128)(2,1)} custom-call(s32[2]{0:T(128)} %pad_add_fusion.1.place_ref, f32[16]{0:T(128)} %decay_ref.7, bf16[128,2048]{1,0:T(8,128)(2,1)} %q_ref.5, f32[128,2048]{1,0:T(8,128)} %near_part.1.near_ref, bf16[128,2048]{1,0:T(8,128)(2,1)} %gate_ref.3, f32[1,2048]{1,0:T(1,128)} %bitcast.209, ...), custom_call_target="tpu_custom_call" | custom-call | tf_op jit(solution)/shard_map/mix_heads/pallas_call | solution.py:175
  54.4 1.7 collective-permute-start.10
  56.1 1.7 collective-permute-start.12
  58.4 2.7 %mix_heads.3 = bf16[128,1024]{1,0:T(8,128)(2,1)} custom-call(s32[2]{0:T(128)} %pad_add_fusion.1.place_ref, f32[16]{0:T(128)} %decay_ref.7, bf16[128,2048]{1,0:T(8,128)(2,1)} %q_ref.5, f32[128,2048]{1,0:T(8,128)} %near_part.1.near_ref, bf16[128,2048]{1,0:T(8,128)(2,1)} %gate_ref.3, f32[1,2048]{1,0:T(1,128)} %bitcast.210, ...), custom_call_target="tpu_custom_call" | custom-call | tf_op jit(solution)/shard_map/mix_heads/pallas_call | solution.py:175
  61.1 0.8 collective-permute-start.11
  62.0 1.2 collective-permute-start.13
  63.1 2.0 %fusion.63 = f32[128,768]{1,0:T(8,128)S(1)} fusion(bf16[128,1024]{1,0:T(8,128)(2,1)} %mix_heads.3, bf16[2048,768]{1,0:T(8,128)(2,1)} %param.21), kind=kOutput, calls=%fused_computation.85 | convolution fusion | flops 201326592 | bytes 2228224 | tf_op jit(solution)/shard_map/dot_general | solution.py:209
  65.2 1.8 fusion.22
  67.0 0.9 collective-permute-start.14
  67.9 1.0 collective-permute-start.16
  68.8 2.2 %collective-permute-done.13 = bf16[128,1024]{1,0:T(8,128)(2,1)S(1)} collective-permute-done((bf16[128,1024]{1,0:T(8,128)(2,1)}, bf16[128,1024]{1,0:T(8,128)(2,1)S(1)}, u32[]{:S(2)}, u32[]{:S(2)}) %collective-permute-start.13) | collective-permute-done | bytes 262176 | tf_op jit(solution)/shard_map/ppermute | solution.py:212
  71.0 2.7 %collective-permute-start.15 = (bf16[128,1024]{1,0:T(8,128)(2,1)S(1)}, bf16[128,1024]{1,0:T(8,128)(2,1)S(1)}, u32[]{:S(2)}, u32[]{:S(2)}) collective-permute-start(bf16[128,1024]{1,0:T(8,128)(2,1)S(1)} %collective-permute-done.13), channel_id=1, source_target_pairs={{0,4},{4,0},{8,12},{12,8},{16,20},{20,16},{24,28},{28,24},{1,5},{5... | collective-permute-start | bytes 786440 | tf_op jit(solution)/shard_map/ppermute | solution.py:207
  75.4 3.3 %collective-permute-done.16 = bf16[128,1024]{1,0:T(8,128)(2,1)S(1)} collective-permute-done((bf16[128,1024]{1,0:T(8,128)(2,1)S(1)}, bf16[128,1024]{1,0:T(8,128)(2,1)S(1)}, u32[]{:S(2)}, u32[]{:S(2)}) %collective-permute-start.16) | collective-permute-done | bytes 262176 | tf_op jit(solution)/shard_map/ppermute | solution.py:212
  78.7 1.4 collective-permute-start.18
  80.1 3.8 %collective-permute-done.17 = bf16[128,1024]{1,0:T(8,128)(2,1)S(1)} collective-permute-done((bf16[128,1024]{1,0:T(8,128)(2,1)S(1)}, bf16[128,1024]{1,0:T(8,128)(2,1)S(1)}, u32[]{:S(2)}, u32[]{:S(2)}) %collective-permute-start.17) | collective-permute-done | bytes 262176 | tf_op jit(solution)/shard_map/ppermute | solution.py:212
  83.9 1.8 collective-permute-start.19
  87.4 0.9 collective-permute-done.20
  88.3 1.3 collective-permute-start.22
  89.6 4.8 %collective-permute-done.21 = bf16[128,1024]{1,0:T(8,128)(2,1)S(1)} collective-permute-done((bf16[128,1024]{1,0:T(8,128)(2,1)S(1)}, bf16[128,1024]{1,0:T(8,128)(2,1)S(1)}, u32[]{:S(2)}, u32[]{:S(2)}) %collective-permute-start.21) | collective-permute-done | bytes 262176 | tf_op jit(solution)/shard_map/ppermute | solution.py:212
  96.1 4.6 %collective-permute-done.23 = bf16[128,1024]{1,0:T(8,128)(2,1)S(1)} collective-permute-done((bf16[128,1024]{1,0:T(8,128)(2,1)S(1)}, bf16[128,1024]{1,0:T(8,128)(2,1)S(1)}, u32[]{:S(2)}, u32[]{:S(2)}) %collective-permute-start.23) | collective-permute-done | bytes 262176 | tf_op jit(solution)/shard_map/ppermute | solution.py:207
  102.3 1.4 collective-permute-done.33
  103.7 1.6 collective-permute-start.34
  105.3 1.0 pad_maximum_fusion
  106.3 2.4 %collective-permute-done.34 = bf16[1,64,768]{2,1,0:T(8,128)(2,1)S(1)} collective-permute-done((bf16[1,64,768]{2,1,0:T(8,128)(2,1)S(1)}, bf16[1,64,768]{2,1,0:T(8,128)(2,1)S(1)}, u32[]{:S(2)}, u32[]{:S(2)}) %collective-permute-start.34) | collective-permute-done | bytes 98336 | tf_op jit(solution)/shard_map/ppermute | solution.py:221
  109.0 1.4 collective-permute-start.36
  110.4 5.0 %collective-permute-done.36 = bf16[64,768]{1,0:T(8,128)(2,1)S(1)} collective-permute-done((bf16[64,768]{1,0:T(8,128)(2,1)S(1)}, bf16[64,768]{1,0:T(8,128)(2,1)S(1)}, u32[]{:S(2)}, u32[]{:S(2)}) %collective-permute-start.36) | collective-permute-done | bytes 98336 | tf_op jit(solution)/shard_map/ppermute | solution.py:243
  115.4 1.8 collective-permute-start.37
  117.2 6.4 %collective-permute-done.38 = bf16[64,768]{1,0:T(8,128)(2,1)S(1)} collective-permute-done((bf16[64,768]{1,0:T(8,128)(2,1)S(1)}, bf16[64,768]{1,0:T(8,128)(2,1)S(1)}, u32[]{:S(2)}, u32[]{:S(2)}) %collective-permute-start.38) | collective-permute-done | bytes 98336 | tf_op jit(solution)/shard_map/ppermute | solution.py:243
  123.9 6.4 %collective-permute-done.40 = bf16[64,768]{1,0:T(8,128)(2,1)S(1)} collective-permute-done((bf16[64,768]{1,0:T(8,128)(2,1)S(1)}, bf16[64,768]{1,0:T(8,128)(2,1)S(1)}, u32[]{:S(2)}, u32[]{:S(2)}) %collective-permute-start.40) | collective-permute-done | bytes 98336 | tf_op jit(solution)/shard_map/ppermute | solution.py:243
  130.3 1.8 collective-permute-start.41
  132.1 2.8 %collective-permute-done.41 = bf16[64,768]{1,0:T(8,128)(2,1)S(1)} collective-permute-done((bf16[64,768]{1,0:T(8,128)(2,1)S(1)}, bf16[64,768]{1,0:T(8,128)(2,1)S(1)}, u32[]{:S(2)}, u32[]{:S(2)}) %collective-permute-start.41) | collective-permute-done | bytes 98336 | tf_op jit(solution)/shard_map/ppermute | solution.py:241
  136.3 1.1 fusion.39
  137.4 1.6 collective-permute-start.25
  138.9 7.5 %fusion.4 = f32[64,1152]{1,0:T(8,128)S(1)} fusion(bf16[64,6144]{1,0:T(8,128)(2,1)S(1)} %bitcast.202, bf16[1,6144,1152]{2,1,0:T(8,128)(2,1)} %param.25), kind=kOutput, calls=%fused_computation.6 | convolution fusion | flops 905969664 | bytes 15237120 | tf_op jit(solution)/shard_map/dot_general | solution.py:248
  146.4 1.1 fusion.38
  147.6 1.9 collective-permute-start.26
  149.5 14.9 %fusion.9 = bf16[8,8,6144]{2,1,0:T(8,128)(2,1)} fusion(bf16[1,1152,6144]{2,1,0:T(8,128)(2,1)} %param.27, bf16[64,6144]{1,0:T(8,128)(2,1)S(1)} %bitcast.203, bf16[1,6144,1152]{2,1,0:T(8,128)(2,1)} %param.26, f32[64,1152]{1,0:T(8,128)S(1)} %fusion.4), kind=kOutput, calls=%fused_computation.9 | convolution fusion | flops 1812774912 | bytes 30179328 | tf_op jit(solution)/shard_map/dot_general | solution.py:251
  164.4 3.5 %all-to-all-start.1 = ((bf16[8,8,6144]{2,1,0:T(8,128)(2,1)}), bf16[8,8,6144]{2,1,0:T(8,128)(2,1)S(1)}, u32[]{:S(2)}, u32[]{:S(2)}) async-start(bf16[8,8,6144]{2,1,0:T(8,128)(2,1)} %fusion.9), calls=%async_computation.1 | async-start | bytes 1572864 | tf_op jit(solution)/shard_map/all_to_all | solution.py:252
  167.9 3.8 %collective-permute-start.27 = (bf16[32,768]{1,0:T(8,128)(2,1)S(1)}, bf16[32,768]{1,0:T(8,128)(2,1)S(1)}, u32[]{:S(2)}, u32[]{:S(2)}) collective-permute-start(bf16[32,768]{1,0:T(8,128)(2,1)S(1)} %get-tuple-element.27), channel_id=1, source_target_pairs={{0,24},{4,28},{8,0},{12,4},{16,8},{20,12},{24,16},{28,20},{1,25},{... | collective-permute-start | bytes 147464 | tf_op jit(solution)/shard_map/ppermute | solution.py:266
  171.7 1.5 collective-permute-start.28
  173.1 2.9 %collective-permute-start.30 = (bf16[32,768]{1,0:T(8,128)(2,1)S(1)}, bf16[32,768]{1,0:T(8,128)(2,1)S(1)}, u32[]{:S(2)}, u32[]{:S(2)}) collective-permute-start(bf16[32,768]{1,0:T(8,128)(2,1)S(1)} %get-tuple-element.24), channel_id=1, source_target_pairs={{0,20},{4,16},{8,28},{12,24},{16,4},{20,0},{24,12},{28,8},{1,21},{... | collective-permute-start | bytes 147464 | tf_op jit(solution)/shard_map/ppermute | solution.py:266
  176.0 1.5 collective-permute-start.31
  177.8 12.3 %collective-permute-start.32 = (bf16[32,768]{1,0:T(8,128)(2,1)S(1)}, bf16[32,768]{1,0:T(8,128)(2,1)S(1)}, u32[]{:S(2)}, u32[]{:S(2)}) collective-permute-start(bf16[32,768]{1,0:T(8,128)(2,1)S(1)} %get-tuple-element.22), channel_id=1, source_target_pairs={{0,12},{4,8},{8,20},{12,16},{16,28},{20,24},{24,4},{28,0},{1,13},{... | collective-permute-start | bytes 147464 | tf_op jit(solution)/shard_map/ppermute | solution.py:266
  190.1 1.0 collective-permute-done.30
  191.1 0.7 collective-permute-done.32
  192.6 1.8 add_convert_fusion
  194.5 0.7 fusion.85
  (146 shorter events, 14.4 us)
Async XLA Ops:
  3.6 13.0 %copy-start.6 = (f32[16]{0:T(128)S(1)}, f32[16]{0:T(128)}, u32[]{:S(2)}) copy-start(f32[16]{0:T(128)} %decay_ref.7) | copy-start | bytes 196
  3.6 13.6 %copy-start.7 = (s32[128,2]{0,1:T(2,128)S(1)}, s32[128,2]{0,1:T(2,128)}, u32[]{:S(2)}) copy-start(s32[128,2]{0,1:T(2,128)} %param.23) | copy-start | bytes 3076
  3.6 13.6 %copy-start.8 = (f32[128,2]{0,1:T(2,128)S(1)}, f32[128,2]{0,1:T(2,128)}, u32[]{:S(2)}) copy-start(f32[128,2]{0,1:T(2,128)} %param.24) | copy-start | bytes 3076
  3.6 13.8 %copy-start.1 = (bf16[512,128]{1,0:T(8,128)(2,1)S(1)}, bf16[512,128]{1,0:T(8,128)(2,1)}, u32[]{:S(2)}) copy-start(bf16[512,128]{1,0:T(8,128)(2,1)} %get-tuple-element.6) | copy-start | bytes 393220
  3.6 17.9 %copy-start = (bf16[512,128]{1,0:T(8,128)(2,1)S(1)}, bf16[512,128]{1,0:T(8,128)(2,1)}, u32[]{:S(2)}) copy-start(bf16[512,128]{1,0:T(8,128)(2,1)} %get-tuple-element.8) | copy-start | bytes 393220
  3.6 13.8 %collective-permute-start = (bf16[512,128]{1,0:T(8,128)(2,1)}, bf16[512,128]{1,0:T(8,128)(2,1)S(1)}, u32[]{:S(2)}, u32[]{:S(2)}) collective-permute-start(bf16[512,128]{1,0:T(8,128)(2,1)} %get-tuple-element.7), channel_id=1, source_target_pairs={{0,4},{4,0},{8,12},{12,8},{16,20},{20,16},{24,28},{28,24},{1,5},{5... | collective-permute-start | bytes 393224 | tf_op jit(solution)/shard_map/ppermute | solution.py:161
  6.6 14.9 %collective-permute-start.5 = (bf16[512,128]{1,0:T(8,128)(2,1)}, bf16[512,128]{1,0:T(8,128)(2,1)S(1)}, u32[]{:S(2)}, u32[]{:S(2)}) collective-permute-start(bf16[512,128]{1,0:T(8,128)(2,1)} %get-tuple-element.9), channel_id=1, source_target_pairs={{0,4},{4,0},{8,12},{12,8},{16,20},{20,16},{24,28},{28,24},{1,5},{5... | collective-permute-start | bytes 393224 | tf_op jit(solution)/shard_map/ppermute | solution.py:161
  10.2 27.1 %all-to-all-start = ((bf16[8,16,768]{2,1,0:T(8,128)(2,1)}), bf16[8,16,768]{2,1,0:T(8,128)(2,1)S(1)}, u32[]{:S(2)}, u32[]{:S(2)}) async-start(bf16[8,16,768]{2,1,0:T(8,128)(2,1)} %pad_maximum_fusion.1), calls=%async_computation | async-start | bytes 393216 | tf_op jit(solution)/shard_map/all_to_all | solution.py:187
  17.6 16.3 %copy-start.5 = (f32[6144]{0:T(1024)S(1)}, f32[6144]{0:T(1024)}, u32[]{:S(2)}) copy-start(f32[6144]{0:T(1024)} %param.22) | copy-start | bytes 73732
  17.6 7.5 %collective-permute-start.1 = (bf16[512,128]{1,0:T(8,128)(2,1)S(1)}, bf16[512,128]{1,0:T(8,128)(2,1)S(1)}, u32[]{:S(2)}, u32[]{:S(2)}) collective-permute-start(bf16[512,128]{1,0:T(8,128)(2,1)S(1)} %fusion.74), channel_id=1, source_target_pairs={{0,8},{4,12},{8,16},{12,20},{16,24},{20,28},{1,9},{5,13},{9,17},{1... | collective-permute-start | bytes 393224 | tf_op jit(solution)/shard_map/ppermute | solution.py:168
  21.7 12.3 %collective-permute-start.6 = (bf16[512,128]{1,0:T(8,128)(2,1)S(1)}, bf16[512,128]{1,0:T(8,128)(2,1)S(1)}, u32[]{:S(2)}, u32[]{:S(2)}) collective-permute-start(bf16[512,128]{1,0:T(8,128)(2,1)S(1)} %fusion.76), channel_id=1, source_target_pairs={{0,8},{4,12},{8,16},{12,20},{16,24},{20,28},{1,9},{5,13},{9,17},{1... | collective-permute-start | bytes 393224 | tf_op jit(solution)/shard_map/ppermute | solution.py:168
  25.1 12.4 %collective-permute-start.2 = (bf16[512,128]{1,0:T(8,128)(2,1)S(1)}, bf16[512,128]{1,0:T(8,128)(2,1)S(1)}, u32[]{:S(2)}, u32[]{:S(2)}) collective-permute-start(bf16[512,128]{1,0:T(8,128)(2,1)S(1)} %collective-permute-done.1), channel_id=1, source_target_pairs={{0,8},{4,12},{8,16},{12,20},{16,24},{20,28},{1,9},{5,13},{9,17},{1... | collective-permute-start | bytes 393224 | tf_op jit(solution)/shard_map/ppermute | solution.py:168
  33.9 7.9 %collective-permute-start.7 = (bf16[512,128]{1,0:T(8,128)(2,1)S(1)}, bf16[512,128]{1,0:T(8,128)(2,1)S(1)}, u32[]{:S(2)}, u32[]{:S(2)}) collective-permute-start(bf16[512,128]{1,0:T(8,128)(2,1)S(1)} %collective-permute-done.6), channel_id=1, source_target_pairs={{0,8},{4,12},{8,16},{12,20},{16,24},{20,28},{1,9},{5,13},{9,17},{1... | collective-permute-start | bytes 393224 | tf_op jit(solution)/shard_map/ppermute | solution.py:168
  37.4 7.5 %collective-permute-start.3 = (bf16[512,128]{1,0:T(8,128)(2,1)S(1)}, bf16[512,128]{1,0:T(8,128)(2,1)S(1)}, u32[]{:S(2)}, u32[]{:S(2)}) collective-permute-start(bf16[512,128]{1,0:T(8,128)(2,1)S(1)} %collective-permute-done.2), channel_id=1, source_target_pairs={{0,8},{4,12},{8,16},{12,20},{16,24},{20,28},{1,9},{5,13},{9,17},{1... | collective-permute-start | bytes 393224 | tf_op jit(solution)/shard_map/ppermute | solution.py:168
  41.8 5.9 %collective-permute-start.8 = (bf16[512,128]{1,0:T(8,128)(2,1)S(1)}, bf16[512,128]{1,0:T(8,128)(2,1)S(1)}, u32[]{:S(2)}, u32[]{:S(2)}) collective-permute-start(bf16[512,128]{1,0:T(8,128)(2,1)S(1)} %collective-permute-done.7), channel_id=1, source_target_pairs={{0,8},{4,12},{8,16},{12,20},{16,24},{20,28},{1,9},{5,13},{9,17},{1... | collective-permute-start | bytes 393224 | tf_op jit(solution)/shard_map/ppermute | solution.py:168
  46.0 5.0 %collective-permute-start.4 = (bf16[512,128]{1,0:T(8,128)(2,1)S(1)}, bf16[512,128]{1,0:T(8,128)(2,1)S(1)}, u32[]{:S(2)}, u32[]{:S(2)}) collective-permute-start(bf16[512,128]{1,0:T(8,128)(2,1)S(1)} %get-tuple-element.16), channel_id=1, source_target_pairs={{0,4},{4,0},{8,12},{12,8},{16,20},{20,16},{24,28},{28,24},{1,5},{5... | collective-permute-start | bytes 393224 | tf_op jit(solution)/shard_map/ppermute | solution.py:173
  48.7 9.0 %collective-permute-start.9 = (bf16[512,128]{1,0:T(8,128)(2,1)S(1)}, bf16[512,128]{1,0:T(8,128)(2,1)S(1)}, u32[]{:S(2)}, u32[]{:S(2)}) collective-permute-start(bf16[512,128]{1,0:T(8,128)(2,1)S(1)} %get-tuple-element.18), channel_id=1, source_target_pairs={{0,4},{4,0},{8,12},{12,8},{16,20},{20,16},{24,28},{28,24},{1,5},{5... | collective-permute-start | bytes 393224 | tf_op jit(solution)/shard_map/ppermute | solution.py:173
  51.0 0.7 copy-start.3
  54.4 20.2 %collective-permute-start.10 = (bf16[128,1024]{1,0:T(8,128)(2,1)}, bf16[128,1024]{1,0:T(8,128)(2,1)S(1)}, u32[]{:S(2)}, u32[]{:S(2)}) collective-permute-start(bf16[128,1024]{1,0:T(8,128)(2,1)} %mix_heads.2), channel_id=1, source_target_pairs={{0,4},{4,0},{8,12},{12,8},{16,20},{20,16},{24,28},{28,24},{1,5},{5... | collective-permute-start | bytes 786440 | tf_op jit(solution)/shard_map/ppermute | solution.py:207
  56.1 10.9 %collective-permute-start.12 = (bf16[128,1024]{1,0:T(8,128)(2,1)}, bf16[128,1024]{1,0:T(8,128)(2,1)S(1)}, u32[]{:S(2)}, u32[]{:S(2)}) collective-permute-start(bf16[128,1024]{1,0:T(8,128)(2,1)} %mix_heads.2), channel_id=1, source_target_pairs={{0,8},{4,12},{8,16},{12,20},{16,24},{20,28},{24,0},{28,4},{1,9},{5... | collective-permute-start | bytes 786440 | tf_op jit(solution)/shard_map/ppermute | solution.py:212
  57.7 0.7 copy-start.4
  61.1 4.0 %copy-start.2 = (bf16[128,1024]{1,0:T(8,128)(2,1)S(1)}, bf16[128,1024]{1,0:T(8,128)(2,1)}, u32[]{:S(2)}) copy-start(bf16[128,1024]{1,0:T(8,128)(2,1)} %mix_heads.2) | copy-start | bytes 786436
  61.1 13.0 %collective-permute-start.11 = (bf16[128,1024]{1,0:T(8,128)(2,1)}, bf16[128,1024]{1,0:T(8,128)(2,1)S(1)}, u32[]{:S(2)}, u32[]{:S(2)}) collective-permute-start(bf16[128,1024]{1,0:T(8,128)(2,1)} %mix_heads.3), channel_id=1, source_target_pairs={{0,4},{4,0},{8,12},{12,8},{16,20},{20,16},{24,28},{28,24},{1,5},{5... | collective-permute-start | bytes 786440 | tf_op jit(solution)/shard_map/ppermute | solution.py:207
  62.0 9.1 %collective-permute-start.13 = (bf16[128,1024]{1,0:T(8,128)(2,1)}, bf16[128,1024]{1,0:T(8,128)(2,1)S(1)}, u32[]{:S(2)}, u32[]{:S(2)}) collective-permute-start(bf16[128,1024]{1,0:T(8,128)(2,1)} %mix_heads.3), channel_id=1, source_target_pairs={{0,8},{4,12},{8,16},{12,20},{16,24},{20,28},{24,0},{28,4},{1,9},{5... | collective-permute-start | bytes 786440 | tf_op jit(solution)/shard_map/ppermute | solution.py:212
  63.1 10.6 %copy-start.9 = (bf16[2048,768]{1,0:T(8,128)(2,1)S(1)}, bf16[2048,768]{1,0:T(8,128)(2,1)}, u32[]{:S(2)}) copy-start(bf16[2048,768]{1,0:T(8,128)(2,1)} %param.21) | copy-start | bytes 9437188
  67.0 19.6 %collective-permute-start.14 = (bf16[128,1024]{1,0:T(8,128)(2,1)S(1)}, bf16[128,1024]{1,0:T(8,128)(2,1)S(1)}, u32[]{:S(2)}, u32[]{:S(2)}) collective-permute-start(bf16[128,1024]{1,0:T(8,128)(2,1)S(1)} %collective-permute-done.12), channel_id=1, source_target_pairs={{0,4},{4,0},{8,12},{12,8},{16,20},{20,16},{24,28},{28,24},{1,5},{5... | collective-permute-start | bytes 786440 | tf_op jit(solution)/shard_map/ppermute | solution.py:207
  67.9 10.8 %collective-permute-start.16 = (bf16[128,1024]{1,0:T(8,128)(2,1)S(1)}, bf16[128,1024]{1,0:T(8,128)(2,1)S(1)}, u32[]{:S(2)}, u32[]{:S(2)}) collective-permute-start(bf16[128,1024]{1,0:T(8,128)(2,1)S(1)} %collective-permute-done.12), channel_id=1, source_target_pairs={{0,8},{4,12},{8,16},{12,20},{16,24},{20,28},{24,0},{28,4},{1,9},{5... | collective-permute-start | bytes 786440 | tf_op jit(solution)/shard_map/ppermute | solution.py:212
  71.0 15.1 %collective-permute-start.15 = (bf16[128,1024]{1,0:T(8,128)(2,1)S(1)}, bf16[128,1024]{1,0:T(8,128)(2,1)S(1)}, u32[]{:S(2)}, u32[]{:S(2)}) collective-permute-start(bf16[128,1024]{1,0:T(8,128)(2,1)S(1)} %collective-permute-done.13), channel_id=1, source_target_pairs={{0,4},{4,0},{8,12},{12,8},{16,20},{20,16},{24,28},{28,24},{1,5},{5... | collective-permute-start | bytes 786440 | tf_op jit(solution)/shard_map/ppermute | solution.py:207
  74.1 9.8 %collective-permute-start.17 = (bf16[128,1024]{1,0:T(8,128)(2,1)S(1)}, bf16[128,1024]{1,0:T(8,128)(2,1)S(1)}, u32[]{:S(2)}, u32[]{:S(2)}) collective-permute-start(bf16[128,1024]{1,0:T(8,128)(2,1)S(1)} %collective-permute-done.13), channel_id=1, source_target_pairs={{0,8},{4,12},{8,16},{12,20},{16,24},{20,28},{24,0},{28,4},{1,9},{5... | collective-permute-start | bytes 786440 | tf_op jit(solution)/shard_map/ppermute | solution.py:212
  78.7 16.7 %collective-permute-start.18 = (bf16[128,1024]{1,0:T(8,128)(2,1)S(1)}, bf16[128,1024]{1,0:T(8,128)(2,1)S(1)}, u32[]{:S(2)}, u32[]{:S(2)}) collective-permute-start(bf16[128,1024]{1,0:T(8,128)(2,1)S(1)} %collective-permute-done.16), channel_id=1, source_target_pairs={{0,4},{4,0},{8,12},{12,8},{16,20},{20,16},{24,28},{28,24},{1,5},{5... | collective-permute-start | bytes 786440 | tf_op jit(solution)/shard_map/ppermute | solution.py:207
  80.1 8.2 %collective-permute-start.20 = (bf16[128,1024]{1,0:T(8,128)(2,1)S(1)}, bf16[128,1024]{1,0:T(8,128)(2,1)S(1)}, u32[]{:S(2)}, u32[]{:S(2)}) collective-permute-start(bf16[128,1024]{1,0:T(8,128)(2,1)S(1)} %collective-permute-done.16), channel_id=1, source_target_pairs={{0,8},{4,12},{8,16},{12,20},{16,24},{20,28},{24,0},{28,4},{1,9},{5... | collective-permute-start | bytes 786440 | tf_op jit(solution)/shard_map/ppermute | solution.py:212
  83.9 11.0 %collective-permute-start.19 = (bf16[128,1024]{1,0:T(8,128)(2,1)S(1)}, bf16[128,1024]{1,0:T(8,128)(2,1)S(1)}, u32[]{:S(2)}, u32[]{:S(2)}) collective-permute-start(bf16[128,1024]{1,0:T(8,128)(2,1)S(1)} %collective-permute-done.17), channel_id=1, source_target_pairs={{0,4},{4,0},{8,12},{12,8},{16,20},{20,16},{24,28},{28,24},{1,5},{5... | collective-permute-start | bytes 786440 | tf_op jit(solution)/shard_map/ppermute | solution.py:207
  86.1 8.2 %collective-permute-start.21 = (bf16[128,1024]{1,0:T(8,128)(2,1)S(1)}, bf16[128,1024]{1,0:T(8,128)(2,1)S(1)}, u32[]{:S(2)}, u32[]{:S(2)}) collective-permute-start(bf16[128,1024]{1,0:T(8,128)(2,1)S(1)} %collective-permute-done.17), channel_id=1, source_target_pairs={{0,8},{4,12},{8,16},{12,20},{16,24},{20,28},{24,0},{28,4},{1,9},{5... | collective-permute-start | bytes 786440 | tf_op jit(solution)/shard_map/ppermute | solution.py:212
  88.3 12.8 %collective-permute-start.22 = (bf16[128,1024]{1,0:T(8,128)(2,1)S(1)}, bf16[128,1024]{1,0:T(8,128)(2,1)S(1)}, u32[]{:S(2)}, u32[]{:S(2)}) collective-permute-start(bf16[128,1024]{1,0:T(8,128)(2,1)S(1)} %collective-permute-done.20), channel_id=1, source_target_pairs={{0,4},{4,0},{8,12},{12,8},{16,20},{20,16},{24,28},{28,24},{1,5},{5... | collective-permute-start | bytes 786440 | tf_op jit(solution)/shard_map/ppermute | solution.py:207
  94.3 6.4 %collective-permute-start.23 = (bf16[128,1024]{1,0:T(8,128)(2,1)S(1)}, bf16[128,1024]{1,0:T(8,128)(2,1)S(1)}, u32[]{:S(2)}, u32[]{:S(2)}) collective-permute-start(bf16[128,1024]{1,0:T(8,128)(2,1)S(1)} %collective-permute-done.21), channel_id=1, source_target_pairs={{0,4},{4,0},{8,12},{12,8},{16,20},{20,16},{24,28},{28,24},{1,5},{5... | collective-permute-start | bytes 786440 | tf_op jit(solution)/shard_map/ppermute | solution.py:207
  102.2 1.5 collective-permute-start.33
  103.7 4.9 %collective-permute-start.34 = (bf16[1,64,768]{2,1,0:T(8,128)(2,1)S(1)}, bf16[1,64,768]{2,1,0:T(8,128)(2,1)S(1)}, u32[]{:S(2)}, u32[]{:S(2)}) collective-permute-start(bf16[1,64,768]{2,1,0:T(8,128)(2,1)S(1)} %fusion.84), channel_id=1, source_target_pairs={{0,2},{1,3},{2,0},{3,1},{4,6},{5,7},{6,4},{7,5},{8,10},{9,11},{10,... | collective-permute-start | bytes 294920 | tf_op jit(solution)/shard_map/ppermute | solution.py:221
  106.3 30.0 %collective-permute-start.24 = (bf16[2,8,32,768]{3,2,1,0:T(8,128)(2,1)}, bf16[2,8,32,768]{3,2,1,0:T(8,128)(2,1)}, u32[]{:S(2)}, u32[]{:S(2)}) collective-permute-start(bf16[2,8,32,768]{3,2,1,0:T(8,128)(2,1)} %pad_maximum_fusion), channel_id=1, source_target_pairs={{0,1},{1,0},{2,3},{3,2},{4,5},{5,4},{6,7},{7,6},{8,9},{9,8},{10,11... | collective-permute-start | bytes 2359304 | tf_op jit(solution)/shard_map/ppermute | solution.py:221
  108.7 8.5 %collective-permute-start.35 = (bf16[64,768]{1,0:T(8,128)(2,1)S(1)}, bf16[64,768]{1,0:T(8,128)(2,1)S(1)}, u32[]{:S(2)}, u32[]{:S(2)}) collective-permute-start(bf16[64,768]{1,0:T(8,128)(2,1)S(1)} %fusion.83), channel_id=1, source_target_pairs={{0,4},{4,0},{8,12},{12,8},{16,20},{20,16},{24,28},{28,24},{1,5},{5... | collective-permute-start | bytes 294920 | tf_op jit(solution)/shard_map/ppermute | solution.py:241
  109.0 6.4 %collective-permute-start.36 = (bf16[64,768]{1,0:T(8,128)(2,1)S(1)}, bf16[64,768]{1,0:T(8,128)(2,1)S(1)}, u32[]{:S(2)}, u32[]{:S(2)}) collective-permute-start(bf16[64,768]{1,0:T(8,128)(2,1)S(1)} %fusion.83), channel_id=1, source_target_pairs={{0,8},{4,12},{8,16},{12,20},{16,24},{20,28},{24,0},{28,4},{1,9},{5... | collective-permute-start | bytes 294920 | tf_op jit(solution)/shard_map/ppermute | solution.py:243
  115.4 8.4 %collective-permute-start.37 = (bf16[64,768]{1,0:T(8,128)(2,1)S(1)}, bf16[64,768]{1,0:T(8,128)(2,1)S(1)}, u32[]{:S(2)}, u32[]{:S(2)}) collective-permute-start(bf16[64,768]{1,0:T(8,128)(2,1)S(1)} %collective-permute-done.36), channel_id=1, source_target_pairs={{0,4},{4,0},{8,12},{12,8},{16,20},{20,16},{24,28},{28,24},{1,5},{5... | collective-permute-start | bytes 294920 | tf_op jit(solution)/shard_map/ppermute | solution.py:241
  117.2 6.4 %collective-permute-start.38 = (bf16[64,768]{1,0:T(8,128)(2,1)S(1)}, bf16[64,768]{1,0:T(8,128)(2,1)S(1)}, u32[]{:S(2)}, u32[]{:S(2)}) collective-permute-start(bf16[64,768]{1,0:T(8,128)(2,1)S(1)} %collective-permute-done.36), channel_id=1, source_target_pairs={{0,8},{4,12},{8,16},{12,20},{16,24},{20,28},{24,0},{28,4},{1,9},{5... | collective-permute-start | bytes 294920 | tf_op jit(solution)/shard_map/ppermute | solution.py:243
  123.6 8.4 %collective-permute-start.39 = (bf16[64,768]{1,0:T(8,128)(2,1)S(1)}, bf16[64,768]{1,0:T(8,128)(2,1)S(1)}, u32[]{:S(2)}, u32[]{:S(2)}) collective-permute-start(bf16[64,768]{1,0:T(8,128)(2,1)S(1)} %collective-permute-done.38), channel_id=1, source_target_pairs={{0,4},{4,0},{8,12},{12,8},{16,20},{20,16},{24,28},{28,24},{1,5},{5... | collective-permute-start | bytes 294920 | tf_op jit(solution)/shard_map/ppermute | solution.py:241
  123.9 6.4 %collective-permute-start.40 = (bf16[64,768]{1,0:T(8,128)(2,1)S(1)}, bf16[64,768]{1,0:T(8,128)(2,1)S(1)}, u32[]{:S(2)}, u32[]{:S(2)}) collective-permute-start(bf16[64,768]{1,0:T(8,128)(2,1)S(1)} %collective-permute-done.38), channel_id=1, source_target_pairs={{0,8},{4,12},{8,16},{12,20},{16,24},{20,28},{24,0},{28,4},{1,9},{5... | collective-permute-start | bytes 294920 | tf_op jit(solution)/shard_map/ppermute | solution.py:243
  130.3 4.6 %collective-permute-start.41 = (bf16[64,768]{1,0:T(8,128)(2,1)S(1)}, bf16[64,768]{1,0:T(8,128)(2,1)S(1)}, u32[]{:S(2)}, u32[]{:S(2)}) collective-permute-start(bf16[64,768]{1,0:T(8,128)(2,1)S(1)} %collective-permute-done.40), channel_id=1, source_target_pairs={{0,4},{4,0},{8,12},{12,8},{16,20},{20,16},{24,28},{28,24},{1,5},{5... | collective-permute-start | bytes 294920 | tf_op jit(solution)/shard_map/ppermute | solution.py:241
  137.4 9.0 %collective-permute-start.25 = (bf16[1,8,32,768]{3,2,1,0:T(8,128)(2,1)S(1)}, bf16[1,8,32,768]{3,2,1,0:T(8,128)(2,1)S(1)}, u32[]{:S(2)}, u32[]{:S(2)}) collective-permute-start(bf16[1,8,32,768]{3,2,1,0:T(8,128)(2,1)S(1)} %fusion.39), channel_id=1, source_target_pairs={{0,2},{1,3},{2,0},{3,1},{4,6},{5,7},{6,4},{7,5},{8,10},{9,11},{10,... | collective-permute-start | bytes 1179656 | tf_op jit(solution)/shard_map/ppermute | solution.py:221
  147.6 28.4 %collective-permute-start.26 = (bf16[32,768]{1,0:T(8,128)(2,1)S(1)}, bf16[32,768]{1,0:T(8,128)(2,1)S(1)}, u32[]{:S(2)}, u32[]{:S(2)}) collective-permute-start(bf16[32,768]{1,0:T(8,128)(2,1)S(1)} %get-tuple-element.28), channel_id=1, source_target_pairs={{0,4},{4,0},{8,12},{12,8},{16,20},{20,16},{24,28},{28,24},{1,5},{5... | collective-permute-start | bytes 147464 | tf_op jit(solution)/shard_map/ppermute | solution.py:266
  164.4 30.1 %all-to-all-start.1 = ((bf16[8,8,6144]{2,1,0:T(8,128)(2,1)}), bf16[8,8,6144]{2,1,0:T(8,128)(2,1)S(1)}, u32[]{:S(2)}, u32[]{:S(2)}) async-start(bf16[8,8,6144]{2,1,0:T(8,128)(2,1)} %fusion.9), calls=%async_computation.1 | async-start | bytes 1572864 | tf_op jit(solution)/shard_map/all_to_all | solution.py:252
  167.9 9.9 %collective-permute-start.27 = (bf16[32,768]{1,0:T(8,128)(2,1)S(1)}, bf16[32,768]{1,0:T(8,128)(2,1)S(1)}, u32[]{:S(2)}, u32[]{:S(2)}) collective-permute-start(bf16[32,768]{1,0:T(8,128)(2,1)S(1)} %get-tuple-element.27), channel_id=1, source_target_pairs={{0,24},{4,28},{8,0},{12,4},{16,8},{20,12},{24,16},{28,20},{1,25},{... | collective-permute-start | bytes 147464 | tf_op jit(solution)/shard_map/ppermute | solution.py:266
  171.7 18.4 %collective-permute-start.28 = (bf16[32,768]{1,0:T(8,128)(2,1)S(1)}, bf16[32,768]{1,0:T(8,128)(2,1)S(1)}, u32[]{:S(2)}, u32[]{:S(2)}) collective-permute-start(bf16[32,768]{1,0:T(8,128)(2,1)S(1)} %get-tuple-element.26), channel_id=1, source_target_pairs={{0,28},{4,24},{8,4},{12,0},{16,12},{20,8},{24,20},{28,16},{1,29},{... | collective-permute-start | bytes 147464 | tf_op jit(solution)/shard_map/ppermute | solution.py:266
  173.1 17.0 %collective-permute-start.29 = (bf16[32,768]{1,0:T(8,128)(2,1)S(1)}, bf16[32,768]{1,0:T(8,128)(2,1)S(1)}, u32[]{:S(2)}, u32[]{:S(2)}) collective-permute-start(bf16[32,768]{1,0:T(8,128)(2,1)S(1)} %get-tuple-element.25), channel_id=1, source_target_pairs={{0,16},{4,20},{8,24},{12,28},{16,0},{20,4},{24,8},{28,12},{1,17},{... | collective-permute-start | bytes 147464 | tf_op jit(solution)/shard_map/ppermute | solution.py:266
  173.1 18.0 %collective-permute-start.30 = (bf16[32,768]{1,0:T(8,128)(2,1)S(1)}, bf16[32,768]{1,0:T(8,128)(2,1)S(1)}, u32[]{:S(2)}, u32[]{:S(2)}) collective-permute-start(bf16[32,768]{1,0:T(8,128)(2,1)S(1)} %get-tuple-element.24), channel_id=1, source_target_pairs={{0,20},{4,16},{8,28},{12,24},{16,4},{20,0},{24,12},{28,8},{1,21},{... | collective-permute-start | bytes 147464 | tf_op jit(solution)/shard_map/ppermute | solution.py:266
  176.0 15.1 %collective-permute-start.31 = (bf16[32,768]{1,0:T(8,128)(2,1)S(1)}, bf16[32,768]{1,0:T(8,128)(2,1)S(1)}, u32[]{:S(2)}, u32[]{:S(2)}) collective-permute-start(bf16[32,768]{1,0:T(8,128)(2,1)S(1)} %get-tuple-element.23), channel_id=1, source_target_pairs={{0,8},{4,12},{8,16},{12,20},{16,24},{20,28},{24,0},{28,4},{1,9},{5... | collective-permute-start | bytes 147464 | tf_op jit(solution)/shard_map/ppermute | solution.py:266
  177.8 14.0 %collective-permute-start.32 = (bf16[32,768]{1,0:T(8,128)(2,1)S(1)}, bf16[32,768]{1,0:T(8,128)(2,1)S(1)}, u32[]{:S(2)}, u32[]{:S(2)}) collective-permute-start(bf16[32,768]{1,0:T(8,128)(2,1)S(1)} %get-tuple-element.22), channel_id=1, source_target_pairs={{0,12},{4,8},{8,20},{12,16},{16,28},{20,24},{24,4},{28,0},{1,13},{... | collective-permute-start | bytes 147464 | tf_op jit(solution)/shard_map/ppermute | solution.py:266

commit v2 on v1

v2 whole, which is shorter than its diff:
```python
import functools

import jax
import jax.numpy as jnp
from jax import lax
from jax.experimental import pallas as pl
from jax.experimental.pallas import tpu as pltpu
from jax.sharding import PartitionSpec as P

CHUNKS = 2
F32 = jnp.float32
BF16 = jnp.bfloat16
VMEM = pl.BlockSpec(memory_space=pltpu.VMEM)
SMEM = pl.BlockSpec(memory_space=pltpu.SMEM)
HBM = pl.BlockSpec(memory_space=pltpu.HBM)


def limit(mib):
    return pltpu.CompilerParams(vmem_limit_bytes=mib * 2**20)


def rows_iota(shape):
    return lax.broadcasted_iota(jnp.int32, shape, 0).astype(F32)


def cols_iota(shape):
    return lax.broadcasted_iota(jnp.int32, shape, 1).astype(F32)


def lanes(head, size):
    return pl.ds(pl.multiple_of(head * size, size), size)


def after(value, *others):
    return lax.optimization_barrier((value, *others))[0]


def state_kernel(per_half, place_ref, decay_ref, k_ref, v_ref, *outs):
    pair = place_ref[0]
    tok, size = k_ref.shape[0], outs[0].shape[2]
    back = (tok - 1.0) - rows_iota((tok, size))
    for chunk in range(CHUNKS):
        for which in (1, 0):
            half = pair if which == 0 else 1 - pair
            heads = [chunk * 2 * per_half + half * per_half + l for l in range(per_half)]
            keys = [
                (k_ref[:, lanes(h, size)].astype(F32) * jnp.exp(-decay_ref[h] * back)).astype(BF16)
                for h in heads
            ]
            states = [
                lax.dot_general(
                    k,
                    v_ref[:, lanes(h, size)],
                    (((0,), (0,)), ((), ())),
                    preferred_element_type=F32,
                )
                for k, h in zip(keys, heads)
            ]
            for l, state in enumerate(states):
                outs[chunk * 2 + which][l] = state.astype(BF16)


def near_kernel(chunk, heads, decay_ref, q_ref, k_ref, v_ref, gate_ref, gain_ref, near_ref, scale_ref, query_ref):
    tok = q_ref.shape[0]
    size = near_ref.shape[1] // heads
    gap = rows_iota((tok, tok)) - cols_iota((tok, tok))
    ahead = jnp.maximum(gap, 0.0)
    for first in range(0, heads, 4):
        local = range(first, min(first + 4, heads))
        at = [slice((chunk * heads + l) * size, (chunk * heads + l + 1) * size) for l in local]
        scores = [
            lax.dot_general(
                q_ref[:, s], k_ref[:, s], (((1,), (1,)), ((), ())), preferred_element_type=F32
            )
            for s in at
        ]
        weights = []
        for l, score in zip(local, scores):
            mask = jnp.where(gap >= 0.0, jnp.exp(-decay_ref[chunk * heads + l] * ahead), 0.0)
            weights.append((score * mask).astype(BF16))
        for l, s, w in zip(local, at, weights):
            near_ref[:, l * size : (l + 1) * size] = jnp.dot(
                w, v_ref[:, s], preferred_element_type=F32
            )
    own = slice(chunk * heads * size, (chunk + 1) * heads * size)
    gate = gate_ref[:, own].astype(F32)
    scale_ref[...] = gain_ref[:, own] / (1.0 + jnp.exp(-gate))
    query_ref[...] = q_ref[:, own]


def mix_kernel(
    chunk, per_half, own_rows, place_ref, decay_ref, q_ref, near_ref, scale_ref, mine_ref, other_ref, out_ref
):
    pair, own = place_ref[0], place_ref[1]
    size = mine_ref.shape[2]
    tok = q_ref.shape[0]
    ahead = rows_iota((tok, size)) + 1.0
    for which in range(2):
        prior = mine_ref if which == 0 else other_ref
        half = pair if which == 0 else 1 - pair
        local = [half * per_half + l for l in range(per_half)]
        far = [
            jnp.dot(q_ref[:, lanes(h, size)], prior[l], preferred_element_type=F32)
            for l, h in enumerate(local)
        ]
        mixed = []
        for h, part in zip(local, far):
            decay = decay_ref[chunk * 2 * per_half + h]
            attended = near_ref[:, lanes(h, size)] + part * jnp.exp(-decay * ahead)
            inverse = lax.rsqrt(jnp.mean(attended * attended, axis=1, keepdims=True) + 1e-06)
            mixed.append((attended * inverse * scale_ref[:, lanes(h, size)]).astype(BF16))
        for h, rows in zip(local, mixed):
            for block in range(tok // own_rows):
                to = pl.multiple_of((block ^ own) * own_rows, own_rows)
                out_ref[pl.ds(to, own_rows), lanes(h, size)] = rows[
                    block * own_rows : (block + 1) * own_rows
                ]


def stage_kernel(first, w_ref, out_ref):
    pltpu.sync_copy(w_ref.at[0, pl.ds(first, out_ref.shape[0]), :], out_ref)


def ffn_kernel(n, parts, blocks, order_ref, *refs):
    pieces, refs = refs[:n], refs[n:]
    gain_ref, refs = refs[0], refs[1:]
    gates, ups, refs = refs[:parts], refs[parts : 2 * parts], refs[2 * parts :]
    down_ref, out_ref, rows_ref, down_buf, sems = refs
    step = out_ref.shape[1] // blocks
    copies = [
        pltpu.make_async_copy(
            down_ref.at[0, :, pl.ds(i * step, step)], down_buf.at[i], sems.at[i]
        )
        for i in range(blocks)
    ]
    for copy in copies:
        copy.start()
    cols = pieces[0].shape[1]
    total = 0.0
    for piece in pieces:
        wide = piece[...].astype(F32)
        total = total + jnp.sum(wide * wide, axis=1, keepdims=True)
    inverse = lax.rsqrt(total * (1.0 / (n * cols)) + 1e-06)
    for i, piece in enumerate(pieces):
        at = lanes(order_ref[i], cols) if n > 1 else slice(None)
        rows_ref[:, at] = (piece[...].astype(F32) * inverse * gain_ref[:, at]).astype(BF16)
    gate = up = None
    span = gates[0].shape[0]
    for i in range(parts):
        for j in range(0, span, span // 4):
            rows = rows_ref[:, i * span + j : i * span + j + span // 4]
            g = jnp.dot(rows, gates[i][j : j + span // 4, :], preferred_element_type=F32)
            u = jnp.dot(rows, ups[i][j : j + span // 4, :], preferred_element_type=F32)
            gate = g if gate is None else gate + g
            up = u if up is None else up + u
    activated = (gate / (1.0 + jnp.exp(-gate)) * up).astype(BF16)
    for i, copy in enumerate(copies):
        copy.wait()
        out_ref[:, i * step : (i + 1) * step] = jnp.dot(
            activated, down_buf[i], preferred_element_type=F32
        ).astype(BF16)


def per_device(
    stream_in,
    queries,
    key_proj,
    values,
    attn_gate,
    decay_rates,
    attn_gain,
    out_weight,
    ffn_gain,
    routing,
    route_weights,
    w_gate,
    w_up,
    w_down,
):
    tok, width = stream_in.shape
    heads = decay_rates.shape[0]
    size = queries.shape[1] // heads
    n_exp, n_ctx = lax.axis_size("exp"), lax.axis_size("ctx")
    own, place = lax.axis_index("exp"), lax.axis_index("ctx")
    groups = n_ctx // 2
    group, pair = place // 2, place % 2
    cap = tok // 16
    own_rows = tok // n_exp
    cols = out_weight.shape[1]
    hidden_units = w_gate.shape[2]
    per_half = heads // (2 * CHUNKS)
    per_chunk = heads // CHUNKS
    wide = per_chunk * size
    swap = [(i, i ^ 1) for i in range(n_ctx)]
    here = jnp.stack([pair, own]).astype(jnp.int32)

    def swapped(value):
        return lax.ppermute(value, "ctx", swap)

    def shifted(value, by):
        to = [(i, (i + 2 * by) % n_ctx) for i in range(n_ctx)]
        return lax.ppermute(value, "ctx", to)

    states = pl.pallas_call(
        functools.partial(state_kernel, per_half),
        out_shape=[jax.ShapeDtypeStruct((per_half, size, size), BF16)] * (2 * CHUNKS),
        in_specs=[SMEM, SMEM, VMEM, VMEM],
        out_specs=[VMEM] * (2 * CHUNKS),
        compiler_params=limit(8),
        name="shard_state",
    )(here, decay_rates, key_proj, values)

    def near_part(chunk, start):
        return pl.pallas_call(
            functools.partial(near_kernel, chunk, per_chunk),
            out_shape=[
                jax.ShapeDtypeStruct((tok, wide), F32),
                jax.ShapeDtypeStruct((tok, wide), F32),
                jax.ShapeDtypeStruct((tok, wide), BF16),
            ],
            in_specs=[SMEM] + [VMEM] * 5,
            out_specs=[VMEM] * 3,
            compiler_params=limit(8),
            name="near_part",
        )(after(decay_rates, start), queries, key_proj, values, attn_gate, attn_gain[None, :])

    rates, lowers, spans, windows, priors, nears = [], [], [], [], [], []
    for chunk in range(CHUNKS):
        keep, send = states[2 * chunk], states[2 * chunk + 1]
        got = swapped(send)
        nears.append(near_part(chunk, states[0] if chunk == 0 else windows[0]))
        first = chunk * per_chunk + pair * per_half
        rate = lax.dynamic_slice_in_dim(decay_rates, first, per_half, 0)[:, None, None]
        span = jnp.exp(-rate * tok)
        lower = jnp.where(pair == 0, keep, got).astype(F32)
        upper = jnp.where(pair == 0, got, keep).astype(F32)
        windows.append((span * lower + upper).astype(BF16))
        rates.append(rate)
        spans.append(span)
        lowers.append(lower)
        priors.append(jnp.zeros(lower.shape, F32))
    reach = 1
    while reach < groups:
        line = [(i, i + 2 * reach) for i in range(n_ctx - 2 * reach)]
        for chunk in range(CHUNKS):
            got = lax.ppermute(windows[chunk], "ctx", line).astype(F32)
            factor = jnp.exp(-rates[chunk] * (2 * tok * (reach - 1)))
            priors[chunk] = priors[chunk] + factor * got
            if 2 * reach < groups:
                factor = jnp.exp(-rates[chunk] * (2 * tok * reach))
                windows[chunk] = (windows[chunk].astype(F32) + factor * got).astype(BF16)
        reach *= 2
    mixed = []
    for chunk in range(CHUNKS):
        prior = priors[chunk]
        second = spans[chunk] * prior + lowers[chunk]
        mine = jnp.where(pair == 0, prior, second).astype(BF16)
        other = swapped(jnp.where(pair == 0, second, prior).astype(BF16))
        near, scale, query = nears[chunk]
        mixed.append(
            pl.pallas_call(
                functools.partial(mix_kernel, chunk, per_half, own_rows),
                out_shape=jax.ShapeDtypeStruct((tok, wide), BF16),
                in_specs=[SMEM, SMEM] + [VMEM] * 5,
                out_specs=VMEM,
                compiler_params=limit(8),
                name="mix_heads",
            )(here, decay_rates, query, near, scale, mine, other)
        )

    routing = after(routing, mixed[0])
    hit = routing[:, :, None] == jnp.arange(n_exp, dtype=jnp.int32)
    member = jnp.any(hit, axis=1)
    gate_of = jnp.sum(jnp.where(hit, route_weights[:, :, None], 0.0), axis=1)
    position = jnp.arange(tok, dtype=jnp.int32)
    before = (position[:, None] > position[None, :]).astype(BF16)
    rank = jnp.dot(before, member.astype(BF16), preferred_element_type=F32)
    pick = member[:, :, None] & (rank[:, :, None] == jnp.arange(cap, dtype=F32))
    number = jnp.sum(jnp.where(pick, (position + 1).astype(F32)[:, None, None], 0.0), axis=0)
    own_pick = lax.dynamic_index_in_dim(pick, own, 1, keepdims=False)
    own_weight = jnp.sum(
        jnp.where(own_pick, lax.dynamic_index_in_dim(gate_of, own, 1), 0.0), axis=0
    )
    stream_slots = lax.dot_general(
        own_pick.astype(BF16), stream_in, (((0,), (0,)), ((), ())), preferred_element_type=F32
    ).astype(BF16)
    parcel = stream_slots.reshape(cap, n_ctx, cols).transpose(1, 0, 2)
    label = jnp.pad(number.reshape(1, n_exp * cap), ((0, cap - 1), (0, cols - n_exp * cap)))
    label = jnp.broadcast_to(label.astype(BF16)[None], (n_ctx, cap, cols))
    parcel = jnp.concatenate([parcel, label], axis=1)

    totals = [None] * n_ctx
    arrived = None
    staged = {}
    parts = 2
    for chunk in range(CHUNKS):
        weight = out_weight[chunk * wide : (chunk + 1) * wide]
        current, crossed = mixed[chunk], None
        for step in range(groups):
            if chunk % 2 and step == 1:
                crossed = shifted(crossed, 1)
            else:
                crossed = swapped(current)
            for y, rows in enumerate((current, crossed)):
                at = 2 * step + y
                part = jnp.dot(rows, weight, preferred_element_type=F32)
                totals[at] = part if totals[at] is None else totals[at] + part
            if step + 1 < groups:
                current = shifted(current, 1)
            if chunk == CHUNKS - 1 and step < parts:
                for name, w in (("gate", w_gate), ("up", w_up)):
                    staged[name, step] = pl.pallas_call(
                        functools.partial(stage_kernel, step * (width // parts)),
                        out_shape=pltpu.VMEM((width // parts, hidden_units), BF16),
                        in_specs=[HBM],
                        out_specs=VMEM,
                        compiler_params=limit(2),
                        name="stage_weight",
                    )(pltpu.with_memory_space_constraint(after(w, current), pltpu.HBM))
        if chunk == 0:
            arrived = lax.all_to_all(
                after(parcel, current), "ctx", split_axis=0, concat_axis=0, tiled=True
            )
    partial = jnp.concatenate([t.astype(BF16) for t in totals], axis=0)

    stream_rows = arrived[:, :cap].reshape(n_ctx * cap, cols)
    token = arrived[:, cap, : n_exp * cap].astype(jnp.int32).reshape(n_ctx, n_exp, cap) - 1
    shard = jnp.arange(n_ctx, dtype=jnp.int32)
    block = ((group - shard // 2) % groups) * 2 + (pair ^ (shard % 2))
    token = jnp.stack(
        [lax.dynamic_index_in_dim(token, own ^ j, 1, keepdims=False) for j in range(n_exp)]
    )
    column = block[None, :, None] * tok + ((token // own_rows) ^ own) * own_rows + token % own_rows
    column = jnp.where(token >= 0, column, -1).reshape(-1)
    chosen = (column[:, None] == jnp.arange(n_ctx * tok, dtype=jnp.int32)[None, :]).astype(BF16)

    def add_groups(parts):
        bit = 1
        parts = list(parts)
        while bit < n_exp:
            far = [j for j in range(0, n_exp, bit) if j & bit]
            sent = jnp.stack([parts[j // bit] for j in far])
            got = lax.ppermute(sent, "exp", [(i, i ^ bit) for i in range(n_exp)])
            parts = [
                parts[j // bit - 1].astype(F32) + got[n].astype(F32) for n, j in enumerate(far)
            ]
            bit *= 2
            if bit < n_exp:
                parts = [p.astype(BF16) for p in parts]
        return parts[0]

    slot_rows = jnp.dot(chosen, partial, preferred_element_type=F32).astype(BF16)
    slot_total = add_groups(slot_rows.reshape(n_exp, n_ctx * cap, cols))
    hidden = (slot_total + stream_rows.astype(F32)).astype(BF16)

    pieces = {0: hidden}
    bit = 1
    while bit < groups:
        for r in range(bit):
            pieces[r | bit] = lax.ppermute(
                pieces[r], "ctx", [(i, i ^ (2 * bit)) for i in range(n_ctx)]
            )
        bit *= 2
    pieces = [p for r in range(groups) for p in (pieces[r], swapped(pieces[r]))]
    source = (place ^ shard).astype(jnp.int32)
    if cols % 128:
        pieces = [jnp.take(jnp.stack(pieces), source, axis=0).transpose(1, 0, 2).reshape(-1, width)]
    blocks = 8
    down = pl.pallas_call(
        functools.partial(ffn_kernel, len(pieces), parts, blocks),
        out_shape=jax.ShapeDtypeStruct((n_ctx * cap, width), BF16),
        in_specs=[SMEM] + [VMEM] * (len(pieces) + 1 + 2 * parts) + [HBM],
        out_specs=VMEM,
        scratch_shapes=[
            pltpu.VMEM((n_ctx * cap, width), BF16),
            pltpu.VMEM((blocks, hidden_units, width // blocks), BF16),
            pltpu.SemaphoreType.DMA((blocks,)),
        ],
        compiler_params=limit(24),
        name="expert",
    )(
        source,
        *pieces,
        ffn_gain[None, :],
        *(
            pltpu.with_memory_space_constraint(staged[name, i], pltpu.VMEM)
            for name in ("gate", "up")
            for i in range(parts)
        ),
        pltpu.with_memory_space_constraint(w_down, pltpu.HBM),
    )
    received = lax.all_to_all(
        down.reshape(n_ctx, cap, width), "ctx", split_axis=0, concat_axis=0, tiled=True
    )
    summed = jnp.sum(received.astype(F32), axis=0)
    expert_out = (summed * own_weight[:, None]).astype(BF16).reshape(1, 1, cap, width)

    bulk = after(partial, hidden).reshape(groups, 2, n_exp, own_rows, cols)
    bulk = add_groups([bulk[:, :, j] for j in range(n_exp)]).astype(BF16)
    bulk = [bulk[:, 0], swapped(bulk[:, 1])]
    bulk = [jnp.stack([bulk[0][k], bulk[1][k]]) for k in range(groups)]
    bit = 1
    while bit < groups:
        moving = [k for k in range(groups) if k & bit]
        moved = shifted(jnp.stack([bulk[k] for k in moving]), -bit)
        for n, k in enumerate(moving):
            bulk[k] = moved[n]
        bit *= 2
    order = ((shard // 2 - group) % groups) * 2 + (pair ^ (shard % 2))
    projected = jnp.take(jnp.concatenate(bulk), order, axis=0).transpose(1, 0, 2)
    projected = projected.reshape(own_rows, width)
    stream_own = lax.dynamic_slice_in_dim(stream_in, own * own_rows, own_rows, 0)
    residual_out = (stream_own.astype(F32) + projected.astype(F32)).astype(BF16)
    return (residual_out, expert_out)


def solution(mesh):
    return jax.shard_map(
        per_device,
        mesh=mesh,
        in_specs=(
            P("ctx", None),
            P("ctx", "exp"),
            P("ctx", "exp"),
            P("ctx", "exp"),
            P("ctx", "exp"),
            P("exp"),
            P("exp"),
            P("exp", "ctx"),
            P(),
            P("ctx", None),
            P("ctx", None),
            P("exp", None, "ctx"),
            P("exp", None, "ctx"),
            P("exp", "ctx", None),
        ),
        out_specs=(P(("ctx", "exp"), None), P("ctx", "exp", None, None)),
        check_vma=False,
    )
```

time: 196 us -> 192 us (0.980)
  Pallas kernels: 12.8 us -> 29.2 us
  matrix products: 34 us -> 22.4 us
  starting transfers between devices: 85 us -> 73.9 us
  other arithmetic: 11.5 us -> 7 us
  waiting for transfers between devices: 46.7 us -> 51.1 us
    dot_general x2 -> x0, matrix products: 22.4 us -> none  [the longest x1 14.9 us: per_device(): jnp.dot(activated, w_down[0], preferred_element_type=F32).astype(BF16)]
    pallas_call x1 -> x7, Pallas kernels: 4.94 us -> 26.3 us  [the longest x4 12 us: per_device(): pl.pallas_call(functools.partial(stage_kernel, step * (width // parts)),...]
    dot_general x16, matrix products: 9.13 us -> 19.9 us  [per_device(): part = jnp.dot(rows, weight, preferred_element_type=F32)]
    ppermute x38 -> x32, starting transfers between devices: 72 us -> 63.1 us  [the longest x9 19 us: shifted(): return lax.ppermute(value, 'ctx', to)]
    pallas_call x2, Pallas kernels: 5.5 us -> 1.89 us  [per_device(): pl.pallas_call(functools.partial(mix_kernel, chunk, per_half, own_rows),...]
    ppermute x4, waiting for transfers between devices: 3.74 us -> 6.97 us  [add_groups(): got = lax.ppermute(sent, 'exp', [(i, i ^ bit) for i in range(n_exp)])]
    all_to_all x1, starting transfers between devices: 6.26 us -> 3.57 us  [per_device(): lax.all_to_all(after(parcel, current), 'ctx', split_axis=0, concat_axis=0...]
    ppermute x38 -> x32, waiting for transfers between devices: 43 us -> 44.2 us  [the longest x9 24.2 us: shifted(): return lax.ppermute(value, 'ctx', to)]
  transfers between devices with their start and end apart: 44 -> 38, of which waited for: 16 -> 17; matrix products, arithmetic and copies ran while one was open for 22% -> 13% of each run, Pallas kernels for 5% -> 15%
where the time goes in v2:
time: 192 us; the launch traced here: 190 us
  starting transfers between devices  73.9 us (38%)
  waiting for transfers between devices  51.1 us (27%)
  Pallas kernels  29.2 us (15%)
  matrix products  22.4 us (12%)
  other arithmetic  7 us (4%)
  local copies, waits for them, and re-layouts  5.16 us (3%)
    ppermute x9, waiting for transfers between devices, shifted(): return lax.ppermute(value, 'ctx', to)  24.2 us
    dot_general x16, matrix products, per_device(): part = jnp.dot(rows, weight, preferred_element_type=F32)  19.9 us
    ppermute x9, starting transfers between devices, shifted(): return lax.ppermute(value, 'ctx', to)  19 us
    ppermute x16, starting transfers between devices, swapped(): return lax.ppermute(value, 'ctx', swap)  18.7 us
    ppermute x4, starting transfers between devices, per_device(): got = lax.ppermute(windows[chunk], 'ctx', line).astype(F32)  18 us
    ppermute x16, waiting for transfers between devices, swapped(): return lax.ppermute(value, 'ctx', swap)  16.1 us
    pallas_call x4, Pallas kernels, per_device(): pl.pallas_call(functools.partial(stage_kernel, step * (width // parts)),...  12 us
    pallas_call x1, Pallas kernels, per_device(): pl.pallas_call(functools.partial(ffn_kernel, len(pieces), parts, blocks),...  11.9 us
  transfers between devices with their start and end apart: 38, of which 17 were waited for; matrix products, arithmetic and copies ran while one was open for 13% of the time, Pallas kernels for 15%

profile of v2, /device:TPU:0, one launch (start us, length us, event | category | flops | bytes accessed | tf_op | source)
XLA Modules:
  0.0 190.1 jit_solution(17970282997603685499)
XLA Ops:
  0.7 1.0 copy-done
  1.8 1.0 copy-done.2
  3.5 1.0 shard_state.1
  4.5 3.0 %collective-permute-start = (bf16[4,128,128]{2,1,0:T(8,128)(2,1)S(1)}, bf16[4,128,128]{2,1,0:T(8,128)(2,1)S(1)}, u32[]{:S(2)}, u32[]{:S(2)}) collective-permute-start(bf16[4,128,128]{2,1,0:T(8,128)(2,1)S(1)} %get-tuple-element.26), channel_id=1, source_target_pairs={{0,4},{4,0},{8,12},{12,8},{16,20},{20,16},{24,28},{28,24},{1,5},{5... | collective-permute-start | bytes 393224 | tf_op jit(solution)/shard_map/ppermute | solution.py:198
  7.7 4.2 %collective-permute-done = bf16[4,128,128]{2,1,0:T(8,128)(2,1)S(1)} collective-permute-done((bf16[4,128,128]{2,1,0:T(8,128)(2,1)S(1)}, bf16[4,128,128]{2,1,0:T(8,128)(2,1)S(1)}, u32[]{:S(2)}, u32[]{:S(2)}) %collective-permute-start) | collective-permute-done | bytes 131104 | tf_op jit(solution)/shard_map/ppermute | solution.py:198
  12.0 4.2 %collective-permute-start.1 = (bf16[4,128,128]{2,1,0:T(8,128)(2,1)S(1)}, bf16[4,128,128]{2,1,0:T(8,128)(2,1)S(1)}, u32[]{:S(2)}, u32[]{:S(2)}) collective-permute-start(bf16[4,128,128]{2,1,0:T(8,128)(2,1)S(1)} %fusion.45), channel_id=1, source_target_pairs={{0,8},{4,12},{8,16},{12,20},{16,24},{20,28},{1,9},{5,13},{9,17},{1... | collective-permute-start | bytes 393224 | tf_op jit(solution)/shard_map/ppermute | solution.py:246
  16.3 3.5 %collective-permute-start.5 = (bf16[4,128,128]{2,1,0:T(8,128)(2,1)S(1)}, bf16[4,128,128]{2,1,0:T(8,128)(2,1)S(1)}, u32[]{:S(2)}, u32[]{:S(2)}) collective-permute-start(bf16[4,128,128]{2,1,0:T(8,128)(2,1)S(1)} %fusion.50), channel_id=1, source_target_pairs={{0,8},{4,12},{8,16},{12,20},{16,24},{20,28},{1,9},{5,13},{9,17},{1... | collective-permute-start | bytes 393224 | tf_op jit(solution)/shard_map/ppermute | solution.py:246
  20.0 5.4 %collective-permute-start.2 = (bf16[4,128,128]{2,1,0:T(8,128)(2,1)S(1)}, bf16[4,128,128]{2,1,0:T(8,128)(2,1)S(1)}, u32[]{:S(2)}, u32[]{:S(2)}) collective-permute-start(bf16[4,128,128]{2,1,0:T(8,128)(2,1)S(1)} %fusion.48), channel_id=1, source_target_pairs={{0,16},{4,20},{8,24},{12,28},{1,17},{5,21},{9,25},{13,29},{2,18},{... | collective-permute-start | bytes 393224 | tf_op jit(solution)/shard_map/ppermute | solution.py:246
  25.5 5.0 %collective-permute-start.6 = (bf16[4,128,128]{2,1,0:T(8,128)(2,1)S(1)}, bf16[4,128,128]{2,1,0:T(8,128)(2,1)S(1)}, u32[]{:S(2)}, u32[]{:S(2)}) collective-permute-start(bf16[4,128,128]{2,1,0:T(8,128)(2,1)S(1)} %fusion.53), channel_id=1, source_target_pairs={{0,16},{4,20},{8,24},{12,28},{1,17},{5,21},{9,25},{13,29},{2,18},{... | collective-permute-start | bytes 393224 | tf_op jit(solution)/shard_map/ppermute | solution.py:246
  30.7 1.6 collective-permute-start.3
  33.2 1.6 collective-permute-start.7
  35.0 1.2 near_part.2
  36.2 1.2 near_part.3
  39.2 2.8 %collective-permute-start.11 = (bf16[128,1024]{1,0:T(8,128)(2,1)S(1)}, bf16[128,1024]{1,0:T(8,128)(2,1)S(1)}, u32[]{:S(2)}, u32[]{:S(2)}) collective-permute-start(bf16[128,1024]{1,0:T(8,128)(2,1)S(1)} %mix_heads.3), channel_id=1, source_target_pairs={{0,8},{4,12},{8,16},{12,20},{16,24},{20,28},{24,0},{28,4},{1,9},{5... | collective-permute-start | bytes 786440 | tf_op jit(solution)/shard_map/ppermute | solution.py:202
  42.0 1.7 collective-permute-start.9
  44.6 1.1 collective-permute-start.10
  46.3 1.1 fusion.34
  48.8 2.8 %fusion.1 = bf16[1024,768]{1,0:T(8,128)(2,1)} fusion(f32[128,768]{1,0:T(8,128)S(1)} %copy-done.16, bf16[128,1024]{1,0:T(8,128)(2,1)S(1)} %mix_heads.2, bf16[2048,768]{1,0:T(8,128)(2,1)} %param.21), kind=kOutput, calls=%fused_computation.13 | convolution fusion | flops 201523200 | bytes 2424832 | tf_op jit(solution)/shard_map/dot_general | solution.py:306
  51.6 3.8 %collective-permute-done.10 = bf16[128,1024]{1,0:T(8,128)(2,1)S(1)} collective-permute-done((bf16[128,1024]{1,0:T(8,128)(2,1)S(1)}, bf16[128,1024]{1,0:T(8,128)(2,1)S(1)}, u32[]{:S(2)}, u32[]{:S(2)}) %collective-permute-start.10) | collective-permute-done | bytes 262176 | tf_op jit(solution)/shard_map/ppermute | solution.py:202
  55.9 2.2 %collective-permute-start.13 = (bf16[128,1024]{1,0:T(8,128)(2,1)S(1)}, bf16[128,1024]{1,0:T(8,128)(2,1)S(1)}, u32[]{:S(2)}, u32[]{:S(2)}) collective-permute-start(bf16[128,1024]{1,0:T(8,128)(2,1)S(1)} %collective-permute-done.9), channel_id=1, source_target_pairs={{0,8},{4,12},{8,16},{12,20},{16,24},{20,28},{24,0},{28,4},{1,9},{5... | collective-permute-start | bytes 786440 | tf_op jit(solution)/shard_map/ppermute | solution.py:202
  58.5 2.1 %collective-permute-start.15 = (bf16[128,1024]{1,0:T(8,128)(2,1)S(1)}, bf16[128,1024]{1,0:T(8,128)(2,1)}, u32[]{:S(2)}, u32[]{:S(2)}) collective-permute-start(bf16[128,1024]{1,0:T(8,128)(2,1)S(1)} %collective-permute-done.11), channel_id=1, source_target_pairs={{0,8},{4,12},{8,16},{12,20},{16,24},{20,28},{24,0},{28,4},{1,9},{5... | collective-permute-start | bytes 786440 | tf_op jit(solution)/shard_map/ppermute | solution.py:202
  61.1 2.0 %fusion.3 = bf16[1024,768]{1,0:T(8,128)(2,1)} fusion(bf16[1024,768]{1,0:T(8,128)(2,1)} %fusion.1, f32[128,768]{1,0:T(8,128)S(1)} %fusion.32, bf16[128,1024]{1,0:T(8,128)(2,1)} %collective-permute-done.8, bf16[2048,768]{1,0:T(8,128)(2,1)S(1)} %copy-done.14), kind=kOutput, calls=%fused_computation.15 | convolution fusion | flops 201523200 | bytes 2424832 | tf_op jit(solution)/shard_map/dot_general | solution.py:306
  63.1 1.1 fusion.5
  64.1 8.8 %collective-permute-done.15 = bf16[128,1024]{1,0:T(8,128)(2,1)} collective-permute-done((bf16[128,1024]{1,0:T(8,128)(2,1)S(1)}, bf16[128,1024]{1,0:T(8,128)(2,1)}, u32[]{:S(2)}, u32[]{:S(2)}) %collective-permute-start.15) | collective-permute-done | bytes 262176 | tf_op jit(solution)/shard_map/ppermute | solution.py:202
  73.1 2.6 %collective-permute-start.18 = (bf16[128,1024]{1,0:T(8,128)(2,1)S(1)}, bf16[128,1024]{1,0:T(8,128)(2,1)}, u32[]{:S(2)}, u32[]{:S(2)}) collective-permute-start(bf16[128,1024]{1,0:T(8,128)(2,1)S(1)} %collective-permute-done.14), channel_id=1, source_target_pairs={{0,8},{4,12},{8,16},{12,20},{16,24},{20,28},{24,0},{28,4},{1,9},{5... | collective-permute-start | bytes 786440 | tf_op jit(solution)/shard_map/ppermute | solution.py:202
  75.7 1.3 fusion.26
  77.1 1.6 collective-permute-start.16
  79.1 1.1 fusion.7
  80.2 1.1 fusion.9
  81.2 4.0 %collective-permute-done.18 = bf16[128,1024]{1,0:T(8,128)(2,1)} collective-permute-done((bf16[128,1024]{1,0:T(8,128)(2,1)S(1)}, bf16[128,1024]{1,0:T(8,128)(2,1)}, u32[]{:S(2)}, u32[]{:S(2)}) %collective-permute-start.18) | collective-permute-done | bytes 262176 | tf_op jit(solution)/shard_map/ppermute | solution.py:202
  85.2 3.6 %all-to-all-start = ((bf16[8,16,768]{2,1,0:T(8,128)(2,1)}), bf16[8,16,768]{2,1,0:T(8,128)(2,1)S(1)}, u32[]{:S(2)}, u32[]{:S(2)}) async-start(bf16[8,16,768]{2,1,0:T(8,128)(2,1)} %pad_maximum_fusion.1), calls=%async_computation | async-start | bytes 393216 | tf_op jit(solution)/shard_map/all_to_all | solution.py:321
  88.8 1.7 collective-permute-start.20
  90.9 1.9 %fusion.22 = f32[128,768]{1,0:T(8,128)S(1)} fusion(bf16[128,1024]{1,0:T(8,128)(2,1)S(1)} %collective-permute-done.19, bf16[2048,768]{1,0:T(8,128)(2,1)} %param.21), kind=kOutput, calls=%fused_computation.54 | convolution fusion | flops 201326592 | bytes 2228224 | tf_op jit(solution)/shard_map/dot_general | solution.py:306
  92.8 1.9 fusion.24
  94.7 1.1 fusion.11
  95.8 2.0 %fusion.13 = bf16[1024,768]{1,0:T(8,128)(2,1)} fusion(bf16[1024,768]{1,0:T(8,128)(2,1)} %fusion.11, f32[128,768]{1,0:T(8,128)S(1)} %fusion.22, bf16[128,1024]{1,0:T(8,128)(2,1)} %collective-permute-done.18, bf16[2048,768]{1,0:T(8,128)(2,1)S(1)} %copy-done.15), kind=kOutput, calls=%fused_computation.25 | convolution fusion | flops 201523200 | bytes 2424832 | tf_op jit(solution)/shard_map/dot_general | solution.py:306
  97.8 1.2 collective-permute-done.21
  99.4 1.1 fusion.15
  100.7 2.0 %convolution_convert_fusion.1 = bf16[256,768]{1,0:T(8,128)(2,1)S(1)} fusion(bf16[1024,768]{1,0:T(8,128)(2,1)} %fusion.15, s32[256]{0:T(256)S(1)} %compare_select_fusion.8), kind=kOutput, calls=%fused_computation.3 | convolution fusion | flops 403111936 | bytes 1967104 | tf_op jit(solution)/shard_map/dot_general | solution.py:352
  102.9 1.4 collective-permute-done.22
  104.4 1.6 collective-permute-start.23
  106.0 3.3 %collective-permute-done.23 = bf16[1,64,768]{2,1,0:T(8,128)(2,1)S(1)} collective-permute-done((bf16[1,64,768]{2,1,0:T(8,128)(2,1)S(1)}, bf16[1,64,768]{2,1,0:T(8,128)(2,1)S(1)}, u32[]{:S(2)}, u32[]{:S(2)}) %collective-permute-start.23) | collective-permute-done | bytes 98336 | tf_op jit(solution)/shard_map/ppermute | solution.py:343
  109.3 1.2 slice_bitcast_fusion.3
  110.7 2.2 %collective-permute-done.24 = bf16[2,4,2,32,768]{4,3,2,1,0:T(8,128)(2,1)S(1)} collective-permute-done((bf16[2,4,2,32,768]{4,3,2,1,0:T(8,128)(2,1)S(1)}, bf16[2,4,2,32,768]{4,3,2,1,0:T(8,128)(2,1)S(1)}, u32[]{:S(2)}, u32[]{:S(2)}) %collective-permute-start.24) | collective-permute-done | bytes 786464 | tf_op jit(solution)/shard_map/ppermute | solution.py:343
  113.0 1.8 fusion.17
  114.8 1.5 collective-permute-start.25
  116.3 1.7 collective-permute-start.30
  118.0 2.3 %collective-permute-start.32 = (bf16[64,768]{1,0:T(8,128)(2,1)S(1)}, bf16[64,768]{1,0:T(8,128)(2,1)S(1)}, u32[]{:S(2)}, u32[]{:S(2)}) collective-permute-start(bf16[64,768]{1,0:T(8,128)(2,1)S(1)} %fusion.54.refs_0_), channel_id=1, source_target_pairs={{0,16},{4,20},{8,24},{12,28},{16,0},{20,4},{24,8},{28,12},{1,17},{... | collective-permute-start | bytes 294920 | tf_op jit(solution)/shard_map/ppermute | solution.py:360
  121.0 3.3 %collective-permute-start.34 = (bf16[64,768]{1,0:T(8,128)(2,1)S(1)}, bf16[64,768]{1,0:T(8,128)(2,1)S(1)}, u32[]{:S(2)}, u32[]{:S(2)}) collective-permute-start(bf16[64,768]{1,0:T(8,128)(2,1)S(1)} %collective-permute-done.30.refs_2_), channel_id=1, source_target_pairs={{0,16},{4,20},{8,24},{12,28},{16,0},{20,4},{24,8},{28,12},{1,17},{... | collective-permute-start | bytes 294920 | tf_op jit(solution)/shard_map/ppermute | solution.py:360
  125.3 1.1 collective-permute-start.31
  126.4 1.9 collective-permute-done.32.refs_4_
  130.6 3.0 %stage_weight.4.refs_9_ = bf16[3072,1152]{1,0:T(8,128)(2,1)S(1)} custom-call(bf16[1,6144,1152]{2,1,0:T(8,128)(2,1)} %w_ref.1), custom_call_target="tpu_custom_call" | custom-call | tf_op jit(solution)/shard_map/stage_weight/pallas_call | solution.py:312
  133.6 3.0 %stage_weight.6.refs_11_ = bf16[3072,1152]{1,0:T(8,128)(2,1)S(1)} custom-call(bf16[1,6144,1152]{2,1,0:T(8,128)(2,1)} %w_ref.3), custom_call_target="tpu_custom_call" | custom-call | tf_op jit(solution)/shard_map/stage_weight/pallas_call | solution.py:312
  136.6 3.0 %stage_weight.5.refs_10_ = bf16[3072,1152]{1,0:T(8,128)(2,1)S(1)} custom-call(bf16[1,6144,1152]{2,1,0:T(8,128)(2,1)} %w_ref.1), custom_call_target="tpu_custom_call" | custom-call | tf_op jit(solution)/shard_map/stage_weight/pallas_call | solution.py:312
  139.6 3.0 %stage_weight.7.refs_12_ = bf16[3072,1152]{1,0:T(8,128)(2,1)S(1)} custom-call(bf16[1,6144,1152]{2,1,0:T(8,128)(2,1)} %w_ref.3), custom_call_target="tpu_custom_call" | custom-call | tf_op jit(solution)/shard_map/stage_weight/pallas_call | solution.py:312
  142.6 11.9 %expert.1 = bf16[64,6144]{1,0:T(8,128)(2,1)} custom-call(s32[8]{0:T(128)S(1)} %iota_xor_fusion.order_ref, bf16[64,768]{1,0:T(8,128)(2,1)S(1)} %fusion.54.refs_0_, bf16[64,768]{1,0:T(8,128)(2,1)S(1)} %collective-permute-done.29.refs_1_, bf16[64,768]{1,0:T(8,128)(2,1)S(1)} %collective-permute-done.30.refs_2_, ...), custom_call_target="tpu_custom_call" | custom-call | tf_op jit(solution)/shard_map/expert/pallas_call | solution.py:369
  154.5 4.0 %all-to-all-start.1 = ((bf16[8,8,6144]{2,1,0:T(8,128)(2,1)}), bf16[8,8,6144]{2,1,0:T(8,128)(2,1)S(1)}, u32[]{:S(2)}, u32[]{:S(2)}) async-start(bf16[8,8,6144]{2,1,0:T(8,128)(2,1)} %bitcast.37), calls=%async_computation.1 | async-start | bytes 1572864 | tf_op jit(solution)/shard_map/all_to_all | solution.py:392
  158.5 1.1 fusion.16
  159.7 2.1 %collective-permute-start.26 = (bf16[4,32,768]{2,1,0:T(8,128)(2,1)S(1)}, bf16[4,32,768]{2,1,0:T(8,128)(2,1)S(1)}, u32[]{:S(2)}, u32[]{:S(2)}) collective-permute-start(bf16[4,32,768]{2,1,0:T(8,128)(2,1)S(1)} %slice_bitcast_fusion.5), channel_id=1, source_target_pairs={{0,4},{4,0},{8,12},{12,8},{16,20},{20,16},{24,28},{28,24},{1,5},{5... | collective-permute-start | bytes 589832 | tf_op jit(solution)/shard_map/ppermute | solution.py:198
  161.8 9.9 %collective-permute-done.26 = bf16[4,32,768]{2,1,0:T(8,128)(2,1)S(1)} collective-permute-done((bf16[4,32,768]{2,1,0:T(8,128)(2,1)S(1)}, bf16[4,32,768]{2,1,0:T(8,128)(2,1)S(1)}, u32[]{:S(2)}, u32[]{:S(2)}) %collective-permute-start.26) | collective-permute-done | bytes 196640 | tf_op jit(solution)/shard_map/ppermute | solution.py:198
  171.8 4.4 %collective-permute-start.27 = (bf16[2,2,32,768]{3,2,1,0:T(8,128)(2,1)S(1)}, bf16[2,2,32,768]{3,2,1,0:T(8,128)(2,1)S(1)}, u32[]{:S(2)}, u32[]{:S(2)}) collective-permute-start(bf16[2,2,32,768]{3,2,1,0:T(8,128)(2,1)S(1)} %pad_maximum_fusion.3), channel_id=1, source_target_pairs={{0,24},{4,28},{8,0},{12,4},{16,8},{20,12},{24,16},{28,20},{1,25},{... | collective-permute-start | bytes 589832 | tf_op jit(solution)/shard_map/ppermute | solution.py:202
  176.3 3.2 %collective-permute-done.27 = bf16[2,2,32,768]{3,2,1,0:T(8,128)(2,1)S(1)} collective-permute-done((bf16[2,2,32,768]{3,2,1,0:T(8,128)(2,1)S(1)}, bf16[2,2,32,768]{3,2,1,0:T(8,128)(2,1)S(1)}, u32[]{:S(2)}, u32[]{:S(2)}) %collective-permute-start.27) | collective-permute-done | bytes 196640 | tf_op jit(solution)/shard_map/ppermute | solution.py:202
  179.6 3.7 %collective-permute-start.28 = (bf16[2,2,32,768]{3,2,1,0:T(8,128)(2,1)S(1)}, bf16[2,2,32,768]{3,2,1,0:T(8,128)(2,1)S(1)}, u32[]{:S(2)}, u32[]{:S(2)}) collective-permute-start(bf16[2,2,32,768]{3,2,1,0:T(8,128)(2,1)S(1)} %pad_maximum_fusion.4), channel_id=1, source_target_pairs={{0,16},{4,20},{8,24},{12,28},{16,0},{20,4},{24,8},{28,12},{1,17},{... | collective-permute-start | bytes 589832 | tf_op jit(solution)/shard_map/ppermute | solution.py:202
  184.1 4.3 %collective-permute-done.28 = bf16[2,2,32,768]{3,2,1,0:T(8,128)(2,1)S(1)} collective-permute-done((bf16[2,2,32,768]{3,2,1,0:T(8,128)(2,1)S(1)}, bf16[2,2,32,768]{3,2,1,0:T(8,128)(2,1)S(1)}, u32[]{:S(2)}, u32[]{:S(2)}) %collective-permute-start.28) | collective-permute-done | bytes 196640 | tf_op jit(solution)/shard_map/ppermute | solution.py:202
  (133 shorter events, 17.0 us)
Async XLA Ops:
  0.7 1.0 copy-start
  1.8 1.0 copy-start.2
  2.8 0.7 copy-start.7
  4.5 7.4 %collective-permute-start = (bf16[4,128,128]{2,1,0:T(8,128)(2,1)S(1)}, bf16[4,128,128]{2,1,0:T(8,128)(2,1)S(1)}, u32[]{:S(2)}, u32[]{:S(2)}) collective-permute-start(bf16[4,128,128]{2,1,0:T(8,128)(2,1)S(1)} %get-tuple-element.26), channel_id=1, source_target_pairs={{0,4},{4,0},{8,12},{12,8},{16,20},{20,16},{24,28},{28,24},{1,5},{5... | collective-permute-start | bytes 393224 | tf_op jit(solution)/shard_map/ppermute | solution.py:198
  7.5 8.6 %collective-permute-start.4 = (bf16[4,128,128]{2,1,0:T(8,128)(2,1)S(1)}, bf16[4,128,128]{2,1,0:T(8,128)(2,1)S(1)}, u32[]{:S(2)}, u32[]{:S(2)}) collective-permute-start(bf16[4,128,128]{2,1,0:T(8,128)(2,1)S(1)} %get-tuple-element.32), channel_id=1, source_target_pairs={{0,4},{4,0},{8,12},{12,8},{16,20},{20,16},{24,28},{28,24},{1,5},{5... | collective-permute-start | bytes 393224 | tf_op jit(solution)/shard_map/ppermute | solution.py:198
  11.9 23.1 %copy-start.1 = (bf16[128,2048]{1,0:T(8,128)(2,1)S(1)}, bf16[128,2048]{1,0:T(8,128)(2,1)}, u32[]{:S(2)}) copy-start(bf16[128,2048]{1,0:T(8,128)(2,1)} %k_ref.5) | copy-start | bytes 1572868
  11.9 23.1 %copy-start.3 = (bf16[128,2048]{1,0:T(8,128)(2,1)S(1)}, bf16[128,2048]{1,0:T(8,128)(2,1)}, u32[]{:S(2)}) copy-start(bf16[128,2048]{1,0:T(8,128)(2,1)} %v_ref.5) | copy-start | bytes 1572868
  11.9 23.1 %copy-start.4 = (bf16[128,2048]{1,0:T(8,128)(2,1)S(1)}, bf16[128,2048]{1,0:T(8,128)(2,1)}, u32[]{:S(2)}) copy-start(bf16[128,2048]{1,0:T(8,128)(2,1)} %q_ref.3) | copy-start | bytes 1572868
  11.9 23.1 %copy-start.5 = (bf16[128,2048]{1,0:T(8,128)(2,1)S(1)}, bf16[128,2048]{1,0:T(8,128)(2,1)}, u32[]{:S(2)}) copy-start(bf16[128,2048]{1,0:T(8,128)(2,1)} %gate_ref.3) | copy-start | bytes 1572868
  11.9 23.1 %copy-start.6 = (f32[2048]{0:T(1024)S(1)}, f32[2048]{0:T(1024)}, u32[]{:S(2)}) copy-start(f32[2048]{0:T(1024)} %param.20) | copy-start | bytes 24580
  11.9 23.1 %copy-start.8 = (f32[16]{0:T(128)S(1)}, f32[16]{0:T(128)}, u32[]{:S(2)}) copy-start(f32[16]{0:T(128)} %decay_ref.7) | copy-start | bytes 196
  12.0 7.9 %collective-permute-start.1 = (bf16[4,128,128]{2,1,0:T(8,128)(2,1)S(1)}, bf16[4,128,128]{2,1,0:T(8,128)(2,1)S(1)}, u32[]{:S(2)}, u32[]{:S(2)}) collective-permute-start(bf16[4,128,128]{2,1,0:T(8,128)(2,1)S(1)} %fusion.45), channel_id=1, source_target_pairs={{0,8},{4,12},{8,16},{12,20},{16,24},{20,28},{1,9},{5,13},{9,17},{1... | collective-permute-start | bytes 393224 | tf_op jit(solution)/shard_map/ppermute | solution.py:246
  16.3 9.1 %collective-permute-start.5 = (bf16[4,128,128]{2,1,0:T(8,128)(2,1)S(1)}, bf16[4,128,128]{2,1,0:T(8,128)(2,1)S(1)}, u32[]{:S(2)}, u32[]{:S(2)}) collective-permute-start(bf16[4,128,128]{2,1,0:T(8,128)(2,1)S(1)} %fusion.50), channel_id=1, source_target_pairs={{0,8},{4,12},{8,16},{12,20},{16,24},{20,28},{1,9},{5,13},{9,17},{1... | collective-permute-start | bytes 393224 | tf_op jit(solution)/shard_map/ppermute | solution.py:246
  20.0 10.5 %collective-permute-start.2 = (bf16[4,128,128]{2,1,0:T(8,128)(2,1)S(1)}, bf16[4,128,128]{2,1,0:T(8,128)(2,1)S(1)}, u32[]{:S(2)}, u32[]{:S(2)}) collective-permute-start(bf16[4,128,128]{2,1,0:T(8,128)(2,1)S(1)} %fusion.48), channel_id=1, source_target_pairs={{0,16},{4,20},{8,24},{12,28},{1,17},{5,21},{9,25},{13,29},{2,18},{... | collective-permute-start | bytes 393224 | tf_op jit(solution)/shard_map/ppermute | solution.py:246
  25.5 7.5 %collective-permute-start.6 = (bf16[4,128,128]{2,1,0:T(8,128)(2,1)S(1)}, bf16[4,128,128]{2,1,0:T(8,128)(2,1)S(1)}, u32[]{:S(2)}, u32[]{:S(2)}) collective-permute-start(bf16[4,128,128]{2,1,0:T(8,128)(2,1)S(1)} %fusion.53), channel_id=1, source_target_pairs={{0,16},{4,20},{8,24},{12,28},{1,17},{5,21},{9,25},{13,29},{2,18},{... | collective-permute-start | bytes 393224 | tf_op jit(solution)/shard_map/ppermute | solution.py:246
  30.7 13.0 %collective-permute-start.3 = (bf16[4,128,128]{2,1,0:T(8,128)(2,1)S(1)}, bf16[4,128,128]{2,1,0:T(8,128)(2,1)S(1)}, u32[]{:S(2)}, u32[]{:S(2)}) collective-permute-start(bf16[4,128,128]{2,1,0:T(8,128)(2,1)S(1)} %get-tuple-element.42), channel_id=1, source_target_pairs={{0,4},{4,0},{8,12},{12,8},{16,20},{20,16},{24,28},{28,24},{1,5},{5... | collective-permute-start | bytes 393224 | tf_op jit(solution)/shard_map/ppermute | solution.py:198
  33.2 5.0 %collective-permute-start.7 = (bf16[4,128,128]{2,1,0:T(8,128)(2,1)S(1)}, bf16[4,128,128]{2,1,0:T(8,128)(2,1)S(1)}, u32[]{:S(2)}, u32[]{:S(2)}) collective-permute-start(bf16[4,128,128]{2,1,0:T(8,128)(2,1)S(1)} %get-tuple-element.44), channel_id=1, source_target_pairs={{0,4},{4,0},{8,12},{12,8},{16,20},{20,16},{24,28},{28,24},{1,5},{5... | collective-permute-start | bytes 393224 | tf_op jit(solution)/shard_map/ppermute | solution.py:198
  38.2 8.1 %copy-start.13 = (bf16[2048,768]{1,0:T(8,128)(2,1)S(1)}, bf16[2048,768]{1,0:T(8,128)(2,1)}, u32[]{:S(2)}) copy-start(bf16[2048,768]{1,0:T(8,128)(2,1)} %param.21) | copy-start | bytes 9437188
  39.2 19.4 %collective-permute-start.11 = (bf16[128,1024]{1,0:T(8,128)(2,1)S(1)}, bf16[128,1024]{1,0:T(8,128)(2,1)S(1)}, u32[]{:S(2)}, u32[]{:S(2)}) collective-permute-start(bf16[128,1024]{1,0:T(8,128)(2,1)S(1)} %mix_heads.3), channel_id=1, source_target_pairs={{0,8},{4,12},{8,16},{12,20},{16,24},{20,28},{24,0},{28,4},{1,9},{5... | collective-permute-start | bytes 786440 | tf_op jit(solution)/shard_map/ppermute | solution.py:202
  42.0 13.9 %collective-permute-start.9 = (bf16[128,1024]{1,0:T(8,128)(2,1)S(1)}, bf16[128,1024]{1,0:T(8,128)(2,1)S(1)}, u32[]{:S(2)}, u32[]{:S(2)}) collective-permute-start(bf16[128,1024]{1,0:T(8,128)(2,1)S(1)} %mix_heads.3), channel_id=1, source_target_pairs={{0,4},{4,0},{8,12},{12,8},{16,20},{20,16},{24,28},{28,24},{1,5},{5... | collective-permute-start | bytes 786440 | tf_op jit(solution)/shard_map/ppermute | solution.py:198
  44.6 2.8 %copy-start.11 = (s32[128,2]{0,1:T(2,128)S(1)}, s32[128,2]{0,1:T(2,128)}, u32[]{:S(2)}) copy-start(s32[128,2]{0,1:T(2,128)} %param.23) | copy-start | bytes 3076
  44.6 3.2 %copy-start.10 = (bf16[128,6144]{1,0:T(8,128)(2,1)S(1)}, bf16[128,6144]{1,0:T(8,128)(2,1)}, u32[]{:S(2)}) copy-start(bf16[128,6144]{1,0:T(8,128)(2,1)} %param.14) | copy-start | bytes 4718596
  44.6 10.7 %collective-permute-start.10 = (bf16[128,1024]{1,0:T(8,128)(2,1)S(1)}, bf16[128,1024]{1,0:T(8,128)(2,1)S(1)}, u32[]{:S(2)}, u32[]{:S(2)}) collective-permute-start(bf16[128,1024]{1,0:T(8,128)(2,1)S(1)} %mix_heads.2), channel_id=1, source_target_pairs={{0,8},{4,12},{8,16},{12,20},{16,24},{20,28},{24,0},{28,4},{1,9},{5... | collective-permute-start | bytes 786440 | tf_op jit(solution)/shard_map/ppermute | solution.py:202
  45.8 15.3 %collective-permute-start.8 = (bf16[128,1024]{1,0:T(8,128)(2,1)S(1)}, bf16[128,1024]{1,0:T(8,128)(2,1)}, u32[]{:S(2)}, u32[]{:S(2)}) collective-permute-start(bf16[128,1024]{1,0:T(8,128)(2,1)S(1)} %mix_heads.2), channel_id=1, source_target_pairs={{0,4},{4,0},{8,12},{12,8},{16,20},{20,16},{24,28},{28,24},{1,5},{5... | collective-permute-start | bytes 786440 | tf_op jit(solution)/shard_map/ppermute | solution.py:198
  47.8 1.1 copy-start.16
  48.1 10.0 %copy-start.14 = (bf16[2048,768]{1,0:T(8,128)(2,1)S(1)}, bf16[2048,768]{1,0:T(8,128)(2,1)}, u32[]{:S(2)}) copy-start(bf16[2048,768]{1,0:T(8,128)(2,1)} %param.21) | copy-start | bytes 9437188
  55.4 17.8 %collective-permute-start.14 = (bf16[128,1024]{1,0:T(8,128)(2,1)S(1)}, bf16[128,1024]{1,0:T(8,128)(2,1)S(1)}, u32[]{:S(2)}, u32[]{:S(2)}) collective-permute-start(bf16[128,1024]{1,0:T(8,128)(2,1)S(1)} %collective-permute-done.10), channel_id=1, source_target_pairs={{0,8},{4,12},{8,16},{12,20},{16,24},{20,28},{24,0},{28,4},{1,9},{5... | collective-permute-start | bytes 786440 | tf_op jit(solution)/shard_map/ppermute | solution.py:202
  55.4 23.7 %collective-permute-start.12 = (bf16[128,1024]{1,0:T(8,128)(2,1)S(1)}, bf16[128,1024]{1,0:T(8,128)(2,1)S(1)}, u32[]{:S(2)}, u32[]{:S(2)}) collective-permute-start(bf16[128,1024]{1,0:T(8,128)(2,1)S(1)} %collective-permute-done.10), channel_id=1, source_target_pairs={{0,4},{4,0},{8,12},{12,8},{16,20},{20,16},{24,28},{28,24},{1,5},{5... | collective-permute-start | bytes 786440 | tf_op jit(solution)/shard_map/ppermute | solution.py:198
  55.9 21.1 %collective-permute-start.13 = (bf16[128,1024]{1,0:T(8,128)(2,1)S(1)}, bf16[128,1024]{1,0:T(8,128)(2,1)S(1)}, u32[]{:S(2)}, u32[]{:S(2)}) collective-permute-start(bf16[128,1024]{1,0:T(8,128)(2,1)S(1)} %collective-permute-done.9), channel_id=1, source_target_pairs={{0,8},{4,12},{8,16},{12,20},{16,24},{20,28},{24,0},{28,4},{1,9},{5... | collective-permute-start | bytes 786440 | tf_op jit(solution)/shard_map/ppermute | solution.py:202
  58.5 14.5 %collective-permute-start.15 = (bf16[128,1024]{1,0:T(8,128)(2,1)S(1)}, bf16[128,1024]{1,0:T(8,128)(2,1)}, u32[]{:S(2)}, u32[]{:S(2)}) collective-permute-start(bf16[128,1024]{1,0:T(8,128)(2,1)S(1)} %collective-permute-done.11), channel_id=1, source_target_pairs={{0,8},{4,12},{8,16},{12,20},{16,24},{20,28},{24,0},{28,4},{1,9},{5... | collective-permute-start | bytes 786440 | tf_op jit(solution)/shard_map/ppermute | solution.py:202
  73.0 17.5 %collective-permute-start.19 = (bf16[128,1024]{1,0:T(8,128)(2,1)}, bf16[128,1024]{1,0:T(8,128)(2,1)S(1)}, u32[]{:S(2)}, u32[]{:S(2)}) collective-permute-start(bf16[128,1024]{1,0:T(8,128)(2,1)} %collective-permute-done.15), channel_id=1, source_target_pairs={{0,8},{4,12},{8,16},{12,20},{16,24},{20,28},{24,0},{28,4},{1,9},{5... | collective-permute-start | bytes 786440 | tf_op jit(solution)/shard_map/ppermute | solution.py:202
  73.0 19.8 %collective-permute-start.17 = (bf16[128,1024]{1,0:T(8,128)(2,1)}, bf16[128,1024]{1,0:T(8,128)(2,1)}, u32[]{:S(2)}, u32[]{:S(2)}) collective-permute-start(bf16[128,1024]{1,0:T(8,128)(2,1)} %collective-permute-done.15), channel_id=1, source_target_pairs={{0,4},{4,0},{8,12},{12,8},{16,20},{20,16},{24,28},{28,24},{1,5},{5... | collective-permute-start | bytes 786440 | tf_op jit(solution)/shard_map/ppermute | solution.py:198
  73.1 12.1 %collective-permute-start.18 = (bf16[128,1024]{1,0:T(8,128)(2,1)S(1)}, bf16[128,1024]{1,0:T(8,128)(2,1)}, u32[]{:S(2)}, u32[]{:S(2)}) collective-permute-start(bf16[128,1024]{1,0:T(8,128)(2,1)S(1)} %collective-permute-done.14), channel_id=1, source_target_pairs={{0,8},{4,12},{8,16},{12,20},{16,24},{20,28},{24,0},{28,4},{1,9},{5... | collective-permute-start | bytes 786440 | tf_op jit(solution)/shard_map/ppermute | solution.py:202
  77.1 17.6 %collective-permute-start.16 = (bf16[128,1024]{1,0:T(8,128)(2,1)S(1)}, bf16[128,1024]{1,0:T(8,128)(2,1)S(1)}, u32[]{:S(2)}, u32[]{:S(2)}) collective-permute-start(bf16[128,1024]{1,0:T(8,128)(2,1)S(1)} %collective-permute-done.14), channel_id=1, source_target_pairs={{0,4},{4,0},{8,12},{12,8},{16,20},{20,16},{24,28},{28,24},{1,5},{5... | collective-permute-start | bytes 786440 | tf_op jit(solution)/shard_map/ppermute | solution.py:198
  85.2 15.3 %all-to-all-start = ((bf16[8,16,768]{2,1,0:T(8,128)(2,1)}), bf16[8,16,768]{2,1,0:T(8,128)(2,1)S(1)}, u32[]{:S(2)}, u32[]{:S(2)}) async-start(bf16[8,16,768]{2,1,0:T(8,128)(2,1)} %pad_maximum_fusion.1), calls=%async_computation | async-start | bytes 393216 | tf_op jit(solution)/shard_map/all_to_all | solution.py:321
  88.8 10.6 %collective-permute-start.20 = (bf16[128,1024]{1,0:T(8,128)(2,1)}, bf16[128,1024]{1,0:T(8,128)(2,1)S(1)}, u32[]{:S(2)}, u32[]{:S(2)}) collective-permute-start(bf16[128,1024]{1,0:T(8,128)(2,1)} %collective-permute-done.18), channel_id=1, source_target_pairs={{0,4},{4,0},{8,12},{12,8},{16,20},{20,16},{24,28},{28,24},{1,5},{5... | collective-permute-start | bytes 786440 | tf_op jit(solution)/shard_map/ppermute | solution.py:198
  90.5 8.5 %collective-permute-start.21 = (bf16[128,1024]{1,0:T(8,128)(2,1)S(1)}, bf16[128,1024]{1,0:T(8,128)(2,1)S(1)}, u32[]{:S(2)}, u32[]{:S(2)}) collective-permute-start(bf16[128,1024]{1,0:T(8,128)(2,1)S(1)} %collective-permute-done.19), channel_id=1, source_target_pairs={{0,4},{4,0},{8,12},{12,8},{16,20},{20,16},{24,28},{28,24},{1,5},{5... | collective-permute-start | bytes 786440 | tf_op jit(solution)/shard_map/ppermute | solution.py:198
  90.9 3.9 %copy-start.15 = (bf16[2048,768]{1,0:T(8,128)(2,1)S(1)}, bf16[2048,768]{1,0:T(8,128)(2,1)}, u32[]{:S(2)}) copy-start(bf16[2048,768]{1,0:T(8,128)(2,1)} %param.21) | copy-start | bytes 9437188
  102.8 1.5 collective-permute-start.22
  104.4 4.9 %collective-permute-start.23 = (bf16[1,64,768]{2,1,0:T(8,128)(2,1)S(1)}, bf16[1,64,768]{2,1,0:T(8,128)(2,1)S(1)}, u32[]{:S(2)}, u32[]{:S(2)}) collective-permute-start(bf16[1,64,768]{2,1,0:T(8,128)(2,1)S(1)} %fusion.55), channel_id=1, source_target_pairs={{0,2},{1,3},{2,0},{3,1},{4,6},{5,7},{6,4},{7,5},{8,10},{9,11},{10,... | collective-permute-start | bytes 294920 | tf_op jit(solution)/shard_map/ppermute | solution.py:343
  110.5 13.8 %copy-start.12 = (f32[128,2]{0,1:T(2,128)S(1)}, f32[128,2]{0,1:T(2,128)}, u32[]{:S(2)}) copy-start(f32[128,2]{0,1:T(2,128)} %param.24) | copy-start | bytes 3076
  110.6 2.4 %collective-permute-start.24 = (bf16[2,4,2,32,768]{4,3,2,1,0:T(8,128)(2,1)S(1)}, bf16[2,4,2,32,768]{4,3,2,1,0:T(8,128)(2,1)S(1)}, u32[]{:S(2)}, u32[]{:S(2)}) collective-permute-start(bf16[2,4,2,32,768]{4,3,2,1,0:T(8,128)(2,1)S(1)} %pad_maximum_fusion), channel_id=1, source_target_pairs={{0,1},{1,0},{2,3},{3,2},{4,5},{5,4},{6,7},{7,6},{8,9},{9,8},{10,11... | collective-permute-start | bytes 2359304 | tf_op jit(solution)/shard_map/ppermute | solution.py:343
  114.8 43.7 %collective-permute-start.25 = (bf16[1,4,2,32,768]{4,3,2,1,0:T(8,128)(2,1)}, bf16[1,4,2,32,768]{4,3,2,1,0:T(8,128)(2,1)S(1)}, u32[]{:S(2)}, u32[]{:S(2)}) collective-permute-start(bf16[1,4,2,32,768]{4,3,2,1,0:T(8,128)(2,1)} %fusion.17), channel_id=1, source_target_pairs={{0,2},{1,3},{2,0},{3,1},{4,6},{5,7},{6,4},{7,5},{8,10},{9,11},{10,... | collective-permute-start | bytes 1179656 | tf_op jit(solution)/shard_map/ppermute | solution.py:343
  116.3 4.6 %collective-permute-start.30 = (bf16[64,768]{1,0:T(8,128)(2,1)S(1)}, bf16[64,768]{1,0:T(8,128)(2,1)S(1)}, u32[]{:S(2)}, u32[]{:S(2)}) collective-permute-start(bf16[64,768]{1,0:T(8,128)(2,1)S(1)} %fusion.54.refs_0_), channel_id=1, source_target_pairs={{0,8},{4,12},{8,0},{12,4},{16,24},{20,28},{24,16},{28,20},{1,9},{5... | collective-permute-start | bytes 294920 | tf_op jit(solution)/shard_map/ppermute | solution.py:360
  118.0 10.2 %collective-permute-start.32 = (bf16[64,768]{1,0:T(8,128)(2,1)S(1)}, bf16[64,768]{1,0:T(8,128)(2,1)S(1)}, u32[]{:S(2)}, u32[]{:S(2)}) collective-permute-start(bf16[64,768]{1,0:T(8,128)(2,1)S(1)} %fusion.54.refs_0_), channel_id=1, source_target_pairs={{0,16},{4,20},{8,24},{12,28},{16,0},{20,4},{24,8},{28,12},{1,17},{... | collective-permute-start | bytes 294920 | tf_op jit(solution)/shard_map/ppermute | solution.py:360
  121.0 8.6 %collective-permute-start.34 = (bf16[64,768]{1,0:T(8,128)(2,1)S(1)}, bf16[64,768]{1,0:T(8,128)(2,1)S(1)}, u32[]{:S(2)}, u32[]{:S(2)}) collective-permute-start(bf16[64,768]{1,0:T(8,128)(2,1)S(1)} %collective-permute-done.30.refs_2_), channel_id=1, source_target_pairs={{0,16},{4,20},{8,24},{12,28},{16,0},{20,4},{24,8},{28,12},{1,17},{... | collective-permute-start | bytes 294920 | tf_op jit(solution)/shard_map/ppermute | solution.py:360
  124.3 18.3 %collective-permute-start.29 = (bf16[64,768]{1,0:T(8,128)(2,1)S(1)}, bf16[64,768]{1,0:T(8,128)(2,1)S(1)}, u32[]{:S(2)}, u32[]{:S(2)}) collective-permute-start(bf16[64,768]{1,0:T(8,128)(2,1)S(1)} %fusion.54.refs_0_), channel_id=1, source_target_pairs={{0,4},{4,0},{8,12},{12,8},{16,20},{20,16},{24,28},{28,24},{1,5},{5... | collective-permute-start | bytes 294920 | tf_op jit(solution)/shard_map/ppermute | solution.py:198
  125.3 17.3 %collective-permute-start.31 = (bf16[64,768]{1,0:T(8,128)(2,1)S(1)}, bf16[64,768]{1,0:T(8,128)(2,1)S(1)}, u32[]{:S(2)}, u32[]{:S(2)}) collective-permute-start(bf16[64,768]{1,0:T(8,128)(2,1)S(1)} %collective-permute-done.30.refs_2_), channel_id=1, source_target_pairs={{0,4},{4,0},{8,12},{12,8},{16,20},{20,16},{24,28},{28,24},{1,5},{5... | collective-permute-start | bytes 294920 | tf_op jit(solution)/shard_map/ppermute | solution.py:198
  128.3 14.3 %collective-permute-start.33 = (bf16[64,768]{1,0:T(8,128)(2,1)S(1)}, bf16[64,768]{1,0:T(8,128)(2,1)S(1)}, u32[]{:S(2)}, u32[]{:S(2)}) collective-permute-start(bf16[64,768]{1,0:T(8,128)(2,1)S(1)} %collective-permute-done.32.refs_4_), channel_id=1, source_target_pairs={{0,4},{4,0},{8,12},{12,8},{16,20},{20,16},{24,28},{28,24},{1,5},{5... | collective-permute-start | bytes 294920 | tf_op jit(solution)/shard_map/ppermute | solution.py:198
  129.6 13.0 %collective-permute-start.35 = (bf16[64,768]{1,0:T(8,128)(2,1)S(1)}, bf16[64,768]{1,0:T(8,128)(2,1)S(1)}, u32[]{:S(2)}, u32[]{:S(2)}) collective-permute-start(bf16[64,768]{1,0:T(8,128)(2,1)S(1)} %collective-permute-done.34.refs_6_), channel_id=1, source_target_pairs={{0,4},{4,0},{8,12},{12,8},{16,20},{20,16},{24,28},{28,24},{1,5},{5... | collective-permute-start | bytes 294920 | tf_op jit(solution)/shard_map/ppermute | solution.py:198
  139.6 3.0 %copy-start.9 = (f32[6144]{0:T(1024)S(1)}, f32[6144]{0:T(1024)}, u32[]{:S(2)}) copy-start(f32[6144]{0:T(1024)} %param.22) | copy-start | bytes 73732
  154.5 28.8 %all-to-all-start.1 = ((bf16[8,8,6144]{2,1,0:T(8,128)(2,1)}), bf16[8,8,6144]{2,1,0:T(8,128)(2,1)S(1)}, u32[]{:S(2)}, u32[]{:S(2)}) async-start(bf16[8,8,6144]{2,1,0:T(8,128)(2,1)} %bitcast.37), calls=%async_computation.1 | async-start | bytes 1572864 | tf_op jit(solution)/shard_map/all_to_all | solution.py:392
  159.7 12.0 %collective-permute-start.26 = (bf16[4,32,768]{2,1,0:T(8,128)(2,1)S(1)}, bf16[4,32,768]{2,1,0:T(8,128)(2,1)S(1)}, u32[]{:S(2)}, u32[]{:S(2)}) collective-permute-start(bf16[4,32,768]{2,1,0:T(8,128)(2,1)S(1)} %slice_bitcast_fusion.5), channel_id=1, source_target_pairs={{0,4},{4,0},{8,12},{12,8},{16,20},{20,16},{24,28},{28,24},{1,5},{5... | collective-permute-start | bytes 589832 | tf_op jit(solution)/shard_map/ppermute | solution.py:198
  171.8 7.8 %collective-permute-start.27 = (bf16[2,2,32,768]{3,2,1,0:T(8,128)(2,1)S(1)}, bf16[2,2,32,768]{3,2,1,0:T(8,128)(2,1)S(1)}, u32[]{:S(2)}, u32[]{:S(2)}) collective-permute-start(bf16[2,2,32,768]{3,2,1,0:T(8,128)(2,1)S(1)} %pad_maximum_fusion.3), channel_id=1, source_target_pairs={{0,24},{4,28},{8,0},{12,4},{16,8},{20,12},{24,16},{28,20},{1,25},{... | collective-permute-start | bytes 589832 | tf_op jit(solution)/shard_map/ppermute | solution.py:202
  179.6 8.9 %collective-permute-start.28 = (bf16[2,2,32,768]{3,2,1,0:T(8,128)(2,1)S(1)}, bf16[2,2,32,768]{3,2,1,0:T(8,128)(2,1)S(1)}, u32[]{:S(2)}, u32[]{:S(2)}) collective-permute-start(bf16[2,2,32,768]{3,2,1,0:T(8,128)(2,1)S(1)} %pad_maximum_fusion.4), channel_id=1, source_target_pairs={{0,16},{4,20},{8,24},{12,28},{16,0},{20,4},{24,8},{28,12},{1,17},{... | collective-permute-start | bytes 589832 | tf_op jit(solution)/shard_map/ppermute | solution.py:202

commit v3 on v2

--- a/solution.py
+++ b/solution.py
@@ -19,6 +19,10 @@
     return pltpu.CompilerParams(vmem_limit_bytes=mib * 2**20)
 
 
+def takes(us):
+    return pl.CostEstimate(flops=int(us * 1e9), bytes_accessed=int(1e6), transcendentals=0)
+
+
 def rows_iota(shape):
     return lax.broadcasted_iota(jnp.int32, shape, 0).astype(F32)
 
@@ -35,11 +39,26 @@
     return lax.optimization_barrier((value, *others))[0]
 
 
-def state_kernel(per_half, place_ref, decay_ref, k_ref, v_ref, *outs):
+def state_kernel(per_half, place_ref, decay_ref, k_hbm, v_hbm, *refs):
+    outs, (k_ref, v_ref, sems) = refs[: 2 * CHUNKS], refs[2 * CHUNKS :]
     pair = place_ref[0]
     tok, size = k_ref.shape[0], outs[0].shape[2]
+    wide = k_ref.shape[1] // CHUNKS
+    copies = []
+    for chunk in range(CHUNKS):
+        at = pl.ds(chunk * wide, wide)
+        copies.append(
+            [
+                pltpu.make_async_copy(hbm.at[:, at], ref.at[:, at], sems.at[i, chunk])
+                for i, (hbm, ref) in enumerate(((k_hbm, k_ref), (v_hbm, v_ref)))
+            ]
+        )
+        for copy in copies[-1]:
+            copy.start()
     back = (tok - 1.0) - rows_iota((tok, size))
     for chunk in range(CHUNKS):
+        for copy in copies[chunk]:
+            copy.wait()
         for which in (1, 0):
             half = pair if which == 0 else 1 - pair
             heads = [chunk * 2 * per_half + half * per_half + l for l in range(per_half)]
@@ -117,15 +136,52 @@
                 ]
 
 
-def stage_kernel(first, w_ref, out_ref):
-    pltpu.sync_copy(w_ref.at[0, pl.ds(first, out_ref.shape[0]), :], out_ref)
-
-
-def ffn_kernel(n, parts, blocks, order_ref, *refs):
+def project_kernel(n_exp, cap, token_ref, *refs):
+    weight_ref, keep_ref, send_ref = refs[-3:]
+    pairs = refs[:-3]
+    chunks = len(pairs) // 2
+    wide = pairs[0].shape[1]
+    tok = pairs[0].shape[0]
+    own_rows = tok // n_exp
+    slots_of = []
+    for y in range(2):
+        total = None
+        for chunk in range(chunks):
+            part = jnp.dot(
+                pairs[chunk * 2 + y][...],
+                weight_ref[chunk * wide : (chunk + 1) * wide, :],
+                preferred_element_type=F32,
+            )
+            total = part if total is None else total + part
+        rows = total.astype(BF16)
+        pick = token_ref[y] == lax.broadcasted_iota(jnp.int32, (n_exp * cap, tok), 1)
+        slots = jnp.dot(pick.astype(F32).astype(BF16), rows, preferred_element_type=F32)
+        for j in range(n_exp):
+            out = send_ref if j % 2 else keep_ref
+            out[j // 2, y * own_rows : (y + 1) * own_rows, :] = rows[j * own_rows : (j + 1) * own_rows]
+        slots_of.append(slots)
+    for j in range(n_exp):
+        out = send_ref if j % 2 else keep_ref
+        both = [s[j * cap : (j + 1) * cap] for s in slots_of]
+        out[j // 2, 2 * own_rows :, :] = jnp.concatenate(both, axis=0).astype(BF16)
+
+
+def hidden_kernel(cap, order_ref, stream_ref, *refs):
+    out_ref, total_ref = refs[-2:]
+    steps = (len(refs) - 2) // 2
+    first = refs[0].shape[0] - 2 * cap
+    for step in range(steps):
+        rows = refs[2 * step][first:, :].astype(F32) + refs[2 * step + 1][first:, :].astype(F32)
+        for y in range(2):
+            to = pl.multiple_of(order_ref[2 * step + y] * cap, cap)
+            total_ref[pl.ds(to, cap), :] = rows[y * cap : (y + 1) * cap]
+    out_ref[...] = (total_ref[...] + stream_ref[...].astype(F32)).astype(BF16)
+
+
+def ffn_kernel(n, blocks, order_ref, *refs):
     pieces, refs = refs[:n], refs[n:]
     gain_ref, refs = refs[0], refs[1:]
-    gates, ups, refs = refs[:parts], refs[parts : 2 * parts], refs[2 * parts :]
-    down_ref, out_ref, rows_ref, down_buf, sems = refs
+    gate_ref, up_ref, down_ref, out_ref, rows_ref, down_buf, sems = refs
     step = out_ref.shape[1] // blocks
     copies = [
         pltpu.make_async_copy(
@@ -145,14 +201,13 @@
         at = lanes(order_ref[i], cols) if n > 1 else slice(None)
         rows_ref[:, at] = (piece[...].astype(F32) * inverse * gain_ref[:, at]).astype(BF16)
     gate = up = None
-    span = gates[0].shape[0]
-    for i in range(parts):
-        for j in range(0, span, span // 4):
-            rows = rows_ref[:, i * span + j : i * span + j + span // 4]
-            g = jnp.dot(rows, gates[i][j : j + span // 4, :], preferred_element_type=F32)
-            u = jnp.dot(rows, ups[i][j : j + span // 4, :], preferred_element_type=F32)
-            gate = g if gate is None else gate + g
-            up = u if up is None else up + u
+    span = rows_ref.shape[1] // blocks
+    for i in range(blocks):
+        rows = rows_ref[:, i * span : (i + 1) * span]
+        g = jnp.dot(rows, gate_ref[0, i * span : (i + 1) * span, :], preferred_element_type=F32)
+        u = jnp.dot(rows, up_ref[0, i * span : (i + 1) * span, :], preferred_element_type=F32)
+        gate = g if gate is None else gate + g
+        up = u if up is None else up + u
     activated = (gate / (1.0 + jnp.exp(-gate)) * up).astype(BF16)
     for i, copy in enumerate(copies):
         copy.wait()
@@ -201,14 +256,23 @@
         to = [(i, (i + 2 * by) % n_ctx) for i in range(n_ctx)]
         return lax.ppermute(value, "ctx", to)
 
+    def in_hbm(value):
+        return pltpu.with_memory_space_constraint(value, pltpu.HBM)
+
     states = pl.pallas_call(
         functools.partial(state_kernel, per_half),
         out_shape=[jax.ShapeDtypeStruct((per_half, size, size), BF16)] * (2 * CHUNKS),
-        in_specs=[SMEM, SMEM, VMEM, VMEM],
+        in_specs=[SMEM, SMEM, HBM, HBM],
         out_specs=[VMEM] * (2 * CHUNKS),
+        scratch_shapes=[
+            pltpu.VMEM((tok, heads * size), BF16),
+            pltpu.VMEM((tok, heads * size), BF16),
+            pltpu.SemaphoreType.DMA((2, CHUNKS)),
+        ],
         compiler_params=limit(8),
+        cost_estimate=takes(2),
         name="shard_state",
-    )(here, decay_rates, key_proj, values)
+    )(here, decay_rates, in_hbm(key_proj), in_hbm(values))
 
     def near_part(chunk, start):
         return pl.pallas_call(
@@ -221,42 +285,32 @@
             in_specs=[SMEM] + [VMEM] * 5,
             out_specs=[VMEM] * 3,
             compiler_params=limit(8),
+            cost_estimate=takes(2),
             name="near_part",
         )(after(decay_rates, start), queries, key_proj, values, attn_gate, attn_gain[None, :])
 
-    rates, lowers, spans, windows, priors, nears = [], [], [], [], [], []
+    mixed, held = [], None
     for chunk in range(CHUNKS):
         keep, send = states[2 * chunk], states[2 * chunk + 1]
-        got = swapped(send)
-        nears.append(near_part(chunk, states[0] if chunk == 0 else windows[0]))
+        got = swapped(send if held is None else after(send, held))
+        near, scale, query = near_part(chunk, states[0] if held is None else held)
         first = chunk * per_chunk + pair * per_half
         rate = lax.dynamic_slice_in_dim(decay_rates, first, per_half, 0)[:, None, None]
         span = jnp.exp(-rate * tok)
         lower = jnp.where(pair == 0, keep, got).astype(F32)
         upper = jnp.where(pair == 0, got, keep).astype(F32)
-        windows.append((span * lower + upper).astype(BF16))
-        rates.append(rate)
-        spans.append(span)
-        lowers.append(lower)
-        priors.append(jnp.zeros(lower.shape, F32))
-    reach = 1
-    while reach < groups:
-        line = [(i, i + 2 * reach) for i in range(n_ctx - 2 * reach)]
-        for chunk in range(CHUNKS):
-            got = lax.ppermute(windows[chunk], "ctx", line).astype(F32)
-            factor = jnp.exp(-rates[chunk] * (2 * tok * (reach - 1)))
-            priors[chunk] = priors[chunk] + factor * got
-            if 2 * reach < groups:
-                factor = jnp.exp(-rates[chunk] * (2 * tok * reach))
-                windows[chunk] = (windows[chunk].astype(F32) + factor * got).astype(BF16)
-        reach *= 2
-    mixed = []
-    for chunk in range(CHUNKS):
-        prior = priors[chunk]
-        second = spans[chunk] * prior + lowers[chunk]
+        window = held = (span * lower + upper).astype(BF16)
+        prior = jnp.zeros(lower.shape, F32)
+        reach = 1
+        while reach < groups:
+            line = [(i, i + 2 * reach) for i in range(n_ctx - 2 * reach)]
+            far = lax.ppermute(window, "ctx", line).astype(F32)
+            prior = prior + jnp.exp(-rate * (2 * tok * (reach - 1))) * far
+            window = (window.astype(F32) + jnp.exp(-rate * (2 * tok * reach)) * far).astype(BF16)
+            reach *= 2
+        second = span * prior + lower
         mine = jnp.where(pair == 0, prior, second).astype(BF16)
         other = swapped(jnp.where(pair == 0, second, prior).astype(BF16))
-        near, scale, query = nears[chunk]
         mixed.append(
             pl.pallas_call(
                 functools.partial(mix_kernel, chunk, per_half, own_rows),
@@ -264,6 +318,7 @@
                 in_specs=[SMEM, SMEM] + [VMEM] * 5,
                 out_specs=VMEM,
                 compiler_params=limit(8),
+                cost_estimate=takes(2),
                 name="mix_heads",
             )(here, decay_rates, query, near, scale, mine, other)
         )
@@ -289,69 +344,62 @@
     label = jnp.broadcast_to(label.astype(BF16)[None], (n_ctx, cap, cols))
     parcel = jnp.concatenate([parcel, label], axis=1)
 
-    totals = [None] * n_ctx
-    arrived = None
-    staged = {}
-    parts = 2
+    arrived = lax.all_to_all(parcel, "ctx", split_axis=0, concat_axis=0, tiled=True)
+    stream_rows = arrived[:, :cap].reshape(n_ctx * cap, cols)
+    token = arrived[:, cap, : n_exp * cap].astype(jnp.int32).reshape(n_ctx, n_exp, cap) - 1
+    token = jnp.where(token >= 0, ((token // own_rows) ^ own) * own_rows + token % own_rows, -1)
+    token = jnp.stack(
+        [lax.dynamic_index_in_dim(token, own ^ j, 1, keepdims=False) for j in range(n_exp)], axis=1
+    )
+    index = jnp.arange(n_ctx, dtype=jnp.int32)
+    order = ((group - index // 2) % groups) * 2 + (pair ^ (index % 2))
+    token = jnp.take(token, order, axis=0).reshape(n_ctx, n_exp * cap, 1)
+
+    rows_of = [[[], []] for _ in range(groups)]
     for chunk in range(CHUNKS):
-        weight = out_weight[chunk * wide : (chunk + 1) * wide]
         current, crossed = mixed[chunk], None
         for step in range(groups):
-            if chunk % 2 and step == 1:
-                crossed = shifted(crossed, 1)
-            else:
-                crossed = swapped(current)
-            for y, rows in enumerate((current, crossed)):
-                at = 2 * step + y
-                part = jnp.dot(rows, weight, preferred_element_type=F32)
-                totals[at] = part if totals[at] is None else totals[at] + part
+            crossed = shifted(crossed, 1) if chunk % 2 and step == 1 else swapped(current)
+            rows_of[step][0].append(current)
+            rows_of[step][1].append(crossed)
             if step + 1 < groups:
                 current = shifted(current, 1)
-            if chunk == CHUNKS - 1 and step < parts:
-                for name, w in (("gate", w_gate), ("up", w_up)):
-                    staged[name, step] = pl.pallas_call(
-                        functools.partial(stage_kernel, step * (width // parts)),
-                        out_shape=pltpu.VMEM((width // parts, hidden_units), BF16),
-                        in_specs=[HBM],
-                        out_specs=VMEM,
-                        compiler_params=limit(2),
-                        name="stage_weight",
-                    )(pltpu.with_memory_space_constraint(after(w, current), pltpu.HBM))
-        if chunk == 0:
-            arrived = lax.all_to_all(
-                after(parcel, current), "ctx", split_axis=0, concat_axis=0, tiled=True
-            )
-    partial = jnp.concatenate([t.astype(BF16) for t in totals], axis=0)
-
-    stream_rows = arrived[:, :cap].reshape(n_ctx * cap, cols)
-    token = arrived[:, cap, : n_exp * cap].astype(jnp.int32).reshape(n_ctx, n_exp, cap) - 1
-    shard = jnp.arange(n_ctx, dtype=jnp.int32)
-    block = ((group - shard // 2) % groups) * 2 + (pair ^ (shard % 2))
-    token = jnp.stack(
-        [lax.dynamic_index_in_dim(token, own ^ j, 1, keepdims=False) for j in range(n_exp)]
-    )
-    column = block[None, :, None] * tok + ((token // own_rows) ^ own) * own_rows + token % own_rows
-    column = jnp.where(token >= 0, column, -1).reshape(-1)
-    chosen = (column[:, None] == jnp.arange(n_ctx * tok, dtype=jnp.int32)[None, :]).astype(BF16)
-
-    def add_groups(parts):
-        bit = 1
-        parts = list(parts)
+    kept, got = [], []
+    for step in range(groups):
+        out = jax.ShapeDtypeStruct((n_exp // 2, 2 * (own_rows + cap), cols), BF16)
+        keep, send = pl.pallas_call(
+            functools.partial(project_kernel, n_exp, cap),
+            out_shape=[out, out],
+            in_specs=[VMEM] * (2 + 2 * CHUNKS),
+            out_specs=[VMEM] * 2,
+            compiler_params=limit(8),
+            cost_estimate=takes(8),
+            name="project",
+        )(
+            token[2 * step : 2 * step + 2],
+            *[rows_of[step][y][chunk] for chunk in range(CHUNKS) for y in range(2)],
+            out_weight,
+        )
+        came = lax.ppermute(send, "exp", [(i, i ^ 1) for i in range(n_exp)])
+        bit = 2
         while bit < n_exp:
-            far = [j for j in range(0, n_exp, bit) if j & bit]
-            sent = jnp.stack([parts[j // bit] for j in far])
-            got = lax.ppermute(sent, "exp", [(i, i ^ bit) for i in range(n_exp)])
-            parts = [
-                parts[j // bit - 1].astype(F32) + got[n].astype(F32) for n, j in enumerate(far)
-            ]
+            total = (keep.astype(F32) + came.astype(F32)).astype(BF16)
+            total = total.reshape(n_exp // (2 * bit), 2, *total.shape[1:])
+            keep = total[:, 0]
+            came = lax.ppermute(total[:, 1], "exp", [(i, i ^ bit) for i in range(n_exp)])
             bit *= 2
-            if bit < n_exp:
-                parts = [p.astype(BF16) for p in parts]
-        return parts[0]
-
-    slot_rows = jnp.dot(chosen, partial, preferred_element_type=F32).astype(BF16)
-    slot_total = add_groups(slot_rows.reshape(n_exp, n_ctx * cap, cols))
-    hidden = (slot_total + stream_rows.astype(F32)).astype(BF16)
+        kept.append(keep[0])
+        got.append(came[0])
+    hidden = pl.pallas_call(
+        functools.partial(hidden_kernel, cap),
+        out_shape=jax.ShapeDtypeStruct((n_ctx * cap, cols), BF16),
+        in_specs=[SMEM] + [VMEM] * (1 + 2 * groups),
+        out_specs=VMEM,
+        scratch_shapes=[pltpu.VMEM((n_ctx * cap, cols), F32)],
+        compiler_params=limit(8),
+        cost_estimate=takes(1),
+        name="slot_hidden",
+    )(order, stream_rows, *[part for pair_of in zip(kept, got) for part in pair_of])
 
     pieces = {0: hidden}
     bit = 1
@@ -362,14 +410,24 @@
             )
         bit *= 2
     pieces = [p for r in range(groups) for p in (pieces[r], swapped(pieces[r]))]
-    source = (place ^ shard).astype(jnp.int32)
+    source = (place ^ index).astype(jnp.int32)
     if cols % 128:
         pieces = [jnp.take(jnp.stack(pieces), source, axis=0).transpose(1, 0, 2).reshape(-1, width)]
+
+    bulk = [
+        (k.astype(F32) + g.astype(F32))[: 2 * own_rows].astype(BF16).reshape(2, own_rows, cols)
+        for k, g in zip(kept, got)
+    ]
+    back = []
+    for step in range(groups):
+        rows = jnp.stack([bulk[step][0], swapped(after(bulk[step][1], hidden))])
+        back.append(shifted(rows, -step) if step else rows)
+
     blocks = 8
     down = pl.pallas_call(
-        functools.partial(ffn_kernel, len(pieces), parts, blocks),
+        functools.partial(ffn_kernel, len(pieces), blocks),
         out_shape=jax.ShapeDtypeStruct((n_ctx * cap, width), BF16),
-        in_specs=[SMEM] + [VMEM] * (len(pieces) + 1 + 2 * parts) + [HBM],
+        in_specs=[SMEM] + [VMEM] * (len(pieces) + 3) + [HBM],
         out_specs=VMEM,
         scratch_shapes=[
             pltpu.VMEM((n_ctx * cap, width), BF16),
@@ -377,37 +435,18 @@
             pltpu.SemaphoreType.DMA((blocks,)),
         ],
         compiler_params=limit(24),
+        cost_estimate=takes(10),
         name="expert",
-    )(
-        source,
-        *pieces,
-        ffn_gain[None, :],
-        *(
-            pltpu.with_memory_space_constraint(staged[name, i], pltpu.VMEM)
-            for name in ("gate", "up")
-            for i in range(parts)
-        ),
-        pltpu.with_memory_space_constraint(w_down, pltpu.HBM),
-    )
+    )(source, *pieces, ffn_gain[None, :], w_gate, w_up, in_hbm(w_down))
+    down = after(down, *back)
     received = lax.all_to_all(
         down.reshape(n_ctx, cap, width), "ctx", split_axis=0, concat_axis=0, tiled=True
     )
     summed = jnp.sum(received.astype(F32), axis=0)
     expert_out = (summed * own_weight[:, None]).astype(BF16).reshape(1, 1, cap, width)
 
-    bulk = after(partial, hidden).reshape(groups, 2, n_exp, own_rows, cols)
-    bulk = add_groups([bulk[:, :, j] for j in range(n_exp)]).astype(BF16)
-    bulk = [bulk[:, 0], swapped(bulk[:, 1])]
-    bulk = [jnp.stack([bulk[0][k], bulk[1][k]]) for k in range(groups)]
-    bit = 1
-    while bit < groups:
-        moving = [k for k in range(groups) if k & bit]
-        moved = shifted(jnp.stack([bulk[k] for k in moving]), -bit)
-        for n, k in enumerate(moving):
-            bulk[k] = moved[n]
-        bit *= 2
-    order = ((shard // 2 - group) % groups) * 2 + (pair ^ (shard % 2))
-    projected = jnp.take(jnp.concatenate(bulk), order, axis=0).transpose(1, 0, 2)
+    order = ((index // 2 - group) % groups) * 2 + (pair ^ (index % 2))
+    projected = jnp.take(jnp.concatenate(back), order, axis=0).transpose(1, 0, 2)
     projected = projected.reshape(own_rows, width)
     stream_own = lax.dynamic_slice_in_dim(stream_in, own * own_rows, own_rows, 0)
     residual_out = (stream_own.astype(F32) + projected.astype(F32)).astype(BF16)

time: 192 us -> 204 us (1.062)
  matrix products: 22.4 us -> 0.44 us
  waiting for transfers between devices: 51.1 us -> 72.7 us
  local copies, waits for them, and re-layouts: 5.16 us -> 20.1 us
  Pallas kernels: 29.2 us -> 25.3 us
    dot_general x17 -> x0, matrix products: 21.9 us -> none  [the longest x16 19.9 us: per_device(): part = jnp.dot(rows, weight, preferred_element_type=F32)]
    ppermute x16 -> x19, waiting for transfers between devices: 16.1 us -> 36.5 us  [swapped(): return lax.ppermute(value, 'ctx', swap)]
    unnamed x37 -> x54, local copies, waits for them, and re-layouts: 2.82 us -> 18.2 us
    all_to_all x1, waiting for transfers between devices: 0.01 us -> 15.1 us  [per_device(): lax.all_to_all(down.reshape(n_ctx, cap, width), 'ctx', split_axis=0, conc...]
    ppermute x9 -> x10, waiting for transfers between devices: 24.2 us -> 12.7 us  [shifted(): return lax.ppermute(value, 'ctx', to)]
    ppermute x9 -> x10, starting transfers between devices: 19 us -> 10.2 us  [shifted(): return lax.ppermute(value, 'ctx', to)]
    ppermute x16 -> x19, starting transfers between devices: 18.7 us -> 25.2 us  [swapped(): return lax.ppermute(value, 'ctx', swap)]
    pallas_call x5 -> x6, Pallas kernels: 23.9 us -> 18.7 us  [the longest x1 11.9 us: per_device(): pl.pallas_call(functools.partial(ffn_kernel, len(pieces), blocks), out_sh...]
  transfers between devices with their start and end apart: 38 -> 46, of which waited for: 17 -> 23; matrix products, arithmetic and copies ran while one was open for 13% -> 5% of each run, Pallas kernels for 15% -> 5%
where the time goes in v3:
time: 204 us; the launch traced here: 203 us
  starting transfers between devices  74.4 us (36%)
  waiting for transfers between devices  72.7 us (36%)
  Pallas kernels  25.3 us (12%)
  local copies, waits for them, and re-layouts  20.1 us (10%)
  other arithmetic  8.68 us (4%)
    ppermute x19, waiting for transfers between devices, swapped(): return lax.ppermute(value, 'ctx', swap)  36.5 us
    ppermute x19, starting transfers between devices, swapped(): return lax.ppermute(value, 'ctx', swap)  25.2 us
    ppermute x4, starting transfers between devices, per_device(): far = lax.ppermute(window, 'ctx', line).astype(F32)  19.3 us
    unnamed x54, local copies, waits for them, and re-layouts  18.2 us
    all_to_all x1, waiting for transfers between devices, per_device(): lax.all_to_all(down.reshape(n_ctx, cap, width), 'ctx', split_axis=0, conc...  15.1 us
    ppermute x10, waiting for transfers between devices, shifted(): return lax.ppermute(value, 'ctx', to)  12.7 us
    pallas_call x1, Pallas kernels, per_device(): pl.pallas_call(functools.partial(ffn_kernel, len(pieces), blocks), out_sh...  11.9 us
    ppermute x10, starting transfers between devices, shifted(): return lax.ppermute(value, 'ctx', to)  10.2 us
  transfers between devices with their start and end apart: 46, of which 23 were waited for; matrix products, arithmetic and copies ran while one was open for 5% of the time, Pallas kernels for 5%

profile of v3, /device:TPU:0, one launch (start us, length us, event | category | flops | bytes accessed | tf_op | source)
XLA Modules:
  0.0 202.9 jit_solution(13733565016757876967)
XLA Ops:
  1.4 2.3 %shard_state.1 = (bf16[4,128,128]{2,1,0:T(8,128)(2,1)S(1)}, bf16[4,128,128]{2,1,0:T(8,128)(2,1)S(1)}, bf16[4,128,128]{2,1,0:T(8,128)(2,1)S(1)}, bf16[4,128,128]{2,1,0:T(8,128)(2,1)S(1)}) custom-call(s32[2]{0:T(128)S(1)} %pad_add_fusion.1.place_ref, f32[16]{0:T(128)S(1)} %copy-done.3, bf16[128,2048]{1,0:T(8,128)(2,1)} %k_ref.3, bf16[128,2048]{1,0:T(8,128)(2,1)} %v_ref.3), custom_call_target="tpu_custom_call" | custom-call | flops 2000000000 | bytes 1000000 | tf_op jit(solution)/shard_map/shard_state/pallas_call | solution.py:262
  3.7 3.0 %collective-permute-start = (bf16[4,128,128]{2,1,0:T(8,128)(2,1)S(1)}, bf16[4,128,128]{2,1,0:T(8,128)(2,1)S(1)}, u32[]{:S(2)}, u32[]{:S(2)}) collective-permute-start(bf16[4,128,128]{2,1,0:T(8,128)(2,1)S(1)} %get-tuple-element.34), channel_id=1, source_target_pairs={{0,4},{4,0},{8,12},{12,8},{16,20},{20,16},{24,28},{28,24},{1,5},{5... | collective-permute-start | bytes 393224 | tf_op jit(solution)/shard_map/ppermute | solution.py:253
  7.0 1.2 near_part.2
  10.4 4.4 %collective-permute-start.1 = (bf16[4,128,128]{2,1,0:T(8,128)(2,1)S(1)}, bf16[4,128,128]{2,1,0:T(8,128)(2,1)}, u32[]{:S(2)}, u32[]{:S(2)}) collective-permute-start(bf16[4,128,128]{2,1,0:T(8,128)(2,1)S(1)} %fusion.1), channel_id=1, source_target_pairs={{0,8},{4,12},{8,16},{12,20},{16,24},{20,28},{1,9},{5,13},{9,17},{1... | collective-permute-start | bytes 393224 | tf_op jit(solution)/shard_map/ppermute | solution.py:307
  14.7 1.6 collective-permute-start.5
  16.6 1.0 fusion.4
  17.6 5.5 %collective-permute-start.2 = (bf16[4,128,128]{2,1,0:T(8,128)(2,1)S(1)}, bf16[4,128,128]{2,1,0:T(8,128)(2,1)S(1)}, u32[]{:S(2)}, u32[]{:S(2)}) collective-permute-start(bf16[4,128,128]{2,1,0:T(8,128)(2,1)S(1)} %fusion.4), channel_id=1, source_target_pairs={{0,16},{4,20},{8,24},{12,28},{1,17},{5,21},{9,25},{13,29},{2,18},{... | collective-permute-start | bytes 393224 | tf_op jit(solution)/shard_map/ppermute | solution.py:307
  23.2 3.5 %collective-permute-start.6 = (bf16[4,128,128]{2,1,0:T(8,128)(2,1)S(1)}, bf16[4,128,128]{2,1,0:T(8,128)(2,1)S(1)}, u32[]{:S(2)}, u32[]{:S(2)}) collective-permute-start(bf16[4,128,128]{2,1,0:T(8,128)(2,1)S(1)} %fusion.6), channel_id=1, source_target_pairs={{0,8},{4,12},{8,16},{12,20},{16,24},{20,28},{1,9},{5,13},{9,17},{1... | collective-permute-start | bytes 393224 | tf_op jit(solution)/shard_map/ppermute | solution.py:307
  26.8 1.1 select_convert_fusion.2
  27.8 1.6 collective-permute-start.3
  30.2 6.0 %collective-permute-start.7 = (bf16[4,128,128]{2,1,0:T(8,128)(2,1)}, bf16[4,128,128]{2,1,0:T(8,128)(2,1)}, u32[]{:S(2)}, u32[]{:S(2)}) collective-permute-start(bf16[4,128,128]{2,1,0:T(8,128)(2,1)} %fusion.9), channel_id=1, source_target_pairs={{0,16},{4,20},{8,24},{12,28},{1,17},{5,21},{9,25},{13,29},{2,18},{... | collective-permute-start | bytes 393224 | tf_op jit(solution)/shard_map/ppermute | solution.py:307
  36.2 1.0 mix_heads.2.refs_0_
  38.8 4.5 %all-to-all-start = ((bf16[8,16,768]{2,1,0:T(8,128)(2,1)}), bf16[8,16,768]{2,1,0:T(8,128)(2,1)S(1)}, u32[]{:S(2)}, u32[]{:S(2)}) async-start(bf16[8,16,768]{2,1,0:T(8,128)(2,1)} %pad_maximum_fusion), calls=%async_computation | async-start | bytes 393216 | tf_op jit(solution)/shard_map/all_to_all | solution.py:347
  43.4 1.1 select_convert_fusion
  44.4 2.1 %collective-permute-start.8 = (bf16[4,128,128]{2,1,0:T(8,128)(2,1)S(1)}, bf16[4,128,128]{2,1,0:T(8,128)(2,1)S(1)}, u32[]{:S(2)}, u32[]{:S(2)}) collective-permute-start(bf16[4,128,128]{2,1,0:T(8,128)(2,1)S(1)} %get-tuple-element.58), channel_id=1, source_target_pairs={{0,4},{4,0},{8,12},{12,8},{16,20},{20,16},{24,28},{28,24},{1,5},{5... | collective-permute-start | bytes 393224 | tf_op jit(solution)/shard_map/ppermute | solution.py:253
  46.5 1.2 near_part.3
  47.8 2.0 collective-permute-start.12
  49.8 1.7 collective-permute-done.8.other_ref
  51.5 1.0 mix_heads.3.refs_2_
  52.4 2.0 collective-permute-start.9
  54.4 1.3 collective-permute-start.14
  55.7 2.8 %all-to-all-done = bf16[8,16,768]{2,1,0:T(8,128)(2,1)S(1)} async-done(((bf16[8,16,768]{2,1,0:T(8,128)(2,1)}), bf16[8,16,768]{2,1,0:T(8,128)(2,1)S(1)}, u32[]{:S(2)}, u32[]{:S(2)}) %all-to-all-start) | async-done | bytes 196640 | tf_op jit(solution)/shard_map/all_to_all | solution.py:347
  60.2 1.9 copy-done.5
  62.1 1.5 project.4
  63.9 3.6 %collective-permute-start.13 = (bf16[128,1024]{1,0:T(8,128)(2,1)S(1)}, bf16[128,1024]{1,0:T(8,128)(2,1)S(1)}, u32[]{:S(2)}, u32[]{:S(2)}) collective-permute-start(bf16[128,1024]{1,0:T(8,128)(2,1)S(1)} %collective-permute-done.12.refs_0_), channel_id=1, source_target_pairs={{0,4},{4,0},{8,12},{12,8},{16,20},{20,16},{24,28},{28,24},{1,5},{5... | collective-permute-start | bytes 786440 | tf_op jit(solution)/shard_map/ppermute | solution.py:253
  67.6 1.1 collective-permute-start.20
  68.9 1.6 collective-permute-start.11
  70.4 4.1 %collective-permute-done.13.refs_1_ = bf16[128,1024]{1,0:T(8,128)(2,1)S(1)} collective-permute-done((bf16[128,1024]{1,0:T(8,128)(2,1)S(1)}, bf16[128,1024]{1,0:T(8,128)(2,1)S(1)}, u32[]{:S(2)}, u32[]{:S(2)}) %collective-permute-start.13) | collective-permute-done | bytes 262176 | tf_op jit(solution)/shard_map/ppermute | solution.py:253
  74.5 9.6 %collective-permute-done.15.refs_3_ = bf16[128,1024]{1,0:T(8,128)(2,1)S(1)} collective-permute-done((bf16[128,1024]{1,0:T(8,128)(2,1)S(1)}, bf16[128,1024]{1,0:T(8,128)(2,1)S(1)}, u32[]{:S(2)}, u32[]{:S(2)}) %collective-permute-start.15) | collective-permute-done | bytes 262176 | tf_op jit(solution)/shard_map/ppermute | solution.py:257
  84.1 1.9 copy-done.6
  86.0 1.5 project.5
  87.9 1.1 collective-permute-done.20.refs_2_
  90.0 1.6 collective-permute-start.17
  91.6 5.4 %collective-permute-done.19.refs_1_ = bf16[128,1024]{1,0:T(8,128)(2,1)S(1)} collective-permute-done((bf16[128,1024]{1,0:T(8,128)(2,1)S(1)}, bf16[128,1024]{1,0:T(8,128)(2,1)S(1)}, u32[]{:S(2)}, u32[]{:S(2)}) %collective-permute-start.19) | collective-permute-done | bytes 262176 | tf_op jit(solution)/shard_map/ppermute | solution.py:253
  96.9 5.2 %collective-permute-done.21.refs_3_ = bf16[128,1024]{1,0:T(8,128)(2,1)S(1)} collective-permute-done((bf16[128,1024]{1,0:T(8,128)(2,1)S(1)}, bf16[128,1024]{1,0:T(8,128)(2,1)S(1)}, u32[]{:S(2)}, u32[]{:S(2)}) %collective-permute-start.21) | collective-permute-done | bytes 262176 | tf_op jit(solution)/shard_map/ppermute | solution.py:253
  102.2 1.9 copy-done.7
  104.1 1.6 project.6
  106.1 1.7 collective-permute-start.27
  108.0 1.6 collective-permute-start.23
  109.5 5.4 %collective-permute-done.25.refs_1_ = bf16[128,1024]{1,0:T(8,128)(2,1)S(1)} collective-permute-done((bf16[128,1024]{1,0:T(8,128)(2,1)S(1)}, bf16[128,1024]{1,0:T(8,128)(2,1)S(1)}, u32[]{:S(2)}, u32[]{:S(2)}) %collective-permute-start.25) | collective-permute-done | bytes 262176 | tf_op jit(solution)/shard_map/ppermute | solution.py:253
  114.9 5.2 %collective-permute-done.27.refs_3_ = bf16[128,1024]{1,0:T(8,128)(2,1)S(1)} collective-permute-done((bf16[128,1024]{1,0:T(8,128)(2,1)S(1)}, bf16[128,1024]{1,0:T(8,128)(2,1)S(1)}, u32[]{:S(2)}, u32[]{:S(2)}) %collective-permute-start.27) | collective-permute-done | bytes 262176 | tf_op jit(solution)/shard_map/ppermute | solution.py:253
  120.1 1.6 project.7
  121.8 1.4 collective-permute-done.28
  123.3 1.6 collective-permute-start.29
  124.9 3.9 %collective-permute-done.29 = bf16[1,80,768]{2,1,0:T(8,128)(2,1)S(1)} collective-permute-done((bf16[1,80,768]{2,1,0:T(8,128)(2,1)S(1)}, bf16[1,80,768]{2,1,0:T(8,128)(2,1)S(1)}, u32[]{:S(2)}, u32[]{:S(2)}) %collective-permute-start.29) | collective-permute-done | bytes 122912 | tf_op jit(solution)/shard_map/ppermute | solution.py:389
  129.8 1.7 collective-permute-start.30
  131.9 3.1 %collective-permute-done.30 = bf16[32,768]{1,0:T(8,128)(2,1)S(1)} collective-permute-done((bf16[32,768]{1,0:T(8,128)(2,1)S(1)}, bf16[32,768]{1,0:T(8,128)(2,1)S(1)}, u32[]{:S(2)}, u32[]{:S(2)}) %collective-permute-start.30) | collective-permute-done | bytes 49184 | tf_op jit(solution)/shard_map/ppermute | solution.py:253
  136.0 1.1 collective-permute-start.35
  137.1 2.0 collective-permute-done.33
  139.1 3.2 %collective-permute-start.32 = (bf16[2,32,768]{2,1,0:T(8,128)(2,1)S(1)}, bf16[2,32,768]{2,1,0:T(8,128)(2,1)S(1)}, u32[]{:S(2)}, u32[]{:S(2)}) collective-permute-start(bf16[2,32,768]{2,1,0:T(8,128)(2,1)S(1)} %pad_maximum_fusion.1), channel_id=1, source_target_pairs={{0,24},{4,28},{8,0},{12,4},{16,8},{20,12},{24,16},{28,20},{1,25},{... | collective-permute-start | bytes 294920 | tf_op jit(solution)/shard_map/ppermute | solution.py:257
  142.7 2.2 %collective-permute-start.36 = (bf16[2,32,768]{2,1,0:T(8,128)(2,1)S(1)}, bf16[2,32,768]{2,1,0:T(8,128)(2,1)S(1)}, u32[]{:S(2)}, u32[]{:S(2)}) collective-permute-start(bf16[2,32,768]{2,1,0:T(8,128)(2,1)S(1)} %pad_maximum_fusion.3), channel_id=1, source_target_pairs={{0,8},{4,12},{8,16},{12,20},{16,24},{20,28},{24,0},{28,4},{1,9},{5... | collective-permute-start | bytes 294920 | tf_op jit(solution)/shard_map/ppermute | solution.py:257
  145.4 1.0 collective-permute-start.39
  146.4 2.9 %collective-permute-start.42 = (bf16[64,768]{1,0:T(8,128)(2,1)S(1)}, bf16[64,768]{1,0:T(8,128)(2,1)S(1)}, u32[]{:S(2)}, u32[]{:S(2)}) collective-permute-start(bf16[64,768]{1,0:T(8,128)(2,1)S(1)} %collective-permute-done.38.refs_2_), channel_id=1, source_target_pairs={{0,16},{4,20},{8,24},{12,28},{16,0},{20,4},{24,8},{28,12},{1,17},{... | collective-permute-start | bytes 294920 | tf_op jit(solution)/shard_map/ppermute | solution.py:408
  149.3 1.5 collective-permute-done.34
  150.9 1.8 collective-permute-start.41
  152.7 1.0 collective-permute-start.43
  154.3 1.1 collective-permute-done.41.refs_5_
  155.5 1.9 collective-permute-done.43.refs_7_
  157.4 5.0 %copy-done = bf16[1,6144,1152]{2,1,0:T(8,128)(2,1)S(1)} copy-done((bf16[1,6144,1152]{2,1,0:T(8,128)(2,1)S(1)}, bf16[1,6144,1152]{2,1,0:T(8,128)(2,1)}, u32[]{:S(2)}) %copy-start) | copy-done | bytes 14155800
  162.4 5.0 %copy-done.1 = bf16[1,6144,1152]{2,1,0:T(8,128)(2,1)S(1)} copy-done((bf16[1,6144,1152]{2,1,0:T(8,128)(2,1)S(1)}, bf16[1,6144,1152]{2,1,0:T(8,128)(2,1)}, u32[]{:S(2)}) %copy-start.1) | copy-done | bytes 14155800
  167.4 11.9 %expert.1 = bf16[64,6144]{1,0:T(8,128)(2,1)} custom-call(s32[8]{0:T(128)S(1)} %iota_xor_fusion.order_ref, bf16[64,768]{1,0:T(8,128)(2,1)S(1)} %slot_hidden.1.refs_0_, bf16[64,768]{1,0:T(8,128)(2,1)S(1)} %collective-permute-done.37.refs_1_, bf16[64,768]{1,0:T(8,128)(2,1)S(1)} %collective-permute-done.38.refs_2_, ...), custom_call_target="tpu_custom_call" | custom-call | flops 10000000000 | bytes 1000000 | tf_op jit(solution)/shard_map/expert/pallas_call | solution.py:427
  179.3 5.6 %all-to-all-start.1 = ((bf16[8,8,6144]{2,1,0:T(8,128)(2,1)}), bf16[8,8,6144]{2,1,0:T(8,128)(2,1)S(1)}, u32[]{:S(2)}, u32[]{:S(2)}) async-start(bf16[8,8,6144]{2,1,0:T(8,128)(2,1)} %bitcast.35), calls=%async_computation.1 | async-start | bytes 1572864 | tf_op jit(solution)/shard_map/all_to_all | solution.py:442
  185.1 1.8 add_convert_fusion
  186.9 15.1 %all-to-all-done.1 = bf16[8,8,6144]{2,1,0:T(8,128)(2,1)S(1)} async-done(((bf16[8,8,6144]{2,1,0:T(8,128)(2,1)}), bf16[8,8,6144]{2,1,0:T(8,128)(2,1)S(1)}, u32[]{:S(2)}, u32[]{:S(2)}) %all-to-all-start.1) | async-done | bytes 786464 | tf_op jit(solution)/shard_map/all_to_all | solution.py:442
  (160 shorter events, 15.0 us)
Async XLA Ops:
  1.4 5.5 %copy-start.4 = (f32[16]{0:T(128)S(1)}, f32[16]{0:T(128)}, u32[]{:S(2)}) copy-start(f32[16]{0:T(128)} %decay_ref.7) | copy-start | bytes 196
  1.4 5.6 %copy-start.9 = (bf16[128,2048]{1,0:T(8,128)(2,1)S(1)}, bf16[128,2048]{1,0:T(8,128)(2,1)}, u32[]{:S(2)}) copy-start(bf16[128,2048]{1,0:T(8,128)(2,1)} %q_ref.3) | copy-start | bytes 1572868
  1.4 5.6 %copy-start.10 = (bf16[128,2048]{1,0:T(8,128)(2,1)S(1)}, bf16[128,2048]{1,0:T(8,128)(2,1)}, u32[]{:S(2)}) copy-start(bf16[128,2048]{1,0:T(8,128)(2,1)} %k_ref.3) | copy-start | bytes 1572868
  1.4 5.6 %copy-start.11 = (bf16[128,2048]{1,0:T(8,128)(2,1)S(1)}, bf16[128,2048]{1,0:T(8,128)(2,1)}, u32[]{:S(2)}) copy-start(bf16[128,2048]{1,0:T(8,128)(2,1)} %v_ref.3) | copy-start | bytes 1572868
  1.4 5.6 %copy-start.12 = (bf16[128,2048]{1,0:T(8,128)(2,1)S(1)}, bf16[128,2048]{1,0:T(8,128)(2,1)}, u32[]{:S(2)}) copy-start(bf16[128,2048]{1,0:T(8,128)(2,1)} %gate_ref.3) | copy-start | bytes 1572868
  1.4 5.6 %copy-start.13 = (f32[2048]{0:T(1024)S(1)}, f32[2048]{0:T(1024)}, u32[]{:S(2)}) copy-start(f32[2048]{0:T(1024)} %param.20) | copy-start | bytes 24580
  3.7 6.5 %collective-permute-start = (bf16[4,128,128]{2,1,0:T(8,128)(2,1)S(1)}, bf16[4,128,128]{2,1,0:T(8,128)(2,1)S(1)}, u32[]{:S(2)}, u32[]{:S(2)}) collective-permute-start(bf16[4,128,128]{2,1,0:T(8,128)(2,1)S(1)} %get-tuple-element.34), channel_id=1, source_target_pairs={{0,4},{4,0},{8,12},{12,8},{16,20},{20,16},{24,28},{28,24},{1,5},{5... | collective-permute-start | bytes 393224 | tf_op jit(solution)/shard_map/ppermute | solution.py:253
  10.4 6.2 %collective-permute-start.1 = (bf16[4,128,128]{2,1,0:T(8,128)(2,1)S(1)}, bf16[4,128,128]{2,1,0:T(8,128)(2,1)}, u32[]{:S(2)}, u32[]{:S(2)}) collective-permute-start(bf16[4,128,128]{2,1,0:T(8,128)(2,1)S(1)} %fusion.1), channel_id=1, source_target_pairs={{0,8},{4,12},{8,16},{12,20},{16,24},{20,28},{1,9},{5,13},{9,17},{1... | collective-permute-start | bytes 393224 | tf_op jit(solution)/shard_map/ppermute | solution.py:307
  14.7 21.4 %copy-start.15 = (f32[128,1024]{1,0:T(8,128)S(1)}, f32[128,1024]{1,0:T(8,128)}, u32[]{:S(2)}) copy-start(f32[128,1024]{1,0:T(8,128)} %copy-done.14) | copy-start | bytes 1572868
  14.7 21.4 %copy-start.17 = (bf16[128,1024]{1,0:T(8,128)(2,1)S(1)}, bf16[128,1024]{1,0:T(8,128)(2,1)}, u32[]{:S(2)}) copy-start(bf16[128,1024]{1,0:T(8,128)(2,1)} %copy-done.16) | copy-start | bytes 786436
  14.7 8.3 %collective-permute-start.5 = (bf16[4,128,128]{2,1,0:T(8,128)(2,1)S(1)}, bf16[4,128,128]{2,1,0:T(8,128)(2,1)S(1)}, u32[]{:S(2)}, u32[]{:S(2)}) collective-permute-start(bf16[4,128,128]{2,1,0:T(8,128)(2,1)S(1)} %get-tuple-element.42), channel_id=1, source_target_pairs={{0,4},{4,0},{8,12},{12,8},{16,20},{20,16},{24,28},{28,24},{1,5},{5... | collective-permute-start | bytes 393224 | tf_op jit(solution)/shard_map/ppermute | solution.py:253
  17.6 9.2 %collective-permute-start.2 = (bf16[4,128,128]{2,1,0:T(8,128)(2,1)S(1)}, bf16[4,128,128]{2,1,0:T(8,128)(2,1)S(1)}, u32[]{:S(2)}, u32[]{:S(2)}) collective-permute-start(bf16[4,128,128]{2,1,0:T(8,128)(2,1)S(1)} %fusion.4), channel_id=1, source_target_pairs={{0,16},{4,20},{8,24},{12,28},{1,17},{5,21},{9,25},{13,29},{2,18},{... | collective-permute-start | bytes 393224 | tf_op jit(solution)/shard_map/ppermute | solution.py:307
  23.1 3.7 %copy-start.19 = (bf16[4,128,128]{2,1,0:T(8,128)(2,1)}, bf16[4,128,128]{2,1,0:T(8,128)(2,1)S(1)}, u32[]{:S(2)}) copy-start(bf16[4,128,128]{2,1,0:T(8,128)(2,1)S(1)} %collective-permute-done.5) | copy-start | bytes 393220
  23.2 6.2 %collective-permute-start.6 = (bf16[4,128,128]{2,1,0:T(8,128)(2,1)S(1)}, bf16[4,128,128]{2,1,0:T(8,128)(2,1)S(1)}, u32[]{:S(2)}, u32[]{:S(2)}) collective-permute-start(bf16[4,128,128]{2,1,0:T(8,128)(2,1)S(1)} %fusion.6), channel_id=1, source_target_pairs={{0,8},{4,12},{8,16},{12,20},{16,24},{20,28},{1,9},{5,13},{9,17},{1... | collective-permute-start | bytes 393224 | tf_op jit(solution)/shard_map/ppermute | solution.py:307
  27.8 8.3 %collective-permute-start.3 = (bf16[4,128,128]{2,1,0:T(8,128)(2,1)S(1)}, bf16[4,128,128]{2,1,0:T(8,128)(2,1)S(1)}, u32[]{:S(2)}, u32[]{:S(2)}) collective-permute-start(bf16[4,128,128]{2,1,0:T(8,128)(2,1)S(1)} %get-tuple-element.60), channel_id=1, source_target_pairs={{0,4},{4,0},{8,12},{12,8},{16,20},{20,16},{24,28},{28,24},{1,5},{5... | collective-permute-start | bytes 393224 | tf_op jit(solution)/shard_map/ppermute | solution.py:253
  29.4 6.7 %copy-start.21 = (bf16[4,128,128]{2,1,0:T(8,128)(2,1)}, bf16[4,128,128]{2,1,0:T(8,128)(2,1)S(1)}, u32[]{:S(2)}) copy-start(bf16[4,128,128]{2,1,0:T(8,128)(2,1)S(1)} %collective-permute-done.6) | copy-start | bytes 393220
  30.2 13.1 %collective-permute-start.7 = (bf16[4,128,128]{2,1,0:T(8,128)(2,1)}, bf16[4,128,128]{2,1,0:T(8,128)(2,1)}, u32[]{:S(2)}, u32[]{:S(2)}) collective-permute-start(bf16[4,128,128]{2,1,0:T(8,128)(2,1)} %fusion.9), channel_id=1, source_target_pairs={{0,16},{4,20},{8,24},{12,28},{1,17},{5,21},{9,25},{13,29},{2,18},{... | collective-permute-start | bytes 393224 | tf_op jit(solution)/shard_map/ppermute | solution.py:307
  37.2 6.2 %copy-start.20 = (bf16[4,128,128]{2,1,0:T(8,128)(2,1)S(1)}, bf16[4,128,128]{2,1,0:T(8,128)(2,1)}, u32[]{:S(2)}) copy-start(bf16[4,128,128]{2,1,0:T(8,128)(2,1)} %copy-done.19) | copy-start | bytes 393220
  37.2 6.2 %copy-start.22 = (bf16[4,128,128]{2,1,0:T(8,128)(2,1)S(1)}, bf16[4,128,128]{2,1,0:T(8,128)(2,1)}, u32[]{:S(2)}) copy-start(bf16[4,128,128]{2,1,0:T(8,128)(2,1)} %copy-done.21) | copy-start | bytes 393220
  38.8 19.7 %all-to-all-start = ((bf16[8,16,768]{2,1,0:T(8,128)(2,1)}), bf16[8,16,768]{2,1,0:T(8,128)(2,1)S(1)}, u32[]{:S(2)}, u32[]{:S(2)}) async-start(bf16[8,16,768]{2,1,0:T(8,128)(2,1)} %pad_maximum_fusion), calls=%async_computation | async-start | bytes 393216 | tf_op jit(solution)/shard_map/all_to_all | solution.py:347
  44.4 7.0 %collective-permute-start.8 = (bf16[4,128,128]{2,1,0:T(8,128)(2,1)S(1)}, bf16[4,128,128]{2,1,0:T(8,128)(2,1)S(1)}, u32[]{:S(2)}, u32[]{:S(2)}) collective-permute-start(bf16[4,128,128]{2,1,0:T(8,128)(2,1)S(1)} %get-tuple-element.58), channel_id=1, source_target_pairs={{0,4},{4,0},{8,12},{12,8},{16,20},{20,16},{24,28},{28,24},{1,5},{5... | collective-permute-start | bytes 393224 | tf_op jit(solution)/shard_map/ppermute | solution.py:253
  47.7 11.8 %collective-permute-start.4 = (bf16[128,1024]{1,0:T(8,128)(2,1)S(1)}, bf16[128,1024]{1,0:T(8,128)(2,1)S(1)}, u32[]{:S(2)}, u32[]{:S(2)}) collective-permute-start(bf16[128,1024]{1,0:T(8,128)(2,1)S(1)} %mix_heads.2.refs_0_), channel_id=1, source_target_pairs={{0,4},{4,0},{8,12},{12,8},{16,20},{20,16},{24,28},{28,24},{1,5},{5... | collective-permute-start | bytes 786440 | tf_op jit(solution)/shard_map/ppermute | solution.py:253
  47.8 16.1 %collective-permute-start.12 = (bf16[128,1024]{1,0:T(8,128)(2,1)S(1)}, bf16[128,1024]{1,0:T(8,128)(2,1)S(1)}, u32[]{:S(2)}, u32[]{:S(2)}) collective-permute-start(bf16[128,1024]{1,0:T(8,128)(2,1)S(1)} %mix_heads.2.refs_0_), channel_id=1, source_target_pairs={{0,8},{4,12},{8,16},{12,20},{16,24},{20,28},{24,0},{28,4},{1,9},{5... | collective-permute-start | bytes 786440 | tf_op jit(solution)/shard_map/ppermute | solution.py:257
  52.4 7.8 %collective-permute-start.9 = (bf16[128,1024]{1,0:T(8,128)(2,1)S(1)}, bf16[128,1024]{1,0:T(8,128)(2,1)S(1)}, u32[]{:S(2)}, u32[]{:S(2)}) collective-permute-start(bf16[128,1024]{1,0:T(8,128)(2,1)S(1)} %mix_heads.3.refs_2_), channel_id=1, source_target_pairs={{0,4},{4,0},{8,12},{12,8},{16,20},{20,16},{24,28},{28,24},{1,5},{5... | collective-permute-start | bytes 786440 | tf_op jit(solution)/shard_map/ppermute | solution.py:253
  54.4 13.2 %collective-permute-start.14 = (bf16[128,1024]{1,0:T(8,128)(2,1)S(1)}, bf16[128,1024]{1,0:T(8,128)(2,1)S(1)}, u32[]{:S(2)}, u32[]{:S(2)}) collective-permute-start(bf16[128,1024]{1,0:T(8,128)(2,1)S(1)} %mix_heads.3.refs_2_), channel_id=1, source_target_pairs={{0,8},{4,12},{8,16},{12,20},{16,24},{20,28},{24,0},{28,4},{1,9},{5... | collective-permute-start | bytes 786440 | tf_op jit(solution)/shard_map/ppermute | solution.py:257
  59.4 4.3 %copy-start.24 = (f32[128,2]{0,1:T(2,128)S(1)}, f32[128,2]{0,1:T(2,128)}, u32[]{:S(2)}) copy-start(f32[128,2]{0,1:T(2,128)} %param.24) | copy-start | bytes 3076
  60.2 1.9 copy-start.5
  63.6 5.1 %collective-permute-start.10 = (bf16[2,80,768]{2,1,0:T(8,128)(2,1)S(1)}, bf16[2,80,768]{2,1,0:T(8,128)(2,1)S(1)}, u32[]{:S(2)}, u32[]{:S(2)}) collective-permute-start(bf16[2,80,768]{2,1,0:T(8,128)(2,1)S(1)} %get-tuple-element.44), channel_id=1, source_target_pairs={{0,1},{1,0},{2,3},{3,2},{4,5},{5,4},{6,7},{7,6},{8,9},{9,8},{10,11... | collective-permute-start | bytes 737288 | tf_op jit(solution)/shard_map/ppermute | solution.py:383
  63.9 10.6 %collective-permute-start.13 = (bf16[128,1024]{1,0:T(8,128)(2,1)S(1)}, bf16[128,1024]{1,0:T(8,128)(2,1)S(1)}, u32[]{:S(2)}, u32[]{:S(2)}) collective-permute-start(bf16[128,1024]{1,0:T(8,128)(2,1)S(1)} %collective-permute-done.12.refs_0_), channel_id=1, source_target_pairs={{0,4},{4,0},{8,12},{12,8},{16,20},{20,16},{24,28},{28,24},{1,5},{5... | collective-permute-start | bytes 786440 | tf_op jit(solution)/shard_map/ppermute | solution.py:253
  67.5 20.3 %collective-permute-start.18 = (bf16[128,1024]{1,0:T(8,128)(2,1)S(1)}, bf16[128,1024]{1,0:T(8,128)(2,1)S(1)}, u32[]{:S(2)}, u32[]{:S(2)}) collective-permute-start(bf16[128,1024]{1,0:T(8,128)(2,1)S(1)} %collective-permute-done.12.refs_0_), channel_id=1, source_target_pairs={{0,8},{4,12},{8,16},{12,20},{16,24},{20,28},{24,0},{28,4},{1,9},{5... | collective-permute-start | bytes 786440 | tf_op jit(solution)/shard_map/ppermute | solution.py:257
  67.6 16.5 %collective-permute-start.15 = (bf16[128,1024]{1,0:T(8,128)(2,1)S(1)}, bf16[128,1024]{1,0:T(8,128)(2,1)S(1)}, u32[]{:S(2)}, u32[]{:S(2)}) collective-permute-start(bf16[128,1024]{1,0:T(8,128)(2,1)S(1)} %collective-permute-done.9.refs_3_), channel_id=1, source_target_pairs={{0,8},{4,12},{8,16},{12,20},{16,24},{20,28},{24,0},{28,4},{1,9},{5... | collective-permute-start | bytes 786440 | tf_op jit(solution)/shard_map/ppermute | solution.py:257
  67.6 21.4 %collective-permute-start.20 = (bf16[128,1024]{1,0:T(8,128)(2,1)S(1)}, bf16[128,1024]{1,0:T(8,128)(2,1)S(1)}, u32[]{:S(2)}, u32[]{:S(2)}) collective-permute-start(bf16[128,1024]{1,0:T(8,128)(2,1)S(1)} %collective-permute-done.14.refs_2_), channel_id=1, source_target_pairs={{0,8},{4,12},{8,16},{12,20},{16,24},{20,28},{24,0},{28,4},{1,9},{5... | collective-permute-start | bytes 786440 | tf_op jit(solution)/shard_map/ppermute | solution.py:257
  68.9 21.0 %collective-permute-start.11 = (bf16[1,80,768]{2,1,0:T(8,128)(2,1)S(1)}, bf16[1,80,768]{2,1,0:T(8,128)(2,1)S(1)}, u32[]{:S(2)}, u32[]{:S(2)}) collective-permute-start(bf16[1,80,768]{2,1,0:T(8,128)(2,1)S(1)} %get-tuple-element.69), channel_id=1, source_target_pairs={{0,2},{1,3},{2,0},{3,1},{4,6},{5,7},{6,4},{7,5},{8,10},{9,11},{10,... | collective-permute-start | bytes 368648 | tf_op jit(solution)/shard_map/ppermute | solution.py:389
  87.5 2.4 %collective-permute-start.16 = (bf16[2,80,768]{2,1,0:T(8,128)(2,1)S(1)}, bf16[2,80,768]{2,1,0:T(8,128)(2,1)S(1)}, u32[]{:S(2)}, u32[]{:S(2)}) collective-permute-start(bf16[2,80,768]{2,1,0:T(8,128)(2,1)S(1)} %get-tuple-element.46), channel_id=1, source_target_pairs={{0,1},{1,0},{2,3},{3,2},{4,5},{5,4},{6,7},{7,6},{8,9},{9,8},{10,11... | collective-permute-start | bytes 737288 | tf_op jit(solution)/shard_map/ppermute | solution.py:383
  87.8 9.2 %collective-permute-start.19 = (bf16[128,1024]{1,0:T(8,128)(2,1)S(1)}, bf16[128,1024]{1,0:T(8,128)(2,1)S(1)}, u32[]{:S(2)}, u32[]{:S(2)}) collective-permute-start(bf16[128,1024]{1,0:T(8,128)(2,1)S(1)} %collective-permute-done.18.refs_0_), channel_id=1, source_target_pairs={{0,4},{4,0},{8,12},{12,8},{16,20},{20,16},{24,28},{28,24},{1,5},{5... | collective-permute-start | bytes 786440 | tf_op jit(solution)/shard_map/ppermute | solution.py:253
  87.9 17.9 %collective-permute-start.24 = (bf16[128,1024]{1,0:T(8,128)(2,1)S(1)}, bf16[128,1024]{1,0:T(8,128)(2,1)S(1)}, u32[]{:S(2)}, u32[]{:S(2)}) collective-permute-start(bf16[128,1024]{1,0:T(8,128)(2,1)S(1)} %collective-permute-done.18.refs_0_), channel_id=1, source_target_pairs={{0,8},{4,12},{8,16},{12,20},{16,24},{20,28},{24,0},{28,4},{1,9},{5... | collective-permute-start | bytes 786440 | tf_op jit(solution)/shard_map/ppermute | solution.py:257
  89.0 13.2 %collective-permute-start.21 = (bf16[128,1024]{1,0:T(8,128)(2,1)S(1)}, bf16[128,1024]{1,0:T(8,128)(2,1)S(1)}, u32[]{:S(2)}, u32[]{:S(2)}) collective-permute-start(bf16[128,1024]{1,0:T(8,128)(2,1)S(1)} %collective-permute-done.20.refs_2_), channel_id=1, source_target_pairs={{0,4},{4,0},{8,12},{12,8},{16,20},{20,16},{24,28},{28,24},{1,5},{5... | collective-permute-start | bytes 786440 | tf_op jit(solution)/shard_map/ppermute | solution.py:253
  89.9 16.2 %collective-permute-start.26 = (bf16[128,1024]{1,0:T(8,128)(2,1)S(1)}, bf16[128,1024]{1,0:T(8,128)(2,1)S(1)}, u32[]{:S(2)}, u32[]{:S(2)}) collective-permute-start(bf16[128,1024]{1,0:T(8,128)(2,1)S(1)} %collective-permute-done.20.refs_2_), channel_id=1, source_target_pairs={{0,8},{4,12},{8,16},{12,20},{16,24},{20,28},{24,0},{28,4},{1,9},{5... | collective-permute-start | bytes 786440 | tf_op jit(solution)/shard_map/ppermute | solution.py:257
  90.0 17.8 %collective-permute-start.17 = (bf16[1,80,768]{2,1,0:T(8,128)(2,1)S(1)}, bf16[1,80,768]{2,1,0:T(8,128)(2,1)S(1)}, u32[]{:S(2)}, u32[]{:S(2)}) collective-permute-start(bf16[1,80,768]{2,1,0:T(8,128)(2,1)S(1)} %get-tuple-element.66), channel_id=1, source_target_pairs={{0,2},{1,3},{2,0},{3,1},{4,6},{5,7},{6,4},{7,5},{8,10},{9,11},{10,... | collective-permute-start | bytes 368648 | tf_op jit(solution)/shard_map/ppermute | solution.py:389
  104.1 16.1 %copy-start.8 = (bf16[2048,768]{1,0:T(8,128)(2,1)S(1)}, bf16[2048,768]{1,0:T(8,128)(2,1)}, u32[]{:S(2)}) copy-start(bf16[2048,768]{1,0:T(8,128)(2,1)} %refs_4_.7) | copy-start | bytes 9437188
  105.6 2.3 %collective-permute-start.22 = (bf16[2,80,768]{2,1,0:T(8,128)(2,1)S(1)}, bf16[2,80,768]{2,1,0:T(8,128)(2,1)S(1)}, u32[]{:S(2)}, u32[]{:S(2)}) collective-permute-start(bf16[2,80,768]{2,1,0:T(8,128)(2,1)S(1)} %get-tuple-element.48), channel_id=1, source_target_pairs={{0,1},{1,0},{2,3},{3,2},{4,5},{5,4},{6,7},{7,6},{8,9},{9,8},{10,11... | collective-permute-start | bytes 737288 | tf_op jit(solution)/shard_map/ppermute | solution.py:383
  105.7 9.2 %collective-permute-start.25 = (bf16[128,1024]{1,0:T(8,128)(2,1)S(1)}, bf16[128,1024]{1,0:T(8,128)(2,1)S(1)}, u32[]{:S(2)}, u32[]{:S(2)}) collective-permute-start(bf16[128,1024]{1,0:T(8,128)(2,1)S(1)} %collective-permute-done.24.refs_0_), channel_id=1, source_target_pairs={{0,4},{4,0},{8,12},{12,8},{16,20},{20,16},{24,28},{28,24},{1,5},{5... | collective-permute-start | bytes 786440 | tf_op jit(solution)/shard_map/ppermute | solution.py:253
  106.1 14.0 %collective-permute-start.27 = (bf16[128,1024]{1,0:T(8,128)(2,1)S(1)}, bf16[128,1024]{1,0:T(8,128)(2,1)S(1)}, u32[]{:S(2)}, u32[]{:S(2)}) collective-permute-start(bf16[128,1024]{1,0:T(8,128)(2,1)S(1)} %collective-permute-done.26.refs_2_), channel_id=1, source_target_pairs={{0,4},{4,0},{8,12},{12,8},{16,20},{20,16},{24,28},{28,24},{1,5},{5... | collective-permute-start | bytes 786440 | tf_op jit(solution)/shard_map/ppermute | solution.py:253
  108.0 13.8 %collective-permute-start.23 = (bf16[1,80,768]{2,1,0:T(8,128)(2,1)S(1)}, bf16[1,80,768]{2,1,0:T(8,128)(2,1)S(1)}, u32[]{:S(2)}, u32[]{:S(2)}) collective-permute-start(bf16[1,80,768]{2,1,0:T(8,128)(2,1)S(1)} %get-tuple-element.64), channel_id=1, source_target_pairs={{0,2},{1,3},{2,0},{3,1},{4,6},{5,7},{6,4},{7,5},{8,10},{9,11},{10,... | collective-permute-start | bytes 368648 | tf_op jit(solution)/shard_map/ppermute | solution.py:389
  121.7 1.6 collective-permute-start.28
  123.3 5.4 %collective-permute-start.29 = (bf16[1,80,768]{2,1,0:T(8,128)(2,1)S(1)}, bf16[1,80,768]{2,1,0:T(8,128)(2,1)S(1)}, u32[]{:S(2)}, u32[]{:S(2)}) collective-permute-start(bf16[1,80,768]{2,1,0:T(8,128)(2,1)S(1)} %get-tuple-element.62), channel_id=1, source_target_pairs={{0,2},{1,3},{2,0},{3,1},{4,6},{5,7},{6,4},{7,5},{8,10},{9,11},{10,... | collective-permute-start | bytes 368648 | tf_op jit(solution)/shard_map/ppermute | solution.py:389
  129.4 28.0 %copy-start.2 = (f32[6144]{0:T(1024)S(1)}, f32[6144]{0:T(1024)}, u32[]{:S(2)}) copy-start(f32[6144]{0:T(1024)} %param.22) | copy-start | bytes 73732
  129.4 24.9 %collective-permute-start.37 = (bf16[64,768]{1,0:T(8,128)(2,1)S(1)}, bf16[64,768]{1,0:T(8,128)(2,1)S(1)}, u32[]{:S(2)}, u32[]{:S(2)}) collective-permute-start(bf16[64,768]{1,0:T(8,128)(2,1)S(1)} %slot_hidden.1.refs_0_), channel_id=1, source_target_pairs={{0,4},{4,0},{8,12},{12,8},{16,20},{20,16},{24,28},{28,24},{1,5},{5... | collective-permute-start | bytes 294920 | tf_op jit(solution)/shard_map/ppermute | solution.py:253
  129.7 12.9 %collective-permute-start.38 = (bf16[64,768]{1,0:T(8,128)(2,1)S(1)}, bf16[64,768]{1,0:T(8,128)(2,1)S(1)}, u32[]{:S(2)}, u32[]{:S(2)}) collective-permute-start(bf16[64,768]{1,0:T(8,128)(2,1)S(1)} %slot_hidden.1.refs_0_), channel_id=1, source_target_pairs={{0,8},{4,12},{8,0},{12,4},{16,24},{20,28},{24,16},{28,20},{1,9},{5... | collective-permute-start | bytes 294920 | tf_op jit(solution)/shard_map/ppermute | solution.py:408
  129.7 16.7 %collective-permute-start.40 = (bf16[64,768]{1,0:T(8,128)(2,1)S(1)}, bf16[64,768]{1,0:T(8,128)(2,1)S(1)}, u32[]{:S(2)}, u32[]{:S(2)}) collective-permute-start(bf16[64,768]{1,0:T(8,128)(2,1)S(1)} %slot_hidden.1.refs_0_), channel_id=1, source_target_pairs={{0,16},{4,20},{8,24},{12,28},{16,0},{20,4},{24,8},{28,12},{1,17},{... | collective-permute-start | bytes 294920 | tf_op jit(solution)/shard_map/ppermute | solution.py:408
  129.8 5.2 %collective-permute-start.30 = (bf16[32,768]{1,0:T(8,128)(2,1)S(1)}, bf16[32,768]{1,0:T(8,128)(2,1)S(1)}, u32[]{:S(2)}, u32[]{:S(2)}) collective-permute-start(bf16[32,768]{1,0:T(8,128)(2,1)S(1)} %slice.153), channel_id=1, source_target_pairs={{0,4},{4,0},{8,12},{12,8},{16,20},{20,16},{24,28},{28,24},{1,5},{5... | collective-permute-start | bytes 147464 | tf_op jit(solution)/shard_map/ppermute | solution.py:253
  131.6 4.4 %collective-permute-start.31 = (bf16[32,768]{1,0:T(8,128)(2,1)S(1)}, bf16[32,768]{1,0:T(8,128)(2,1)S(1)}, u32[]{:S(2)}, u32[]{:S(2)}) collective-permute-start(bf16[32,768]{1,0:T(8,128)(2,1)S(1)} %get-tuple-element.52), channel_id=1, source_target_pairs={{0,4},{4,0},{8,12},{12,8},{16,20},{20,16},{24,28},{28,24},{1,5},{5... | collective-permute-start | bytes 147464 | tf_op jit(solution)/shard_map/ppermute | solution.py:253
  135.0 4.1 %collective-permute-start.33 = (bf16[32,768]{1,0:T(8,128)(2,1)S(1)}, bf16[32,768]{1,0:T(8,128)(2,1)S(1)}, u32[]{:S(2)}, u32[]{:S(2)}) collective-permute-start(bf16[32,768]{1,0:T(8,128)(2,1)S(1)} %get-tuple-element.53), channel_id=1, source_target_pairs={{0,4},{4,0},{8,12},{12,8},{16,20},{20,16},{24,28},{28,24},{1,5},{5... | collective-permute-start | bytes 147464 | tf_op jit(solution)/shard_map/ppermute | solution.py:253
  136.0 6.3 %collective-permute-start.35 = (bf16[32,768]{1,0:T(8,128)(2,1)S(1)}, bf16[32,768]{1,0:T(8,128)(2,1)S(1)}, u32[]{:S(2)}, u32[]{:S(2)}) collective-permute-start(bf16[32,768]{1,0:T(8,128)(2,1)S(1)} %get-tuple-element.54), channel_id=1, source_target_pairs={{0,4},{4,0},{8,12},{12,8},{16,20},{20,16},{24,28},{28,24},{1,5},{5... | collective-permute-start | bytes 147464 | tf_op jit(solution)/shard_map/ppermute | solution.py:253
  139.1 6.2 %collective-permute-start.32 = (bf16[2,32,768]{2,1,0:T(8,128)(2,1)S(1)}, bf16[2,32,768]{2,1,0:T(8,128)(2,1)S(1)}, u32[]{:S(2)}, u32[]{:S(2)}) collective-permute-start(bf16[2,32,768]{2,1,0:T(8,128)(2,1)S(1)} %pad_maximum_fusion.1), channel_id=1, source_target_pairs={{0,24},{4,28},{8,0},{12,4},{16,8},{20,12},{24,16},{28,20},{1,25},{... | collective-permute-start | bytes 294920 | tf_op jit(solution)/shard_map/ppermute | solution.py:257
  142.3 8.5 %collective-permute-start.34 = (bf16[2,32,768]{2,1,0:T(8,128)(2,1)S(1)}, bf16[2,32,768]{2,1,0:T(8,128)(2,1)S(1)}, u32[]{:S(2)}, u32[]{:S(2)}) collective-permute-start(bf16[2,32,768]{2,1,0:T(8,128)(2,1)S(1)} %pad_maximum_fusion.2), channel_id=1, source_target_pairs={{0,16},{4,20},{8,24},{12,28},{16,0},{20,4},{24,8},{28,12},{1,17},{... | collective-permute-start | bytes 294920 | tf_op jit(solution)/shard_map/ppermute | solution.py:257
  142.7 11.1 %collective-permute-start.36 = (bf16[2,32,768]{2,1,0:T(8,128)(2,1)S(1)}, bf16[2,32,768]{2,1,0:T(8,128)(2,1)S(1)}, u32[]{:S(2)}, u32[]{:S(2)}) collective-permute-start(bf16[2,32,768]{2,1,0:T(8,128)(2,1)S(1)} %pad_maximum_fusion.3), channel_id=1, source_target_pairs={{0,8},{4,12},{8,16},{12,20},{16,24},{20,28},{24,0},{28,4},{1,9},{5... | collective-permute-start | bytes 294920 | tf_op jit(solution)/shard_map/ppermute | solution.py:257
  145.4 9.0 %collective-permute-start.39 = (bf16[64,768]{1,0:T(8,128)(2,1)S(1)}, bf16[64,768]{1,0:T(8,128)(2,1)S(1)}, u32[]{:S(2)}, u32[]{:S(2)}) collective-permute-start(bf16[64,768]{1,0:T(8,128)(2,1)S(1)} %collective-permute-done.38.refs_2_), channel_id=1, source_target_pairs={{0,4},{4,0},{8,12},{12,8},{16,20},{20,16},{24,28},{28,24},{1,5},{5... | collective-permute-start | bytes 294920 | tf_op jit(solution)/shard_map/ppermute | solution.py:253
  146.4 6.3 %collective-permute-start.42 = (bf16[64,768]{1,0:T(8,128)(2,1)S(1)}, bf16[64,768]{1,0:T(8,128)(2,1)S(1)}, u32[]{:S(2)}, u32[]{:S(2)}) collective-permute-start(bf16[64,768]{1,0:T(8,128)(2,1)S(1)} %collective-permute-done.38.refs_2_), channel_id=1, source_target_pairs={{0,16},{4,20},{8,24},{12,28},{16,0},{20,4},{24,8},{28,12},{1,17},{... | collective-permute-start | bytes 294920 | tf_op jit(solution)/shard_map/ppermute | solution.py:408
  150.9 4.6 %collective-permute-start.41 = (bf16[64,768]{1,0:T(8,128)(2,1)S(1)}, bf16[64,768]{1,0:T(8,128)(2,1)S(1)}, u32[]{:S(2)}, u32[]{:S(2)}) collective-permute-start(bf16[64,768]{1,0:T(8,128)(2,1)S(1)} %collective-permute-done.40.refs_4_), channel_id=1, source_target_pairs={{0,4},{4,0},{8,12},{12,8},{16,20},{20,16},{24,28},{28,24},{1,5},{5... | collective-permute-start | bytes 294920 | tf_op jit(solution)/shard_map/ppermute | solution.py:253
  152.7 4.7 %collective-permute-start.43 = (bf16[64,768]{1,0:T(8,128)(2,1)S(1)}, bf16[64,768]{1,0:T(8,128)(2,1)S(1)}, u32[]{:S(2)}, u32[]{:S(2)}) collective-permute-start(bf16[64,768]{1,0:T(8,128)(2,1)S(1)} %collective-permute-done.42.refs_6_), channel_id=1, source_target_pairs={{0,4},{4,0},{8,12},{12,8},{16,20},{20,16},{24,28},{28,24},{1,5},{5... | collective-permute-start | bytes 294920 | tf_op jit(solution)/shard_map/ppermute | solution.py:253
  157.4 5.0 %copy-start = (bf16[1,6144,1152]{2,1,0:T(8,128)(2,1)S(1)}, bf16[1,6144,1152]{2,1,0:T(8,128)(2,1)}, u32[]{:S(2)}) copy-start(bf16[1,6144,1152]{2,1,0:T(8,128)(2,1)} %refs_9_.1) | copy-start | bytes 42467332
  162.4 5.0 %copy-start.1 = (bf16[1,6144,1152]{2,1,0:T(8,128)(2,1)S(1)}, bf16[1,6144,1152]{2,1,0:T(8,128)(2,1)}, u32[]{:S(2)}) copy-start(bf16[1,6144,1152]{2,1,0:T(8,128)(2,1)} %refs_10_.1) | copy-start | bytes 42467332
  179.3 22.7 %all-to-all-start.1 = ((bf16[8,8,6144]{2,1,0:T(8,128)(2,1)}), bf16[8,8,6144]{2,1,0:T(8,128)(2,1)S(1)}, u32[]{:S(2)}, u32[]{:S(2)}) async-start(bf16[8,8,6144]{2,1,0:T(8,128)(2,1)} %bitcast.35), calls=%async_computation.1 | async-start | bytes 1572864 | tf_op jit(solution)/shard_map/all_to_all | solution.py:442
  (7 other events, 8.4 us)

commit v4 on v3

--- a/solution.py
+++ b/solution.py
@@ -136,14 +136,12 @@
                 ]
 
 
-def project_kernel(n_exp, cap, token_ref, *refs):
-    weight_ref, keep_ref, send_ref = refs[-3:]
+def project_kernel(n_exp, *refs):
+    weight_ref, outs = refs[-3], refs[-2:]
     pairs = refs[:-3]
     chunks = len(pairs) // 2
     wide = pairs[0].shape[1]
-    tok = pairs[0].shape[0]
-    own_rows = tok // n_exp
-    slots_of = []
+    own_rows = pairs[0].shape[0] // n_exp
     for y in range(2):
         total = None
         for chunk in range(chunks):
@@ -154,42 +152,53 @@
             )
             total = part if total is None else total + part
         rows = total.astype(BF16)
-        pick = token_ref[y] == lax.broadcasted_iota(jnp.int32, (n_exp * cap, tok), 1)
-        slots = jnp.dot(pick.astype(F32).astype(BF16), rows, preferred_element_type=F32)
         for j in range(n_exp):
-            out = send_ref if j % 2 else keep_ref
-            out[j // 2, y * own_rows : (y + 1) * own_rows, :] = rows[j * own_rows : (j + 1) * own_rows]
-        slots_of.append(slots)
-    for j in range(n_exp):
-        out = send_ref if j % 2 else keep_ref
-        both = [s[j * cap : (j + 1) * cap] for s in slots_of]
-        out[j // 2, 2 * own_rows :, :] = jnp.concatenate(both, axis=0).astype(BF16)
-
-
-def hidden_kernel(cap, order_ref, stream_ref, *refs):
-    out_ref, total_ref = refs[-2:]
-    steps = (len(refs) - 2) // 2
-    first = refs[0].shape[0] - 2 * cap
-    for step in range(steps):
-        rows = refs[2 * step][first:, :].astype(F32) + refs[2 * step + 1][first:, :].astype(F32)
-        for y in range(2):
-            to = pl.multiple_of(order_ref[2 * step + y] * cap, cap)
-            total_ref[pl.ds(to, cap), :] = rows[y * cap : (y + 1) * cap]
+            outs[j % 2][j // 2, y * own_rows : (y + 1) * own_rows, :] = rows[
+                j * own_rows : (j + 1) * own_rows
+            ]
+
+
+def select_kernel(n_exp, cap, row_ref, *refs):
+    parts, outs = refs[:-2], refs[-2:]
+    for step in range(len(parts) // 2):
+        both = parts[2 * step : 2 * step + 2]
+        rows = jnp.concatenate([p[i] for p in both for i in range(n_exp // 2)], axis=0)
+        slots = n_exp * 2 * cap
+        pick = row_ref[step] == lax.broadcasted_iota(jnp.int32, (slots, rows.shape[0]), 1)
+        found = jnp.dot(pick.astype(F32).astype(BF16), rows, preferred_element_type=F32)
+        found = found.astype(BF16)
+        for j in range(n_exp):
+            outs[j % 2][j // 2, 2 * cap * step : 2 * cap * (step + 1), :] = found[
+                2 * cap * j : 2 * cap * (j + 1)
+            ]
+
+
+def hidden_kernel(cap, order_ref, stream_ref, mine_ref, came_ref, out_ref, total_ref):
+    rows = mine_ref[...].astype(F32) + came_ref[...].astype(F32)
+    for i in range(rows.shape[0] // cap):
+        to = pl.multiple_of(order_ref[i] * cap, cap)
+        total_ref[pl.ds(to, cap), :] = rows[i * cap : (i + 1) * cap]
     out_ref[...] = (total_ref[...] + stream_ref[...].astype(F32)).astype(BF16)
 
 
 def ffn_kernel(n, blocks, order_ref, *refs):
     pieces, refs = refs[:n], refs[n:]
-    gain_ref, refs = refs[0], refs[1:]
-    gate_ref, up_ref, down_ref, out_ref, rows_ref, down_buf, sems = refs
+    gain_ref, gate_ref, up_ref, down_ref, out_ref, rows_ref, up_buf, down_buf, sems = refs
+    rows_step = up_buf.shape[1]
     step = out_ref.shape[1] // blocks
-    copies = [
+    ups = [
         pltpu.make_async_copy(
-            down_ref.at[0, :, pl.ds(i * step, step)], down_buf.at[i], sems.at[i]
+            up_ref.at[0, pl.ds(i * rows_step, rows_step), :], up_buf.at[i], sems.at[0, i]
         )
         for i in range(blocks)
     ]
-    for copy in copies:
+    downs = [
+        pltpu.make_async_copy(
+            down_ref.at[0, :, pl.ds(i * step, step)], down_buf.at[i], sems.at[1, i]
+        )
+        for i in range(blocks)
+    ]
+    for copy in ups + downs:
         copy.start()
     cols = pieces[0].shape[1]
     total = 0.0
@@ -200,16 +209,18 @@
     for i, piece in enumerate(pieces):
         at = lanes(order_ref[i], cols) if n > 1 else slice(None)
         rows_ref[:, at] = (piece[...].astype(F32) * inverse * gain_ref[:, at]).astype(BF16)
+    spans = [slice(i * rows_step, (i + 1) * rows_step) for i in range(blocks)]
     gate = up = None
-    span = rows_ref.shape[1] // blocks
-    for i in range(blocks):
-        rows = rows_ref[:, i * span : (i + 1) * span]
-        g = jnp.dot(rows, gate_ref[0, i * span : (i + 1) * span, :], preferred_element_type=F32)
-        u = jnp.dot(rows, up_ref[0, i * span : (i + 1) * span, :], preferred_element_type=F32)
+    for at in spans:
+        g = jnp.dot(rows_ref[:, at], gate_ref[0, at, :], preferred_element_type=F32)
         gate = g if gate is None else gate + g
+    gate = gate / (1.0 + jnp.exp(-gate))
+    for i, at in enumerate(spans):
+        ups[i].wait()
+        u = jnp.dot(rows_ref[:, at], up_buf[i], preferred_element_type=F32)
         up = u if up is None else up + u
-    activated = (gate / (1.0 + jnp.exp(-gate)) * up).astype(BF16)
-    for i, copy in enumerate(copies):
+    activated = (gate * up).astype(BF16)
+    for i, copy in enumerate(downs):
         copy.wait()
         out_ref[:, i * step : (i + 1) * step] = jnp.dot(
             activated, down_buf[i], preferred_element_type=F32
@@ -270,7 +281,7 @@
             pltpu.SemaphoreType.DMA((2, CHUNKS)),
         ],
         compiler_params=limit(8),
-        cost_estimate=takes(2),
+        cost_estimate=takes(1),
         name="shard_state",
     )(here, decay_rates, in_hbm(key_proj), in_hbm(values))
 
@@ -285,45 +296,11 @@
             in_specs=[SMEM] + [VMEM] * 5,
             out_specs=[VMEM] * 3,
             compiler_params=limit(8),
-            cost_estimate=takes(2),
+            cost_estimate=takes(1),
             name="near_part",
         )(after(decay_rates, start), queries, key_proj, values, attn_gate, attn_gain[None, :])
 
-    mixed, held = [], None
-    for chunk in range(CHUNKS):
-        keep, send = states[2 * chunk], states[2 * chunk + 1]
-        got = swapped(send if held is None else after(send, held))
-        near, scale, query = near_part(chunk, states[0] if held is None else held)
-        first = chunk * per_chunk + pair * per_half
-        rate = lax.dynamic_slice_in_dim(decay_rates, first, per_half, 0)[:, None, None]
-        span = jnp.exp(-rate * tok)
-        lower = jnp.where(pair == 0, keep, got).astype(F32)
-        upper = jnp.where(pair == 0, got, keep).astype(F32)
-        window = held = (span * lower + upper).astype(BF16)
-        prior = jnp.zeros(lower.shape, F32)
-        reach = 1
-        while reach < groups:
-            line = [(i, i + 2 * reach) for i in range(n_ctx - 2 * reach)]
-            far = lax.ppermute(window, "ctx", line).astype(F32)
-            prior = prior + jnp.exp(-rate * (2 * tok * (reach - 1))) * far
-            window = (window.astype(F32) + jnp.exp(-rate * (2 * tok * reach)) * far).astype(BF16)
-            reach *= 2
-        second = span * prior + lower
-        mine = jnp.where(pair == 0, prior, second).astype(BF16)
-        other = swapped(jnp.where(pair == 0, second, prior).astype(BF16))
-        mixed.append(
-            pl.pallas_call(
-                functools.partial(mix_kernel, chunk, per_half, own_rows),
-                out_shape=jax.ShapeDtypeStruct((tok, wide), BF16),
-                in_specs=[SMEM, SMEM] + [VMEM] * 5,
-                out_specs=VMEM,
-                compiler_params=limit(8),
-                cost_estimate=takes(2),
-                name="mix_heads",
-            )(here, decay_rates, query, near, scale, mine, other)
-        )
-
-    routing = after(routing, mixed[0])
+    routing = after(routing, states[0])
     hit = routing[:, :, None] == jnp.arange(n_exp, dtype=jnp.int32)
     member = jnp.any(hit, axis=1)
     gate_of = jnp.sum(jnp.where(hit, route_weights[:, :, None], 0.0), axis=1)
@@ -344,42 +321,106 @@
     label = jnp.broadcast_to(label.astype(BF16)[None], (n_ctx, cap, cols))
     parcel = jnp.concatenate([parcel, label], axis=1)
 
-    arrived = lax.all_to_all(parcel, "ctx", split_axis=0, concat_axis=0, tiled=True)
+
+    mixed, held = [], None
+    for chunk in range(CHUNKS):
+        keep, send = states[2 * chunk], states[2 * chunk + 1]
+        got = swapped(send if held is None else after(send, held))
+        first = chunk * per_chunk + pair * per_half
+        rate = lax.dynamic_slice_in_dim(decay_rates, first, per_half, 0)[:, None, None]
+        span = jnp.exp(-rate * tok)
+        lower = jnp.where(pair == 0, keep, got).astype(F32)
+        upper = jnp.where(pair == 0, got, keep).astype(F32)
+        window = held = (span * lower + upper).astype(BF16)
+        prior = jnp.zeros(lower.shape, F32)
+        reach = 1
+        while reach < groups:
+            line = [(i, i + 2 * reach) for i in range(n_ctx - 2 * reach)]
+            far = lax.ppermute(window, "ctx", line).astype(F32)
+            prior = prior + jnp.exp(-rate * (2 * tok * (reach - 1))) * far
+            window = (window.astype(F32) + jnp.exp(-rate * (2 * tok * reach)) * far).astype(BF16)
+            reach *= 2
+        near, scale, query = near_part(chunk, far)
+        second = span * prior + lower
+        mine = jnp.where(pair == 0, prior, second).astype(BF16)
+        if chunk == 0:
+            mine = after(mine, parcel)
+        other = swapped(jnp.where(pair == 0, second, prior).astype(BF16))
+        mixed.append(
+            pl.pallas_call(
+                functools.partial(mix_kernel, chunk, per_half, own_rows),
+                out_shape=jax.ShapeDtypeStruct((tok, wide), BF16),
+                in_specs=[SMEM, SMEM] + [VMEM] * 5,
+                out_specs=VMEM,
+                compiler_params=limit(8),
+                cost_estimate=takes(1),
+                name="mix_heads",
+            )(here, decay_rates, query, near, scale, mine, other)
+        )
+
+    ring = [[m] for m in mixed]
+    cross = [[None] * groups for _ in mixed]
+    swaps = []
+    for step in range(groups):
+        for chunk in range(CHUNKS):
+            if step + 1 < groups:
+                ring[chunk].append(shifted(ring[chunk][step], 1))
+        for chunk in range(CHUNKS):
+            if chunk % 2 == 0 or step != 1:
+                held = swaps[-2:-1] if len(swaps) > 1 else []
+                cross[chunk][step] = swapped(after(ring[chunk][step], *held))
+                swaps.append(cross[chunk][step])
+    for chunk in range(1, CHUNKS, 2):
+        cross[chunk][1] = shifted(after(cross[chunk][0], ring[chunk - 1][-1]), 1)
+    rows_of = [
+        [[r[step] for r in ring], [c[step] for c in cross]] for step in range(groups)
+    ]
+
+    arrived = lax.all_to_all(
+        after(parcel, ring[0][-1]), "ctx", split_axis=0, concat_axis=0, tiled=True
+    )
     stream_rows = arrived[:, :cap].reshape(n_ctx * cap, cols)
     token = arrived[:, cap, : n_exp * cap].astype(jnp.int32).reshape(n_ctx, n_exp, cap) - 1
-    token = jnp.where(token >= 0, ((token // own_rows) ^ own) * own_rows + token % own_rows, -1)
-    token = jnp.stack(
-        [lax.dynamic_index_in_dim(token, own ^ j, 1, keepdims=False) for j in range(n_exp)], axis=1
-    )
     index = jnp.arange(n_ctx, dtype=jnp.int32)
     order = ((group - index // 2) % groups) * 2 + (pair ^ (index % 2))
-    token = jnp.take(token, order, axis=0).reshape(n_ctx, n_exp * cap, 1)
-
-    rows_of = [[[], []] for _ in range(groups)]
-    for chunk in range(CHUNKS):
-        current, crossed = mixed[chunk], None
-        for step in range(groups):
-            crossed = shifted(crossed, 1) if chunk % 2 and step == 1 else swapped(current)
-            rows_of[step][0].append(current)
-            rows_of[step][1].append(crossed)
-            if step + 1 < groups:
-                current = shifted(current, 1)
-    kept, got = [], []
+    turned = (token // own_rows) ^ own
+    row = (turned % 2 * (n_exp // 2) + turned // 2) * 2 + (index % 2 ^ pair)[:, None, None]
+    row = jnp.where(token >= 0, row * own_rows + token % own_rows, -1)
+    row = jnp.stack(
+        [lax.dynamic_index_in_dim(row, own ^ j, 1, keepdims=False) for j in range(n_exp)], axis=1
+    )
+    row = jnp.take(row, order, axis=0).reshape(groups, 2, n_exp, cap)
+    row = row.transpose(0, 2, 1, 3).reshape(groups, n_exp * 2 * cap, 1)
+
+    parts = []
     for step in range(groups):
-        out = jax.ShapeDtypeStruct((n_exp // 2, 2 * (own_rows + cap), cols), BF16)
-        keep, send = pl.pallas_call(
-            functools.partial(project_kernel, n_exp, cap),
-            out_shape=[out, out],
-            in_specs=[VMEM] * (2 + 2 * CHUNKS),
-            out_specs=[VMEM] * 2,
-            compiler_params=limit(8),
-            cost_estimate=takes(8),
-            name="project",
-        )(
-            token[2 * step : 2 * step + 2],
-            *[rows_of[step][y][chunk] for chunk in range(CHUNKS) for y in range(2)],
-            out_weight,
+        weight = out_weight
+        if step + 1 < groups:
+            weight = after(weight, cross[0][-1])
+        rows = jax.ShapeDtypeStruct((n_exp // 2, 2 * own_rows, cols), BF16)
+        parts.append(
+            pl.pallas_call(
+                functools.partial(project_kernel, n_exp),
+                out_shape=[rows, rows],
+                in_specs=[VMEM] * (1 + 2 * CHUNKS),
+                out_specs=[VMEM] * 2,
+                compiler_params=limit(8),
+                cost_estimate=takes(1.5),
+                name="project",
+            )(*[rows_of[step][y][chunk] for chunk in range(CHUNKS) for y in range(2)], weight)
         )
+    slots = jax.ShapeDtypeStruct((n_exp // 2, n_ctx * cap, cols), BF16)
+    slot_parts = pl.pallas_call(
+        functools.partial(select_kernel, n_exp, cap),
+        out_shape=[slots, slots],
+        in_specs=[VMEM] * (1 + 2 * groups),
+        out_specs=[VMEM] * 2,
+        compiler_params=limit(8),
+        cost_estimate=takes(1),
+        name="slot_rows",
+    )(row, *[p for both in parts for p in both])
+
+    def add_groups(keep, send):
         came = lax.ppermute(send, "exp", [(i, i ^ 1) for i in range(n_exp)])
         bit = 2
         while bit < n_exp:
@@ -388,18 +429,18 @@
             keep = total[:, 0]
             came = lax.ppermute(total[:, 1], "exp", [(i, i ^ bit) for i in range(n_exp)])
             bit *= 2
-        kept.append(keep[0])
-        got.append(came[0])
+        return keep[0], came[0]
+
     hidden = pl.pallas_call(
         functools.partial(hidden_kernel, cap),
         out_shape=jax.ShapeDtypeStruct((n_ctx * cap, cols), BF16),
-        in_specs=[SMEM] + [VMEM] * (1 + 2 * groups),
+        in_specs=[SMEM] + [VMEM] * 3,
         out_specs=VMEM,
         scratch_shapes=[pltpu.VMEM((n_ctx * cap, cols), F32)],
         compiler_params=limit(8),
-        cost_estimate=takes(1),
+        cost_estimate=takes(15),
         name="slot_hidden",
-    )(order, stream_rows, *[part for pair_of in zip(kept, got) for part in pair_of])
+    )(order, stream_rows, *add_groups(*slot_parts))
 
     pieces = {0: hidden}
     bit = 1
@@ -410,41 +451,40 @@
             )
         bit *= 2
     pieces = [p for r in range(groups) for p in (pieces[r], swapped(pieces[r]))]
+    late = pieces[-3:-1]
     source = (place ^ index).astype(jnp.int32)
     if cols % 128:
         pieces = [jnp.take(jnp.stack(pieces), source, axis=0).transpose(1, 0, 2).reshape(-1, width)]
 
-    bulk = [
-        (k.astype(F32) + g.astype(F32))[: 2 * own_rows].astype(BF16).reshape(2, own_rows, cols)
-        for k, g in zip(kept, got)
-    ]
-    back = []
-    for step in range(groups):
-        rows = jnp.stack([bulk[step][0], swapped(after(bulk[step][1], hidden))])
-        back.append(shifted(rows, -step) if step else rows)
+    bulk_parts = [jnp.concatenate([p[i] for p in parts], axis=1) for i in (0, 1)]
+    mine, came = add_groups(bulk_parts[0], after(bulk_parts[1], *late))
+    bulk = (mine.astype(F32) + came.astype(F32)).astype(BF16)
+    bulk = bulk.reshape(groups, 2, own_rows, cols)
 
     blocks = 8
     down = pl.pallas_call(
         functools.partial(ffn_kernel, len(pieces), blocks),
         out_shape=jax.ShapeDtypeStruct((n_ctx * cap, width), BF16),
-        in_specs=[SMEM] + [VMEM] * (len(pieces) + 3) + [HBM],
+        in_specs=[SMEM] + [VMEM] * (len(pieces) + 2) + [HBM, HBM],
         out_specs=VMEM,
         scratch_shapes=[
             pltpu.VMEM((n_ctx * cap, width), BF16),
+            pltpu.VMEM((blocks, width // blocks, hidden_units), BF16),
             pltpu.VMEM((blocks, hidden_units, width // blocks), BF16),
-            pltpu.SemaphoreType.DMA((blocks,)),
+            pltpu.SemaphoreType.DMA((2, blocks)),
         ],
-        compiler_params=limit(24),
+        compiler_params=limit(36),
         cost_estimate=takes(10),
         name="expert",
-    )(source, *pieces, ffn_gain[None, :], w_gate, w_up, in_hbm(w_down))
-    down = after(down, *back)
+    )(source, *pieces, ffn_gain[None, :], w_gate, in_hbm(w_up), in_hbm(w_down))
     received = lax.all_to_all(
         down.reshape(n_ctx, cap, width), "ctx", split_axis=0, concat_axis=0, tiled=True
     )
     summed = jnp.sum(received.astype(F32), axis=0)
     expert_out = (summed * own_weight[:, None]).astype(BF16).reshape(1, 1, cap, width)
 
+    turned = jnp.stack([bulk[:, 0], swapped(bulk[:, 1])], axis=1)
+    back = [turned[0]] + [shifted(turned[k], -k) for k in range(1, groups)]
     order = ((index // 2 - group) % groups) * 2 + (pair ^ (index % 2))
     projected = jnp.take(jnp.concatenate(back), order, axis=0).transpose(1, 0, 2)
     projected = projected.reshape(own_rows, width)

time: 204 us -> 173 us (0.85)
  waiting for transfers between devices: 72.7 us -> 54.2 us
  starting transfers between devices: 74.4 us -> 68.5 us
  local copies, waits for them, and re-layouts: 20.1 us -> 15.3 us
    ppermute x19 -> x16, waiting for transfers between devices: 36.5 us -> 14.6 us  [swapped(): return lax.ppermute(value, 'ctx', swap)]
    all_to_all x1, waiting for transfers between devices: 15.1 us -> 0.01 us  [per_device(): lax.all_to_all(down.reshape(n_ctx, cap, width), 'ctx', split_axis=0, conc...]
    ppermute x10, waiting for transfers between devices: 12.7 us -> 21.1 us  [shifted(): return lax.ppermute(value, 'ctx', to)]
    ppermute x8 -> x4, waiting for transfers between devices: 5.31 us -> 12.2 us  [the longest x2 10.8 us: add_groups(): lax.ppermute(total[:, 1], 'exp', [(i, i ^ bit) for i in range(n_exp)])]
    ppermute x3, waiting for transfers between devices: 0.01 us -> 5.53 us  [per_device(): lax.ppermute(pieces[r], 'ctx', [(i, i ^ 2 * bit) for i in range(n_ctx)])]
    unnamed x54 -> x39, local copies, waits for them, and re-layouts: 18.2 us -> 12.8 us
    ppermute x19 -> x16, starting transfers between devices: 25.2 us -> 21.7 us  [swapped(): return lax.ppermute(value, 'ctx', swap)]
    ppermute x8 -> x4, starting transfers between devices: 6.51 us -> 3.2 us  [the longest x2 3.13 us: add_groups(): lax.ppermute(total[:, 1], 'exp', [(i, i ^ bit) for i in range(n_exp)])]
  transfers between devices with their start and end apart: 46 -> 39, of which waited for: 23 -> 20; matrix products, arithmetic and copies ran while one was open for 5% -> 4% of each run, Pallas kernels for 5% -> 12%
where the time goes in v4:
time: 173 us; the launch traced here: 172 us
  starting transfers between devices  68.5 us (40%)
  waiting for transfers between devices  54.2 us (31%)
  Pallas kernels  25.4 us (15%)
  local copies, waits for them, and re-layouts  15.3 us (9%)
  other arithmetic  7.3 us (4%)
    ppermute x16, starting transfers between devices, swapped(): return lax.ppermute(value, 'ctx', swap)  21.7 us
    ppermute x10, waiting for transfers between devices, shifted(): return lax.ppermute(value, 'ctx', to)  21.1 us
    ppermute x4, starting transfers between devices, per_device(): far = lax.ppermute(window, 'ctx', line).astype(F32)  18.1 us
    ppermute x16, waiting for transfers between devices, swapped(): return lax.ppermute(value, 'ctx', swap)  14.6 us
    ppermute x10, starting transfers between devices, shifted(): return lax.ppermute(value, 'ctx', to)  12.9 us
    unnamed x39, local copies, waits for them, and re-layouts  12.8 us
    pallas_call x1, Pallas kernels, per_device(): pl.pallas_call(functools.partial(ffn_kernel, len(pieces), blocks), out_sh...  11.9 us
    ppermute x2, waiting for transfers between devices, add_groups(): lax.ppermute(total[:, 1], 'exp', [(i, i ^ bit) for i in range(n_exp)])  10.8 us
  transfers between devices with their start and end apart: 39, of which 20 were waited for; matrix products, arithmetic and copies ran while one was open for 4% of the time, Pallas kernels for 12%

profile of v4, /device:TPU:0, one launch (start us, length us, event | category | flops | bytes accessed | tf_op | source)
XLA Modules:
  0.0 172.3 jit_solution(13422302259837326814)
XLA Ops:
  1.4 2.2 %shard_state.1 = (bf16[4,128,128]{2,1,0:T(8,128)(2,1)S(1)}, bf16[4,128,128]{2,1,0:T(8,128)(2,1)S(1)}, bf16[4,128,128]{2,1,0:T(8,128)(2,1)S(1)}, bf16[4,128,128]{2,1,0:T(8,128)(2,1)S(1)}) custom-call(s32[2]{0:T(128)S(1)} %pad_add_fusion.1.place_ref, f32[16]{0:T(128)S(1)} %copy-done.2, bf16[128,2048]{1,0:T(8,128)(2,1)} %k_ref.3, bf16[128,2048]{1,0:T(8,128)(2,1)} %v_ref.3), custom_call_target="tpu_custom_call" | custom-call | flops 1000000000 | bytes 1000000 | tf_op jit(solution)/shard_map/shard_state/pallas_call | solution.py:273
  3.6 3.0 %collective-permute-start = (bf16[4,128,128]{2,1,0:T(8,128)(2,1)S(1)}, bf16[4,128,128]{2,1,0:T(8,128)(2,1)S(1)}, u32[]{:S(2)}, u32[]{:S(2)}) collective-permute-start(bf16[4,128,128]{2,1,0:T(8,128)(2,1)S(1)} %get-tuple-element.37), channel_id=1, source_target_pairs={{0,4},{4,0},{8,12},{12,8},{16,20},{20,16},{24,28},{28,24},{1,5},{5... | collective-permute-start | bytes 393224 | tf_op jit(solution)/shard_map/ppermute | solution.py:264
  7.3 2.8 %collective-permute-done = bf16[4,128,128]{2,1,0:T(8,128)(2,1)S(1)} collective-permute-done((bf16[4,128,128]{2,1,0:T(8,128)(2,1)S(1)}, bf16[4,128,128]{2,1,0:T(8,128)(2,1)S(1)}, u32[]{:S(2)}, u32[]{:S(2)}) %collective-permute-start) | collective-permute-done | bytes 131104 | tf_op jit(solution)/shard_map/ppermute | solution.py:264
  10.3 3.7 %collective-permute-start.1 = (bf16[4,128,128]{2,1,0:T(8,128)(2,1)S(1)}, bf16[4,128,128]{2,1,0:T(8,128)(2,1)S(1)}, u32[]{:S(2)}, u32[]{:S(2)}) collective-permute-start(bf16[4,128,128]{2,1,0:T(8,128)(2,1)S(1)} %fusion.3), channel_id=1, source_target_pairs={{0,8},{4,12},{8,16},{12,20},{16,24},{20,28},{1,9},{5,13},{9,17},{1... | collective-permute-start | bytes 393224 | tf_op jit(solution)/shard_map/ppermute | solution.py:339
  14.9 1.5 collective-permute-start.5
  16.6 5.4 %collective-permute-start.2 = (bf16[4,128,128]{2,1,0:T(8,128)(2,1)S(1)}, bf16[4,128,128]{2,1,0:T(8,128)(2,1)S(1)}, u32[]{:S(2)}, u32[]{:S(2)}) collective-permute-start(bf16[4,128,128]{2,1,0:T(8,128)(2,1)S(1)} %fusion.5), channel_id=1, source_target_pairs={{0,16},{4,20},{8,24},{12,28},{1,17},{5,21},{9,25},{13,29},{2,18},{... | collective-permute-start | bytes 393224 | tf_op jit(solution)/shard_map/ppermute | solution.py:339
  22.1 3.5 %collective-permute-start.6 = (bf16[4,128,128]{2,1,0:T(8,128)(2,1)S(1)}, bf16[4,128,128]{2,1,0:T(8,128)(2,1)S(1)}, u32[]{:S(2)}, u32[]{:S(2)}) collective-permute-start(bf16[4,128,128]{2,1,0:T(8,128)(2,1)S(1)} %fusion.8), channel_id=1, source_target_pairs={{0,8},{4,12},{8,16},{12,20},{16,24},{20,28},{1,9},{5,13},{9,17},{1... | collective-permute-start | bytes 393224 | tf_op jit(solution)/shard_map/ppermute | solution.py:339
  25.8 1.6 collective-permute-start.3
  28.2 5.6 %collective-permute-start.7 = (bf16[4,128,128]{2,1,0:T(8,128)(2,1)S(1)}, bf16[4,128,128]{2,1,0:T(8,128)(2,1)S(1)}, u32[]{:S(2)}, u32[]{:S(2)}) collective-permute-start(bf16[4,128,128]{2,1,0:T(8,128)(2,1)S(1)} %fusion.10), channel_id=1, source_target_pairs={{0,16},{4,20},{8,24},{12,28},{1,17},{5,21},{9,25},{13,29},{2,18},{... | collective-permute-start | bytes 393224 | tf_op jit(solution)/shard_map/ppermute | solution.py:339
  33.8 1.2 near_part.2
  35.0 1.0 mix_heads.2.refs_0_
  36.0 1.9 %collective-permute-start.10 = (bf16[128,1024]{1,0:T(8,128)(2,1)S(1)}, bf16[128,1024]{1,0:T(8,128)(2,1)S(1)}, u32[]{:S(2)}, u32[]{:S(2)}) collective-permute-start(bf16[128,1024]{1,0:T(8,128)(2,1)S(1)} %mix_heads.2.refs_0_), channel_id=1, source_target_pairs={{0,8},{4,12},{8,16},{12,20},{16,24},{20,28},{24,0},{28,4},{1,9},{5... | collective-permute-start | bytes 786440 | tf_op jit(solution)/shard_map/ppermute | solution.py:268
  38.0 1.3 collective-permute-start.8
  39.3 1.2 near_part.3
  40.5 0.8 collective-permute-start.4
  41.4 3.2 %collective-permute-done.8.other_ref = bf16[4,128,128]{2,1,0:T(8,128)(2,1)S(1)} collective-permute-done((bf16[4,128,128]{2,1,0:T(8,128)(2,1)S(1)}, bf16[4,128,128]{2,1,0:T(8,128)(2,1)S(1)}, u32[]{:S(2)}, u32[]{:S(2)}) %collective-permute-start.8) | collective-permute-done | bytes 131104 | tf_op jit(solution)/shard_map/ppermute | solution.py:264
  44.5 1.0 mix_heads.3.refs_2_
  45.5 1.9 %collective-permute-start.16 = (bf16[128,1024]{1,0:T(8,128)(2,1)S(1)}, bf16[128,1024]{1,0:T(8,128)(2,1)S(1)}, u32[]{:S(2)}, u32[]{:S(2)}) collective-permute-start(bf16[128,1024]{1,0:T(8,128)(2,1)S(1)} %mix_heads.3.refs_2_), channel_id=1, source_target_pairs={{0,8},{4,12},{8,16},{12,20},{16,24},{20,28},{24,0},{28,4},{1,9},{5... | collective-permute-start | bytes 786440 | tf_op jit(solution)/shard_map/ppermute | solution.py:268
  48.0 2.0 %collective-permute-start.11 = (bf16[128,1024]{1,0:T(8,128)(2,1)S(1)}, bf16[128,1024]{1,0:T(8,128)(2,1)S(1)}, u32[]{:S(2)}, u32[]{:S(2)}) collective-permute-start(bf16[128,1024]{1,0:T(8,128)(2,1)S(1)} %collective-permute-done.10.refs_0_), channel_id=1, source_target_pairs={{0,8},{4,12},{8,16},{12,20},{16,24},{20,28},{24,0},{28,4},{1,9},{5... | collective-permute-start | bytes 786440 | tf_op jit(solution)/shard_map/ppermute | solution.py:268
  50.1 1.1 collective-permute-start.15
  51.2 6.8 %collective-permute-done.16.refs_2_ = bf16[128,1024]{1,0:T(8,128)(2,1)S(1)} collective-permute-done((bf16[128,1024]{1,0:T(8,128)(2,1)S(1)}, bf16[128,1024]{1,0:T(8,128)(2,1)S(1)}, u32[]{:S(2)}, u32[]{:S(2)}) %collective-permute-start.16) | collective-permute-done | bytes 262176 | tf_op jit(solution)/shard_map/ppermute | solution.py:268
  58.1 4.6 %collective-permute-done.11.refs_0_ = bf16[128,1024]{1,0:T(8,128)(2,1)S(1)} collective-permute-done((bf16[128,1024]{1,0:T(8,128)(2,1)S(1)}, bf16[128,1024]{1,0:T(8,128)(2,1)S(1)}, u32[]{:S(2)}, u32[]{:S(2)}) %collective-permute-start.11) | collective-permute-done | bytes 262176 | tf_op jit(solution)/shard_map/ppermute | solution.py:268
  62.7 1.9 %collective-permute-start.13 = (bf16[128,1024]{1,0:T(8,128)(2,1)S(1)}, bf16[128,1024]{1,0:T(8,128)(2,1)S(1)}, u32[]{:S(2)}, u32[]{:S(2)}) collective-permute-start(bf16[128,1024]{1,0:T(8,128)(2,1)S(1)} %collective-permute-done.11.refs_0_), channel_id=1, source_target_pairs={{0,4},{4,0},{8,12},{12,8},{16,20},{20,16},{24,28},{28,24},{1,5},{5... | collective-permute-start | bytes 786440 | tf_op jit(solution)/shard_map/ppermute | solution.py:264
  64.6 3.6 %collective-permute-done.18.refs_2_ = bf16[128,1024]{1,0:T(8,128)(2,1)} collective-permute-done((bf16[128,1024]{1,0:T(8,128)(2,1)S(1)}, bf16[128,1024]{1,0:T(8,128)(2,1)}, u32[]{:S(2)}, u32[]{:S(2)}) %collective-permute-start.18) | collective-permute-done | bytes 262176 | tf_op jit(solution)/shard_map/ppermute | solution.py:268
  68.2 1.5 collective-permute-start.19
  69.7 1.2 collective-permute-done.12.refs_0_
  71.6 2.0 %collective-permute-start.14 = (bf16[128,1024]{1,0:T(8,128)(2,1)S(1)}, bf16[128,1024]{1,0:T(8,128)(2,1)S(1)}, u32[]{:S(2)}, u32[]{:S(2)}) collective-permute-start(bf16[128,1024]{1,0:T(8,128)(2,1)S(1)} %collective-permute-done.12.refs_0_), channel_id=1, source_target_pairs={{0,4},{4,0},{8,12},{12,8},{16,20},{20,16},{24,28},{28,24},{1,5},{5... | collective-permute-start | bytes 786440 | tf_op jit(solution)/shard_map/ppermute | solution.py:264
  73.7 4.0 %all-to-all-start = ((bf16[8,16,768]{2,1,0:T(8,128)(2,1)}), bf16[8,16,768]{2,1,0:T(8,128)(2,1)}, u32[]{:S(2)}, u32[]{:S(2)}) async-start(bf16[8,16,768]{2,1,0:T(8,128)(2,1)} %pad_maximum_fusion.2), calls=%async_computation | async-start | bytes 393216 | tf_op jit(solution)/shard_map/all_to_all | solution.py:379
  77.7 2.0 %collective-permute-start.17 = (bf16[128,1024]{1,0:T(8,128)(2,1)S(1)}, bf16[128,1024]{1,0:T(8,128)(2,1)S(1)}, u32[]{:S(2)}, u32[]{:S(2)}) collective-permute-start(bf16[128,1024]{1,0:T(8,128)(2,1)S(1)} %collective-permute-done.9.refs_3_), channel_id=1, source_target_pairs={{0,8},{4,12},{8,16},{12,20},{16,24},{20,28},{24,0},{28,4},{1,9},{5... | collective-permute-start | bytes 786440 | tf_op jit(solution)/shard_map/ppermute | solution.py:268
  79.7 1.5 collective-permute-start.21
  81.9 1.9 %copy-done.4 = bf16[2048,768]{1,0:T(8,128)(2,1)S(1)} copy-done((bf16[2048,768]{1,0:T(8,128)(2,1)S(1)}, bf16[2048,768]{1,0:T(8,128)(2,1)}, u32[]{:S(2)}) %copy-start.4) | copy-done | bytes 3145752
  83.8 1.0 project.4
  84.8 0.9 copy-done.5
  85.7 0.9 copy-done.14
  86.6 2.0 %project.6 = (bf16[2,64,768]{2,1,0:T(8,128)(2,1)S(1)}, bf16[2,64,768]{2,1,0:T(8,128)(2,1)S(1)}) custom-call(bf16[128,1024]{1,0:T(8,128)(2,1)S(1)} %collective-permute-done.11.refs_0_, bf16[128,1024]{1,0:T(8,128)(2,1)S(1)} %copy-done.14, bf16[128,1024]{1,0:T(8,128)(2,1)} %collective-permute-done.18.refs_2_, ...), custom_call_target="tpu_custom_call" | custom-call | flops 1500000000 | bytes 1000000 | tf_op jit(solution)/shard_map/project/pallas_call | solution.py:402
  88.7 1.0 project.5
  91.5 1.9 %copy-done.6 = bf16[2048,768]{1,0:T(8,128)(2,1)S(1)} copy-done((bf16[2048,768]{1,0:T(8,128)(2,1)S(1)}, bf16[2048,768]{1,0:T(8,128)(2,1)}, u32[]{:S(2)}) %copy-start.6) | copy-done | bytes 3145752
  93.3 2.0 %project.7 = (bf16[2,64,768]{2,1,0:T(8,128)(2,1)S(1)}, bf16[2,64,768]{2,1,0:T(8,128)(2,1)S(1)}) custom-call(bf16[128,1024]{1,0:T(8,128)(2,1)S(1)} %collective-permute-done.12.refs_0_, bf16[128,1024]{1,0:T(8,128)(2,1)S(1)} %copy-done.12, bf16[128,1024]{1,0:T(8,128)(2,1)S(1)} %collective-permute-done.20.refs_2_, ...), custom_call_target="tpu_custom_call" | custom-call | flops 1500000000 | bytes 1000000 | tf_op jit(solution)/shard_map/project/pallas_call | solution.py:402
  95.8 1.4 collective-permute-done.22
  97.3 1.6 collective-permute-start.23
  98.9 0.9 slice_bitcast_fusion.5.stream_ref
  99.8 2.4 %collective-permute-done.23 = bf16[1,64,768]{2,1,0:T(8,128)(2,1)S(1)} collective-permute-done((bf16[1,64,768]{2,1,0:T(8,128)(2,1)S(1)}, bf16[1,64,768]{2,1,0:T(8,128)(2,1)S(1)}, u32[]{:S(2)}, u32[]{:S(2)}) %collective-permute-start.23) | collective-permute-done | bytes 98336 | tf_op jit(solution)/shard_map/ppermute | solution.py:430
  102.8 1.5 collective-permute-start.26
  104.3 1.5 collective-permute-start.24
  105.8 2.6 %collective-permute-done.26.refs_2_ = bf16[64,768]{1,0:T(8,128)(2,1)S(1)} collective-permute-done((bf16[64,768]{1,0:T(8,128)(2,1)S(1)}, bf16[64,768]{1,0:T(8,128)(2,1)S(1)}, u32[]{:S(2)}, u32[]{:S(2)}) %collective-permute-start.26) | collective-permute-done | bytes 98336 | tf_op jit(solution)/shard_map/ppermute | solution.py:449
  108.4 1.9 %collective-permute-start.27 = (bf16[64,768]{1,0:T(8,128)(2,1)S(1)}, bf16[64,768]{1,0:T(8,128)(2,1)S(1)}, u32[]{:S(2)}, u32[]{:S(2)}) collective-permute-start(bf16[64,768]{1,0:T(8,128)(2,1)S(1)} %collective-permute-done.26.refs_2_), channel_id=1, source_target_pairs={{0,16},{4,20},{8,24},{12,28},{16,0},{20,4},{24,8},{28,12},{1,17},{... | collective-permute-start | bytes 294920 | tf_op jit(solution)/shard_map/ppermute | solution.py:449
  110.9 1.5 collective-permute-start.35
  113.0 2.3 %collective-permute-done.27.refs_6_ = bf16[64,768]{1,0:T(8,128)(2,1)S(1)} collective-permute-done((bf16[64,768]{1,0:T(8,128)(2,1)S(1)}, bf16[64,768]{1,0:T(8,128)(2,1)S(1)}, u32[]{:S(2)}, u32[]{:S(2)}) %collective-permute-start.27) | collective-permute-done | bytes 98336 | tf_op jit(solution)/shard_map/ppermute | solution.py:449
  115.3 0.9 collective-permute-start.36
  116.3 1.9 %collective-permute-done.25.refs_5_ = bf16[64,768]{1,0:T(8,128)(2,1)S(1)} collective-permute-done((bf16[64,768]{1,0:T(8,128)(2,1)S(1)}, bf16[64,768]{1,0:T(8,128)(2,1)S(1)}, u32[]{:S(2)}, u32[]{:S(2)}) %collective-permute-start.25) | collective-permute-done | bytes 98336 | tf_op jit(solution)/shard_map/ppermute | solution.py:264
  118.2 1.7 collective-permute-done.36.refs_7_
  119.9 5.0 %copy-done = bf16[1,6144,1152]{2,1,0:T(8,128)(2,1)S(1)} copy-done((bf16[1,6144,1152]{2,1,0:T(8,128)(2,1)S(1)}, bf16[1,6144,1152]{2,1,0:T(8,128)(2,1)}, u32[]{:S(2)}) %copy-start) | copy-done | bytes 14155800
  124.9 11.9 %expert.1 = bf16[64,6144]{1,0:T(8,128)(2,1)} custom-call(s32[8]{0:T(128)S(1)} %iota_xor_fusion.order_ref, bf16[64,768]{1,0:T(8,128)(2,1)S(1)} %slot_hidden.1.refs_0_, bf16[64,768]{1,0:T(8,128)(2,1)S(1)} %collective-permute-done.34.refs_1_, bf16[64,768]{1,0:T(8,128)(2,1)S(1)} %collective-permute-done.26.refs_2_, ...), custom_call_target="tpu_custom_call" | custom-call | flops 10000000000 | bytes 1000000 | tf_op jit(solution)/shard_map/expert/pallas_call | solution.py:465
  136.8 3.7 %all-to-all-start.1 = ((bf16[8,8,6144]{2,1,0:T(8,128)(2,1)}), bf16[8,8,6144]{2,1,0:T(8,128)(2,1)S(1)}, u32[]{:S(2)}, u32[]{:S(2)}) async-start(bf16[8,8,6144]{2,1,0:T(8,128)(2,1)} %bitcast.27), calls=%async_computation.1 | async-start | bytes 1572864 | tf_op jit(solution)/shard_map/all_to_all | solution.py:480
  140.5 1.3 fusion
  141.9 1.6 collective-permute-start.29
  143.5 8.4 %collective-permute-done.29 = bf16[1,256,768]{2,1,0:T(8,128)(2,1)S(1)} collective-permute-done((bf16[1,256,768]{2,1,0:T(8,128)(2,1)S(1)}, bf16[1,256,768]{2,1,0:T(8,128)(2,1)S(1)}, u32[]{:S(2)}, u32[]{:S(2)}) %collective-permute-start.29) | collective-permute-done | bytes 393248 | tf_op jit(solution)/shard_map/ppermute | solution.py:430
  152.0 1.8 %collective-permute-start.30 = (bf16[4,32,768]{2,1,0:T(8,128)(2,1)S(1)}, bf16[4,32,768]{2,1,0:T(8,128)(2,1)S(1)}, u32[]{:S(2)}, u32[]{:S(2)}) collective-permute-start(bf16[4,32,768]{2,1,0:T(8,128)(2,1)S(1)} %get-tuple-element.81), channel_id=1, source_target_pairs={{0,4},{4,0},{8,12},{12,8},{16,20},{20,16},{24,28},{28,24},{1,5},{5... | collective-permute-start | bytes 589832 | tf_op jit(solution)/shard_map/ppermute | solution.py:264
  153.9 4.8 %collective-permute-done.30 = bf16[4,32,768]{2,1,0:T(8,128)(2,1)S(1)} collective-permute-done((bf16[4,32,768]{2,1,0:T(8,128)(2,1)S(1)}, bf16[4,32,768]{2,1,0:T(8,128)(2,1)S(1)}, u32[]{:S(2)}, u32[]{:S(2)}) %collective-permute-start.30) | collective-permute-done | bytes 196640 | tf_op jit(solution)/shard_map/ppermute | solution.py:264
  158.7 2.6 %collective-permute-start.31 = (bf16[2,32,768]{2,1,0:T(8,128)(2,1)S(1)}, bf16[2,32,768]{2,1,0:T(8,128)(2,1)S(1)}, u32[]{:S(2)}, u32[]{:S(2)}) collective-permute-start(bf16[2,32,768]{2,1,0:T(8,128)(2,1)S(1)} %get-tuple-element.77), channel_id=1, source_target_pairs={{0,24},{4,28},{8,0},{12,4},{16,8},{20,12},{24,16},{28,20},{1,25},{... | collective-permute-start | bytes 294920 | tf_op jit(solution)/shard_map/ppermute | solution.py:268
  161.4 1.1 collective-permute-start.32
  162.5 1.5 collective-permute-start.33
  164.8 4.8 %collective-permute-done.32 = bf16[2,32,768]{2,1,0:T(8,128)(2,1)S(1)} collective-permute-done((bf16[2,32,768]{2,1,0:T(8,128)(2,1)S(1)}, bf16[2,32,768]{2,1,0:T(8,128)(2,1)S(1)}, u32[]{:S(2)}, u32[]{:S(2)}) %collective-permute-start.32) | collective-permute-done | bytes 98336 | tf_op jit(solution)/shard_map/ppermute | solution.py:268
  170.5 1.8 %add_convert_fusion.1 = bf16[32,6144]{1,0:T(8,128)(2,1)} fusion(f32[32,6144]{1,0:T(8,128)S(1)} %bitcast.71, bf16[128,6144]{1,0:T(8,128)(2,1)} %param.14, s32[]{:T(128)S(6)} %select_n.248), kind=kLoop, calls=%fused_computation.10 | loop fusion | flops 589824 | bytes 1572868 | tf_op jit(solution)/shard_map/convert_element_type | solution.py:492
  (120 shorter events, 12.4 us)
Async XLA Ops:
  0.7 0.7 copy-start.2
  1.4 5.3 %copy-start.17 = (s32[128,2]{0,1:T(2,128)S(1)}, s32[128,2]{0,1:T(2,128)}, u32[]{:S(2)}) copy-start(s32[128,2]{0,1:T(2,128)} %param.23) | copy-start | bytes 3076
  1.4 5.5 %copy-start.16 = (bf16[128,6144]{1,0:T(8,128)(2,1)S(1)}, bf16[128,6144]{1,0:T(8,128)(2,1)}, u32[]{:S(2)}) copy-start(bf16[128,6144]{1,0:T(8,128)(2,1)} %param.14) | copy-start | bytes 4718596
  3.6 3.6 %copy-start.3 = (f32[16]{0:T(128)S(1)}, f32[16]{0:T(128)}, u32[]{:S(2)}) copy-start(f32[16]{0:T(128)} %decay_ref.7) | copy-start | bytes 196
  3.6 6.5 %collective-permute-start = (bf16[4,128,128]{2,1,0:T(8,128)(2,1)S(1)}, bf16[4,128,128]{2,1,0:T(8,128)(2,1)S(1)}, u32[]{:S(2)}, u32[]{:S(2)}) collective-permute-start(bf16[4,128,128]{2,1,0:T(8,128)(2,1)S(1)} %get-tuple-element.37), channel_id=1, source_target_pairs={{0,4},{4,0},{8,12},{12,8},{16,20},{20,16},{24,28},{28,24},{1,5},{5... | collective-permute-start | bytes 393224 | tf_op jit(solution)/shard_map/ppermute | solution.py:264
  7.2 26.6 %copy-start.7 = (bf16[128,2048]{1,0:T(8,128)(2,1)S(1)}, bf16[128,2048]{1,0:T(8,128)(2,1)}, u32[]{:S(2)}) copy-start(bf16[128,2048]{1,0:T(8,128)(2,1)} %q_ref.3) | copy-start | bytes 1572868
  7.2 26.6 %copy-start.8 = (bf16[128,2048]{1,0:T(8,128)(2,1)S(1)}, bf16[128,2048]{1,0:T(8,128)(2,1)}, u32[]{:S(2)}) copy-start(bf16[128,2048]{1,0:T(8,128)(2,1)} %k_ref.3) | copy-start | bytes 1572868
  7.2 26.6 %copy-start.9 = (bf16[128,2048]{1,0:T(8,128)(2,1)S(1)}, bf16[128,2048]{1,0:T(8,128)(2,1)}, u32[]{:S(2)}) copy-start(bf16[128,2048]{1,0:T(8,128)(2,1)} %v_ref.3) | copy-start | bytes 1572868
  7.2 26.6 %copy-start.10 = (bf16[128,2048]{1,0:T(8,128)(2,1)S(1)}, bf16[128,2048]{1,0:T(8,128)(2,1)}, u32[]{:S(2)}) copy-start(bf16[128,2048]{1,0:T(8,128)(2,1)} %gate_ref.3) | copy-start | bytes 1572868
  7.2 26.6 %copy-start.15 = (f32[2048]{0:T(1024)S(1)}, f32[2048]{0:T(1024)}, u32[]{:S(2)}) copy-start(f32[2048]{0:T(1024)} %param.20) | copy-start | bytes 24580
  10.3 6.2 %collective-permute-start.1 = (bf16[4,128,128]{2,1,0:T(8,128)(2,1)S(1)}, bf16[4,128,128]{2,1,0:T(8,128)(2,1)S(1)}, u32[]{:S(2)}, u32[]{:S(2)}) collective-permute-start(bf16[4,128,128]{2,1,0:T(8,128)(2,1)S(1)} %fusion.3), channel_id=1, source_target_pairs={{0,8},{4,12},{8,16},{12,20},{16,24},{20,28},{1,9},{5,13},{9,17},{1... | collective-permute-start | bytes 393224 | tf_op jit(solution)/shard_map/ppermute | solution.py:339
  14.9 7.1 %collective-permute-start.5 = (bf16[4,128,128]{2,1,0:T(8,128)(2,1)S(1)}, bf16[4,128,128]{2,1,0:T(8,128)(2,1)S(1)}, u32[]{:S(2)}, u32[]{:S(2)}) collective-permute-start(bf16[4,128,128]{2,1,0:T(8,128)(2,1)S(1)} %get-tuple-element.46), channel_id=1, source_target_pairs={{0,4},{4,0},{8,12},{12,8},{16,20},{20,16},{24,28},{28,24},{1,5},{5... | collective-permute-start | bytes 393224 | tf_op jit(solution)/shard_map/ppermute | solution.py:264
  16.6 9.1 %collective-permute-start.2 = (bf16[4,128,128]{2,1,0:T(8,128)(2,1)S(1)}, bf16[4,128,128]{2,1,0:T(8,128)(2,1)S(1)}, u32[]{:S(2)}, u32[]{:S(2)}) collective-permute-start(bf16[4,128,128]{2,1,0:T(8,128)(2,1)S(1)} %fusion.5), channel_id=1, source_target_pairs={{0,16},{4,20},{8,24},{12,28},{1,17},{5,21},{9,25},{13,29},{2,18},{... | collective-permute-start | bytes 393224 | tf_op jit(solution)/shard_map/ppermute | solution.py:339
  22.1 6.0 %collective-permute-start.6 = (bf16[4,128,128]{2,1,0:T(8,128)(2,1)S(1)}, bf16[4,128,128]{2,1,0:T(8,128)(2,1)S(1)}, u32[]{:S(2)}, u32[]{:S(2)}) collective-permute-start(bf16[4,128,128]{2,1,0:T(8,128)(2,1)S(1)} %fusion.8), channel_id=1, source_target_pairs={{0,8},{4,12},{8,16},{12,20},{16,24},{20,28},{1,9},{5,13},{9,17},{1... | collective-permute-start | bytes 393224 | tf_op jit(solution)/shard_map/ppermute | solution.py:339
  25.8 9.2 %collective-permute-start.3 = (bf16[4,128,128]{2,1,0:T(8,128)(2,1)S(1)}, bf16[4,128,128]{2,1,0:T(8,128)(2,1)S(1)}, u32[]{:S(2)}, u32[]{:S(2)}) collective-permute-start(bf16[4,128,128]{2,1,0:T(8,128)(2,1)S(1)} %get-tuple-element.74), channel_id=1, source_target_pairs={{0,4},{4,0},{8,12},{12,8},{16,20},{20,16},{24,28},{28,24},{1,5},{5... | collective-permute-start | bytes 393224 | tf_op jit(solution)/shard_map/ppermute | solution.py:264
  28.2 9.7 %collective-permute-start.7 = (bf16[4,128,128]{2,1,0:T(8,128)(2,1)S(1)}, bf16[4,128,128]{2,1,0:T(8,128)(2,1)S(1)}, u32[]{:S(2)}, u32[]{:S(2)}) collective-permute-start(bf16[4,128,128]{2,1,0:T(8,128)(2,1)S(1)} %fusion.10), channel_id=1, source_target_pairs={{0,16},{4,20},{8,24},{12,28},{1,17},{5,21},{9,25},{13,29},{2,18},{... | collective-permute-start | bytes 393224 | tf_op jit(solution)/shard_map/ppermute | solution.py:339
  36.0 12.0 %collective-permute-start.10 = (bf16[128,1024]{1,0:T(8,128)(2,1)S(1)}, bf16[128,1024]{1,0:T(8,128)(2,1)S(1)}, u32[]{:S(2)}, u32[]{:S(2)}) collective-permute-start(bf16[128,1024]{1,0:T(8,128)(2,1)S(1)} %mix_heads.2.refs_0_), channel_id=1, source_target_pairs={{0,8},{4,12},{8,16},{12,20},{16,24},{20,28},{24,0},{28,4},{1,9},{5... | collective-permute-start | bytes 786440 | tf_op jit(solution)/shard_map/ppermute | solution.py:268
  38.0 6.5 %collective-permute-start.8 = (bf16[4,128,128]{2,1,0:T(8,128)(2,1)S(1)}, bf16[4,128,128]{2,1,0:T(8,128)(2,1)S(1)}, u32[]{:S(2)}, u32[]{:S(2)}) collective-permute-start(bf16[4,128,128]{2,1,0:T(8,128)(2,1)S(1)} %get-tuple-element.72), channel_id=1, source_target_pairs={{0,4},{4,0},{8,12},{12,8},{16,20},{20,16},{24,28},{28,24},{1,5},{5... | collective-permute-start | bytes 393224 | tf_op jit(solution)/shard_map/ppermute | solution.py:264
  40.5 9.6 %collective-permute-start.4 = (bf16[128,1024]{1,0:T(8,128)(2,1)S(1)}, bf16[128,1024]{1,0:T(8,128)(2,1)S(1)}, u32[]{:S(2)}, u32[]{:S(2)}) collective-permute-start(bf16[128,1024]{1,0:T(8,128)(2,1)S(1)} %mix_heads.2.refs_0_), channel_id=1, source_target_pairs={{0,4},{4,0},{8,12},{12,8},{16,20},{20,16},{24,28},{28,24},{1,5},{5... | collective-permute-start | bytes 786440 | tf_op jit(solution)/shard_map/ppermute | solution.py:264
  45.5 12.6 %collective-permute-start.16 = (bf16[128,1024]{1,0:T(8,128)(2,1)S(1)}, bf16[128,1024]{1,0:T(8,128)(2,1)S(1)}, u32[]{:S(2)}, u32[]{:S(2)}) collective-permute-start(bf16[128,1024]{1,0:T(8,128)(2,1)S(1)} %mix_heads.3.refs_2_), channel_id=1, source_target_pairs={{0,8},{4,12},{8,16},{12,20},{16,24},{20,28},{24,0},{28,4},{1,9},{5... | collective-permute-start | bytes 786440 | tf_op jit(solution)/shard_map/ppermute | solution.py:268
  47.3 10.8 %collective-permute-start.9 = (bf16[128,1024]{1,0:T(8,128)(2,1)S(1)}, bf16[128,1024]{1,0:T(8,128)(2,1)S(1)}, u32[]{:S(2)}, u32[]{:S(2)}) collective-permute-start(bf16[128,1024]{1,0:T(8,128)(2,1)S(1)} %mix_heads.3.refs_2_), channel_id=1, source_target_pairs={{0,4},{4,0},{8,12},{12,8},{16,20},{20,16},{24,28},{28,24},{1,5},{5... | collective-permute-start | bytes 786440 | tf_op jit(solution)/shard_map/ppermute | solution.py:264
  48.0 14.7 %collective-permute-start.11 = (bf16[128,1024]{1,0:T(8,128)(2,1)S(1)}, bf16[128,1024]{1,0:T(8,128)(2,1)S(1)}, u32[]{:S(2)}, u32[]{:S(2)}) collective-permute-start(bf16[128,1024]{1,0:T(8,128)(2,1)S(1)} %collective-permute-done.10.refs_0_), channel_id=1, source_target_pairs={{0,8},{4,12},{8,16},{12,20},{16,24},{20,28},{24,0},{28,4},{1,9},{5... | collective-permute-start | bytes 786440 | tf_op jit(solution)/shard_map/ppermute | solution.py:268
  50.1 14.5 %collective-permute-start.15 = (bf16[128,1024]{1,0:T(8,128)(2,1)S(1)}, bf16[128,1024]{1,0:T(8,128)(2,1)S(1)}, u32[]{:S(2)}, u32[]{:S(2)}) collective-permute-start(bf16[128,1024]{1,0:T(8,128)(2,1)S(1)} %collective-permute-done.10.refs_0_), channel_id=1, source_target_pairs={{0,4},{4,0},{8,12},{12,8},{16,20},{20,16},{24,28},{28,24},{1,5},{5... | collective-permute-start | bytes 786440 | tf_op jit(solution)/shard_map/ppermute | solution.py:264
  58.1 10.1 %collective-permute-start.18 = (bf16[128,1024]{1,0:T(8,128)(2,1)S(1)}, bf16[128,1024]{1,0:T(8,128)(2,1)}, u32[]{:S(2)}, u32[]{:S(2)}) collective-permute-start(bf16[128,1024]{1,0:T(8,128)(2,1)S(1)} %collective-permute-done.16.refs_2_), channel_id=1, source_target_pairs={{0,8},{4,12},{8,16},{12,20},{16,24},{20,28},{24,0},{28,4},{1,9},{5... | collective-permute-start | bytes 786440 | tf_op jit(solution)/shard_map/ppermute | solution.py:268
  62.7 8.2 %collective-permute-start.12 = (bf16[128,1024]{1,0:T(8,128)(2,1)S(1)}, bf16[128,1024]{1,0:T(8,128)(2,1)S(1)}, u32[]{:S(2)}, u32[]{:S(2)}) collective-permute-start(bf16[128,1024]{1,0:T(8,128)(2,1)S(1)} %collective-permute-done.11.refs_0_), channel_id=1, source_target_pairs={{0,8},{4,12},{8,16},{12,20},{16,24},{20,28},{24,0},{28,4},{1,9},{5... | collective-permute-start | bytes 786440 | tf_op jit(solution)/shard_map/ppermute | solution.py:268
  62.7 8.2 %collective-permute-start.13 = (bf16[128,1024]{1,0:T(8,128)(2,1)S(1)}, bf16[128,1024]{1,0:T(8,128)(2,1)S(1)}, u32[]{:S(2)}, u32[]{:S(2)}) collective-permute-start(bf16[128,1024]{1,0:T(8,128)(2,1)S(1)} %collective-permute-done.11.refs_0_), channel_id=1, source_target_pairs={{0,4},{4,0},{8,12},{12,8},{16,20},{20,16},{24,28},{28,24},{1,5},{5... | collective-permute-start | bytes 786440 | tf_op jit(solution)/shard_map/ppermute | solution.py:264
  68.2 11.5 %collective-permute-start.19 = (bf16[128,1024]{1,0:T(8,128)(2,1)}, bf16[128,1024]{1,0:T(8,128)(2,1)}, u32[]{:S(2)}, u32[]{:S(2)}) collective-permute-start(bf16[128,1024]{1,0:T(8,128)(2,1)} %collective-permute-done.18.refs_2_), channel_id=1, source_target_pairs={{0,4},{4,0},{8,12},{12,8},{16,20},{20,16},{24,28},{28,24},{1,5},{5... | collective-permute-start | bytes 786440 | tf_op jit(solution)/shard_map/ppermute | solution.py:264
  69.7 10.0 %collective-permute-start.20 = (bf16[128,1024]{1,0:T(8,128)(2,1)}, bf16[128,1024]{1,0:T(8,128)(2,1)S(1)}, u32[]{:S(2)}, u32[]{:S(2)}) collective-permute-start(bf16[128,1024]{1,0:T(8,128)(2,1)} %collective-permute-done.18.refs_2_), channel_id=1, source_target_pairs={{0,8},{4,12},{8,16},{12,20},{16,24},{20,28},{24,0},{28,4},{1,9},{5... | collective-permute-start | bytes 786440 | tf_op jit(solution)/shard_map/ppermute | solution.py:268
  70.9 0.7 copy-start.13
  71.6 9.5 %collective-permute-start.14 = (bf16[128,1024]{1,0:T(8,128)(2,1)S(1)}, bf16[128,1024]{1,0:T(8,128)(2,1)S(1)}, u32[]{:S(2)}, u32[]{:S(2)}) collective-permute-start(bf16[128,1024]{1,0:T(8,128)(2,1)S(1)} %collective-permute-done.12.refs_0_), channel_id=1, source_target_pairs={{0,4},{4,0},{8,12},{12,8},{16,20},{20,16},{24,28},{28,24},{1,5},{5... | collective-permute-start | bytes 786440 | tf_op jit(solution)/shard_map/ppermute | solution.py:264
  73.7 16.0 %all-to-all-start = ((bf16[8,16,768]{2,1,0:T(8,128)(2,1)}), bf16[8,16,768]{2,1,0:T(8,128)(2,1)}, u32[]{:S(2)}, u32[]{:S(2)}) async-start(bf16[8,16,768]{2,1,0:T(8,128)(2,1)} %pad_maximum_fusion.2), calls=%async_computation | async-start | bytes 393216 | tf_op jit(solution)/shard_map/all_to_all | solution.py:379
  77.7 10.9 %collective-permute-start.17 = (bf16[128,1024]{1,0:T(8,128)(2,1)S(1)}, bf16[128,1024]{1,0:T(8,128)(2,1)S(1)}, u32[]{:S(2)}, u32[]{:S(2)}) collective-permute-start(bf16[128,1024]{1,0:T(8,128)(2,1)S(1)} %collective-permute-done.9.refs_3_), channel_id=1, source_target_pairs={{0,8},{4,12},{8,16},{12,20},{16,24},{20,28},{24,0},{28,4},{1,9},{5... | collective-permute-start | bytes 786440 | tf_op jit(solution)/shard_map/ppermute | solution.py:268
  79.7 11.7 %collective-permute-start.21 = (bf16[128,1024]{1,0:T(8,128)(2,1)S(1)}, bf16[128,1024]{1,0:T(8,128)(2,1)}, u32[]{:S(2)}, u32[]{:S(2)}) collective-permute-start(bf16[128,1024]{1,0:T(8,128)(2,1)S(1)} %collective-permute-done.20.refs_2_), channel_id=1, source_target_pairs={{0,4},{4,0},{8,12},{12,8},{16,20},{20,16},{24,28},{28,24},{1,5},{5... | collective-permute-start | bytes 786440 | tf_op jit(solution)/shard_map/ppermute | solution.py:264
  81.2 0.7 copy-start.11
  81.9 1.9 %copy-start.4 = (bf16[2048,768]{1,0:T(8,128)(2,1)S(1)}, bf16[2048,768]{1,0:T(8,128)(2,1)}, u32[]{:S(2)}) copy-start(bf16[2048,768]{1,0:T(8,128)(2,1)} %refs_4_.4) | copy-start | bytes 9437188
  83.8 1.9 %copy-start.5 = (bf16[2048,768]{1,0:T(8,128)(2,1)S(1)}, bf16[2048,768]{1,0:T(8,128)(2,1)}, u32[]{:S(2)}) copy-start(bf16[2048,768]{1,0:T(8,128)(2,1)} %refs_4_.4) | copy-start | bytes 9437188
  85.7 0.9 copy-start.14
  88.6 2.8 %copy-start.12 = (bf16[128,1024]{1,0:T(8,128)(2,1)S(1)}, bf16[128,1024]{1,0:T(8,128)(2,1)}, u32[]{:S(2)}) copy-start(bf16[128,1024]{1,0:T(8,128)(2,1)} %copy-done.11) | copy-start | bytes 786436
  91.4 1.9 %copy-start.6 = (bf16[2048,768]{1,0:T(8,128)(2,1)S(1)}, bf16[2048,768]{1,0:T(8,128)(2,1)}, u32[]{:S(2)}) copy-start(bf16[2048,768]{1,0:T(8,128)(2,1)} %refs_4_.4) | copy-start | bytes 9437188
  95.7 1.5 collective-permute-start.22
  97.3 4.9 %collective-permute-start.23 = (bf16[1,64,768]{2,1,0:T(8,128)(2,1)S(1)}, bf16[1,64,768]{2,1,0:T(8,128)(2,1)S(1)}, u32[]{:S(2)}, u32[]{:S(2)}) collective-permute-start(bf16[1,64,768]{2,1,0:T(8,128)(2,1)S(1)} %get-tuple-element.82), channel_id=1, source_target_pairs={{0,2},{1,3},{2,0},{3,1},{4,6},{5,7},{6,4},{7,5},{8,10},{9,11},{10,... | collective-permute-start | bytes 294920 | tf_op jit(solution)/shard_map/ppermute | solution.py:430
  102.8 17.1 %copy-start.1 = (f32[6144]{0:T(1024)S(1)}, f32[6144]{0:T(1024)}, u32[]{:S(2)}) copy-start(f32[6144]{0:T(1024)} %param.22) | copy-start | bytes 73732
  102.8 5.6 %collective-permute-start.26 = (bf16[64,768]{1,0:T(8,128)(2,1)S(1)}, bf16[64,768]{1,0:T(8,128)(2,1)S(1)}, u32[]{:S(2)}, u32[]{:S(2)}) collective-permute-start(bf16[64,768]{1,0:T(8,128)(2,1)S(1)} %slot_hidden.1.refs_0_), channel_id=1, source_target_pairs={{0,8},{4,12},{8,0},{12,4},{16,24},{20,28},{24,16},{28,20},{1,9},{5... | collective-permute-start | bytes 294920 | tf_op jit(solution)/shard_map/ppermute | solution.py:449
  104.3 8.6 %collective-permute-start.24 = (bf16[64,768]{1,0:T(8,128)(2,1)S(1)}, bf16[64,768]{1,0:T(8,128)(2,1)S(1)}, u32[]{:S(2)}, u32[]{:S(2)}) collective-permute-start(bf16[64,768]{1,0:T(8,128)(2,1)S(1)} %slot_hidden.1.refs_0_), channel_id=1, source_target_pairs={{0,16},{4,20},{8,24},{12,28},{16,0},{20,4},{24,8},{28,12},{1,17},{... | collective-permute-start | bytes 294920 | tf_op jit(solution)/shard_map/ppermute | solution.py:449
  108.4 6.9 %collective-permute-start.27 = (bf16[64,768]{1,0:T(8,128)(2,1)S(1)}, bf16[64,768]{1,0:T(8,128)(2,1)S(1)}, u32[]{:S(2)}, u32[]{:S(2)}) collective-permute-start(bf16[64,768]{1,0:T(8,128)(2,1)S(1)} %collective-permute-done.26.refs_2_), channel_id=1, source_target_pairs={{0,16},{4,20},{8,24},{12,28},{16,0},{20,4},{24,8},{28,12},{1,17},{... | collective-permute-start | bytes 294920 | tf_op jit(solution)/shard_map/ppermute | solution.py:449
  110.3 7.9 %collective-permute-start.34 = (bf16[64,768]{1,0:T(8,128)(2,1)S(1)}, bf16[64,768]{1,0:T(8,128)(2,1)S(1)}, u32[]{:S(2)}, u32[]{:S(2)}) collective-permute-start(bf16[64,768]{1,0:T(8,128)(2,1)S(1)} %slot_hidden.1.refs_0_), channel_id=1, source_target_pairs={{0,4},{4,0},{8,12},{12,8},{16,20},{20,16},{24,28},{28,24},{1,5},{5... | collective-permute-start | bytes 294920 | tf_op jit(solution)/shard_map/ppermute | solution.py:264
  110.9 7.3 %collective-permute-start.35 = (bf16[64,768]{1,0:T(8,128)(2,1)S(1)}, bf16[64,768]{1,0:T(8,128)(2,1)S(1)}, u32[]{:S(2)}, u32[]{:S(2)}) collective-permute-start(bf16[64,768]{1,0:T(8,128)(2,1)S(1)} %collective-permute-done.26.refs_2_), channel_id=1, source_target_pairs={{0,4},{4,0},{8,12},{12,8},{16,20},{20,16},{24,28},{28,24},{1,5},{5... | collective-permute-start | bytes 294920 | tf_op jit(solution)/shard_map/ppermute | solution.py:264
  113.0 5.2 %collective-permute-start.25 = (bf16[64,768]{1,0:T(8,128)(2,1)S(1)}, bf16[64,768]{1,0:T(8,128)(2,1)S(1)}, u32[]{:S(2)}, u32[]{:S(2)}) collective-permute-start(bf16[64,768]{1,0:T(8,128)(2,1)S(1)} %collective-permute-done.24.refs_4_), channel_id=1, source_target_pairs={{0,4},{4,0},{8,12},{12,8},{16,20},{20,16},{24,28},{28,24},{1,5},{5... | collective-permute-start | bytes 294920 | tf_op jit(solution)/shard_map/ppermute | solution.py:264
  115.3 4.6 %collective-permute-start.36 = (bf16[64,768]{1,0:T(8,128)(2,1)S(1)}, bf16[64,768]{1,0:T(8,128)(2,1)S(1)}, u32[]{:S(2)}, u32[]{:S(2)}) collective-permute-start(bf16[64,768]{1,0:T(8,128)(2,1)S(1)} %collective-permute-done.27.refs_6_), channel_id=1, source_target_pairs={{0,4},{4,0},{8,12},{12,8},{16,20},{20,16},{24,28},{28,24},{1,5},{5... | collective-permute-start | bytes 294920 | tf_op jit(solution)/shard_map/ppermute | solution.py:264
  118.2 22.3 %collective-permute-start.28 = (bf16[2,256,768]{2,1,0:T(8,128)(2,1)S(1)}, bf16[2,256,768]{2,1,0:T(8,128)(2,1)}, u32[]{:S(2)}, u32[]{:S(2)}) collective-permute-start(bf16[2,256,768]{2,1,0:T(8,128)(2,1)S(1)} %pad_maximum_fusion), channel_id=1, source_target_pairs={{0,1},{1,0},{2,3},{3,2},{4,5},{5,4},{6,7},{7,6},{8,9},{9,8},{10,11... | collective-permute-start | bytes 2359304 | tf_op jit(solution)/shard_map/ppermute | solution.py:424
  119.9 5.0 %copy-start = (bf16[1,6144,1152]{2,1,0:T(8,128)(2,1)S(1)}, bf16[1,6144,1152]{2,1,0:T(8,128)(2,1)}, u32[]{:S(2)}) copy-start(bf16[1,6144,1152]{2,1,0:T(8,128)(2,1)} %refs_9_.1) | copy-start | bytes 42467332
  136.8 27.2 %all-to-all-start.1 = ((bf16[8,8,6144]{2,1,0:T(8,128)(2,1)}), bf16[8,8,6144]{2,1,0:T(8,128)(2,1)S(1)}, u32[]{:S(2)}, u32[]{:S(2)}) async-start(bf16[8,8,6144]{2,1,0:T(8,128)(2,1)} %bitcast.27), calls=%async_computation.1 | async-start | bytes 1572864 | tf_op jit(solution)/shard_map/all_to_all | solution.py:480
  140.5 3.0 %copy-start.18 = (f32[128,2]{0,1:T(2,128)S(1)}, f32[128,2]{0,1:T(2,128)}, u32[]{:S(2)}) copy-start(f32[128,2]{0,1:T(2,128)} %param.24) | copy-start | bytes 3076
  141.9 10.0 %collective-permute-start.29 = (bf16[1,256,768]{2,1,0:T(8,128)(2,1)S(1)}, bf16[1,256,768]{2,1,0:T(8,128)(2,1)S(1)}, u32[]{:S(2)}, u32[]{:S(2)}) collective-permute-start(bf16[1,256,768]{2,1,0:T(8,128)(2,1)S(1)} %get-tuple-element.71), channel_id=1, source_target_pairs={{0,2},{1,3},{2,0},{3,1},{4,6},{5,7},{6,4},{7,5},{8,10},{9,11},{10,... | collective-permute-start | bytes 1179656 | tf_op jit(solution)/shard_map/ppermute | solution.py:430
  152.0 6.7 %collective-permute-start.30 = (bf16[4,32,768]{2,1,0:T(8,128)(2,1)S(1)}, bf16[4,32,768]{2,1,0:T(8,128)(2,1)S(1)}, u32[]{:S(2)}, u32[]{:S(2)}) collective-permute-start(bf16[4,32,768]{2,1,0:T(8,128)(2,1)S(1)} %get-tuple-element.81), channel_id=1, source_target_pairs={{0,4},{4,0},{8,12},{12,8},{16,20},{20,16},{24,28},{28,24},{1,5},{5... | collective-permute-start | bytes 589832 | tf_op jit(solution)/shard_map/ppermute | solution.py:264
  158.7 6.1 %collective-permute-start.31 = (bf16[2,32,768]{2,1,0:T(8,128)(2,1)S(1)}, bf16[2,32,768]{2,1,0:T(8,128)(2,1)S(1)}, u32[]{:S(2)}, u32[]{:S(2)}) collective-permute-start(bf16[2,32,768]{2,1,0:T(8,128)(2,1)S(1)} %get-tuple-element.77), channel_id=1, source_target_pairs={{0,24},{4,28},{8,0},{12,4},{16,8},{20,12},{24,16},{28,20},{1,25},{... | collective-permute-start | bytes 294920 | tf_op jit(solution)/shard_map/ppermute | solution.py:268
  161.4 8.3 %collective-permute-start.32 = (bf16[2,32,768]{2,1,0:T(8,128)(2,1)S(1)}, bf16[2,32,768]{2,1,0:T(8,128)(2,1)S(1)}, u32[]{:S(2)}, u32[]{:S(2)}) collective-permute-start(bf16[2,32,768]{2,1,0:T(8,128)(2,1)S(1)} %get-tuple-element.79), channel_id=1, source_target_pairs={{0,16},{4,20},{8,24},{12,28},{16,0},{20,4},{24,8},{28,12},{1,17},{... | collective-permute-start | bytes 294920 | tf_op jit(solution)/shard_map/ppermute | solution.py:268
  162.5 7.2 %collective-permute-start.33 = (bf16[2,32,768]{2,1,0:T(8,128)(2,1)S(1)}, bf16[2,32,768]{2,1,0:T(8,128)(2,1)S(1)}, u32[]{:S(2)}, u32[]{:S(2)}) collective-permute-start(bf16[2,32,768]{2,1,0:T(8,128)(2,1)S(1)} %get-tuple-element.78), channel_id=1, source_target_pairs={{0,8},{4,12},{8,16},{12,20},{16,24},{20,28},{24,0},{28,4},{1,9},{5... | collective-permute-start | bytes 294920 | tf_op jit(solution)/shard_map/ppermute | solution.py:268

commit v5 on v4

--- a/solution.py
+++ b/solution.py
@@ -158,19 +158,32 @@
             ]
 
 
-def select_kernel(n_exp, cap, row_ref, *refs):
-    parts, outs = refs[:-2], refs[-2:]
-    for step in range(len(parts) // 2):
-        both = parts[2 * step : 2 * step + 2]
-        rows = jnp.concatenate([p[i] for p in both for i in range(n_exp // 2)], axis=0)
-        slots = n_exp * 2 * cap
-        pick = row_ref[step] == lax.broadcasted_iota(jnp.int32, (slots, rows.shape[0]), 1)
-        found = jnp.dot(pick.astype(F32).astype(BF16), rows, preferred_element_type=F32)
-        found = found.astype(BF16)
+def select_kernel(n_exp, cap, chunks, row_ref, *refs):
+    blocks, (weight_ref, keep_ref, send_ref) = refs[:-3], refs[-3:]
+    steps, slots = row_ref.shape[:2]
+    tok, wide = blocks[0].shape
+    picked = [[] for _ in range(chunks)]
+    for step in range(steps):
+        pick = row_ref[step] == lax.broadcasted_iota(jnp.int32, (slots, 2 * tok), 1)
+        pick = pick.astype(F32).astype(BF16)
+        for chunk in range(chunks):
+            rows = [blocks[(step * 2 + y) * chunks + chunk][...] for y in range(2)]
+            rows = jnp.dot(pick, jnp.concatenate(rows, axis=0), preferred_element_type=F32)
+            picked[chunk].append(rows.astype(BF16))
+    total = None
+    for chunk in range(chunks):
+        part = jnp.dot(
+            jnp.concatenate(picked[chunk], axis=0),
+            weight_ref[chunk * wide : (chunk + 1) * wide, :],
+            preferred_element_type=F32,
+        )
+        total = part if total is None else total + part
+    total = total.astype(BF16)
+    for step in range(steps):
         for j in range(n_exp):
-            outs[j % 2][j // 2, 2 * cap * step : 2 * cap * (step + 1), :] = found[
-                2 * cap * j : 2 * cap * (j + 1)
-            ]
+            out = send_ref if j % 2 else keep_ref
+            at = step * slots + 2 * cap * j
+            out[j // 2, 2 * cap * step : 2 * cap * (step + 1), :] = total[at : at + 2 * cap]
 
 
 def hidden_kernel(cap, order_ref, stream_ref, mine_ref, came_ref, out_ref, total_ref):
@@ -183,23 +196,7 @@
 
 def ffn_kernel(n, blocks, order_ref, *refs):
     pieces, refs = refs[:n], refs[n:]
-    gain_ref, gate_ref, up_ref, down_ref, out_ref, rows_ref, up_buf, down_buf, sems = refs
-    rows_step = up_buf.shape[1]
-    step = out_ref.shape[1] // blocks
-    ups = [
-        pltpu.make_async_copy(
-            up_ref.at[0, pl.ds(i * rows_step, rows_step), :], up_buf.at[i], sems.at[0, i]
-        )
-        for i in range(blocks)
-    ]
-    downs = [
-        pltpu.make_async_copy(
-            down_ref.at[0, :, pl.ds(i * step, step)], down_buf.at[i], sems.at[1, i]
-        )
-        for i in range(blocks)
-    ]
-    for copy in ups + downs:
-        copy.start()
+    gain_ref, gate_ref, up_ref, down_ref, out_ref, rows_ref = refs
     cols = pieces[0].shape[1]
     total = 0.0
     for piece in pieces:
@@ -209,21 +206,19 @@
     for i, piece in enumerate(pieces):
         at = lanes(order_ref[i], cols) if n > 1 else slice(None)
         rows_ref[:, at] = (piece[...].astype(F32) * inverse * gain_ref[:, at]).astype(BF16)
-    spans = [slice(i * rows_step, (i + 1) * rows_step) for i in range(blocks)]
+    step = out_ref.shape[1] // blocks
+    spans = [slice(i * step, (i + 1) * step) for i in range(blocks)]
     gate = up = None
     for at in spans:
-        g = jnp.dot(rows_ref[:, at], gate_ref[0, at, :], preferred_element_type=F32)
+        rows = rows_ref[:, at]
+        g = jnp.dot(rows, gate_ref[0, at, :], preferred_element_type=F32)
+        u = jnp.dot(rows, up_ref[0, at, :], preferred_element_type=F32)
         gate = g if gate is None else gate + g
-    gate = gate / (1.0 + jnp.exp(-gate))
-    for i, at in enumerate(spans):
-        ups[i].wait()
-        u = jnp.dot(rows_ref[:, at], up_buf[i], preferred_element_type=F32)
         up = u if up is None else up + u
-    activated = (gate * up).astype(BF16)
-    for i, copy in enumerate(downs):
-        copy.wait()
-        out_ref[:, i * step : (i + 1) * step] = jnp.dot(
-            activated, down_buf[i], preferred_element_type=F32
+    activated = (gate / (1.0 + jnp.exp(-gate)) * up).astype(BF16)
+    for at in spans:
+        out_ref[:, at] = jnp.dot(
+            activated, down_ref[0, :, at], preferred_element_type=F32
         ).astype(BF16)
 
 
@@ -259,6 +254,7 @@
     wide = per_chunk * size
     swap = [(i, i ^ 1) for i in range(n_ctx)]
     here = jnp.stack([pair, own]).astype(jnp.int32)
+    room = 4 * max(1, n_ctx // 8)
 
     def swapped(value):
         return lax.ppermute(value, "ctx", swap)
@@ -280,7 +276,7 @@
             pltpu.VMEM((tok, heads * size), BF16),
             pltpu.SemaphoreType.DMA((2, CHUNKS)),
         ],
-        compiler_params=limit(8),
+        compiler_params=limit(room),
         cost_estimate=takes(1),
         name="shard_state",
     )(here, decay_rates, in_hbm(key_proj), in_hbm(values))
@@ -295,7 +291,7 @@
             ],
             in_specs=[SMEM] + [VMEM] * 5,
             out_specs=[VMEM] * 3,
-            compiler_params=limit(8),
+            compiler_params=limit(room),
             cost_estimate=takes(1),
             name="near_part",
         )(after(decay_rates, start), queries, key_proj, values, attn_gate, attn_gain[None, :])
@@ -352,7 +348,7 @@
                 out_shape=jax.ShapeDtypeStruct((tok, wide), BF16),
                 in_specs=[SMEM, SMEM] + [VMEM] * 5,
                 out_specs=VMEM,
-                compiler_params=limit(8),
+                compiler_params=limit(room),
                 cost_estimate=takes(1),
                 name="mix_heads",
             )(here, decay_rates, query, near, scale, mine, other)
@@ -383,8 +379,7 @@
     token = arrived[:, cap, : n_exp * cap].astype(jnp.int32).reshape(n_ctx, n_exp, cap) - 1
     index = jnp.arange(n_ctx, dtype=jnp.int32)
     order = ((group - index // 2) % groups) * 2 + (pair ^ (index % 2))
-    turned = (token // own_rows) ^ own
-    row = (turned % 2 * (n_exp // 2) + turned // 2) * 2 + (index % 2 ^ pair)[:, None, None]
+    row = (index % 2 ^ pair)[:, None, None] * n_exp + ((token // own_rows) ^ own)
     row = jnp.where(token >= 0, row * own_rows + token % own_rows, -1)
     row = jnp.stack(
         [lax.dynamic_index_in_dim(row, own ^ j, 1, keepdims=False) for j in range(n_exp)], axis=1
@@ -392,11 +387,25 @@
     row = jnp.take(row, order, axis=0).reshape(groups, 2, n_exp, cap)
     row = row.transpose(0, 2, 1, 3).reshape(groups, n_exp * 2 * cap, 1)
 
+    slots = jax.ShapeDtypeStruct((n_exp // 2, n_ctx * cap, cols), BF16)
+    slot_parts = pl.pallas_call(
+        functools.partial(select_kernel, n_exp, cap, CHUNKS),
+        out_shape=[slots, slots],
+        in_specs=[VMEM] * (2 + n_ctx * CHUNKS),
+        out_specs=[VMEM] * 2,
+        compiler_params=limit(room),
+        cost_estimate=takes(1),
+        name="slot_rows",
+    )(
+        row,
+        *[rows_of[i // 2][i % 2][chunk] for i in range(n_ctx) for chunk in range(CHUNKS)],
+        out_weight,
+    )
+
     parts = []
     for step in range(groups):
         weight = out_weight
-        if step + 1 < groups:
-            weight = after(weight, cross[0][-1])
+        weight = after(weight, cross[0][-1] if step + 1 < groups else slot_parts[0])
         rows = jax.ShapeDtypeStruct((n_exp // 2, 2 * own_rows, cols), BF16)
         parts.append(
             pl.pallas_call(
@@ -404,22 +413,11 @@
                 out_shape=[rows, rows],
                 in_specs=[VMEM] * (1 + 2 * CHUNKS),
                 out_specs=[VMEM] * 2,
-                compiler_params=limit(8),
-                cost_estimate=takes(1.5),
+                compiler_params=limit(room),
+                cost_estimate=takes(1.5 if step + 1 < groups else 60),
                 name="project",
             )(*[rows_of[step][y][chunk] for chunk in range(CHUNKS) for y in range(2)], weight)
         )
-    slots = jax.ShapeDtypeStruct((n_exp // 2, n_ctx * cap, cols), BF16)
-    slot_parts = pl.pallas_call(
-        functools.partial(select_kernel, n_exp, cap),
-        out_shape=[slots, slots],
-        in_specs=[VMEM] * (1 + 2 * groups),
-        out_specs=[VMEM] * 2,
-        compiler_params=limit(8),
-        cost_estimate=takes(1),
-        name="slot_rows",
-    )(row, *[p for both in parts for p in both])
-
     def add_groups(keep, send):
         came = lax.ppermute(send, "exp", [(i, i ^ 1) for i in range(n_exp)])
         bit = 2
@@ -437,8 +435,8 @@
         in_specs=[SMEM] + [VMEM] * 3,
         out_specs=VMEM,
         scratch_shapes=[pltpu.VMEM((n_ctx * cap, cols), F32)],
-        compiler_params=limit(8),
-        cost_estimate=takes(15),
+        compiler_params=limit(room),
+        cost_estimate=takes(1),
         name="slot_hidden",
     )(order, stream_rows, *add_groups(*slot_parts))
 
@@ -465,18 +463,15 @@
     down = pl.pallas_call(
         functools.partial(ffn_kernel, len(pieces), blocks),
         out_shape=jax.ShapeDtypeStruct((n_ctx * cap, width), BF16),
-        in_specs=[SMEM] + [VMEM] * (len(pieces) + 2) + [HBM, HBM],
+        in_specs=[SMEM] + [VMEM] * (len(pieces) + 4),
         out_specs=VMEM,
         scratch_shapes=[
             pltpu.VMEM((n_ctx * cap, width), BF16),
-            pltpu.VMEM((blocks, width // blocks, hidden_units), BF16),
-            pltpu.VMEM((blocks, hidden_units, width // blocks), BF16),
-            pltpu.SemaphoreType.DMA((2, blocks)),
         ],
-        compiler_params=limit(36),
+        compiler_params=limit(room),
         cost_estimate=takes(10),
         name="expert",
-    )(source, *pieces, ffn_gain[None, :], w_gate, in_hbm(w_up), in_hbm(w_down))
+    )(source, *pieces, ffn_gain[None, :], w_gate, w_up, w_down)
     received = lax.all_to_all(
         down.reshape(n_ctx, cap, width), "ctx", split_axis=0, concat_axis=0, tiled=True
     )

time: 173 us -> 171 us (0.988)
  local copies, waits for them, and re-layouts: 15.3 us -> 11.6 us
  Pallas kernels: 25.4 us -> 27.9 us
    ppermute x10, waiting for transfers between devices: 21.1 us -> 26.6 us  [shifted(): return lax.ppermute(value, 'ctx', to)]
    unnamed x39 -> x83, local copies, waits for them, and re-layouts: 12.8 us -> 7.83 us
    ppermute x3, waiting for transfers between devices: 5.53 us -> 1.79 us  [per_device(): lax.ppermute(pieces[r], 'ctx', [(i, i ^ 2 * bit) for i in range(n_ctx)])]
    pallas_call x1, Pallas kernels: 0.43 us -> 3.61 us  [per_device(): pl.pallas_call(functools.partial(select_kernel, n_exp, cap, CHUNKS), out_...]
    pallas_call x1, Pallas kernels: 11.9 us -> 8.8 us  [per_device(): pl.pallas_call(functools.partial(ffn_kernel, len(pieces), blocks), out_sh...]
    pallas_call x4, Pallas kernels: 5.97 us -> 8.43 us  [per_device(): pl.pallas_call(functools.partial(project_kernel, n_exp), out_shape=[rows,...]
    ppermute x10, starting transfers between devices: 12.9 us -> 11 us  [shifted(): return lax.ppermute(value, 'ctx', to)]
  transfers between devices with their start and end apart: 39 -> 39, of which waited for: 20 -> 21; matrix products, arithmetic and copies ran while one was open for 4% -> 4% of each run, Pallas kernels for 12% -> 13%
where the time goes in v5:
time: 171 us; the launch traced here: 170 us
  starting transfers between devices  66.8 us (39%)
  waiting for transfers between devices  55.4 us (32%)
  Pallas kernels  27.9 us (16%)
  local copies, waits for them, and re-layouts  11.6 us (7%)
  other arithmetic  6.14 us (4%)
    ppermute x10, waiting for transfers between devices, shifted(): return lax.ppermute(value, 'ctx', to)  26.6 us
    ppermute x16, starting transfers between devices, swapped(): return lax.ppermute(value, 'ctx', swap)  21.6 us
    ppermute x4, starting transfers between devices, per_device(): far = lax.ppermute(window, 'ctx', line).astype(F32)  18.1 us
    ppermute x16, waiting for transfers between devices, swapped(): return lax.ppermute(value, 'ctx', swap)  14.3 us
    ppermute x2, waiting for transfers between devices, add_groups(): lax.ppermute(total[:, 1], 'exp', [(i, i ^ bit) for i in range(n_exp)])  11.4 us
    ppermute x10, starting transfers between devices, shifted(): return lax.ppermute(value, 'ctx', to)  11 us
    pallas_call x1, Pallas kernels, per_device(): pl.pallas_call(functools.partial(ffn_kernel, len(pieces), blocks), out_sh...  8.8 us
    pallas_call x4, Pallas kernels, per_device(): pl.pallas_call(functools.partial(project_kernel, n_exp), out_shape=[rows,...  8.43 us
  transfers between devices with their start and end apart: 39, of which 21 were waited for; matrix products, arithmetic and copies ran while one was open for 4% of the time, Pallas kernels for 13%

profile of v5, /device:TPU:0, one launch (start us, length us, event | category | flops | bytes accessed | tf_op | source)
XLA Modules:
  0.0 169.9 jit_solution(3180982275300527246)
XLA Ops:
  1.4 2.2 %shard_state.1 = (bf16[4,128,128]{2,1,0:T(8,128)(2,1)S(1)}, bf16[4,128,128]{2,1,0:T(8,128)(2,1)S(1)}, bf16[4,128,128]{2,1,0:T(8,128)(2,1)S(1)}, bf16[4,128,128]{2,1,0:T(8,128)(2,1)S(1)}) custom-call(s32[2]{0:T(128)S(1)} %pad_add_fusion.1.place_ref, f32[16]{0:T(128)S(1)} %copy-done.19, bf16[128,2048]{1,0:T(8,128)(2,1)} %k_ref.3, bf16[128,2048]{1,0:T(8,128)(2,1)} %v_ref.3), custom_call_target="tpu_custom_call" | custom-call | flops 1000000000 | bytes 1000000 | tf_op jit(solution)/shard_map/shard_state/pallas_call | solution.py:269
  3.6 3.0 %collective-permute-start = (bf16[4,128,128]{2,1,0:T(8,128)(2,1)S(1)}, bf16[4,128,128]{2,1,0:T(8,128)(2,1)S(1)}, u32[]{:S(2)}, u32[]{:S(2)}) collective-permute-start(bf16[4,128,128]{2,1,0:T(8,128)(2,1)S(1)} %get-tuple-element.38), channel_id=1, source_target_pairs={{0,4},{4,0},{8,12},{12,8},{16,20},{20,16},{24,28},{28,24},{1,5},{5... | collective-permute-start | bytes 393224 | tf_op jit(solution)/shard_map/ppermute | solution.py:260
  7.3 2.8 %collective-permute-done = bf16[4,128,128]{2,1,0:T(8,128)(2,1)S(1)} collective-permute-done((bf16[4,128,128]{2,1,0:T(8,128)(2,1)S(1)}, bf16[4,128,128]{2,1,0:T(8,128)(2,1)S(1)}, u32[]{:S(2)}, u32[]{:S(2)}) %collective-permute-start) | collective-permute-done | bytes 131104 | tf_op jit(solution)/shard_map/ppermute | solution.py:260
  10.3 3.7 %collective-permute-start.1 = (bf16[4,128,128]{2,1,0:T(8,128)(2,1)S(1)}, bf16[4,128,128]{2,1,0:T(8,128)(2,1)S(1)}, u32[]{:S(2)}, u32[]{:S(2)}) collective-permute-start(bf16[4,128,128]{2,1,0:T(8,128)(2,1)S(1)} %fusion.3), channel_id=1, source_target_pairs={{0,8},{4,12},{8,16},{12,20},{16,24},{20,28},{1,9},{5,13},{9,17},{1... | collective-permute-start | bytes 393224 | tf_op jit(solution)/shard_map/ppermute | solution.py:335
  14.9 1.5 collective-permute-start.5
  16.6 5.4 %collective-permute-start.2 = (bf16[4,128,128]{2,1,0:T(8,128)(2,1)S(1)}, bf16[4,128,128]{2,1,0:T(8,128)(2,1)S(1)}, u32[]{:S(2)}, u32[]{:S(2)}) collective-permute-start(bf16[4,128,128]{2,1,0:T(8,128)(2,1)S(1)} %fusion.5), channel_id=1, source_target_pairs={{0,16},{4,20},{8,24},{12,28},{1,17},{5,21},{9,25},{13,29},{2,18},{... | collective-permute-start | bytes 393224 | tf_op jit(solution)/shard_map/ppermute | solution.py:335
  22.1 3.5 %collective-permute-start.6 = (bf16[4,128,128]{2,1,0:T(8,128)(2,1)S(1)}, bf16[4,128,128]{2,1,0:T(8,128)(2,1)S(1)}, u32[]{:S(2)}, u32[]{:S(2)}) collective-permute-start(bf16[4,128,128]{2,1,0:T(8,128)(2,1)S(1)} %fusion.8), channel_id=1, source_target_pairs={{0,8},{4,12},{8,16},{12,20},{16,24},{20,28},{1,9},{5,13},{9,17},{1... | collective-permute-start | bytes 393224 | tf_op jit(solution)/shard_map/ppermute | solution.py:335
  25.8 1.6 collective-permute-start.3
  28.2 5.6 %collective-permute-start.7 = (bf16[4,128,128]{2,1,0:T(8,128)(2,1)S(1)}, bf16[4,128,128]{2,1,0:T(8,128)(2,1)S(1)}, u32[]{:S(2)}, u32[]{:S(2)}) collective-permute-start(bf16[4,128,128]{2,1,0:T(8,128)(2,1)S(1)} %fusion.10), channel_id=1, source_target_pairs={{0,16},{4,20},{8,24},{12,28},{1,17},{5,21},{9,25},{13,29},{2,18},{... | collective-permute-start | bytes 393224 | tf_op jit(solution)/shard_map/ppermute | solution.py:335
  33.8 1.2 near_part.2
  35.0 1.0 mix_heads.2.refs_0_
  36.0 1.8 %collective-permute-start.10 = (bf16[128,1024]{1,0:T(8,128)(2,1)S(1)}, bf16[128,1024]{1,0:T(8,128)(2,1)}, u32[]{:S(2)}, u32[]{:S(2)}) collective-permute-start(bf16[128,1024]{1,0:T(8,128)(2,1)S(1)} %mix_heads.2.refs_0_), channel_id=1, source_target_pairs={{0,8},{4,12},{8,16},{12,20},{16,24},{20,28},{24,0},{28,4},{1,9},{5... | collective-permute-start | bytes 786440 | tf_op jit(solution)/shard_map/ppermute | solution.py:264
  38.0 1.3 collective-permute-start.8
  39.3 1.2 near_part.3
  40.5 0.8 collective-permute-start.4
  41.4 3.0 %collective-permute-done.10.refs_0_.refs_4_ = bf16[128,1024]{1,0:T(8,128)(2,1)} collective-permute-done((bf16[128,1024]{1,0:T(8,128)(2,1)S(1)}, bf16[128,1024]{1,0:T(8,128)(2,1)}, u32[]{:S(2)}, u32[]{:S(2)}) %collective-permute-start.10) | collective-permute-done | bytes 262176 | tf_op jit(solution)/shard_map/ppermute | solution.py:264
  44.5 1.0 mix_heads.3.refs_2_.refs_1_
  45.5 1.6 collective-permute-start.16
  47.1 1.1 collective-permute-start.9
  48.9 6.1 %collective-permute-done.11.refs_0_.refs_8_ = bf16[128,1024]{1,0:T(8,128)(2,1)} collective-permute-done((bf16[128,1024]{1,0:T(8,128)(2,1)}, bf16[128,1024]{1,0:T(8,128)(2,1)}, u32[]{:S(2)}, u32[]{:S(2)}) %collective-permute-start.11) | collective-permute-done | bytes 262176 | tf_op jit(solution)/shard_map/ppermute | solution.py:264
  55.7 1.5 collective-permute-start.15
  57.2 3.4 %collective-permute-done.16.refs_2_.refs_5_ = bf16[128,1024]{1,0:T(8,128)(2,1)} collective-permute-done((bf16[128,1024]{1,0:T(8,128)(2,1)S(1)}, bf16[128,1024]{1,0:T(8,128)(2,1)}, u32[]{:S(2)}, u32[]{:S(2)}) %collective-permute-start.16) | collective-permute-done | bytes 262176 | tf_op jit(solution)/shard_map/ppermute | solution.py:264
  61.3 1.5 collective-permute-start.13
  62.8 2.4 %collective-permute-done.12.refs_12_.refs_0_ = bf16[128,1024]{1,0:T(8,128)(2,1)} collective-permute-done((bf16[128,1024]{1,0:T(8,128)(2,1)}, bf16[128,1024]{1,0:T(8,128)(2,1)}, u32[]{:S(2)}, u32[]{:S(2)}) %collective-permute-start.12) | collective-permute-done | bytes 262176 | tf_op jit(solution)/shard_map/ppermute | solution.py:264
  65.2 4.0 %all-to-all-start = ((bf16[8,16,768]{2,1,0:T(8,128)(2,1)}), bf16[8,16,768]{2,1,0:T(8,128)(2,1)}, u32[]{:S(2)}, u32[]{:S(2)}) async-start(bf16[8,16,768]{2,1,0:T(8,128)(2,1)} %pad_maximum_fusion.2), calls=%async_computation | async-start | bytes 393216 | tf_op jit(solution)/shard_map/all_to_all | solution.py:375
  69.3 1.6 collective-permute-done.18.refs_2_.refs_9_
  70.9 1.5 collective-permute-start.19
  73.3 1.7 %collective-permute-start.17 = (bf16[128,1024]{1,0:T(8,128)(2,1)}, bf16[128,1024]{1,0:T(8,128)(2,1)}, u32[]{:S(2)}, u32[]{:S(2)}) collective-permute-start(bf16[128,1024]{1,0:T(8,128)(2,1)} %copy-done.7), channel_id=1, source_target_pairs={{0,8},{4,12},{8,16},{12,20},{16,24},{20,28},{24,0},{28,4},{1,9},{5... | collective-permute-start | bytes 786440 | tf_op jit(solution)/shard_map/ppermute | solution.py:264
  75.0 5.8 %collective-permute-done.20.refs_13_.refs_2_ = bf16[128,1024]{1,0:T(8,128)(2,1)} collective-permute-done((bf16[128,1024]{1,0:T(8,128)(2,1)}, bf16[128,1024]{1,0:T(8,128)(2,1)}, u32[]{:S(2)}, u32[]{:S(2)}) %collective-permute-start.20) | collective-permute-done | bytes 262176 | tf_op jit(solution)/shard_map/ppermute | solution.py:264
  80.9 1.3 collective-permute-start.21
  82.2 1.9 %collective-permute-done.14.refs_14_.refs_1_ = bf16[128,1024]{1,0:T(8,128)(2,1)} collective-permute-done((bf16[128,1024]{1,0:T(8,128)(2,1)}, bf16[128,1024]{1,0:T(8,128)(2,1)}, u32[]{:S(2)}, u32[]{:S(2)}) %collective-permute-start.14) | collective-permute-done | bytes 262176 | tf_op jit(solution)/shard_map/ppermute | solution.py:260
  86.8 0.8 reshape.310.row_ref
  87.7 0.9 copy-done.2
  88.6 0.9 copy-done.5
  89.6 0.9 copy-done.8
  90.5 3.6 %slot_rows.1 = (bf16[2,64,768]{2,1,0:T(8,128)(2,1)S(1)}, bf16[2,64,768]{2,1,0:T(8,128)(2,1)S(1)}) custom-call(s32[4,64,1]{2,1,0:T(8,128)S(1)} %reshape.310.row_ref, bf16[128,1024]{1,0:T(8,128)(2,1)S(1)} %mix_heads.2.refs_0_, bf16[128,1024]{1,0:T(8,128)(2,1)S(1)} %copy-done.5, bf16[128,1024]{1,0:T(8,128)(2,1)S(1)} %copy-done.2, ...), custom_call_target="tpu_custom_call" | custom-call | flops 1000000000 | bytes 1000000 | tf_op jit(solution)/shard_map/slot_rows/pallas_call | solution.py:391
  94.2 2.2 %project.6 = (bf16[2,64,768]{2,1,0:T(8,128)(2,1)S(1)}, bf16[2,64,768]{2,1,0:T(8,128)(2,1)S(1)}) custom-call(bf16[128,1024]{1,0:T(8,128)(2,1)} %collective-permute-done.11.refs_0_.refs_8_, bf16[128,1024]{1,0:T(8,128)(2,1)} %collective-permute-done.13.refs_1_.refs_10_, bf16[128,1024]{1,0:T(8,128)(2,1)} %collective-permute-done.18.refs_2_.refs_9_, ...), custom_call_target="tpu_custom_call" | custom-call | flops 1500000000 | bytes 1000000 | tf_op jit(solution)/shard_map/project/pallas_call | solution.py:411
  97.1 2.2 %project.5 = (bf16[2,64,768]{2,1,0:T(8,128)(2,1)S(1)}, bf16[2,64,768]{2,1,0:T(8,128)(2,1)S(1)}) custom-call(bf16[128,1024]{1,0:T(8,128)(2,1)} %collective-permute-done.10.refs_0_.refs_4_, bf16[128,1024]{1,0:T(8,128)(2,1)} %collective-permute-done.15.refs_1_.refs_6_, bf16[128,1024]{1,0:T(8,128)(2,1)} %collective-permute-done.16.refs_2_.refs_5_, ...), custom_call_target="tpu_custom_call" | custom-call | flops 1500000000 | bytes 1000000 | tf_op jit(solution)/shard_map/project/pallas_call | solution.py:411
  100.1 1.6 collective-permute-start.23
  101.6 0.9 slice_bitcast_fusion.5.stream_ref
  102.5 2.8 %collective-permute-done.23 = bf16[1,64,768]{2,1,0:T(8,128)(2,1)S(1)} collective-permute-done((bf16[1,64,768]{2,1,0:T(8,128)(2,1)S(1)}, bf16[1,64,768]{2,1,0:T(8,128)(2,1)S(1)}, u32[]{:S(2)}, u32[]{:S(2)}) %collective-permute-start.23) | collective-permute-done | bytes 98336 | tf_op jit(solution)/shard_map/ppermute | solution.py:428
  105.9 1.4 collective-permute-start.26
  107.3 1.0 project.4
  109.1 2.5 %collective-permute-start.24 = (bf16[64,768]{1,0:T(8,128)(2,1)S(1)}, bf16[64,768]{1,0:T(8,128)(2,1)S(1)}, u32[]{:S(2)}, u32[]{:S(2)}) collective-permute-start(bf16[64,768]{1,0:T(8,128)(2,1)S(1)} %slot_hidden.1.refs_0_), channel_id=1, source_target_pairs={{0,16},{4,20},{8,24},{12,28},{16,0},{20,4},{24,8},{28,12},{1,17},{... | collective-permute-start | bytes 294920 | tf_op jit(solution)/shard_map/ppermute | solution.py:447
  111.6 0.8 collective-permute-start.27
  112.4 3.0 %project.7 = (bf16[2,64,768]{2,1,0:T(8,128)(2,1)S(1)}, bf16[2,64,768]{2,1,0:T(8,128)(2,1)S(1)}) custom-call(bf16[128,1024]{1,0:T(8,128)(2,1)} %collective-permute-done.12.refs_12_.refs_0_, bf16[128,1024]{1,0:T(8,128)(2,1)} %collective-permute-done.14.refs_14_.refs_1_, bf16[128,1024]{1,0:T(8,128)(2,1)} %collective-permute-done.20.refs_13_.refs_2_, ...), custom_call_target="tpu_custom_call" | custom-call | flops 60000002048 | bytes 1000000 | tf_op jit(solution)/shard_map/project/pallas_call | solution.py:411
  115.4 1.0 collective-permute-start.34
  116.4 1.1 collective-permute-start.35
  117.5 1.4 collective-permute-done.24.refs_4_
  119.0 1.2 collective-permute-start.25
  120.5 0.8 collective-permute-start.36
  121.4 3.0 %collective-permute-done.25.refs_5_ = bf16[64,768]{1,0:T(8,128)(2,1)S(1)} collective-permute-done((bf16[64,768]{1,0:T(8,128)(2,1)S(1)}, bf16[64,768]{1,0:T(8,128)(2,1)S(1)}, u32[]{:S(2)}, u32[]{:S(2)}) %collective-permute-start.25) | collective-permute-done | bytes 98336 | tf_op jit(solution)/shard_map/ppermute | solution.py:260
  124.5 1.2 collective-permute-done.36.refs_7_
  125.8 8.8 %expert.1 = bf16[64,6144]{1,0:T(8,128)(2,1)} custom-call(s32[8]{0:T(128)S(1)} %iota_xor_fusion.order_ref, bf16[64,768]{1,0:T(8,128)(2,1)S(1)} %slot_hidden.1.refs_0_, bf16[64,768]{1,0:T(8,128)(2,1)S(1)} %collective-permute-done.34.refs_1_, bf16[64,768]{1,0:T(8,128)(2,1)S(1)} %collective-permute-done.26.refs_2_, ...), custom_call_target="tpu_custom_call" | custom-call | flops 10000000000 | bytes 1000000 | tf_op jit(solution)/shard_map/expert/pallas_call | solution.py:463
  134.6 4.2 %all-to-all-start.1 = ((bf16[8,8,6144]{2,1,0:T(8,128)(2,1)}), bf16[8,8,6144]{2,1,0:T(8,128)(2,1)S(1)}, u32[]{:S(2)}, u32[]{:S(2)}) async-start(bf16[8,8,6144]{2,1,0:T(8,128)(2,1)} %bitcast.27), calls=%async_computation.1 | async-start | bytes 1572864 | tf_op jit(solution)/shard_map/all_to_all | solution.py:475
  139.1 1.6 collective-permute-start.29
  140.8 8.6 %collective-permute-done.29 = bf16[1,256,768]{2,1,0:T(8,128)(2,1)S(1)} collective-permute-done((bf16[1,256,768]{2,1,0:T(8,128)(2,1)S(1)}, bf16[1,256,768]{2,1,0:T(8,128)(2,1)S(1)}, u32[]{:S(2)}, u32[]{:S(2)}) %collective-permute-start.29) | collective-permute-done | bytes 393248 | tf_op jit(solution)/shard_map/ppermute | solution.py:428
  149.6 1.8 %collective-permute-start.30 = (bf16[4,32,768]{2,1,0:T(8,128)(2,1)S(1)}, bf16[4,32,768]{2,1,0:T(8,128)(2,1)S(1)}, u32[]{:S(2)}, u32[]{:S(2)}) collective-permute-start(bf16[4,32,768]{2,1,0:T(8,128)(2,1)S(1)} %get-tuple-element.83), channel_id=1, source_target_pairs={{0,4},{4,0},{8,12},{12,8},{16,20},{20,16},{24,28},{28,24},{1,5},{5... | collective-permute-start | bytes 589832 | tf_op jit(solution)/shard_map/ppermute | solution.py:260
  151.5 5.3 %collective-permute-done.30 = bf16[4,32,768]{2,1,0:T(8,128)(2,1)S(1)} collective-permute-done((bf16[4,32,768]{2,1,0:T(8,128)(2,1)S(1)}, bf16[4,32,768]{2,1,0:T(8,128)(2,1)S(1)}, u32[]{:S(2)}, u32[]{:S(2)}) %collective-permute-start.30) | collective-permute-done | bytes 196640 | tf_op jit(solution)/shard_map/ppermute | solution.py:260
  156.8 2.1 %collective-permute-start.31 = (bf16[2,32,768]{2,1,0:T(8,128)(2,1)S(1)}, bf16[2,32,768]{2,1,0:T(8,128)(2,1)S(1)}, u32[]{:S(2)}, u32[]{:S(2)}) collective-permute-start(bf16[2,32,768]{2,1,0:T(8,128)(2,1)S(1)} %get-tuple-element.79), channel_id=1, source_target_pairs={{0,24},{4,28},{8,0},{12,4},{16,8},{20,12},{24,16},{28,20},{1,25},{... | collective-permute-start | bytes 294920 | tf_op jit(solution)/shard_map/ppermute | solution.py:264
  158.9 3.2 %collective-permute-start.32 = (bf16[2,32,768]{2,1,0:T(8,128)(2,1)S(1)}, bf16[2,32,768]{2,1,0:T(8,128)(2,1)S(1)}, u32[]{:S(2)}, u32[]{:S(2)}) collective-permute-start(bf16[2,32,768]{2,1,0:T(8,128)(2,1)S(1)} %get-tuple-element.81), channel_id=1, source_target_pairs={{0,16},{4,20},{8,24},{12,28},{16,0},{20,4},{24,8},{28,12},{1,17},{... | collective-permute-start | bytes 294920 | tf_op jit(solution)/shard_map/ppermute | solution.py:264
  162.9 2.5 %collective-permute-done.33 = bf16[2,32,768]{2,1,0:T(8,128)(2,1)S(1)} collective-permute-done((bf16[2,32,768]{2,1,0:T(8,128)(2,1)S(1)}, bf16[2,32,768]{2,1,0:T(8,128)(2,1)S(1)}, u32[]{:S(2)}, u32[]{:S(2)}) %collective-permute-start.33) | collective-permute-done | bytes 98336 | tf_op jit(solution)/shard_map/ppermute | solution.py:264
  165.4 1.8 %collective-permute-done.32 = bf16[2,32,768]{2,1,0:T(8,128)(2,1)S(1)} collective-permute-done((bf16[2,32,768]{2,1,0:T(8,128)(2,1)S(1)}, bf16[2,32,768]{2,1,0:T(8,128)(2,1)S(1)}, u32[]{:S(2)}, u32[]{:S(2)}) %collective-permute-start.32) | collective-permute-done | bytes 98336 | tf_op jit(solution)/shard_map/ppermute | solution.py:264
  168.0 1.8 %add_convert_fusion.1 = bf16[32,6144]{1,0:T(8,128)(2,1)} fusion(f32[32,6144]{1,0:T(8,128)S(1)} %bitcast.77, bf16[128,6144]{1,0:T(8,128)(2,1)} %param.14, s32[]{:T(128)S(6)} %select_n.241), kind=kLoop, calls=%fused_computation.10 | loop fusion | flops 589824 | bytes 1572868 | tf_op jit(solution)/shard_map/convert_element_type | solution.py:487
  (167 shorter events, 15.4 us)
Async XLA Ops:
  1.4 5.3 %copy-start.27 = (s32[128,2]{0,1:T(2,128)S(1)}, s32[128,2]{0,1:T(2,128)}, u32[]{:S(2)}) copy-start(s32[128,2]{0,1:T(2,128)} %param.23) | copy-start | bytes 3076
  1.4 5.5 %copy-start.26 = (bf16[128,6144]{1,0:T(8,128)(2,1)S(1)}, bf16[128,6144]{1,0:T(8,128)(2,1)}, u32[]{:S(2)}) copy-start(bf16[128,6144]{1,0:T(8,128)(2,1)} %param.14) | copy-start | bytes 4718596
  3.6 6.5 %collective-permute-start = (bf16[4,128,128]{2,1,0:T(8,128)(2,1)S(1)}, bf16[4,128,128]{2,1,0:T(8,128)(2,1)S(1)}, u32[]{:S(2)}, u32[]{:S(2)}) collective-permute-start(bf16[4,128,128]{2,1,0:T(8,128)(2,1)S(1)} %get-tuple-element.38), channel_id=1, source_target_pairs={{0,4},{4,0},{8,12},{12,8},{16,20},{20,16},{24,28},{28,24},{1,5},{5... | collective-permute-start | bytes 393224 | tf_op jit(solution)/shard_map/ppermute | solution.py:260
  7.2 26.6 %copy-start.21 = (bf16[128,2048]{1,0:T(8,128)(2,1)S(1)}, bf16[128,2048]{1,0:T(8,128)(2,1)}, u32[]{:S(2)}) copy-start(bf16[128,2048]{1,0:T(8,128)(2,1)} %q_ref.3) | copy-start | bytes 1572868
  7.2 26.6 %copy-start.22 = (bf16[128,2048]{1,0:T(8,128)(2,1)S(1)}, bf16[128,2048]{1,0:T(8,128)(2,1)}, u32[]{:S(2)}) copy-start(bf16[128,2048]{1,0:T(8,128)(2,1)} %k_ref.3) | copy-start | bytes 1572868
  7.2 26.6 %copy-start.23 = (bf16[128,2048]{1,0:T(8,128)(2,1)S(1)}, bf16[128,2048]{1,0:T(8,128)(2,1)}, u32[]{:S(2)}) copy-start(bf16[128,2048]{1,0:T(8,128)(2,1)} %v_ref.3) | copy-start | bytes 1572868
  7.2 26.6 %copy-start.24 = (bf16[128,2048]{1,0:T(8,128)(2,1)S(1)}, bf16[128,2048]{1,0:T(8,128)(2,1)}, u32[]{:S(2)}) copy-start(bf16[128,2048]{1,0:T(8,128)(2,1)} %gate_ref.3) | copy-start | bytes 1572868
  7.2 26.6 %copy-start.25 = (f32[2048]{0:T(1024)S(1)}, f32[2048]{0:T(1024)}, u32[]{:S(2)}) copy-start(f32[2048]{0:T(1024)} %param.20) | copy-start | bytes 24580
  10.3 6.2 %collective-permute-start.1 = (bf16[4,128,128]{2,1,0:T(8,128)(2,1)S(1)}, bf16[4,128,128]{2,1,0:T(8,128)(2,1)S(1)}, u32[]{:S(2)}, u32[]{:S(2)}) collective-permute-start(bf16[4,128,128]{2,1,0:T(8,128)(2,1)S(1)} %fusion.3), channel_id=1, source_target_pairs={{0,8},{4,12},{8,16},{12,20},{16,24},{20,28},{1,9},{5,13},{9,17},{1... | collective-permute-start | bytes 393224 | tf_op jit(solution)/shard_map/ppermute | solution.py:335
  14.9 7.1 %collective-permute-start.5 = (bf16[4,128,128]{2,1,0:T(8,128)(2,1)S(1)}, bf16[4,128,128]{2,1,0:T(8,128)(2,1)S(1)}, u32[]{:S(2)}, u32[]{:S(2)}) collective-permute-start(bf16[4,128,128]{2,1,0:T(8,128)(2,1)S(1)} %get-tuple-element.47), channel_id=1, source_target_pairs={{0,4},{4,0},{8,12},{12,8},{16,20},{20,16},{24,28},{28,24},{1,5},{5... | collective-permute-start | bytes 393224 | tf_op jit(solution)/shard_map/ppermute | solution.py:260
  16.6 9.1 %collective-permute-start.2 = (bf16[4,128,128]{2,1,0:T(8,128)(2,1)S(1)}, bf16[4,128,128]{2,1,0:T(8,128)(2,1)S(1)}, u32[]{:S(2)}, u32[]{:S(2)}) collective-permute-start(bf16[4,128,128]{2,1,0:T(8,128)(2,1)S(1)} %fusion.5), channel_id=1, source_target_pairs={{0,16},{4,20},{8,24},{12,28},{1,17},{5,21},{9,25},{13,29},{2,18},{... | collective-permute-start | bytes 393224 | tf_op jit(solution)/shard_map/ppermute | solution.py:335
  22.1 6.0 %collective-permute-start.6 = (bf16[4,128,128]{2,1,0:T(8,128)(2,1)S(1)}, bf16[4,128,128]{2,1,0:T(8,128)(2,1)S(1)}, u32[]{:S(2)}, u32[]{:S(2)}) collective-permute-start(bf16[4,128,128]{2,1,0:T(8,128)(2,1)S(1)} %fusion.8), channel_id=1, source_target_pairs={{0,8},{4,12},{8,16},{12,20},{16,24},{20,28},{1,9},{5,13},{9,17},{1... | collective-permute-start | bytes 393224 | tf_op jit(solution)/shard_map/ppermute | solution.py:335
  25.8 9.2 %collective-permute-start.3 = (bf16[4,128,128]{2,1,0:T(8,128)(2,1)S(1)}, bf16[4,128,128]{2,1,0:T(8,128)(2,1)S(1)}, u32[]{:S(2)}, u32[]{:S(2)}) collective-permute-start(bf16[4,128,128]{2,1,0:T(8,128)(2,1)S(1)} %get-tuple-element.76), channel_id=1, source_target_pairs={{0,4},{4,0},{8,12},{12,8},{16,20},{20,16},{24,28},{28,24},{1,5},{5... | collective-permute-start | bytes 393224 | tf_op jit(solution)/shard_map/ppermute | solution.py:260
  28.2 9.6 %collective-permute-start.7 = (bf16[4,128,128]{2,1,0:T(8,128)(2,1)S(1)}, bf16[4,128,128]{2,1,0:T(8,128)(2,1)S(1)}, u32[]{:S(2)}, u32[]{:S(2)}) collective-permute-start(bf16[4,128,128]{2,1,0:T(8,128)(2,1)S(1)} %fusion.10), channel_id=1, source_target_pairs={{0,16},{4,20},{8,24},{12,28},{1,17},{5,21},{9,25},{13,29},{2,18},{... | collective-permute-start | bytes 393224 | tf_op jit(solution)/shard_map/ppermute | solution.py:335
  36.0 8.3 %collective-permute-start.10 = (bf16[128,1024]{1,0:T(8,128)(2,1)S(1)}, bf16[128,1024]{1,0:T(8,128)(2,1)}, u32[]{:S(2)}, u32[]{:S(2)}) collective-permute-start(bf16[128,1024]{1,0:T(8,128)(2,1)S(1)} %mix_heads.2.refs_0_), channel_id=1, source_target_pairs={{0,8},{4,12},{8,16},{12,20},{16,24},{20,28},{24,0},{28,4},{1,9},{5... | collective-permute-start | bytes 786440 | tf_op jit(solution)/shard_map/ppermute | solution.py:264
  38.0 6.5 %collective-permute-start.8 = (bf16[4,128,128]{2,1,0:T(8,128)(2,1)S(1)}, bf16[4,128,128]{2,1,0:T(8,128)(2,1)S(1)}, u32[]{:S(2)}, u32[]{:S(2)}) collective-permute-start(bf16[4,128,128]{2,1,0:T(8,128)(2,1)S(1)} %get-tuple-element.74), channel_id=1, source_target_pairs={{0,4},{4,0},{8,12},{12,8},{16,20},{20,16},{24,28},{28,24},{1,5},{5... | collective-permute-start | bytes 393224 | tf_op jit(solution)/shard_map/ppermute | solution.py:260
  40.5 14.5 %collective-permute-start.4 = (bf16[128,1024]{1,0:T(8,128)(2,1)S(1)}, bf16[128,1024]{1,0:T(8,128)(2,1)S(1)}, u32[]{:S(2)}, u32[]{:S(2)}) collective-permute-start(bf16[128,1024]{1,0:T(8,128)(2,1)S(1)} %mix_heads.2.refs_0_), channel_id=1, source_target_pairs={{0,4},{4,0},{8,12},{12,8},{16,20},{20,16},{24,28},{28,24},{1,5},{5... | collective-permute-start | bytes 786440 | tf_op jit(solution)/shard_map/ppermute | solution.py:260
  44.3 10.7 %collective-permute-start.11 = (bf16[128,1024]{1,0:T(8,128)(2,1)}, bf16[128,1024]{1,0:T(8,128)(2,1)}, u32[]{:S(2)}, u32[]{:S(2)}) collective-permute-start(bf16[128,1024]{1,0:T(8,128)(2,1)} %collective-permute-done.10.refs_0_.refs_4_), channel_id=1, source_target_pairs={{0,8},{4,12},{8,16},{12,20},{16,24},{20,28},{24,0},{28,4},{1,9},{5... | collective-permute-start | bytes 786440 | tf_op jit(solution)/shard_map/ppermute | solution.py:264
  44.5 43.1 %copy-start = (bf16[2048,768]{1,0:T(8,128)(2,1)S(1)}, bf16[2048,768]{1,0:T(8,128)(2,1)}, u32[]{:S(2)}) copy-start(bf16[2048,768]{1,0:T(8,128)(2,1)} %refs_4_.3) | copy-start | bytes 9437188
  45.5 15.1 %collective-permute-start.16 = (bf16[128,1024]{1,0:T(8,128)(2,1)S(1)}, bf16[128,1024]{1,0:T(8,128)(2,1)}, u32[]{:S(2)}, u32[]{:S(2)}) collective-permute-start(bf16[128,1024]{1,0:T(8,128)(2,1)S(1)} %mix_heads.3.refs_2_.refs_1_), channel_id=1, source_target_pairs={{0,8},{4,12},{8,16},{12,20},{16,24},{20,28},{24,0},{28,4},{1,9},{5... | collective-permute-start | bytes 786440 | tf_op jit(solution)/shard_map/ppermute | solution.py:264
  47.1 13.5 %collective-permute-start.9 = (bf16[128,1024]{1,0:T(8,128)(2,1)S(1)}, bf16[128,1024]{1,0:T(8,128)(2,1)S(1)}, u32[]{:S(2)}, u32[]{:S(2)}) collective-permute-start(bf16[128,1024]{1,0:T(8,128)(2,1)S(1)} %mix_heads.3.refs_2_.refs_1_), channel_id=1, source_target_pairs={{0,4},{4,0},{8,12},{12,8},{16,20},{20,16},{24,28},{28,24},{1,5},{5... | collective-permute-start | bytes 786440 | tf_op jit(solution)/shard_map/ppermute | solution.py:260
  55.0 10.2 %collective-permute-start.12 = (bf16[128,1024]{1,0:T(8,128)(2,1)}, bf16[128,1024]{1,0:T(8,128)(2,1)}, u32[]{:S(2)}, u32[]{:S(2)}) collective-permute-start(bf16[128,1024]{1,0:T(8,128)(2,1)} %collective-permute-done.11.refs_0_.refs_8_), channel_id=1, source_target_pairs={{0,8},{4,12},{8,16},{12,20},{16,24},{20,28},{24,0},{28,4},{1,9},{5... | collective-permute-start | bytes 786440 | tf_op jit(solution)/shard_map/ppermute | solution.py:264
  55.7 13.5 %collective-permute-start.15 = (bf16[128,1024]{1,0:T(8,128)(2,1)}, bf16[128,1024]{1,0:T(8,128)(2,1)}, u32[]{:S(2)}, u32[]{:S(2)}) collective-permute-start(bf16[128,1024]{1,0:T(8,128)(2,1)} %collective-permute-done.10.refs_0_.refs_4_), channel_id=1, source_target_pairs={{0,4},{4,0},{8,12},{12,8},{16,20},{20,16},{24,28},{28,24},{1,5},{5... | collective-permute-start | bytes 786440 | tf_op jit(solution)/shard_map/ppermute | solution.py:260
  60.6 10.3 %collective-permute-start.18 = (bf16[128,1024]{1,0:T(8,128)(2,1)}, bf16[128,1024]{1,0:T(8,128)(2,1)}, u32[]{:S(2)}, u32[]{:S(2)}) collective-permute-start(bf16[128,1024]{1,0:T(8,128)(2,1)} %collective-permute-done.16.refs_2_.refs_5_), channel_id=1, source_target_pairs={{0,8},{4,12},{8,16},{12,20},{16,24},{20,28},{24,0},{28,4},{1,9},{5... | collective-permute-start | bytes 786440 | tf_op jit(solution)/shard_map/ppermute | solution.py:264
  61.3 11.4 %collective-permute-start.13 = (bf16[128,1024]{1,0:T(8,128)(2,1)}, bf16[128,1024]{1,0:T(8,128)(2,1)}, u32[]{:S(2)}, u32[]{:S(2)}) collective-permute-start(bf16[128,1024]{1,0:T(8,128)(2,1)} %collective-permute-done.11.refs_0_.refs_8_), channel_id=1, source_target_pairs={{0,4},{4,0},{8,12},{12,8},{16,20},{20,16},{24,28},{28,24},{1,5},{5... | collective-permute-start | bytes 786440 | tf_op jit(solution)/shard_map/ppermute | solution.py:260
  65.2 19.4 %all-to-all-start = ((bf16[8,16,768]{2,1,0:T(8,128)(2,1)}), bf16[8,16,768]{2,1,0:T(8,128)(2,1)}, u32[]{:S(2)}, u32[]{:S(2)}) async-start(bf16[8,16,768]{2,1,0:T(8,128)(2,1)} %pad_maximum_fusion.2), calls=%async_computation | async-start | bytes 393216 | tf_op jit(solution)/shard_map/all_to_all | solution.py:375
  70.9 10.0 %collective-permute-start.19 = (bf16[128,1024]{1,0:T(8,128)(2,1)}, bf16[128,1024]{1,0:T(8,128)(2,1)}, u32[]{:S(2)}, u32[]{:S(2)}) collective-permute-start(bf16[128,1024]{1,0:T(8,128)(2,1)} %collective-permute-done.18.refs_2_.refs_9_), channel_id=1, source_target_pairs={{0,4},{4,0},{8,12},{12,8},{16,20},{20,16},{24,28},{28,24},{1,5},{5... | collective-permute-start | bytes 786440 | tf_op jit(solution)/shard_map/ppermute | solution.py:260
  72.4 8.5 %collective-permute-start.20 = (bf16[128,1024]{1,0:T(8,128)(2,1)}, bf16[128,1024]{1,0:T(8,128)(2,1)}, u32[]{:S(2)}, u32[]{:S(2)}) collective-permute-start(bf16[128,1024]{1,0:T(8,128)(2,1)} %collective-permute-done.18.refs_2_.refs_9_), channel_id=1, source_target_pairs={{0,8},{4,12},{8,16},{12,20},{16,24},{20,28},{24,0},{28,4},{1,9},{5... | collective-permute-start | bytes 786440 | tf_op jit(solution)/shard_map/ppermute | solution.py:264
  72.7 11.4 %collective-permute-start.14 = (bf16[128,1024]{1,0:T(8,128)(2,1)}, bf16[128,1024]{1,0:T(8,128)(2,1)}, u32[]{:S(2)}, u32[]{:S(2)}) collective-permute-start(bf16[128,1024]{1,0:T(8,128)(2,1)} %collective-permute-done.12.refs_12_.refs_0_), channel_id=1, source_target_pairs={{0,4},{4,0},{8,12},{12,8},{16,20},{20,16},{24,28},{28,24},{1,5},{5... | collective-permute-start | bytes 786440 | tf_op jit(solution)/shard_map/ppermute | solution.py:260
  73.3 14.3 %collective-permute-start.17 = (bf16[128,1024]{1,0:T(8,128)(2,1)}, bf16[128,1024]{1,0:T(8,128)(2,1)}, u32[]{:S(2)}, u32[]{:S(2)}) collective-permute-start(bf16[128,1024]{1,0:T(8,128)(2,1)} %copy-done.7), channel_id=1, source_target_pairs={{0,8},{4,12},{8,16},{12,20},{16,24},{20,28},{24,0},{28,4},{1,9},{5... | collective-permute-start | bytes 786440 | tf_op jit(solution)/shard_map/ppermute | solution.py:264
  80.9 6.8 %collective-permute-start.21 = (bf16[128,1024]{1,0:T(8,128)(2,1)}, bf16[128,1024]{1,0:T(8,128)(2,1)}, u32[]{:S(2)}, u32[]{:S(2)}) collective-permute-start(bf16[128,1024]{1,0:T(8,128)(2,1)} %collective-permute-done.20.refs_13_.refs_2_), channel_id=1, source_target_pairs={{0,4},{4,0},{8,12},{12,8},{16,20},{20,16},{24,28},{28,24},{1,5},{5... | collective-permute-start | bytes 786440 | tf_op jit(solution)/shard_map/ppermute | solution.py:260
  94.1 5.9 %collective-permute-start.22 = (bf16[2,64,768]{2,1,0:T(8,128)(2,1)S(1)}, bf16[2,64,768]{2,1,0:T(8,128)(2,1)S(1)}, u32[]{:S(2)}, u32[]{:S(2)}) collective-permute-start(bf16[2,64,768]{2,1,0:T(8,128)(2,1)S(1)} %get-tuple-element.70), channel_id=1, source_target_pairs={{0,1},{1,0},{2,3},{3,2},{4,5},{5,4},{6,7},{7,6},{8,9},{9,8},{10,11... | collective-permute-start | bytes 589832 | tf_op jit(solution)/shard_map/ppermute | solution.py:422
  100.1 5.3 %collective-permute-start.23 = (bf16[1,64,768]{2,1,0:T(8,128)(2,1)S(1)}, bf16[1,64,768]{2,1,0:T(8,128)(2,1)S(1)}, u32[]{:S(2)}, u32[]{:S(2)}) collective-permute-start(bf16[1,64,768]{2,1,0:T(8,128)(2,1)S(1)} %get-tuple-element.84), channel_id=1, source_target_pairs={{0,2},{1,3},{2,0},{3,1},{4,6},{5,7},{6,4},{7,5},{8,10},{9,11},{10,... | collective-permute-start | bytes 294920 | tf_op jit(solution)/shard_map/ppermute | solution.py:428
  105.9 5.7 %collective-permute-start.26 = (bf16[64,768]{1,0:T(8,128)(2,1)S(1)}, bf16[64,768]{1,0:T(8,128)(2,1)S(1)}, u32[]{:S(2)}, u32[]{:S(2)}) collective-permute-start(bf16[64,768]{1,0:T(8,128)(2,1)S(1)} %slot_hidden.1.refs_0_), channel_id=1, source_target_pairs={{0,8},{4,12},{8,0},{12,4},{16,24},{20,28},{24,16},{28,20},{1,9},{5... | collective-permute-start | bytes 294920 | tf_op jit(solution)/shard_map/ppermute | solution.py:447
  107.3 18.4 %slice-start = ((s8[14155776]{0:T(1024)(128)(4,1)}), s8[4194304]{0:T(1024)(128)(4,1)S(1)}, s32[]{:S(2)}) async-start(s8[14155776]{0:T(1024)(128)(4,1)} %bitcast.67), calls=%async_computation.2 | async-start | bytes 8388608
  107.3 18.4 %slice-start.4 = ((s8[14155776]{0:T(1024)(128)(4,1)}), s8[4194304]{0:T(1024)(128)(4,1)S(1)}, s32[]{:S(2)}) async-start(s8[14155776]{0:T(1024)(128)(4,1)} %bitcast.69), calls=%async_computation.6 | async-start | bytes 8388608
  107.3 18.4 %slice-start.8 = ((s8[14155776]{0:T(1024)(128)(4,1)}), s8[4194304]{0:T(1024)(128)(4,1)S(1)}, s32[]{:S(2)}) async-start(s8[14155776]{0:T(1024)(128)(4,1)} %bitcast.71), calls=%async_computation.10 | async-start | bytes 8388608
  109.0 16.7 %slice-start.1 = ((s8[14155776]{0:T(1024)(128)(4,1)}), s8[4194304]{0:T(1024)(128)(4,1)S(1)}, s32[]{:S(2)}) async-start(s8[14155776]{0:T(1024)(128)(4,1)} %bitcast.67), calls=%async_computation.3 | async-start | bytes 8388608
  109.0 16.7 %slice-start.2 = ((s8[14155776]{0:T(1024)(128)(4,1)}), s8[4194304]{0:T(1024)(128)(4,1)S(1)}, s32[]{:S(2)}) async-start(s8[14155776]{0:T(1024)(128)(4,1)} %bitcast.67), calls=%async_computation.4 | async-start | bytes 8388608
  109.0 16.7 %slice-start.3 = ((s8[14155776]{0:T(1024)(128)(4,1)}), s8[1572864]{0:T(1024)(128)(4,1)S(1)}, s32[]{:S(2)}) async-start(s8[14155776]{0:T(1024)(128)(4,1)} %bitcast.67), calls=%async_computation.5 | async-start | bytes 3145728
  109.0 16.7 %slice-start.5 = ((s8[14155776]{0:T(1024)(128)(4,1)}), s8[4194304]{0:T(1024)(128)(4,1)S(1)}, s32[]{:S(2)}) async-start(s8[14155776]{0:T(1024)(128)(4,1)} %bitcast.69), calls=%async_computation.7 | async-start | bytes 8388608
  109.0 16.7 %slice-start.6 = ((s8[14155776]{0:T(1024)(128)(4,1)}), s8[4194304]{0:T(1024)(128)(4,1)S(1)}, s32[]{:S(2)}) async-start(s8[14155776]{0:T(1024)(128)(4,1)} %bitcast.69), calls=%async_computation.8 | async-start | bytes 8388608
  109.1 16.7 %slice-start.7 = ((s8[14155776]{0:T(1024)(128)(4,1)}), s8[1572864]{0:T(1024)(128)(4,1)S(1)}, s32[]{:S(2)}) async-start(s8[14155776]{0:T(1024)(128)(4,1)} %bitcast.69), calls=%async_computation.9 | async-start | bytes 3145728
  109.1 16.7 %slice-start.9 = ((s8[14155776]{0:T(1024)(128)(4,1)}), s8[4194304]{0:T(1024)(128)(4,1)S(1)}, s32[]{:S(2)}) async-start(s8[14155776]{0:T(1024)(128)(4,1)} %bitcast.71), calls=%async_computation.11 | async-start | bytes 8388608
  109.1 16.7 %slice-start.10 = ((s8[14155776]{0:T(1024)(128)(4,1)}), s8[4194304]{0:T(1024)(128)(4,1)S(1)}, s32[]{:S(2)}) async-start(s8[14155776]{0:T(1024)(128)(4,1)} %bitcast.71), calls=%async_computation.12 | async-start | bytes 8388608
  109.1 16.7 %slice-start.11 = ((s8[14155776]{0:T(1024)(128)(4,1)}), s8[1572864]{0:T(1024)(128)(4,1)S(1)}, s32[]{:S(2)}) async-start(s8[14155776]{0:T(1024)(128)(4,1)} %bitcast.71), calls=%async_computation.13 | async-start | bytes 3145728
  109.1 9.9 %collective-permute-start.24 = (bf16[64,768]{1,0:T(8,128)(2,1)S(1)}, bf16[64,768]{1,0:T(8,128)(2,1)S(1)}, u32[]{:S(2)}, u32[]{:S(2)}) collective-permute-start(bf16[64,768]{1,0:T(8,128)(2,1)S(1)} %slot_hidden.1.refs_0_), channel_id=1, source_target_pairs={{0,16},{4,20},{8,24},{12,28},{16,0},{20,4},{24,8},{28,12},{1,17},{... | collective-permute-start | bytes 294920 | tf_op jit(solution)/shard_map/ppermute | solution.py:447
  111.6 8.9 %collective-permute-start.27 = (bf16[64,768]{1,0:T(8,128)(2,1)S(1)}, bf16[64,768]{1,0:T(8,128)(2,1)S(1)}, u32[]{:S(2)}, u32[]{:S(2)}) collective-permute-start(bf16[64,768]{1,0:T(8,128)(2,1)S(1)} %collective-permute-done.26.refs_2_), channel_id=1, source_target_pairs={{0,16},{4,20},{8,24},{12,28},{16,0},{20,4},{24,8},{28,12},{1,17},{... | collective-permute-start | bytes 294920 | tf_op jit(solution)/shard_map/ppermute | solution.py:447
  115.4 19.2 %copy-start.16 = (bf16[2,64,768]{2,1,0:T(8,128)(2,1)}, bf16[2,64,768]{2,1,0:T(8,128)(2,1)S(1)}, u32[]{:S(2)}) copy-start(bf16[2,64,768]{2,1,0:T(8,128)(2,1)S(1)} %get-tuple-element.65) | copy-start | bytes 589828
  115.4 10.4 %copy-start.18 = (f32[6144]{0:T(1024)S(1)}, f32[6144]{0:T(1024)}, u32[]{:S(2)}) copy-start(f32[6144]{0:T(1024)} %param.22) | copy-start | bytes 73732
  115.4 9.0 %collective-permute-start.34 = (bf16[64,768]{1,0:T(8,128)(2,1)S(1)}, bf16[64,768]{1,0:T(8,128)(2,1)S(1)}, u32[]{:S(2)}, u32[]{:S(2)}) collective-permute-start(bf16[64,768]{1,0:T(8,128)(2,1)S(1)} %slot_hidden.1.refs_0_), channel_id=1, source_target_pairs={{0,4},{4,0},{8,12},{12,8},{16,20},{20,16},{24,28},{28,24},{1,5},{5... | collective-permute-start | bytes 294920 | tf_op jit(solution)/shard_map/ppermute | solution.py:260
  116.4 8.0 %collective-permute-start.35 = (bf16[64,768]{1,0:T(8,128)(2,1)S(1)}, bf16[64,768]{1,0:T(8,128)(2,1)S(1)}, u32[]{:S(2)}, u32[]{:S(2)}) collective-permute-start(bf16[64,768]{1,0:T(8,128)(2,1)S(1)} %collective-permute-done.26.refs_2_), channel_id=1, source_target_pairs={{0,4},{4,0},{8,12},{12,8},{16,20},{20,16},{24,28},{28,24},{1,5},{5... | collective-permute-start | bytes 294920 | tf_op jit(solution)/shard_map/ppermute | solution.py:260
  119.0 5.5 %collective-permute-start.25 = (bf16[64,768]{1,0:T(8,128)(2,1)S(1)}, bf16[64,768]{1,0:T(8,128)(2,1)S(1)}, u32[]{:S(2)}, u32[]{:S(2)}) collective-permute-start(bf16[64,768]{1,0:T(8,128)(2,1)S(1)} %collective-permute-done.24.refs_4_), channel_id=1, source_target_pairs={{0,4},{4,0},{8,12},{12,8},{16,20},{20,16},{24,28},{28,24},{1,5},{5... | collective-permute-start | bytes 294920 | tf_op jit(solution)/shard_map/ppermute | solution.py:260
  120.5 5.2 %collective-permute-start.36 = (bf16[64,768]{1,0:T(8,128)(2,1)S(1)}, bf16[64,768]{1,0:T(8,128)(2,1)S(1)}, u32[]{:S(2)}, u32[]{:S(2)}) collective-permute-start(bf16[64,768]{1,0:T(8,128)(2,1)S(1)} %collective-permute-done.27.refs_6_), channel_id=1, source_target_pairs={{0,4},{4,0},{8,12},{12,8},{16,20},{20,16},{24,28},{28,24},{1,5},{5... | collective-permute-start | bytes 294920 | tf_op jit(solution)/shard_map/ppermute | solution.py:260
  124.5 14.3 %collective-permute-start.28 = (bf16[2,256,768]{2,1,0:T(8,128)(2,1)S(1)}, bf16[2,256,768]{2,1,0:T(8,128)(2,1)S(1)}, u32[]{:S(2)}, u32[]{:S(2)}) collective-permute-start(bf16[2,256,768]{2,1,0:T(8,128)(2,1)S(1)} %pad_maximum_fusion), channel_id=1, source_target_pairs={{0,1},{1,0},{2,3},{3,2},{4,5},{5,4},{6,7},{7,6},{8,9},{9,8},{10,11... | collective-permute-start | bytes 2359304 | tf_op jit(solution)/shard_map/ppermute | solution.py:422
  134.6 4.2 %copy-start.13 = (bf16[2,64,768]{2,1,0:T(8,128)(2,1)S(1)}, bf16[2,64,768]{2,1,0:T(8,128)(2,1)}, u32[]{:S(2)}) copy-start(bf16[2,64,768]{2,1,0:T(8,128)(2,1)} %copy-done.12) | copy-start | bytes 589828
  134.6 4.2 %copy-start.15 = (bf16[2,64,768]{2,1,0:T(8,128)(2,1)S(1)}, bf16[2,64,768]{2,1,0:T(8,128)(2,1)}, u32[]{:S(2)}) copy-start(bf16[2,64,768]{2,1,0:T(8,128)(2,1)} %copy-done.14) | copy-start | bytes 589828
  134.6 4.2 %copy-start.17 = (bf16[2,64,768]{2,1,0:T(8,128)(2,1)S(1)}, bf16[2,64,768]{2,1,0:T(8,128)(2,1)}, u32[]{:S(2)}) copy-start(bf16[2,64,768]{2,1,0:T(8,128)(2,1)} %copy-done.16) | copy-start | bytes 589828
  134.6 27.4 %all-to-all-start.1 = ((bf16[8,8,6144]{2,1,0:T(8,128)(2,1)}), bf16[8,8,6144]{2,1,0:T(8,128)(2,1)S(1)}, u32[]{:S(2)}, u32[]{:S(2)}) async-start(bf16[8,8,6144]{2,1,0:T(8,128)(2,1)} %bitcast.27), calls=%async_computation.1 | async-start | bytes 1572864 | tf_op jit(solution)/shard_map/all_to_all | solution.py:475
  139.1 10.3 %collective-permute-start.29 = (bf16[1,256,768]{2,1,0:T(8,128)(2,1)S(1)}, bf16[1,256,768]{2,1,0:T(8,128)(2,1)S(1)}, u32[]{:S(2)}, u32[]{:S(2)}) collective-permute-start(bf16[1,256,768]{2,1,0:T(8,128)(2,1)S(1)} %get-tuple-element.73), channel_id=1, source_target_pairs={{0,2},{1,3},{2,0},{3,1},{4,6},{5,7},{6,4},{7,5},{8,10},{9,11},{10,... | collective-permute-start | bytes 1179656 | tf_op jit(solution)/shard_map/ppermute | solution.py:428
  149.6 7.2 %collective-permute-start.30 = (bf16[4,32,768]{2,1,0:T(8,128)(2,1)S(1)}, bf16[4,32,768]{2,1,0:T(8,128)(2,1)S(1)}, u32[]{:S(2)}, u32[]{:S(2)}) collective-permute-start(bf16[4,32,768]{2,1,0:T(8,128)(2,1)S(1)} %get-tuple-element.83), channel_id=1, source_target_pairs={{0,4},{4,0},{8,12},{12,8},{16,20},{20,16},{24,28},{28,24},{1,5},{5... | collective-permute-start | bytes 589832 | tf_op jit(solution)/shard_map/ppermute | solution.py:260
  156.8 6.2 %collective-permute-start.31 = (bf16[2,32,768]{2,1,0:T(8,128)(2,1)S(1)}, bf16[2,32,768]{2,1,0:T(8,128)(2,1)S(1)}, u32[]{:S(2)}, u32[]{:S(2)}) collective-permute-start(bf16[2,32,768]{2,1,0:T(8,128)(2,1)S(1)} %get-tuple-element.79), channel_id=1, source_target_pairs={{0,24},{4,28},{8,0},{12,4},{16,8},{20,12},{24,16},{28,20},{1,25},{... | collective-permute-start | bytes 294920 | tf_op jit(solution)/shard_map/ppermute | solution.py:264
  158.9 6.5 %collective-permute-start.33 = (bf16[2,32,768]{2,1,0:T(8,128)(2,1)S(1)}, bf16[2,32,768]{2,1,0:T(8,128)(2,1)S(1)}, u32[]{:S(2)}, u32[]{:S(2)}) collective-permute-start(bf16[2,32,768]{2,1,0:T(8,128)(2,1)S(1)} %get-tuple-element.80), channel_id=1, source_target_pairs={{0,8},{4,12},{8,16},{12,20},{16,24},{20,28},{24,0},{28,4},{1,9},{5... | collective-permute-start | bytes 294920 | tf_op jit(solution)/shard_map/ppermute | solution.py:264
  158.9 8.3 %collective-permute-start.32 = (bf16[2,32,768]{2,1,0:T(8,128)(2,1)S(1)}, bf16[2,32,768]{2,1,0:T(8,128)(2,1)S(1)}, u32[]{:S(2)}, u32[]{:S(2)}) collective-permute-start(bf16[2,32,768]{2,1,0:T(8,128)(2,1)S(1)} %get-tuple-element.81), channel_id=1, source_target_pairs={{0,16},{4,20},{8,24},{12,28},{16,0},{20,4},{24,8},{28,12},{1,17},{... | collective-permute-start | bytes 294920 | tf_op jit(solution)/shard_map/ppermute | solution.py:264
  (16 other events, 23.3 us)

commit v6 on v5

--- a/solution.py
+++ b/solution.py
@@ -160,15 +160,20 @@
 
 def select_kernel(n_exp, cap, chunks, row_ref, *refs):
     blocks, (weight_ref, keep_ref, send_ref) = refs[:-3], refs[-3:]
-    steps, slots = row_ref.shape[:2]
+    steps, _, slots = row_ref.shape
     tok, wide = blocks[0].shape
     picked = [[] for _ in range(chunks)]
     for step in range(steps):
-        pick = row_ref[step] == lax.broadcasted_iota(jnp.int32, (slots, 2 * tok), 1)
+        pick = row_ref[step] == lax.broadcasted_iota(jnp.int32, (2 * tok, slots), 0)
         pick = pick.astype(F32).astype(BF16)
         for chunk in range(chunks):
             rows = [blocks[(step * 2 + y) * chunks + chunk][...] for y in range(2)]
-            rows = jnp.dot(pick, jnp.concatenate(rows, axis=0), preferred_element_type=F32)
+            rows = lax.dot_general(
+                pick,
+                jnp.concatenate(rows, axis=0),
+                (((0,), (0,)), ((), ())),
+                preferred_element_type=F32,
+            )
             picked[chunk].append(rows.astype(BF16))
     total = None
     for chunk in range(chunks):
@@ -385,7 +390,7 @@
         [lax.dynamic_index_in_dim(row, own ^ j, 1, keepdims=False) for j in range(n_exp)], axis=1
     )
     row = jnp.take(row, order, axis=0).reshape(groups, 2, n_exp, cap)
-    row = row.transpose(0, 2, 1, 3).reshape(groups, n_exp * 2 * cap, 1)
+    row = row.transpose(0, 2, 1, 3).reshape(groups, 1, n_exp * 2 * cap)
 
     slots = jax.ShapeDtypeStruct((n_exp // 2, n_ctx * cap, cols), BF16)
     slot_parts = pl.pallas_call(

time: 171 us -> 170 us (level)
  transfers between devices with their start and end apart: 39 -> 39, of which waited for: 21 -> 22; matrix products, arithmetic and copies ran while one was open for 4% -> 4% of each run, Pallas kernels for 13% -> 13%
where the time goes in v6:
time: 170 us
  starting transfers between devices  67 us (39%)
  waiting for transfers between devices  56.3 us (33%)
  Pallas kernels  27.9 us (16%)
  local copies, waits for them, and re-layouts  10.3 us (6%)
  other arithmetic  6.14 us (4%)
    ppermute x10, waiting for transfers between devices, shifted(): return lax.ppermute(value, 'ctx', to)  26.6 us
    ppermute x16, starting transfers between devices, swapped(): return lax.ppermute(value, 'ctx', swap)  21.9 us
    ppermute x4, starting transfers between devices, per_device(): far = lax.ppermute(window, 'ctx', line).astype(F32)  18.1 us
    ppermute x16, waiting for transfers between devices, swapped(): return lax.ppermute(value, 'ctx', swap)  15.4 us
    ppermute x2, waiting for transfers between devices, add_groups(): lax.ppermute(total[:, 1], 'exp', [(i, i ^ bit) for i in range(n_exp)])  11.4 us
    ppermute x10, starting transfers between devices, shifted(): return lax.ppermute(value, 'ctx', to)  11 us
    pallas_call x1, Pallas kernels, per_device(): pl.pallas_call(functools.partial(ffn_kernel, len(pieces), blocks), out_sh...  8.8 us
    pallas_call x4, Pallas kernels, per_device(): pl.pallas_call(functools.partial(project_kernel, n_exp), out_shape=[rows,...  8.43 us
  transfers between devices with their start and end apart: 39, of which 22 were waited for; matrix products, arithmetic and copies ran while one was open for 4% of the time, Pallas kernels for 13%

profile of v6, /device:TPU:0, one launch (start us, length us, event | category | flops | bytes accessed | tf_op | source)
XLA Modules:
  0.0 169.6 jit_solution(10972633551796498506)
XLA Ops:
  1.4 2.2 %shard_state.1 = (bf16[4,128,128]{2,1,0:T(8,128)(2,1)S(1)}, bf16[4,128,128]{2,1,0:T(8,128)(2,1)S(1)}, bf16[4,128,128]{2,1,0:T(8,128)(2,1)S(1)}, bf16[4,128,128]{2,1,0:T(8,128)(2,1)S(1)}) custom-call(s32[2]{0:T(128)S(1)} %pad_add_fusion.1.place_ref, f32[16]{0:T(128)S(1)} %copy-done.19, bf16[128,2048]{1,0:T(8,128)(2,1)} %k_ref.3, bf16[128,2048]{1,0:T(8,128)(2,1)} %v_ref.3), custom_call_target="tpu_custom_call" | custom-call | flops 1000000000 | bytes 1000000 | tf_op jit(solution)/shard_map/shard_state/pallas_call | solution.py:274
  3.6 3.0 %collective-permute-start = (bf16[4,128,128]{2,1,0:T(8,128)(2,1)S(1)}, bf16[4,128,128]{2,1,0:T(8,128)(2,1)S(1)}, u32[]{:S(2)}, u32[]{:S(2)}) collective-permute-start(bf16[4,128,128]{2,1,0:T(8,128)(2,1)S(1)} %get-tuple-element.38), channel_id=1, source_target_pairs={{0,4},{4,0},{8,12},{12,8},{16,20},{20,16},{24,28},{28,24},{1,5},{5... | collective-permute-start | bytes 393224 | tf_op jit(solution)/shard_map/ppermute | solution.py:265
  7.3 2.8 %collective-permute-done = bf16[4,128,128]{2,1,0:T(8,128)(2,1)S(1)} collective-permute-done((bf16[4,128,128]{2,1,0:T(8,128)(2,1)S(1)}, bf16[4,128,128]{2,1,0:T(8,128)(2,1)S(1)}, u32[]{:S(2)}, u32[]{:S(2)}) %collective-permute-start) | collective-permute-done | bytes 131104 | tf_op jit(solution)/shard_map/ppermute | solution.py:265
  10.3 3.7 %collective-permute-start.1 = (bf16[4,128,128]{2,1,0:T(8,128)(2,1)S(1)}, bf16[4,128,128]{2,1,0:T(8,128)(2,1)S(1)}, u32[]{:S(2)}, u32[]{:S(2)}) collective-permute-start(bf16[4,128,128]{2,1,0:T(8,128)(2,1)S(1)} %fusion.3), channel_id=1, source_target_pairs={{0,8},{4,12},{8,16},{12,20},{16,24},{20,28},{1,9},{5,13},{9,17},{1... | collective-permute-start | bytes 393224 | tf_op jit(solution)/shard_map/ppermute | solution.py:340
  14.9 1.5 collective-permute-start.5
  16.6 5.4 %collective-permute-start.2 = (bf16[4,128,128]{2,1,0:T(8,128)(2,1)S(1)}, bf16[4,128,128]{2,1,0:T(8,128)(2,1)S(1)}, u32[]{:S(2)}, u32[]{:S(2)}) collective-permute-start(bf16[4,128,128]{2,1,0:T(8,128)(2,1)S(1)} %fusion.5), channel_id=1, source_target_pairs={{0,16},{4,20},{8,24},{12,28},{1,17},{5,21},{9,25},{13,29},{2,18},{... | collective-permute-start | bytes 393224 | tf_op jit(solution)/shard_map/ppermute | solution.py:340
  22.1 3.5 %collective-permute-start.6 = (bf16[4,128,128]{2,1,0:T(8,128)(2,1)S(1)}, bf16[4,128,128]{2,1,0:T(8,128)(2,1)S(1)}, u32[]{:S(2)}, u32[]{:S(2)}) collective-permute-start(bf16[4,128,128]{2,1,0:T(8,128)(2,1)S(1)} %fusion.8), channel_id=1, source_target_pairs={{0,8},{4,12},{8,16},{12,20},{16,24},{20,28},{1,9},{5,13},{9,17},{1... | collective-permute-start | bytes 393224 | tf_op jit(solution)/shard_map/ppermute | solution.py:340
  25.8 1.6 collective-permute-start.3
  28.2 5.6 %collective-permute-start.7 = (bf16[4,128,128]{2,1,0:T(8,128)(2,1)S(1)}, bf16[4,128,128]{2,1,0:T(8,128)(2,1)S(1)}, u32[]{:S(2)}, u32[]{:S(2)}) collective-permute-start(bf16[4,128,128]{2,1,0:T(8,128)(2,1)S(1)} %fusion.10), channel_id=1, source_target_pairs={{0,16},{4,20},{8,24},{12,28},{1,17},{5,21},{9,25},{13,29},{2,18},{... | collective-permute-start | bytes 393224 | tf_op jit(solution)/shard_map/ppermute | solution.py:340
  33.8 1.2 near_part.2
  35.0 1.0 mix_heads.2.refs_0_
  36.0 1.9 %collective-permute-start.10 = (bf16[128,1024]{1,0:T(8,128)(2,1)S(1)}, bf16[128,1024]{1,0:T(8,128)(2,1)}, u32[]{:S(2)}, u32[]{:S(2)}) collective-permute-start(bf16[128,1024]{1,0:T(8,128)(2,1)S(1)} %mix_heads.2.refs_0_), channel_id=1, source_target_pairs={{0,8},{4,12},{8,16},{12,20},{16,24},{20,28},{24,0},{28,4},{1,9},{5... | collective-permute-start | bytes 786440 | tf_op jit(solution)/shard_map/ppermute | solution.py:269
  38.0 1.3 collective-permute-start.8
  39.3 1.2 near_part.3
  40.5 0.8 collective-permute-start.4
  41.4 3.0 %collective-permute-done.10.refs_0_.refs_4_ = bf16[128,1024]{1,0:T(8,128)(2,1)} collective-permute-done((bf16[128,1024]{1,0:T(8,128)(2,1)S(1)}, bf16[128,1024]{1,0:T(8,128)(2,1)}, u32[]{:S(2)}, u32[]{:S(2)}) %collective-permute-start.10) | collective-permute-done | bytes 262176 | tf_op jit(solution)/shard_map/ppermute | solution.py:269
  44.6 1.0 mix_heads.3.refs_2_.refs_1_
  45.5 1.6 collective-permute-start.16
  47.1 1.1 collective-permute-start.9
  48.9 6.1 %collective-permute-done.11.refs_0_.refs_8_ = bf16[128,1024]{1,0:T(8,128)(2,1)} collective-permute-done((bf16[128,1024]{1,0:T(8,128)(2,1)}, bf16[128,1024]{1,0:T(8,128)(2,1)}, u32[]{:S(2)}, u32[]{:S(2)}) %collective-permute-start.11) | collective-permute-done | bytes 262176 | tf_op jit(solution)/shard_map/ppermute | solution.py:269
  55.7 1.5 collective-permute-start.15
  57.2 3.4 %collective-permute-done.16.refs_2_.refs_5_ = bf16[128,1024]{1,0:T(8,128)(2,1)} collective-permute-done((bf16[128,1024]{1,0:T(8,128)(2,1)S(1)}, bf16[128,1024]{1,0:T(8,128)(2,1)}, u32[]{:S(2)}, u32[]{:S(2)}) %collective-permute-start.16) | collective-permute-done | bytes 262176 | tf_op jit(solution)/shard_map/ppermute | solution.py:269
  61.3 1.5 collective-permute-start.13
  62.8 2.4 %collective-permute-done.12.refs_12_.refs_0_ = bf16[128,1024]{1,0:T(8,128)(2,1)} collective-permute-done((bf16[128,1024]{1,0:T(8,128)(2,1)}, bf16[128,1024]{1,0:T(8,128)(2,1)}, u32[]{:S(2)}, u32[]{:S(2)}) %collective-permute-start.12) | collective-permute-done | bytes 262176 | tf_op jit(solution)/shard_map/ppermute | solution.py:269
  65.2 4.0 %all-to-all-start = ((bf16[8,16,768]{2,1,0:T(8,128)(2,1)}), bf16[8,16,768]{2,1,0:T(8,128)(2,1)}, u32[]{:S(2)}, u32[]{:S(2)}) async-start(bf16[8,16,768]{2,1,0:T(8,128)(2,1)} %pad_maximum_fusion.2), calls=%async_computation | async-start | bytes 393216 | tf_op jit(solution)/shard_map/all_to_all | solution.py:380
  69.3 1.6 collective-permute-done.18.refs_2_.refs_9_
  70.9 1.5 collective-permute-start.19
  73.3 1.7 %collective-permute-start.17 = (bf16[128,1024]{1,0:T(8,128)(2,1)}, bf16[128,1024]{1,0:T(8,128)(2,1)}, u32[]{:S(2)}, u32[]{:S(2)}) collective-permute-start(bf16[128,1024]{1,0:T(8,128)(2,1)} %copy-done.7), channel_id=1, source_target_pairs={{0,8},{4,12},{8,16},{12,20},{16,24},{20,28},{24,0},{28,4},{1,9},{5... | collective-permute-start | bytes 786440 | tf_op jit(solution)/shard_map/ppermute | solution.py:269
  75.0 5.9 %collective-permute-done.20.refs_13_.refs_2_ = bf16[128,1024]{1,0:T(8,128)(2,1)} collective-permute-done((bf16[128,1024]{1,0:T(8,128)(2,1)}, bf16[128,1024]{1,0:T(8,128)(2,1)}, u32[]{:S(2)}, u32[]{:S(2)}) %collective-permute-start.20) | collective-permute-done | bytes 262176 | tf_op jit(solution)/shard_map/ppermute | solution.py:269
  80.9 1.3 collective-permute-start.21
  82.2 1.9 %collective-permute-done.14.refs_14_.refs_1_ = bf16[128,1024]{1,0:T(8,128)(2,1)} collective-permute-done((bf16[128,1024]{1,0:T(8,128)(2,1)}, bf16[128,1024]{1,0:T(8,128)(2,1)}, u32[]{:S(2)}, u32[]{:S(2)}) %collective-permute-start.14) | collective-permute-done | bytes 262176 | tf_op jit(solution)/shard_map/ppermute | solution.py:265
  86.3 1.3 collective-permute-done.21.refs_15_.refs_3_
  87.6 0.9 copy-done.2
  88.5 0.9 copy-done.5
  89.5 0.9 copy-done.8
  90.4 3.6 %slot_rows.1 = (bf16[2,64,768]{2,1,0:T(8,128)(2,1)S(1)}, bf16[2,64,768]{2,1,0:T(8,128)(2,1)S(1)}) custom-call(s32[4,1,64]{2,1,0:T(1,128)S(1)} %reshape.286.row_ref, bf16[128,1024]{1,0:T(8,128)(2,1)S(1)} %mix_heads.2.refs_0_, bf16[128,1024]{1,0:T(8,128)(2,1)S(1)} %copy-done.5, bf16[128,1024]{1,0:T(8,128)(2,1)S(1)} %copy-done.2, ...), custom_call_target="tpu_custom_call" | custom-call | flops 1000000000 | bytes 1000000 | tf_op jit(solution)/shard_map/slot_rows/pallas_call | solution.py:396
  94.1 2.2 %project.6 = (bf16[2,64,768]{2,1,0:T(8,128)(2,1)S(1)}, bf16[2,64,768]{2,1,0:T(8,128)(2,1)S(1)}) custom-call(bf16[128,1024]{1,0:T(8,128)(2,1)} %collective-permute-done.11.refs_0_.refs_8_, bf16[128,1024]{1,0:T(8,128)(2,1)} %collective-permute-done.13.refs_1_.refs_10_, bf16[128,1024]{1,0:T(8,128)(2,1)} %collective-permute-done.18.refs_2_.refs_9_, ...), custom_call_target="tpu_custom_call" | custom-call | flops 1500000000 | bytes 1000000 | tf_op jit(solution)/shard_map/project/pallas_call | solution.py:416
  97.0 2.2 %project.5 = (bf16[2,64,768]{2,1,0:T(8,128)(2,1)S(1)}, bf16[2,64,768]{2,1,0:T(8,128)(2,1)S(1)}) custom-call(bf16[128,1024]{1,0:T(8,128)(2,1)} %collective-permute-done.10.refs_0_.refs_4_, bf16[128,1024]{1,0:T(8,128)(2,1)} %collective-permute-done.15.refs_1_.refs_6_, bf16[128,1024]{1,0:T(8,128)(2,1)} %collective-permute-done.16.refs_2_.refs_5_, ...), custom_call_target="tpu_custom_call" | custom-call | flops 1500000000 | bytes 1000000 | tf_op jit(solution)/shard_map/project/pallas_call | solution.py:416
  100.0 1.6 collective-permute-start.23
  101.6 0.9 slice_bitcast_fusion.5.stream_ref
  102.5 2.8 %collective-permute-done.23 = bf16[1,64,768]{2,1,0:T(8,128)(2,1)S(1)} collective-permute-done((bf16[1,64,768]{2,1,0:T(8,128)(2,1)S(1)}, bf16[1,64,768]{2,1,0:T(8,128)(2,1)S(1)}, u32[]{:S(2)}, u32[]{:S(2)}) %collective-permute-start.23) | collective-permute-done | bytes 98336 | tf_op jit(solution)/shard_map/ppermute | solution.py:433
  105.8 1.0 collective-permute-start.26
  106.9 1.0 project.4
  108.6 2.6 %collective-permute-start.24 = (bf16[64,768]{1,0:T(8,128)(2,1)S(1)}, bf16[64,768]{1,0:T(8,128)(2,1)S(1)}, u32[]{:S(2)}, u32[]{:S(2)}) collective-permute-start(bf16[64,768]{1,0:T(8,128)(2,1)S(1)} %slot_hidden.1.refs_0_), channel_id=1, source_target_pairs={{0,16},{4,20},{8,24},{12,28},{16,0},{20,4},{24,8},{28,12},{1,17},{... | collective-permute-start | bytes 294920 | tf_op jit(solution)/shard_map/ppermute | solution.py:452
  111.3 0.8 collective-permute-start.27
  112.1 3.0 %project.7 = (bf16[2,64,768]{2,1,0:T(8,128)(2,1)S(1)}, bf16[2,64,768]{2,1,0:T(8,128)(2,1)S(1)}) custom-call(bf16[128,1024]{1,0:T(8,128)(2,1)} %collective-permute-done.12.refs_12_.refs_0_, bf16[128,1024]{1,0:T(8,128)(2,1)} %collective-permute-done.14.refs_14_.refs_1_, bf16[128,1024]{1,0:T(8,128)(2,1)} %collective-permute-done.20.refs_13_.refs_2_, ...), custom_call_target="tpu_custom_call" | custom-call | flops 60000002048 | bytes 1000000 | tf_op jit(solution)/shard_map/project/pallas_call | solution.py:416
  115.1 1.0 collective-permute-start.34
  116.2 1.1 collective-permute-start.35
  117.2 1.4 collective-permute-done.24.refs_4_
  118.6 1.3 collective-permute-start.25
  120.1 1.0 collective-permute-start.36
  121.1 3.1 %collective-permute-done.25.refs_5_ = bf16[64,768]{1,0:T(8,128)(2,1)S(1)} collective-permute-done((bf16[64,768]{1,0:T(8,128)(2,1)S(1)}, bf16[64,768]{1,0:T(8,128)(2,1)S(1)}, u32[]{:S(2)}, u32[]{:S(2)}) %collective-permute-start.25) | collective-permute-done | bytes 98336 | tf_op jit(solution)/shard_map/ppermute | solution.py:265
  124.2 1.0 collective-permute-done.36.refs_7_
  125.4 8.8 %expert.1 = bf16[64,6144]{1,0:T(8,128)(2,1)} custom-call(s32[8]{0:T(128)S(1)} %iota_xor_fusion.order_ref, bf16[64,768]{1,0:T(8,128)(2,1)S(1)} %slot_hidden.1.refs_0_, bf16[64,768]{1,0:T(8,128)(2,1)S(1)} %collective-permute-done.34.refs_1_, bf16[64,768]{1,0:T(8,128)(2,1)S(1)} %collective-permute-done.26.refs_2_, ...), custom_call_target="tpu_custom_call" | custom-call | flops 10000000000 | bytes 1000000 | tf_op jit(solution)/shard_map/expert/pallas_call | solution.py:468
  134.2 4.3 %all-to-all-start.1 = ((bf16[8,8,6144]{2,1,0:T(8,128)(2,1)}), bf16[8,8,6144]{2,1,0:T(8,128)(2,1)S(1)}, u32[]{:S(2)}, u32[]{:S(2)}) async-start(bf16[8,8,6144]{2,1,0:T(8,128)(2,1)} %bitcast.27), calls=%async_computation.1 | async-start | bytes 1572864 | tf_op jit(solution)/shard_map/all_to_all | solution.py:480
  138.8 1.6 collective-permute-start.29
  140.5 8.6 %collective-permute-done.29 = bf16[1,256,768]{2,1,0:T(8,128)(2,1)S(1)} collective-permute-done((bf16[1,256,768]{2,1,0:T(8,128)(2,1)S(1)}, bf16[1,256,768]{2,1,0:T(8,128)(2,1)S(1)}, u32[]{:S(2)}, u32[]{:S(2)}) %collective-permute-start.29) | collective-permute-done | bytes 393248 | tf_op jit(solution)/shard_map/ppermute | solution.py:433
  149.2 1.8 %collective-permute-start.30 = (bf16[4,32,768]{2,1,0:T(8,128)(2,1)S(1)}, bf16[4,32,768]{2,1,0:T(8,128)(2,1)S(1)}, u32[]{:S(2)}, u32[]{:S(2)}) collective-permute-start(bf16[4,32,768]{2,1,0:T(8,128)(2,1)S(1)} %get-tuple-element.83), channel_id=1, source_target_pairs={{0,4},{4,0},{8,12},{12,8},{16,20},{20,16},{24,28},{28,24},{1,5},{5... | collective-permute-start | bytes 589832 | tf_op jit(solution)/shard_map/ppermute | solution.py:265
  151.2 5.3 %collective-permute-done.30 = bf16[4,32,768]{2,1,0:T(8,128)(2,1)S(1)} collective-permute-done((bf16[4,32,768]{2,1,0:T(8,128)(2,1)S(1)}, bf16[4,32,768]{2,1,0:T(8,128)(2,1)S(1)}, u32[]{:S(2)}, u32[]{:S(2)}) %collective-permute-start.30) | collective-permute-done | bytes 196640 | tf_op jit(solution)/shard_map/ppermute | solution.py:265
  156.5 2.1 %collective-permute-start.31 = (bf16[2,32,768]{2,1,0:T(8,128)(2,1)S(1)}, bf16[2,32,768]{2,1,0:T(8,128)(2,1)S(1)}, u32[]{:S(2)}, u32[]{:S(2)}) collective-permute-start(bf16[2,32,768]{2,1,0:T(8,128)(2,1)S(1)} %get-tuple-element.79), channel_id=1, source_target_pairs={{0,24},{4,28},{8,0},{12,4},{16,8},{20,12},{24,16},{28,20},{1,25},{... | collective-permute-start | bytes 294920 | tf_op jit(solution)/shard_map/ppermute | solution.py:269
  158.6 3.2 %collective-permute-start.32 = (bf16[2,32,768]{2,1,0:T(8,128)(2,1)S(1)}, bf16[2,32,768]{2,1,0:T(8,128)(2,1)S(1)}, u32[]{:S(2)}, u32[]{:S(2)}) collective-permute-start(bf16[2,32,768]{2,1,0:T(8,128)(2,1)S(1)} %get-tuple-element.81), channel_id=1, source_target_pairs={{0,16},{4,20},{8,24},{12,28},{16,0},{20,4},{24,8},{28,12},{1,17},{... | collective-permute-start | bytes 294920 | tf_op jit(solution)/shard_map/ppermute | solution.py:269
  162.6 2.5 %collective-permute-done.33 = bf16[2,32,768]{2,1,0:T(8,128)(2,1)S(1)} collective-permute-done((bf16[2,32,768]{2,1,0:T(8,128)(2,1)S(1)}, bf16[2,32,768]{2,1,0:T(8,128)(2,1)S(1)}, u32[]{:S(2)}, u32[]{:S(2)}) %collective-permute-start.33) | collective-permute-done | bytes 98336 | tf_op jit(solution)/shard_map/ppermute | solution.py:269
  165.1 1.8 %collective-permute-done.32 = bf16[2,32,768]{2,1,0:T(8,128)(2,1)S(1)} collective-permute-done((bf16[2,32,768]{2,1,0:T(8,128)(2,1)S(1)}, bf16[2,32,768]{2,1,0:T(8,128)(2,1)S(1)}, u32[]{:S(2)}, u32[]{:S(2)}) %collective-permute-start.32) | collective-permute-done | bytes 98336 | tf_op jit(solution)/shard_map/ppermute | solution.py:269
  167.7 1.8 %add_convert_fusion.1 = bf16[32,6144]{1,0:T(8,128)(2,1)} fusion(f32[32,6144]{1,0:T(8,128)S(1)} %bitcast.77, bf16[128,6144]{1,0:T(8,128)(2,1)} %param.14, s32[]{:T(128)S(6)} %select_n.241), kind=kLoop, calls=%fused_computation.10 | loop fusion | flops 589824 | bytes 1572868 | tf_op jit(solution)/shard_map/convert_element_type | solution.py:492
  (167 shorter events, 14.6 us)
Async XLA Ops:
  1.4 5.3 %copy-start.27 = (s32[128,2]{0,1:T(2,128)S(1)}, s32[128,2]{0,1:T(2,128)}, u32[]{:S(2)}) copy-start(s32[128,2]{0,1:T(2,128)} %param.23) | copy-start | bytes 3076
  1.4 5.5 %copy-start.26 = (bf16[128,6144]{1,0:T(8,128)(2,1)S(1)}, bf16[128,6144]{1,0:T(8,128)(2,1)}, u32[]{:S(2)}) copy-start(bf16[128,6144]{1,0:T(8,128)(2,1)} %param.14) | copy-start | bytes 4718596
  3.6 6.5 %collective-permute-start = (bf16[4,128,128]{2,1,0:T(8,128)(2,1)S(1)}, bf16[4,128,128]{2,1,0:T(8,128)(2,1)S(1)}, u32[]{:S(2)}, u32[]{:S(2)}) collective-permute-start(bf16[4,128,128]{2,1,0:T(8,128)(2,1)S(1)} %get-tuple-element.38), channel_id=1, source_target_pairs={{0,4},{4,0},{8,12},{12,8},{16,20},{20,16},{24,28},{28,24},{1,5},{5... | collective-permute-start | bytes 393224 | tf_op jit(solution)/shard_map/ppermute | solution.py:265
  7.2 26.6 %copy-start.21 = (bf16[128,2048]{1,0:T(8,128)(2,1)S(1)}, bf16[128,2048]{1,0:T(8,128)(2,1)}, u32[]{:S(2)}) copy-start(bf16[128,2048]{1,0:T(8,128)(2,1)} %q_ref.3) | copy-start | bytes 1572868
  7.2 26.6 %copy-start.22 = (bf16[128,2048]{1,0:T(8,128)(2,1)S(1)}, bf16[128,2048]{1,0:T(8,128)(2,1)}, u32[]{:S(2)}) copy-start(bf16[128,2048]{1,0:T(8,128)(2,1)} %k_ref.3) | copy-start | bytes 1572868
  7.2 26.6 %copy-start.23 = (bf16[128,2048]{1,0:T(8,128)(2,1)S(1)}, bf16[128,2048]{1,0:T(8,128)(2,1)}, u32[]{:S(2)}) copy-start(bf16[128,2048]{1,0:T(8,128)(2,1)} %v_ref.3) | copy-start | bytes 1572868
  7.2 26.6 %copy-start.24 = (bf16[128,2048]{1,0:T(8,128)(2,1)S(1)}, bf16[128,2048]{1,0:T(8,128)(2,1)}, u32[]{:S(2)}) copy-start(bf16[128,2048]{1,0:T(8,128)(2,1)} %gate_ref.3) | copy-start | bytes 1572868
  7.2 26.6 %copy-start.25 = (f32[2048]{0:T(1024)S(1)}, f32[2048]{0:T(1024)}, u32[]{:S(2)}) copy-start(f32[2048]{0:T(1024)} %param.20) | copy-start | bytes 24580
  10.3 6.2 %collective-permute-start.1 = (bf16[4,128,128]{2,1,0:T(8,128)(2,1)S(1)}, bf16[4,128,128]{2,1,0:T(8,128)(2,1)S(1)}, u32[]{:S(2)}, u32[]{:S(2)}) collective-permute-start(bf16[4,128,128]{2,1,0:T(8,128)(2,1)S(1)} %fusion.3), channel_id=1, source_target_pairs={{0,8},{4,12},{8,16},{12,20},{16,24},{20,28},{1,9},{5,13},{9,17},{1... | collective-permute-start | bytes 393224 | tf_op jit(solution)/shard_map/ppermute | solution.py:340
  14.9 7.1 %collective-permute-start.5 = (bf16[4,128,128]{2,1,0:T(8,128)(2,1)S(1)}, bf16[4,128,128]{2,1,0:T(8,128)(2,1)S(1)}, u32[]{:S(2)}, u32[]{:S(2)}) collective-permute-start(bf16[4,128,128]{2,1,0:T(8,128)(2,1)S(1)} %get-tuple-element.47), channel_id=1, source_target_pairs={{0,4},{4,0},{8,12},{12,8},{16,20},{20,16},{24,28},{28,24},{1,5},{5... | collective-permute-start | bytes 393224 | tf_op jit(solution)/shard_map/ppermute | solution.py:265
  16.6 9.1 %collective-permute-start.2 = (bf16[4,128,128]{2,1,0:T(8,128)(2,1)S(1)}, bf16[4,128,128]{2,1,0:T(8,128)(2,1)S(1)}, u32[]{:S(2)}, u32[]{:S(2)}) collective-permute-start(bf16[4,128,128]{2,1,0:T(8,128)(2,1)S(1)} %fusion.5), channel_id=1, source_target_pairs={{0,16},{4,20},{8,24},{12,28},{1,17},{5,21},{9,25},{13,29},{2,18},{... | collective-permute-start | bytes 393224 | tf_op jit(solution)/shard_map/ppermute | solution.py:340
  22.1 6.0 %collective-permute-start.6 = (bf16[4,128,128]{2,1,0:T(8,128)(2,1)S(1)}, bf16[4,128,128]{2,1,0:T(8,128)(2,1)S(1)}, u32[]{:S(2)}, u32[]{:S(2)}) collective-permute-start(bf16[4,128,128]{2,1,0:T(8,128)(2,1)S(1)} %fusion.8), channel_id=1, source_target_pairs={{0,8},{4,12},{8,16},{12,20},{16,24},{20,28},{1,9},{5,13},{9,17},{1... | collective-permute-start | bytes 393224 | tf_op jit(solution)/shard_map/ppermute | solution.py:340
  25.8 9.2 %collective-permute-start.3 = (bf16[4,128,128]{2,1,0:T(8,128)(2,1)S(1)}, bf16[4,128,128]{2,1,0:T(8,128)(2,1)S(1)}, u32[]{:S(2)}, u32[]{:S(2)}) collective-permute-start(bf16[4,128,128]{2,1,0:T(8,128)(2,1)S(1)} %get-tuple-element.76), channel_id=1, source_target_pairs={{0,4},{4,0},{8,12},{12,8},{16,20},{20,16},{24,28},{28,24},{1,5},{5... | collective-permute-start | bytes 393224 | tf_op jit(solution)/shard_map/ppermute | solution.py:265
  28.2 9.7 %collective-permute-start.7 = (bf16[4,128,128]{2,1,0:T(8,128)(2,1)S(1)}, bf16[4,128,128]{2,1,0:T(8,128)(2,1)S(1)}, u32[]{:S(2)}, u32[]{:S(2)}) collective-permute-start(bf16[4,128,128]{2,1,0:T(8,128)(2,1)S(1)} %fusion.10), channel_id=1, source_target_pairs={{0,16},{4,20},{8,24},{12,28},{1,17},{5,21},{9,25},{13,29},{2,18},{... | collective-permute-start | bytes 393224 | tf_op jit(solution)/shard_map/ppermute | solution.py:340
  36.0 8.3 %collective-permute-start.10 = (bf16[128,1024]{1,0:T(8,128)(2,1)S(1)}, bf16[128,1024]{1,0:T(8,128)(2,1)}, u32[]{:S(2)}, u32[]{:S(2)}) collective-permute-start(bf16[128,1024]{1,0:T(8,128)(2,1)S(1)} %mix_heads.2.refs_0_), channel_id=1, source_target_pairs={{0,8},{4,12},{8,16},{12,20},{16,24},{20,28},{24,0},{28,4},{1,9},{5... | collective-permute-start | bytes 786440 | tf_op jit(solution)/shard_map/ppermute | solution.py:269
  38.0 6.5 %collective-permute-start.8 = (bf16[4,128,128]{2,1,0:T(8,128)(2,1)S(1)}, bf16[4,128,128]{2,1,0:T(8,128)(2,1)S(1)}, u32[]{:S(2)}, u32[]{:S(2)}) collective-permute-start(bf16[4,128,128]{2,1,0:T(8,128)(2,1)S(1)} %get-tuple-element.74), channel_id=1, source_target_pairs={{0,4},{4,0},{8,12},{12,8},{16,20},{20,16},{24,28},{28,24},{1,5},{5... | collective-permute-start | bytes 393224 | tf_op jit(solution)/shard_map/ppermute | solution.py:265
  40.5 14.5 %collective-permute-start.4 = (bf16[128,1024]{1,0:T(8,128)(2,1)S(1)}, bf16[128,1024]{1,0:T(8,128)(2,1)S(1)}, u32[]{:S(2)}, u32[]{:S(2)}) collective-permute-start(bf16[128,1024]{1,0:T(8,128)(2,1)S(1)} %mix_heads.2.refs_0_), channel_id=1, source_target_pairs={{0,4},{4,0},{8,12},{12,8},{16,20},{20,16},{24,28},{28,24},{1,5},{5... | collective-permute-start | bytes 786440 | tf_op jit(solution)/shard_map/ppermute | solution.py:265
  44.3 10.7 %collective-permute-start.11 = (bf16[128,1024]{1,0:T(8,128)(2,1)}, bf16[128,1024]{1,0:T(8,128)(2,1)}, u32[]{:S(2)}, u32[]{:S(2)}) collective-permute-start(bf16[128,1024]{1,0:T(8,128)(2,1)} %collective-permute-done.10.refs_0_.refs_4_), channel_id=1, source_target_pairs={{0,8},{4,12},{8,16},{12,20},{16,24},{20,28},{24,0},{28,4},{1,9},{5... | collective-permute-start | bytes 786440 | tf_op jit(solution)/shard_map/ppermute | solution.py:269
  44.6 43.0 %copy-start = (bf16[2048,768]{1,0:T(8,128)(2,1)S(1)}, bf16[2048,768]{1,0:T(8,128)(2,1)}, u32[]{:S(2)}) copy-start(bf16[2048,768]{1,0:T(8,128)(2,1)} %refs_4_.3) | copy-start | bytes 9437188
  45.5 15.1 %collective-permute-start.16 = (bf16[128,1024]{1,0:T(8,128)(2,1)S(1)}, bf16[128,1024]{1,0:T(8,128)(2,1)}, u32[]{:S(2)}, u32[]{:S(2)}) collective-permute-start(bf16[128,1024]{1,0:T(8,128)(2,1)S(1)} %mix_heads.3.refs_2_.refs_1_), channel_id=1, source_target_pairs={{0,8},{4,12},{8,16},{12,20},{16,24},{20,28},{24,0},{28,4},{1,9},{5... | collective-permute-start | bytes 786440 | tf_op jit(solution)/shard_map/ppermute | solution.py:269
  47.1 13.5 %collective-permute-start.9 = (bf16[128,1024]{1,0:T(8,128)(2,1)S(1)}, bf16[128,1024]{1,0:T(8,128)(2,1)S(1)}, u32[]{:S(2)}, u32[]{:S(2)}) collective-permute-start(bf16[128,1024]{1,0:T(8,128)(2,1)S(1)} %mix_heads.3.refs_2_.refs_1_), channel_id=1, source_target_pairs={{0,4},{4,0},{8,12},{12,8},{16,20},{20,16},{24,28},{28,24},{1,5},{5... | collective-permute-start | bytes 786440 | tf_op jit(solution)/shard_map/ppermute | solution.py:265
  55.0 10.2 %collective-permute-start.12 = (bf16[128,1024]{1,0:T(8,128)(2,1)}, bf16[128,1024]{1,0:T(8,128)(2,1)}, u32[]{:S(2)}, u32[]{:S(2)}) collective-permute-start(bf16[128,1024]{1,0:T(8,128)(2,1)} %collective-permute-done.11.refs_0_.refs_8_), channel_id=1, source_target_pairs={{0,8},{4,12},{8,16},{12,20},{16,24},{20,28},{24,0},{28,4},{1,9},{5... | collective-permute-start | bytes 786440 | tf_op jit(solution)/shard_map/ppermute | solution.py:269
  55.7 13.5 %collective-permute-start.15 = (bf16[128,1024]{1,0:T(8,128)(2,1)}, bf16[128,1024]{1,0:T(8,128)(2,1)}, u32[]{:S(2)}, u32[]{:S(2)}) collective-permute-start(bf16[128,1024]{1,0:T(8,128)(2,1)} %collective-permute-done.10.refs_0_.refs_4_), channel_id=1, source_target_pairs={{0,4},{4,0},{8,12},{12,8},{16,20},{20,16},{24,28},{28,24},{1,5},{5... | collective-permute-start | bytes 786440 | tf_op jit(solution)/shard_map/ppermute | solution.py:265
  60.6 10.3 %collective-permute-start.18 = (bf16[128,1024]{1,0:T(8,128)(2,1)}, bf16[128,1024]{1,0:T(8,128)(2,1)}, u32[]{:S(2)}, u32[]{:S(2)}) collective-permute-start(bf16[128,1024]{1,0:T(8,128)(2,1)} %collective-permute-done.16.refs_2_.refs_5_), channel_id=1, source_target_pairs={{0,8},{4,12},{8,16},{12,20},{16,24},{20,28},{24,0},{28,4},{1,9},{5... | collective-permute-start | bytes 786440 | tf_op jit(solution)/shard_map/ppermute | solution.py:269
  61.3 11.4 %collective-permute-start.13 = (bf16[128,1024]{1,0:T(8,128)(2,1)}, bf16[128,1024]{1,0:T(8,128)(2,1)}, u32[]{:S(2)}, u32[]{:S(2)}) collective-permute-start(bf16[128,1024]{1,0:T(8,128)(2,1)} %collective-permute-done.11.refs_0_.refs_8_), channel_id=1, source_target_pairs={{0,4},{4,0},{8,12},{12,8},{16,20},{20,16},{24,28},{28,24},{1,5},{5... | collective-permute-start | bytes 786440 | tf_op jit(solution)/shard_map/ppermute | solution.py:265
  65.2 19.4 %all-to-all-start = ((bf16[8,16,768]{2,1,0:T(8,128)(2,1)}), bf16[8,16,768]{2,1,0:T(8,128)(2,1)}, u32[]{:S(2)}, u32[]{:S(2)}) async-start(bf16[8,16,768]{2,1,0:T(8,128)(2,1)} %pad_maximum_fusion.2), calls=%async_computation | async-start | bytes 393216 | tf_op jit(solution)/shard_map/all_to_all | solution.py:380
  70.9 10.0 %collective-permute-start.19 = (bf16[128,1024]{1,0:T(8,128)(2,1)}, bf16[128,1024]{1,0:T(8,128)(2,1)}, u32[]{:S(2)}, u32[]{:S(2)}) collective-permute-start(bf16[128,1024]{1,0:T(8,128)(2,1)} %collective-permute-done.18.refs_2_.refs_9_), channel_id=1, source_target_pairs={{0,4},{4,0},{8,12},{12,8},{16,20},{20,16},{24,28},{28,24},{1,5},{5... | collective-permute-start | bytes 786440 | tf_op jit(solution)/shard_map/ppermute | solution.py:265
  72.4 8.5 %collective-permute-start.20 = (bf16[128,1024]{1,0:T(8,128)(2,1)}, bf16[128,1024]{1,0:T(8,128)(2,1)}, u32[]{:S(2)}, u32[]{:S(2)}) collective-permute-start(bf16[128,1024]{1,0:T(8,128)(2,1)} %collective-permute-done.18.refs_2_.refs_9_), channel_id=1, source_target_pairs={{0,8},{4,12},{8,16},{12,20},{16,24},{20,28},{24,0},{28,4},{1,9},{5... | collective-permute-start | bytes 786440 | tf_op jit(solution)/shard_map/ppermute | solution.py:269
  72.7 11.4 %collective-permute-start.14 = (bf16[128,1024]{1,0:T(8,128)(2,1)}, bf16[128,1024]{1,0:T(8,128)(2,1)}, u32[]{:S(2)}, u32[]{:S(2)}) collective-permute-start(bf16[128,1024]{1,0:T(8,128)(2,1)} %collective-permute-done.12.refs_12_.refs_0_), channel_id=1, source_target_pairs={{0,4},{4,0},{8,12},{12,8},{16,20},{20,16},{24,28},{28,24},{1,5},{5... | collective-permute-start | bytes 786440 | tf_op jit(solution)/shard_map/ppermute | solution.py:265
  73.3 13.0 %collective-permute-start.17 = (bf16[128,1024]{1,0:T(8,128)(2,1)}, bf16[128,1024]{1,0:T(8,128)(2,1)}, u32[]{:S(2)}, u32[]{:S(2)}) collective-permute-start(bf16[128,1024]{1,0:T(8,128)(2,1)} %copy-done.7), channel_id=1, source_target_pairs={{0,8},{4,12},{8,16},{12,20},{16,24},{20,28},{24,0},{28,4},{1,9},{5... | collective-permute-start | bytes 786440 | tf_op jit(solution)/shard_map/ppermute | solution.py:269
  80.9 6.7 %collective-permute-start.21 = (bf16[128,1024]{1,0:T(8,128)(2,1)}, bf16[128,1024]{1,0:T(8,128)(2,1)}, u32[]{:S(2)}, u32[]{:S(2)}) collective-permute-start(bf16[128,1024]{1,0:T(8,128)(2,1)} %collective-permute-done.20.refs_13_.refs_2_), channel_id=1, source_target_pairs={{0,4},{4,0},{8,12},{12,8},{16,20},{20,16},{24,28},{28,24},{1,5},{5... | collective-permute-start | bytes 786440 | tf_op jit(solution)/shard_map/ppermute | solution.py:265
  94.0 5.9 %collective-permute-start.22 = (bf16[2,64,768]{2,1,0:T(8,128)(2,1)S(1)}, bf16[2,64,768]{2,1,0:T(8,128)(2,1)S(1)}, u32[]{:S(2)}, u32[]{:S(2)}) collective-permute-start(bf16[2,64,768]{2,1,0:T(8,128)(2,1)S(1)} %get-tuple-element.70), channel_id=1, source_target_pairs={{0,1},{1,0},{2,3},{3,2},{4,5},{5,4},{6,7},{7,6},{8,9},{9,8},{10,11... | collective-permute-start | bytes 589832 | tf_op jit(solution)/shard_map/ppermute | solution.py:427
  100.0 5.3 %collective-permute-start.23 = (bf16[1,64,768]{2,1,0:T(8,128)(2,1)S(1)}, bf16[1,64,768]{2,1,0:T(8,128)(2,1)S(1)}, u32[]{:S(2)}, u32[]{:S(2)}) collective-permute-start(bf16[1,64,768]{2,1,0:T(8,128)(2,1)S(1)} %get-tuple-element.84), channel_id=1, source_target_pairs={{0,2},{1,3},{2,0},{3,1},{4,6},{5,7},{6,4},{7,5},{8,10},{9,11},{10,... | collective-permute-start | bytes 294920 | tf_op jit(solution)/shard_map/ppermute | solution.py:433
  105.8 5.5 %collective-permute-start.26 = (bf16[64,768]{1,0:T(8,128)(2,1)S(1)}, bf16[64,768]{1,0:T(8,128)(2,1)S(1)}, u32[]{:S(2)}, u32[]{:S(2)}) collective-permute-start(bf16[64,768]{1,0:T(8,128)(2,1)S(1)} %slot_hidden.1.refs_0_), channel_id=1, source_target_pairs={{0,8},{4,12},{8,0},{12,4},{16,24},{20,28},{24,16},{28,20},{1,9},{5... | collective-permute-start | bytes 294920 | tf_op jit(solution)/shard_map/ppermute | solution.py:452
  106.8 18.4 %slice-start = ((s8[14155776]{0:T(1024)(128)(4,1)}), s8[4194304]{0:T(1024)(128)(4,1)S(1)}, s32[]{:S(2)}) async-start(s8[14155776]{0:T(1024)(128)(4,1)} %bitcast.67), calls=%async_computation.2 | async-start | bytes 8388608
  106.9 18.4 %slice-start.4 = ((s8[14155776]{0:T(1024)(128)(4,1)}), s8[4194304]{0:T(1024)(128)(4,1)S(1)}, s32[]{:S(2)}) async-start(s8[14155776]{0:T(1024)(128)(4,1)} %bitcast.69), calls=%async_computation.6 | async-start | bytes 8388608
  106.9 18.4 %slice-start.8 = ((s8[14155776]{0:T(1024)(128)(4,1)}), s8[4194304]{0:T(1024)(128)(4,1)S(1)}, s32[]{:S(2)}) async-start(s8[14155776]{0:T(1024)(128)(4,1)} %bitcast.71), calls=%async_computation.10 | async-start | bytes 8388608
  108.6 16.7 %slice-start.1 = ((s8[14155776]{0:T(1024)(128)(4,1)}), s8[4194304]{0:T(1024)(128)(4,1)S(1)}, s32[]{:S(2)}) async-start(s8[14155776]{0:T(1024)(128)(4,1)} %bitcast.67), calls=%async_computation.3 | async-start | bytes 8388608
  108.6 16.7 %slice-start.2 = ((s8[14155776]{0:T(1024)(128)(4,1)}), s8[4194304]{0:T(1024)(128)(4,1)S(1)}, s32[]{:S(2)}) async-start(s8[14155776]{0:T(1024)(128)(4,1)} %bitcast.67), calls=%async_computation.4 | async-start | bytes 8388608
  108.6 16.7 %slice-start.3 = ((s8[14155776]{0:T(1024)(128)(4,1)}), s8[1572864]{0:T(1024)(128)(4,1)S(1)}, s32[]{:S(2)}) async-start(s8[14155776]{0:T(1024)(128)(4,1)} %bitcast.67), calls=%async_computation.5 | async-start | bytes 3145728
  108.6 16.7 %slice-start.5 = ((s8[14155776]{0:T(1024)(128)(4,1)}), s8[4194304]{0:T(1024)(128)(4,1)S(1)}, s32[]{:S(2)}) async-start(s8[14155776]{0:T(1024)(128)(4,1)} %bitcast.69), calls=%async_computation.7 | async-start | bytes 8388608
  108.6 16.7 %slice-start.6 = ((s8[14155776]{0:T(1024)(128)(4,1)}), s8[4194304]{0:T(1024)(128)(4,1)S(1)}, s32[]{:S(2)}) async-start(s8[14155776]{0:T(1024)(128)(4,1)} %bitcast.69), calls=%async_computation.8 | async-start | bytes 8388608
  108.6 16.7 %slice-start.7 = ((s8[14155776]{0:T(1024)(128)(4,1)}), s8[1572864]{0:T(1024)(128)(4,1)S(1)}, s32[]{:S(2)}) async-start(s8[14155776]{0:T(1024)(128)(4,1)} %bitcast.69), calls=%async_computation.9 | async-start | bytes 3145728
  108.6 16.7 %slice-start.9 = ((s8[14155776]{0:T(1024)(128)(4,1)}), s8[4194304]{0:T(1024)(128)(4,1)S(1)}, s32[]{:S(2)}) async-start(s8[14155776]{0:T(1024)(128)(4,1)} %bitcast.71), calls=%async_computation.11 | async-start | bytes 8388608
  108.6 16.7 %slice-start.10 = ((s8[14155776]{0:T(1024)(128)(4,1)}), s8[4194304]{0:T(1024)(128)(4,1)S(1)}, s32[]{:S(2)}) async-start(s8[14155776]{0:T(1024)(128)(4,1)} %bitcast.71), calls=%async_computation.12 | async-start | bytes 8388608
  108.6 16.7 %slice-start.11 = ((s8[14155776]{0:T(1024)(128)(4,1)}), s8[1572864]{0:T(1024)(128)(4,1)S(1)}, s32[]{:S(2)}) async-start(s8[14155776]{0:T(1024)(128)(4,1)} %bitcast.71), calls=%async_computation.13 | async-start | bytes 3145728
  108.6 10.0 %collective-permute-start.24 = (bf16[64,768]{1,0:T(8,128)(2,1)S(1)}, bf16[64,768]{1,0:T(8,128)(2,1)S(1)}, u32[]{:S(2)}, u32[]{:S(2)}) collective-permute-start(bf16[64,768]{1,0:T(8,128)(2,1)S(1)} %slot_hidden.1.refs_0_), channel_id=1, source_target_pairs={{0,16},{4,20},{8,24},{12,28},{16,0},{20,4},{24,8},{28,12},{1,17},{... | collective-permute-start | bytes 294920 | tf_op jit(solution)/shard_map/ppermute | solution.py:452
  111.3 8.8 %collective-permute-start.27 = (bf16[64,768]{1,0:T(8,128)(2,1)S(1)}, bf16[64,768]{1,0:T(8,128)(2,1)S(1)}, u32[]{:S(2)}, u32[]{:S(2)}) collective-permute-start(bf16[64,768]{1,0:T(8,128)(2,1)S(1)} %collective-permute-done.26.refs_2_), channel_id=1, source_target_pairs={{0,16},{4,20},{8,24},{12,28},{16,0},{20,4},{24,8},{28,12},{1,17},{... | collective-permute-start | bytes 294920 | tf_op jit(solution)/shard_map/ppermute | solution.py:452
  115.1 19.1 %copy-start.16 = (bf16[2,64,768]{2,1,0:T(8,128)(2,1)}, bf16[2,64,768]{2,1,0:T(8,128)(2,1)S(1)}, u32[]{:S(2)}) copy-start(bf16[2,64,768]{2,1,0:T(8,128)(2,1)S(1)} %get-tuple-element.65) | copy-start | bytes 589828
  115.1 10.2 %copy-start.18 = (f32[6144]{0:T(1024)S(1)}, f32[6144]{0:T(1024)}, u32[]{:S(2)}) copy-start(f32[6144]{0:T(1024)} %param.22) | copy-start | bytes 73732
  115.1 9.1 %collective-permute-start.34 = (bf16[64,768]{1,0:T(8,128)(2,1)S(1)}, bf16[64,768]{1,0:T(8,128)(2,1)S(1)}, u32[]{:S(2)}, u32[]{:S(2)}) collective-permute-start(bf16[64,768]{1,0:T(8,128)(2,1)S(1)} %slot_hidden.1.refs_0_), channel_id=1, source_target_pairs={{0,4},{4,0},{8,12},{12,8},{16,20},{20,16},{24,28},{28,24},{1,5},{5... | collective-permute-start | bytes 294920 | tf_op jit(solution)/shard_map/ppermute | solution.py:265
  116.2 8.1 %collective-permute-start.35 = (bf16[64,768]{1,0:T(8,128)(2,1)S(1)}, bf16[64,768]{1,0:T(8,128)(2,1)S(1)}, u32[]{:S(2)}, u32[]{:S(2)}) collective-permute-start(bf16[64,768]{1,0:T(8,128)(2,1)S(1)} %collective-permute-done.26.refs_2_), channel_id=1, source_target_pairs={{0,4},{4,0},{8,12},{12,8},{16,20},{20,16},{24,28},{28,24},{1,5},{5... | collective-permute-start | bytes 294920 | tf_op jit(solution)/shard_map/ppermute | solution.py:265
  118.6 5.6 %collective-permute-start.25 = (bf16[64,768]{1,0:T(8,128)(2,1)S(1)}, bf16[64,768]{1,0:T(8,128)(2,1)S(1)}, u32[]{:S(2)}, u32[]{:S(2)}) collective-permute-start(bf16[64,768]{1,0:T(8,128)(2,1)S(1)} %collective-permute-done.24.refs_4_), channel_id=1, source_target_pairs={{0,4},{4,0},{8,12},{12,8},{16,20},{20,16},{24,28},{28,24},{1,5},{5... | collective-permute-start | bytes 294920 | tf_op jit(solution)/shard_map/ppermute | solution.py:265
  120.1 5.2 %collective-permute-start.36 = (bf16[64,768]{1,0:T(8,128)(2,1)S(1)}, bf16[64,768]{1,0:T(8,128)(2,1)S(1)}, u32[]{:S(2)}, u32[]{:S(2)}) collective-permute-start(bf16[64,768]{1,0:T(8,128)(2,1)S(1)} %collective-permute-done.27.refs_6_), channel_id=1, source_target_pairs={{0,4},{4,0},{8,12},{12,8},{16,20},{20,16},{24,28},{28,24},{1,5},{5... | collective-permute-start | bytes 294920 | tf_op jit(solution)/shard_map/ppermute | solution.py:265
  124.2 14.3 %collective-permute-start.28 = (bf16[2,256,768]{2,1,0:T(8,128)(2,1)S(1)}, bf16[2,256,768]{2,1,0:T(8,128)(2,1)S(1)}, u32[]{:S(2)}, u32[]{:S(2)}) collective-permute-start(bf16[2,256,768]{2,1,0:T(8,128)(2,1)S(1)} %pad_maximum_fusion), channel_id=1, source_target_pairs={{0,1},{1,0},{2,3},{3,2},{4,5},{5,4},{6,7},{7,6},{8,9},{9,8},{10,11... | collective-permute-start | bytes 2359304 | tf_op jit(solution)/shard_map/ppermute | solution.py:427
  134.2 4.3 %copy-start.13 = (bf16[2,64,768]{2,1,0:T(8,128)(2,1)S(1)}, bf16[2,64,768]{2,1,0:T(8,128)(2,1)}, u32[]{:S(2)}) copy-start(bf16[2,64,768]{2,1,0:T(8,128)(2,1)} %copy-done.12) | copy-start | bytes 589828
  134.2 4.3 %copy-start.15 = (bf16[2,64,768]{2,1,0:T(8,128)(2,1)S(1)}, bf16[2,64,768]{2,1,0:T(8,128)(2,1)}, u32[]{:S(2)}) copy-start(bf16[2,64,768]{2,1,0:T(8,128)(2,1)} %copy-done.14) | copy-start | bytes 589828
  134.2 4.3 %copy-start.17 = (bf16[2,64,768]{2,1,0:T(8,128)(2,1)S(1)}, bf16[2,64,768]{2,1,0:T(8,128)(2,1)}, u32[]{:S(2)}) copy-start(bf16[2,64,768]{2,1,0:T(8,128)(2,1)} %copy-done.16) | copy-start | bytes 589828
  134.2 27.6 %all-to-all-start.1 = ((bf16[8,8,6144]{2,1,0:T(8,128)(2,1)}), bf16[8,8,6144]{2,1,0:T(8,128)(2,1)S(1)}, u32[]{:S(2)}, u32[]{:S(2)}) async-start(bf16[8,8,6144]{2,1,0:T(8,128)(2,1)} %bitcast.27), calls=%async_computation.1 | async-start | bytes 1572864 | tf_op jit(solution)/shard_map/all_to_all | solution.py:480
  138.8 10.3 %collective-permute-start.29 = (bf16[1,256,768]{2,1,0:T(8,128)(2,1)S(1)}, bf16[1,256,768]{2,1,0:T(8,128)(2,1)S(1)}, u32[]{:S(2)}, u32[]{:S(2)}) collective-permute-start(bf16[1,256,768]{2,1,0:T(8,128)(2,1)S(1)} %get-tuple-element.73), channel_id=1, source_target_pairs={{0,2},{1,3},{2,0},{3,1},{4,6},{5,7},{6,4},{7,5},{8,10},{9,11},{10,... | collective-permute-start | bytes 1179656 | tf_op jit(solution)/shard_map/ppermute | solution.py:433
  149.2 7.2 %collective-permute-start.30 = (bf16[4,32,768]{2,1,0:T(8,128)(2,1)S(1)}, bf16[4,32,768]{2,1,0:T(8,128)(2,1)S(1)}, u32[]{:S(2)}, u32[]{:S(2)}) collective-permute-start(bf16[4,32,768]{2,1,0:T(8,128)(2,1)S(1)} %get-tuple-element.83), channel_id=1, source_target_pairs={{0,4},{4,0},{8,12},{12,8},{16,20},{20,16},{24,28},{28,24},{1,5},{5... | collective-permute-start | bytes 589832 | tf_op jit(solution)/shard_map/ppermute | solution.py:265
  156.5 6.2 %collective-permute-start.31 = (bf16[2,32,768]{2,1,0:T(8,128)(2,1)S(1)}, bf16[2,32,768]{2,1,0:T(8,128)(2,1)S(1)}, u32[]{:S(2)}, u32[]{:S(2)}) collective-permute-start(bf16[2,32,768]{2,1,0:T(8,128)(2,1)S(1)} %get-tuple-element.79), channel_id=1, source_target_pairs={{0,24},{4,28},{8,0},{12,4},{16,8},{20,12},{24,16},{28,20},{1,25},{... | collective-permute-start | bytes 294920 | tf_op jit(solution)/shard_map/ppermute | solution.py:269
  158.6 6.5 %collective-permute-start.33 = (bf16[2,32,768]{2,1,0:T(8,128)(2,1)S(1)}, bf16[2,32,768]{2,1,0:T(8,128)(2,1)S(1)}, u32[]{:S(2)}, u32[]{:S(2)}) collective-permute-start(bf16[2,32,768]{2,1,0:T(8,128)(2,1)S(1)} %get-tuple-element.80), channel_id=1, source_target_pairs={{0,8},{4,12},{8,16},{12,20},{16,24},{20,28},{24,0},{28,4},{1,9},{5... | collective-permute-start | bytes 294920 | tf_op jit(solution)/shard_map/ppermute | solution.py:269
  158.6 8.3 %collective-permute-start.32 = (bf16[2,32,768]{2,1,0:T(8,128)(2,1)S(1)}, bf16[2,32,768]{2,1,0:T(8,128)(2,1)S(1)}, u32[]{:S(2)}, u32[]{:S(2)}) collective-permute-start(bf16[2,32,768]{2,1,0:T(8,128)(2,1)S(1)} %get-tuple-element.81), channel_id=1, source_target_pairs={{0,16},{4,20},{8,24},{12,28},{16,0},{20,4},{24,8},{28,12},{1,17},{... | collective-permute-start | bytes 294920 | tf_op jit(solution)/shard_map/ppermute | solution.py:269
  (16 other events, 22.4 us)
